TPU v7x, 32 devices: a whole 2x2x4 slice. The times are simulated.
32 devices in a mesh: parts: 2 (over x), tensor: 16 (over z, y, core).
Axes of the slice: x: 2, y: 2, z: 4, core: 2. Of those that a mesh axis runs over, the one named last changes fastest.
Arguments:
- hidden: bfloat16 [320, 8192], P('parts'), parts along dimension 0, may hold values from -6 to 6
- key_value_weight: bfloat16 [2048, 8192], P('tensor'), may hold values from -0.0625 to 0.0625
- adapter_down_weight: bfloat16 [8192, 16, 128], P('tensor'), may hold values from -0.0625 to 0.0625
- adapter_up_weight: bfloat16 [2048, 16, 64], P('tensor'), may hold values from -0.75 to 0.75
- tenant: int32 [32], P('parts'), parts along dimension 0, may hold values from 0 to 7
- tenant_page_table: int32 [8], replicated, may hold values from 0 to 15, as said below
- request_block_count: int32 [32], P('parts'), parts along dimension 0, may hold values from 1 to 2, 20 in all
- last_block_tokens: int32 [32], P('parts'), parts along dimension 0, may hold values from 1 to 8
- placement: int32 [32], P('parts'), parts along dimension 0, may hold values from 0 to 31, as said below
- key_value_cache: bfloat16 [64, 128, 2048], P(('parts', 'tensor')), parts along dimension 0, may hold values from -4 to 4
- context_length: int32 [64], P(('parts', 'tensor')), parts along dimension 0, may hold values from 2 to 128
- decode_step_query: bfloat16 [4, 64, 8192], P(None, ('parts', 'tensor')), parts along dimension 1, may hold values from -40 to 40
- step_key_value: bfloat16 [4, 64, 2048], P(None, ('parts', 'tensor')), parts along dimension 1, may hold values from -6 to 6
Outputs:
- attended: bfloat16 [4, 64, 8192], P(None, ('parts', 'tensor')), parts along dimension 1
There are 2 independent parts, one for each index of `parts`. A program takes and returns all parts, laid end to end along the dimension named above; an argument that names none is the same for every part. Nothing has to cross between parts.
Inputs may be any that keep to these rules, and one draw needn't show every extreme that they name: `tenant_page_table`: different tenants have different pages. `request_block_count`: the counts sum to 20; each request's blocks follow those of the request before it. Requests go to different devices: placement // 2 differs between requests.
All inputs are finite; a program needn't handle non-finite values.
Results may differ from a plain program's by a relative error of at most 0.0051.
Values may be sent and summed in bfloat16 or wider, within the bound.
No kernel may reach another device: no remote copies, remote signals or barrier semaphores. Data moves between devices by JAX's collectives and lax.ppermute only.
A program may use at most 128 MiB of HBM per device.

v0:
```python
import jax
import jax.numpy as jnp
from jax import lax
from jax.sharding import PartitionSpec as P

HEADS = 64
KVH = 8
HD = 128
BLK = 8
MOSTB = 2


ADAPTER_SCALE = 0.5
NEG_LARGE = -1e30


def select_tenant(products, tenant_hot):
    tokens, tenant_index = tenant_hot.shape
    shaped = products.reshape(tokens, tenant_index, -1)
    return jnp.sum(jnp.where(tenant_hot[:, :, None], shaped, jnp.zeros((), jnp.float32)), axis=1)


def body(
    hidden,
    key_value_weight,
    adapter_down_weight,
    adapter_up_weight,
    tenant,
    tenant_page_table,
    request_block_count,
    last_block_tokens,
    placement,
    key_value_cache,
    context_length,
    decode_step_query,
    step_key_value,
):
    tokens = hidden.shape[0]
    key_value_rows = key_value_weight.shape[0]
    my_index = lax.axis_index("tensor")
    devices = lax.axis_size("tensor")
    requests = tenant.shape[0]
    tenant_index = tenant_page_table.shape[0]
    adapter_rank_size = adapter_up_weight.shape[2]
    device_local_rows = adapter_down_weight.shape[0]
    dec_rows, ctx, kv_width = key_value_cache.shape
    half_width = kv_width // 2
    steps = step_key_value.shape[0]
    capacity = MOSTB * BLK
    req_end = jnp.cumsum(request_block_count)
    req_start = req_end - request_block_count
    block_of = jnp.arange(tokens, dtype=jnp.int32) // BLK
    owner_request = jnp.sum((req_end[None, :] <= block_of[:, None]).astype(jnp.int32), axis=1)
    owner_hot = owner_request[:, None] == jnp.arange(requests, dtype=jnp.int32)[None, :]
    tok_tenant = jnp.sum(jnp.where(owner_hot, tenant[None, :], 0), axis=1)
    tenant_hot = tok_tenant[:, None] == jnp.arange(tenant_index, dtype=jnp.int32)[None, :]
    selected_down_maps = jnp.take(adapter_down_weight, tenant_page_table, axis=1).reshape(
        device_local_rows, -1
    )
    products = jnp.dot(
        hidden,
        lax.all_gather(selected_down_maps, "tensor", axis=0, tiled=True),
        preferred_element_type=jnp.float32,
    )
    shrunk = select_tenant(products, tenant_hot)
    shrunk = shrunk.astype(jnp.bfloat16)
    upper_half = my_index * key_value_rows >= half_width
    shrunk_half = jnp.where(
        upper_half, shrunk[:, adapter_rank_size:], shrunk[:, :adapter_rank_size]
    )
    masked_result = jnp.where(
        tenant_hot[:, :, None], shrunk_half[:, None, :], jnp.zeros((), jnp.bfloat16)
    ).reshape(tokens, tenant_index * adapter_rank_size)
    selected_up_maps = jnp.take(adapter_up_weight, tenant_page_table, axis=1).reshape(
        key_value_rows, tenant_index * adapter_rank_size
    )
    contract_product = (((1,), (1,)), ((), ()))
    base_key_value = lax.dot_general(
        key_value_weight, hidden, contract_product, preferred_element_type=jnp.float32
    )
    adapter_output_delta = lax.dot_general(
        selected_up_maps, masked_result, contract_product, preferred_element_type=jnp.float32
    )
    prefill_key_value = (base_key_value + ADAPTER_SCALE * adapter_output_delta).astype(jnp.bfloat16)
    new_lengths = (request_block_count - 1) * BLK + last_block_tokens
    start_tokens = req_start * BLK
    dest_device = placement // dec_rows
    offsets = jnp.arange(capacity, dtype=jnp.int32)
    my_hit = dest_device == my_index
    my_length = jnp.sum(jnp.where(my_hit, new_lengths, 0))
    my_slot = jnp.sum(jnp.where(my_hit, placement % dec_rows, 0))
    device_hit = dest_device[None, :] == jnp.arange(devices, dtype=jnp.int32)[:, None]
    device_start = jnp.sum(jnp.where(device_hit, start_tokens[None, :], 0), axis=1)
    token_index = jnp.clip(device_start[:, None] + offsets[None, :], 0, tokens - 1).reshape(-1)
    outgoing = jnp.take(prefill_key_value, token_index, axis=1)
    received = lax.all_to_all(outgoing, "tensor", split_axis=1, concat_axis=0, tiled=True)
    cache_keys = key_value_cache[:, :, :half_width].reshape(dec_rows, ctx, KVH, HD)
    cache_values = key_value_cache[:, :, half_width:].reshape(dec_rows, ctx, KVH, HD)
    new_keys = received[:half_width].reshape(KVH, HD, capacity)
    new_values = received[half_width:].reshape(KVH, HD, capacity)
    step_keys = step_key_value[:, :, :half_width].reshape(steps, dec_rows, KVH, HD)
    step_values = step_key_value[:, :, half_width:].reshape(steps, dec_rows, KVH, HD)
    cache_ok = jnp.arange(ctx, dtype=jnp.int32)[None, :] < context_length[:, None]
    new_ok = (jnp.arange(dec_rows, dtype=jnp.int32)[:, None] == my_slot) & (
        offsets[None, :] < my_length
    )
    outputs = []
    for step in range(steps):
        step_ok = jnp.broadcast_to(
            jnp.arange(steps, dtype=jnp.int32)[None, :] <= step, (dec_rows, steps)
        )
        allowed = jnp.concatenate([cache_ok, new_ok, step_ok], axis=1)[:, None, None, :]
        queries = decode_step_query[step].reshape(dec_rows, KVH, HEADS // KVH, HD)
        scores = jnp.concatenate(
            [
                jnp.einsum(
                    "rkgd,rckd->rkgc", queries, cache_keys, preferred_element_type=jnp.float32
                ),
                jnp.einsum("rkgd,kdj->rkgj", queries, new_keys, preferred_element_type=jnp.float32),
                jnp.einsum(
                    "rkgd,srkd->rkgs", queries, step_keys, preferred_element_type=jnp.float32
                ),
            ],
            axis=3,
        ) * HD ** (-0.5)
        scores = jnp.where(allowed, scores, NEG_LARGE)
        highest = jnp.max(scores, axis=3, keepdims=True)
        weights = jnp.exp(scores - highest)
        denominator = jnp.sum(weights, axis=3)
        soft_weights = weights.astype(jnp.bfloat16)
        combined = jnp.einsum(
            "rkgc,rckd->rkgd",
            soft_weights[..., :ctx],
            cache_values,
            preferred_element_type=jnp.float32,
        )
        combined = combined + jnp.einsum(
            "rkgj,kdj->rkgd",
            soft_weights[..., ctx : ctx + capacity],
            new_values,
            preferred_element_type=jnp.float32,
        )
        combined = combined + jnp.einsum(
            "rkgs,srkd->rkgd",
            soft_weights[..., ctx + capacity :],
            step_values,
            preferred_element_type=jnp.float32,
        )
        outputs.append(
            (combined / denominator[..., None]).reshape(dec_rows, HEADS * HD).astype(jnp.bfloat16)
        )
    return jnp.stack(outputs, axis=0)


def solution(mesh):
    return jax.shard_map(
        body,
        mesh=mesh,
        in_specs=(
            P("parts", None),
            P("tensor", None),
            P("tensor", None, None),
            P("tensor", None, None),
            P("parts"),
            P(),
            P("parts"),
            P("parts"),
            P("parts"),
            P(("parts", "tensor"), None, None),
            P(("parts", "tensor")),
            P(None, ("parts", "tensor"), None),
            P(None, ("parts", "tensor"), None),
        ),
        out_specs=P(None, ("parts", "tensor"), None),
        check_vma=False,
    )
```

profile of v0, /device:TPU:0, one launch (start us, length us, event | category | flops | bytes accessed | tf_op | source)
XLA Modules:
  0.0 188.9 jit_solution(12131286958044924257)
XLA Ops:
  6.5 0.8 compare_select_fusion.2
  7.3 0.7 compare_and_fusion.1
  8.0 0.5 copy-done.18
  8.6 4.6 %gather_fusion.1 = bf16[8,512,128]{2,0,1:T(8,128)(2,1)} fusion(bf16[512,16,128]{2,1,0:T(8,128)(2,1)} %param.15, s32[1024]{0:T(1024)S(1)} %pad_clamp_fusion.1), kind=kCustom, calls=%fused_computation.1 | custom fusion | bytes 2097184 | tf_op jit(solution)/shard_map/jit(_take)/gather | solution.py:57
  13.2 2.4 %bitcast_select_fusion = bf16[512,1024]{1,0:T(8,128)(2,1)} fusion(bf16[64,8,8,128]{3,2,1,0:T(8,128)(2,1)} %bitcast.136, pred[1024]{0:T(1024)(128)(4,1)S(1)} %broadcast_bitcast_fusion), kind=kLoop, calls=%fused_computation.44 | loop fusion | flops 524288 | bytes 2098176 | tf_op jit(solution)/shard_map/jit(_take)/select_n | solution.py:57
  15.8 0.1 reduce
  15.9 0.7 fusion.108
  16.6 0.1 select_reduce_fusion.1
  16.9 0.1 convert_reduce_fusion
  17.1 0.1 iota_compare_fusion
  17.2 0.7 copy.116
  17.9 0.6 gather_fusion
  18.5 0.6 pad.15.clone
  19.1 0.6 pad.21.clone
  19.7 0.6 pad.27.clone
  20.2 0.6 pad.9.clone
  20.9 2.1 %fusion.119 = (bf16[2,128,1024]{2,1,0:T(8,128)(2,1)S(1)}, bf16[2,128,1024]{2,1,0:T(8,128)(2,1)}) fusion(bf16[2,128,2048]{2,1,0:T(8,128)(2,1)} %param.22), kind=kLoop, calls=%fused_computation.188 | loop fusion | bytes 2097152 | tf_op jit(solution)/shard_map/slice | solution.py:97
  23.0 1.0 copy.158
  24.1 1.3 copy.159
  25.4 0.6 reshape.243
  26.0 0.8 iota_compare_fusion.8
  26.8 0.7 iota_compare_fusion.9
  27.5 0.6 iota_compare_fusion.3
  28.1 0.6 broadcast_and_fusion
  28.8 0.9 slice_bitcast_fusion.5
  29.7 0.8 fusion.62
  30.5 0.8 fusion.57
  31.2 0.8 fusion.52
  32.0 0.8 fusion.47
  32.8 1.9 %fusion.65 = f32[2,8,8,128]{3,2,1,0:T(8,128)} fusion(bf16[2,128,8,128]{1,3,2,0:T(8,128)(2,1)} %bitcast.132, bf16[1,2,64,128]{3,1,2,0:T(2,128)(2,1)S(1)} %get-tuple-element.12), kind=kOutput, calls=%fused_computation.89 | convolution fusion | flops 4194304 | bytes 622592 | tf_op jit(solution)/shard_map/rkgd,rckd->rkgc/dot_general | solution.py:116
  34.7 1.9 %fusion.60 = f32[2,8,8,128]{3,2,1,0:T(8,128)} fusion(bf16[2,128,8,128]{1,3,2,0:T(8,128)(2,1)} %bitcast.133, bf16[1,2,64,128]{3,1,2,0:T(2,128)(2,1)S(1)} %get-tuple-element.13), kind=kOutput, calls=%fused_computation.84 | convolution fusion | flops 4194304 | bytes 622592 | tf_op jit(solution)/shard_map/rkgd,rckd->rkgc/dot_general | solution.py:116
  36.6 1.9 %fusion.55 = f32[2,8,8,128]{3,2,1,0:T(8,128)} fusion(bf16[2,128,8,128]{1,3,2,0:T(8,128)(2,1)} %bitcast.134, bf16[1,2,64,128]{3,1,2,0:T(2,128)(2,1)S(1)} %get-tuple-element.15), kind=kOutput, calls=%fused_computation.79 | convolution fusion | flops 4194304 | bytes 622592 | tf_op jit(solution)/shard_map/rkgd,rckd->rkgc/dot_general | solution.py:116
  38.5 0.2 fusion.50
  38.7 106.7 %all-gather.2.cloned.1.call-done = bf16[8192,1024]{1,0:T(8,128)(2,1)} async-done(((bf16[512,1024]{1,0:T(8,128)(2,1)}), bf16[8192,1024]{1,0:T(8,128)(2,1)}) %all-gather.2.cloned.1.call-update) | async-done | bytes 16777232 | tf_op jit(solution)/shard_map/all_gather | solution.py:62
  145.4 7.3 %convolution_bitcast_fusion = f32[20,8,8,128]{3,1,2,0:T(8,128)S(1)} fusion(bf16[160,8192]{1,0:T(8,128)(2,1)S(1)} %copy-done, bf16[8192,1024]{1,0:T(8,128)(2,1)} %all-gather.2.cloned.1.call-done), kind=kOutput, calls=%fused_computation.7 | convolution fusion | flops 2684354560 | bytes 20054016 | tf_op jit(solution)/shard_map/dot_general | solution.py:60
  152.7 0.1 copy.162
  152.8 0.3 fusion.26
  153.3 0.9 fusion.12
  154.3 2.4 %fusion.21 = bf16[128,160]{0,1:T(8,128)(2,1)S(1)} fusion(f32[128,160]{0,1:T(8,128)S(1)} %fusion.12, bf16[128,8192]{1,0:T(8,128)(2,1)} %param.14, bf16[160,8192]{1,0:T(8,128)(2,1)S(1)} %copy-done), kind=kOutput, calls=%fused_computation.39 | convolution fusion | flops 335585280 | bytes 4841472 | tf_op jit(solution)/shard_map/dot_general | solution.py:78
  156.8 0.9 gather_fusion.2
  157.6 0.7 broadcast_select_fusion
  158.4 3.5 %all-to-all-start = ((bf16[128,16,16]{0,2,1:T(8,128)(2,1)}), bf16[128,16,16]{0,2,1:T(8,128)(2,1)S(1)}, u32[]{:S(2)}, u32[]{:S(2)}) async-start(bf16[128,16,16]{0,2,1:T(8,128)(2,1)} %broadcast_select_fusion), calls=%async_computation | async-start | bytes 131072 | tf_op jit(solution)/shard_map/all_to_all | solution.py:96
  161.9 6.8 %all-to-all-done = bf16[128,16,16]{0,2,1:T(8,128)(2,1)S(1)} async-done(((bf16[128,16,16]{0,2,1:T(8,128)(2,1)}), bf16[128,16,16]{0,2,1:T(8,128)(2,1)S(1)}, u32[]{:S(2)}, u32[]{:S(2)}) %all-to-all-start) | async-done | bytes 65568 | tf_op jit(solution)/shard_map/all_to_all | solution.py:96
  168.7 0.1 convolution_bitcast_fusion.9
  168.8 0.8 convolution_bitcast_fusion.7
  169.6 0.7 convolution_bitcast_fusion.5
  170.4 0.7 convolution_bitcast_fusion.3
  171.1 1.2 fusion.120
  172.3 0.4 fusion.81
  172.7 0.1 fusion.20
  172.8 0.2 fusion.22
  173.1 1.2 fusion.121
  174.3 0.4 fusion.77
  174.7 0.1 fusion.18
  174.8 0.9 fusion.23
  175.8 1.2 fusion.122
  177.0 0.4 fusion.73
  177.4 0.1 fusion.16
  177.5 0.9 fusion.24
  178.5 1.2 fusion.123
  179.7 0.4 fusion.69
  180.0 0.1 fusion.14
  180.2 0.9 fusion.25
  181.1 0.9 pad_maximum_fusion
  (63 shorter events, 1.0 us)
Async XLA Ops:
  6.5 138.9 %copy-start = (bf16[160,8192]{1,0:T(8,128)(2,1)S(1)}, bf16[160,8192]{1,0:T(8,128)(2,1)}, u32[]{:S(2)}) copy-start(bf16[160,8192]{1,0:T(8,128)(2,1)} %param.13) | copy-start | bytes 7864324
  6.5 138.8 %all-gather.2.cloned.1.call-start = ((), (), s32[]{:S(2)}) async-start(), calls=%async_computation.1 | async-start | bytes 17825792 | tf_op jit(solution)/shard_map/all_gather | solution.py:62
  8.0 0.5 copy-start.18
  13.2 2.5 %copy-start.7 = (s32[16]{0:T(128)S(1)}, s32[16]{0:T(128)}, u32[]{:S(2)}) copy-start(s32[16]{0:T(128)} %param.19) | copy-start | bytes 196
  13.2 2.7 %copy-start.14 = (s32[16]{0:T(128)S(1)}, s32[16]{0:T(128)}, u32[]{:S(2)}) copy-start(s32[16]{0:T(128)} %param.21) | copy-start | bytes 196
  13.2 2.7 %copy-start.15 = (s32[16]{0:T(128)S(1)}, s32[16]{0:T(128)}, u32[]{:S(2)}) copy-start(s32[16]{0:T(128)} %param.20) | copy-start | bytes 196
  13.2 3.8 %copy-start.16 = (s32[16]{0:T(128)S(1)}, s32[16]{0:T(128)}, u32[]{:S(2)}) copy-start(s32[16]{0:T(128)} %param.17) | copy-start | bytes 196
  13.2 4.7 %copy-start.2 = (bf16[128,16,64]{0,2,1:T(8,128)(2,1)S(1)}, bf16[128,16,64]{0,2,1:T(8,128)(2,1)}, u32[]{:S(2)}) copy-start(bf16[128,16,64]{0,2,1:T(8,128)(2,1)} %param.16) | copy-start | bytes 786436
  15.6 8.4 %copy-start.5 = (bf16[4,2,2048]{2,1,0:T(2,128)(2,1)S(1)}, bf16[4,2,2048]{2,1,0:T(2,128)(2,1)}, u32[]{:S(2)}) copy-start(bf16[4,2,2048]{2,1,0:T(2,128)(2,1)} %param.25) | copy-start | bytes 98308
  15.6 11.8 %copy-start.17 = (s32[2]{0:T(128)S(1)}, s32[2]{0:T(128)}, u32[]{:S(2)}) copy-start(s32[2]{0:T(128)} %param.23) | copy-start | bytes 28
  26.0 12.5 %copy-start.1 = (bf16[2,128,1024]{1,2,0:T(8,128)(2,1)S(1)}, bf16[2,128,1024]{1,2,0:T(8,128)(2,1)}, u32[]{:S(2)}) copy-start(bf16[2,128,1024]{1,2,0:T(8,128)(2,1)} %copy.158) | copy-start | bytes 1572868
  154.3 7.6 %copy-start.8 = (pred[148]{0:T(512)(128)(4,1)S(1)}, pred[148]{0:T(512)(128)(4,1)}, u32[]{:S(2)}) copy-start(pred[148]{0:T(512)(128)(4,1)} %pad.15.clone) | copy-start | bytes 448
  154.3 7.6 %copy-start.9 = (pred[148]{0:T(512)(128)(4,1)S(1)}, pred[148]{0:T(512)(128)(4,1)}, u32[]{:S(2)}) copy-start(pred[148]{0:T(512)(128)(4,1)} %pad.21.clone) | copy-start | bytes 448
  154.3 7.6 %copy-start.10 = (pred[148]{0:T(512)(128)(4,1)S(1)}, pred[148]{0:T(512)(128)(4,1)}, u32[]{:S(2)}) copy-start(pred[148]{0:T(512)(128)(4,1)} %pad.27.clone) | copy-start | bytes 448
  154.3 7.6 %copy-start.11 = (pred[148]{0:T(512)(128)(4,1)S(1)}, pred[148]{0:T(512)(128)(4,1)}, u32[]{:S(2)}) copy-start(pred[148]{0:T(512)(128)(4,1)} %pad.9.clone) | copy-start | bytes 448
  154.3 7.6 %copy-start.12 = (pred[2,128]{1,0:T(4,128)(4,1)S(1)}, pred[2,128]{1,0:T(4,128)(4,1)}, u32[]{:S(2)}) copy-start(pred[2,128]{1,0:T(4,128)(4,1)} %iota_compare_fusion.3) | copy-start | bytes 772
  154.3 7.6 %copy-start.13 = (pred[2,16]{1,0:T(4,128)(4,1)S(1)}, pred[2,16]{1,0:T(4,128)(4,1)}, u32[]{:S(2)}) copy-start(pred[2,16]{1,0:T(4,128)(4,1)} %broadcast_and_fusion) | copy-start | bytes 100
  154.3 18.5 %copy-start.6 = (bf16[4,2,8,128]{3,2,1,0:T(8,128)(2,1)S(1)}, bf16[4,2,8,128]{3,2,1,0:T(8,128)(2,1)}, u32[]{:S(2)}) copy-start(bf16[4,2,8,128]{3,2,1,0:T(8,128)(2,1)} %reshape.243) | copy-start | bytes 49156
  158.4 10.4 %all-to-all-start = ((bf16[128,16,16]{0,2,1:T(8,128)(2,1)}), bf16[128,16,16]{0,2,1:T(8,128)(2,1)S(1)}, u32[]{:S(2)}, u32[]{:S(2)}) async-start(bf16[128,16,16]{0,2,1:T(8,128)(2,1)} %broadcast_select_fusion), calls=%async_computation | async-start | bytes 131072 | tf_op jit(solution)/shard_map/all_to_all | solution.py:96
  168.8 9.6 %copy-start.3 = (f32[2,8,8,4]{3,2,1,0:T(8,128)S(1)}, f32[2,8,8,4]{3,2,1,0:T(8,128)}, u32[]{:S(2)}) copy-start(f32[2,8,8,4]{3,2,1,0:T(8,128)} %fusion.47) | copy-start | bytes 6148
  170.3 5.4 %copy-start.4 = (f32[2,8,8,16]{3,2,1,0:T(8,128)S(1)}, f32[2,8,8,16]{3,2,1,0:T(8,128)}, u32[]{:S(2)}) copy-start(f32[2,8,8,16]{3,2,1,0:T(8,128)} %convolution_bitcast_fusion.5) | copy-start | bytes 24580
Sparse Core Ops, SparseCore 0:
  15.8 129.5 all-gather.1
where the time goes:
time: 190 us; the launch traced here: 189 us
  waiting for transfers between devices  113 us (59%)
  matrix products  27.1 us (14%)
  local copies, waits for them, and re-layouts  16.2 us (9%)
  other arithmetic  14.8 us (8%)
  between operations  13.8 us (7%)
  starting transfers between devices  3.5 us (2%)
    all_gather x1, waiting for transfers between devices, body(): lax.all_gather(selected_down_maps, 'tensor', axis=0, tiled=True)  107 us
    dot_general x1, matrix products, body(): jnp.dot(hidden, lax.all_gather(selected_down_maps, 'tensor', axis=0, tile...  7.31 us
    all_to_all x1, waiting for transfers between devices, body(): lax.all_to_all(outgoing, 'tensor', split_axis=1, concat_axis=0, tiled=True)  6.78 us
    dot_general x4, matrix products, body(): jnp.einsum('rkgd,rckd->rkgc', queries, cache_keys, preferred_element_type...  5.97 us
    sub x4, other arithmetic, body(): weights = jnp.exp(scores - highest)  4.83 us
    gather x1, local copies, waits for them, and re-layouts, body(): jnp.take(adapter_down_weight, tenant_page_table, axis=1)  4.58 us
    unnamed x42, local copies, waits for them, and re-layouts  3.94 us
  transfers between devices with their start and end apart: 2, of which 2 were waited for; matrix products, arithmetic and copies ran while one was open for 12% of the time, Pallas kernels for 0%

commit v1 on v0

v1 whole, which is shorter than its diff:
```python
import functools

import jax
import jax.numpy as jnp
from jax import lax
from jax.experimental import pallas as pl
from jax.experimental.pallas import tpu as pltpu
from jax.sharding import PartitionSpec as P

HEADS = 64
KVH = 8
HD = 128
BLK = 8
MOSTB = 2
CAPT = MOSTB * BLK
ADAPTER_SCALE = 0.5
NEG_LARGE = -1e30
VMEM_LIMIT = 60 * 1024 * 1024
WIRE = jnp.float32

SMEM_SPEC = pl.BlockSpec(memory_space=pltpu.SMEM)
VMEM_SPEC = pl.BlockSpec(memory_space=pltpu.VMEM)
ANY_SPEC = pl.BlockSpec(memory_space=pl.ANY)


def up_kernel(dec_rows, tenant, table, placement, up, out, page_of, sems):
    requests = tenant.shape[0]
    devices = out.shape[0]
    for dest in range(devices):
        page_of[dest] = 0
    for r in range(requests):
        page_of[placement[r] // dec_rows] = table[tenant[r]]
    copies = []
    for dest in range(devices):
        copy = pltpu.make_async_copy(up.at[page_of[dest]], out.at[dest], sems.at[dest])
        copy.start()
        copies.append(copy)
    for copy in copies:
        copy.wait()


def project_kernel(
    dec_rows, chunks, tenant, table, counts, placement, hidden, weight, down, out,
    h_s, w_s, d_s, mine_s, sel_s, base_s, part_s, sems,
):
    tokens, width = hidden.shape
    features = weight.shape[0]
    local, pages, rank2 = down.shape
    tenants = table.shape[0]
    requests = tenant.shape[0]
    devices = out.shape[0]
    me = lax.axis_index("tensor")
    step = width // chunks
    dstep = local // chunks

    def my_copy():
        return pltpu.make_async_copy(
            hidden.at[:, pl.ds(pl.multiple_of(me * local, 128), local)], mine_s, sems.at[0, 3]
        )

    my_copy().start()
    d_copies, h_copies, w_copies = [], [], []
    for c in range(chunks):
        d_copies.append(pltpu.make_async_copy(
            down.at[pl.ds(c * dstep, dstep)], d_s.at[pl.ds(c * dstep, dstep)], sems.at[c, 0]))
        h_copies.append(pltpu.make_async_copy(
            hidden.at[:, pl.ds(c * step, step)], h_s.at[c], sems.at[c, 1]))
        w_copies.append(pltpu.make_async_copy(
            weight.at[:, pl.ds(c * step, step)], w_s.at[c], sems.at[c, 2]))
    for c in range(chunks):
        d_copies[c].start()
    for c in range(chunks):
        h_copies[c].start()
        w_copies[c].start()

    rows = lax.broadcasted_iota(jnp.int32, (tenants * 16, 16 * pages), 0)
    cols = lax.broadcasted_iota(jnp.int32, (tenants * 16, 16 * pages), 1)
    page_of_row = jnp.zeros_like(rows)
    for k in range(tenants):
        page_of_row = jnp.where(rows // 16 == k, table[k], page_of_row)
    pick = (rows % 16 == cols // pages) & (cols % pages == page_of_row)
    pick = jnp.where(pick, jnp.float32(1), jnp.float32(0)).astype(jnp.bfloat16)

    for c in range(chunks):
        d_copies[c].wait()
        for b in range(c * dstep // 16, (c + 1) * dstep // 16):
            block = d_s[pl.ds(b * 16, 16)].reshape(16 * pages, rank2)
            chosen = jnp.dot(pick, block, preferred_element_type=jnp.float32)
            sel_s[b] = chosen.astype(jnp.bfloat16)
    my_copy().wait()
    mine = mine_s[...]
    for k in range(tenants):
        maps = sel_s[:, k * 16 : (k + 1) * 16, :].reshape(local, rank2)
        part_s[k, :tokens] = jnp.dot(mine, maps, preferred_element_type=jnp.float32)
        part_s[k, tokens:] = jnp.zeros((BLK, rank2), jnp.float32)

    total = jnp.zeros((tokens, features), jnp.float32)
    for c in range(chunks):
        h_copies[c].wait()
        w_copies[c].wait()
        total = total + lax.dot_general(
            h_s[c], w_s[c], (((1,), (1,)), ((), ())), preferred_element_type=jnp.float32
        )
    base_s[...] = jnp.zeros_like(base_s)
    base_s[:tokens, :features] = total

    if requests < devices:
        out[...] = jnp.zeros_like(out)
    first = jnp.int32(0)
    for r in range(requests):
        dest = placement[r] // dec_rows
        start = pl.multiple_of(first * BLK, BLK)
        out[dest, :, :128] = base_s[pl.ds(start, CAPT), :].astype(out.dtype)
        out[dest, :, 128:] = part_s[tenant[r], pl.ds(start, CAPT), :].astype(out.dtype)
        first = first + counts[r]


def attend_kernel(fused, counts, last, placement, lengths, *refs):
    if fused:
        received, ups, cache, query, steps_kv, out = refs
        base, part = received.at[:, :, :HD], received.at[:, :, HD:]
    else:
        base, part, ups, cache, query, steps_kv, out = refs
    dec_rows, ctx, kv_width = cache.shape
    half_width = kv_width // 2
    step_rows = steps_kv.shape[0]
    steps = step_rows // dec_rows
    rank = ups.shape[1]
    requests = placement.shape[0]
    me = lax.axis_index("tensor")
    group = HEADS // KVH * dec_rows
    q_rows = steps * group

    my_slot = jnp.int32(-1)
    my_length = jnp.int32(0)
    for r in range(requests):
        hit = placement[r] // dec_rows == me
        my_slot = jnp.where(hit, placement[r] % dec_rows, my_slot)
        my_length = jnp.where(hit, (counts[r] - 1) * BLK + last[r], my_length)

    shrunk = part[0].astype(jnp.float32)
    for i in range(1, part.shape[0]):
        shrunk = shrunk + part[i].astype(jnp.float32)
    shrunk = shrunk.astype(jnp.bfloat16)
    halves = (shrunk[:, :rank], shrunk[:, rank:])

    row = lax.broadcasted_iota(jnp.int32, (q_rows, ctx), 0)
    col = lax.broadcasted_iota(jnp.int32, (q_rows, ctx), 1)
    row_slot = row % dec_rows
    cache_ok = [(row_slot == g) & (col < lengths[g]) for g in range(dec_rows)]
    extra = CAPT + 16
    row = lax.broadcasted_iota(jnp.int32, (q_rows, extra), 0)
    col = lax.broadcasted_iota(jnp.int32, (q_rows, extra), 1)
    row_slot = row % dec_rows
    row_step = row // group
    step_col = col - CAPT
    extra_ok = ((col < CAPT) & (row_slot == my_slot) & (col < my_length)) | (
        (step_col >= 0)
        & (step_col < step_rows)
        & (step_col % dec_rows == row_slot)
        & (step_col // dec_rows <= row_step)
    )
    pad = jnp.zeros((16 - step_rows, HD), jnp.bfloat16)

    def fresh(i):
        half = halves[i // KVH]
        delta = jnp.dot(half, ups[i], preferred_element_type=jnp.float32)
        return (base[i].astype(jnp.float32) + ADAPTER_SCALE * delta).astype(jnp.bfloat16)

    nt = (((1,), (1,)), ((), ()))
    scale = HD ** (-0.5)
    for k in range(KVH):
        lanes = pl.ds(k * HD, HD)
        vlanes = pl.ds(half_width + k * HD, HD)
        q = jnp.concatenate(
            [query[pl.ds(s * HEADS * dec_rows + k * group, group), :] for s in range(steps)], axis=0
        )
        extra_keys = jnp.concatenate([fresh(k), steps_kv[:, lanes], pad], axis=0)
        extra_values = jnp.concatenate([fresh(KVH + k), steps_kv[:, vlanes], pad], axis=0)
        scores = []
        for g in range(dec_rows):
            s = lax.dot_general(q, cache[g, :, lanes], nt, preferred_element_type=jnp.float32)
            scores.append(jnp.where(cache_ok[g], s * scale, NEG_LARGE))
        s = lax.dot_general(q, extra_keys, nt, preferred_element_type=jnp.float32)
        scores.append(jnp.where(extra_ok, s * scale, NEG_LARGE))
        top = functools.reduce(
            jnp.maximum, [jnp.max(s, axis=1, keepdims=True) for s in scores]
        )
        weights = [jnp.exp(s - top) for s in scores]
        total = sum(jnp.sum(w, axis=1, keepdims=True) for w in weights)
        values = [cache[g, :, vlanes] for g in range(dec_rows)] + [extra_values]
        mixed = sum(
            jnp.dot(w.astype(jnp.bfloat16), v, preferred_element_type=jnp.float32)
            for w, v in zip(weights, values)
        )
        result = (mixed / total).astype(jnp.bfloat16)
        for s in range(steps):
            out[pl.ds(s * HEADS * dec_rows + k * group, group), :] = result[
                s * group : (s + 1) * group
            ]


def body(
    hidden,
    key_value_weight,
    adapter_down_weight,
    adapter_up_weight,
    tenant,
    tenant_page_table,
    request_block_count,
    last_block_tokens,
    placement,
    key_value_cache,
    context_length,
    decode_step_query,
    step_key_value,
):
    devices = lax.axis_size("tensor")
    tokens, width = hidden.shape
    features = key_value_weight.shape[0]
    local, pages, rank2 = adapter_down_weight.shape
    rank = adapter_up_weight.shape[2]
    tenants = tenant_page_table.shape[0]
    dec_rows, ctx, kv_width = key_value_cache.shape
    steps = step_key_value.shape[0]
    params = pltpu.CompilerParams(vmem_limit_bytes=VMEM_LIMIT)

    up_by_page = jnp.transpose(adapter_up_weight, (1, 2, 0))
    up_out = pl.pallas_call(
        functools.partial(up_kernel, dec_rows),
        out_shape=jax.ShapeDtypeStruct((devices, rank, features), jnp.bfloat16),
        in_specs=[SMEM_SPEC] * 3 + [ANY_SPEC],
        out_specs=ANY_SPEC,
        scratch_shapes=[pltpu.SMEM((devices,), jnp.int32), pltpu.SemaphoreType.DMA((devices,))],
        compiler_params=params,
        name="up_maps",
    )(tenant, tenant_page_table, placement, up_by_page)
    ups = lax.all_to_all(up_out, "tensor", split_axis=0, concat_axis=0, tiled=True)

    chunks = 8
    outgoing = pl.pallas_call(
        functools.partial(project_kernel, dec_rows, chunks),
        out_shape=jax.ShapeDtypeStruct((devices, CAPT, 128 + rank2), WIRE),
        in_specs=[SMEM_SPEC] * 4 + [ANY_SPEC] * 3,
        out_specs=VMEM_SPEC,
        scratch_shapes=[
            pltpu.VMEM((chunks, tokens, width // chunks), jnp.bfloat16),
            pltpu.VMEM((chunks, features, width // chunks), jnp.bfloat16),
            pltpu.VMEM((local, pages, rank2), jnp.bfloat16),
            pltpu.VMEM((tokens, local), jnp.bfloat16),
            pltpu.VMEM((local // 16, tenants * 16, rank2), jnp.bfloat16),
            pltpu.VMEM((tokens + BLK, 128), jnp.float32),
            pltpu.VMEM((tenants, tokens + BLK, rank2), jnp.float32),
            pltpu.SemaphoreType.DMA((chunks, 4)),
        ],
        compiler_params=params,
        name="project",
    )(
        tenant, tenant_page_table, request_block_count, placement,
        hidden, key_value_weight, adapter_down_weight,
    )
    received = lax.all_to_all(outgoing, "tensor", split_axis=0, concat_axis=0, tiled=True)

    heads2 = kv_width // HD
    fused = features == HD
    if fused:
        arrived = (received,)
    else:
        pieces = HD // features
        base = received[:, :, :features].reshape(heads2, pieces, CAPT, features)
        base = base.transpose(0, 2, 1, 3).reshape(heads2, CAPT, HD)
        ups = ups.reshape(heads2, pieces, rank, features)
        ups = ups.transpose(0, 2, 1, 3).reshape(heads2, rank, HD)
        arrived = (base, received[:, :, 128:])

    query = decode_step_query.reshape(steps, dec_rows, HEADS, HD)
    query = query.transpose(0, 2, 1, 3).reshape(steps * HEADS * dec_rows, HD)
    steps_kv = step_key_value.reshape(steps * dec_rows, kv_width)
    attended = pl.pallas_call(
        functools.partial(attend_kernel, fused),
        out_shape=jax.ShapeDtypeStruct((steps * HEADS * dec_rows, HD), jnp.bfloat16),
        in_specs=[SMEM_SPEC] * 4 + [VMEM_SPEC] * (len(arrived) + 4),
        out_specs=VMEM_SPEC,
        compiler_params=params,
        name="attend",
    )(
        request_block_count, last_block_tokens, placement, context_length,
        *arrived, ups, key_value_cache, query, steps_kv,
    )
    attended = attended.reshape(steps, HEADS, dec_rows, HD).transpose(0, 2, 1, 3)
    return attended.reshape(steps, dec_rows, HEADS * HD)


def solution(mesh):
    return jax.shard_map(
        body,
        mesh=mesh,
        in_specs=(
            P("parts", None),
            P("tensor", None),
            P("tensor", None, None),
            P("tensor", None, None),
            P("parts"),
            P(),
            P("parts"),
            P("parts"),
            P("parts"),
            P(("parts", "tensor"), None, None),
            P(("parts", "tensor")),
            P(None, ("parts", "tensor"), None),
            P(None, ("parts", "tensor"), None),
        ),
        out_specs=P(None, ("parts", "tensor"), None),
        check_vma=False,
    )
```

time: 190 us -> 46.5 us (0.24)
  waiting for transfers between devices: 113 us -> 9.48 us
  matrix products: 27.1 us -> 0 us
  Pallas kernels: 0 us -> 21.9 us
  local copies, waits for them, and re-layouts: 16.2 us -> 1.33 us
  other arithmetic: 14.8 us -> 0 us
  between operations: 13.8 us -> 0.04 us
  starting transfers between devices: 3.5 us -> 13.4 us
    all_gather x1 -> x0, waiting for transfers between devices: 107 us -> none  [body(): lax.all_gather(selected_down_maps, 'tensor', axis=0, tiled=True)]
    dot_general x27 -> x0, matrix products: 27.1 us -> none  [the longest x1 7.31 us: body(): jnp.dot(hidden, lax.all_gather(selected_down_maps, 'tensor', axis=0, tile...]
    pallas_call x0 -> x3, Pallas kernels: none -> 21.9 us  [the longest x1 9.97 us: body(): pl.pallas_call(functools.partial(up_kernel, dec_rows), out_shape=jax.Shap...]
    all_to_all x1 -> x2, starting transfers between devices: 3.5 us -> 13.4 us  [the longest x1 7.4 us: body(): lax.all_to_all(outgoing, 'tensor', split_axis=0, concat_axis=0, tiled=True)]
    gather x3 -> x0, local copies, waits for them, and re-layouts: 6 us -> none  [the longest x1 4.58 us: body(): jnp.take(adapter_down_weight, tenant_page_table, axis=1)]
    sub x4 -> x0, other arithmetic: 4.83 us -> none  [body(): weights = jnp.exp(scores - highest)]
    select_n x6 -> x0, other arithmetic: 4.04 us -> none  [the longest x1 2.41 us: body(): jnp.take(adapter_down_weight, tenant_page_table, axis=1)]
    unnamed x42 -> x6, local copies, waits for them, and re-layouts: 3.94 us -> 0.7 us
  transfers between devices with their start and end apart: 2 -> 2, of which waited for: 2 -> 2; matrix products, arithmetic and copies ran while one was open for 12% -> 1% of each run, Pallas kernels for 0% -> 22%
where the time goes in v1:
time: 46.5 us; the launch traced here: 46.1 us
  Pallas kernels  21.9 us (47%)
  starting transfers between devices  13.4 us (29%)
  waiting for transfers between devices  9.48 us (20%)
  local copies, waits for them, and re-layouts  1.33 us (3%)
    pallas_call x1, Pallas kernels, body(): pl.pallas_call(functools.partial(up_kernel, dec_rows), out_shape=jax.Shap...  9.97 us
    all_to_all x1, waiting for transfers between devices, body(): lax.all_to_all(up_out, 'tensor', split_axis=0, concat_axis=0, tiled=True)  9.41 us
    all_to_all x1, starting transfers between devices, body(): lax.all_to_all(outgoing, 'tensor', split_axis=0, concat_axis=0, tiled=True)  7.4 us
    pallas_call x1, Pallas kernels, body(): pl.pallas_call(functools.partial(project_kernel, dec_rows, chunks), out_s...  7.32 us
    all_to_all x1, starting transfers between devices, body(): lax.all_to_all(up_out, 'tensor', split_axis=0, concat_axis=0, tiled=True)  5.96 us
    pallas_call x1, Pallas kernels, body(): pl.pallas_call(functools.partial(attend_kernel, fused), out_shape=jax.Sha...  4.62 us
  transfers between devices with their start and end apart: 2, of which 2 were waited for; matrix products, arithmetic and copies ran while one was open for 1% of the time, Pallas kernels for 22%

profile of v1, /device:TPU:0, one launch (start us, length us, event | category | flops | bytes accessed | tf_op | source)
XLA Modules:
  0.0 46.1 jit_solution(18165715618234207854)
XLA Ops:
  0.0 0.0 copy-start.2
  0.0 7.3 %project.1 = f32[16,16,256]{2,1,0:T(8,128)} custom-call(s32[16]{0:T(128)} %tenant.3, s32[8]{0:T(128)} %table.3, s32[16]{0:T(128)} %counts.3, s32[16]{0:T(128)} %placement.5, bf16[160,8192]{1,0:T(8,128)(2,1)} %hidden.1, bf16[128,8192]{1,0:T(8,128)(2,1)} %weight.1, bf16[512,16,128]{2,1,0:T(8,128)(2,1)} %down.1), custom_call_target="tpu_custom_call" | custom-call | tf_op jit(solution)/shard_map/project/pallas_call | solution.py:241
  7.3 7.4 %all-to-all-start = ((f32[16,16,256]{2,1,0:T(8,128)}), f32[16,16,256]{2,1,0:T(8,128)S(1)}, u32[]{:S(2)}, u32[]{:S(2)}) async-start(f32[16,16,256]{2,1,0:T(8,128)} %project.1), calls=%async_computation | async-start | bytes 524288 | tf_op jit(solution)/shard_map/all_to_all | solution.py:262
  14.7 10.0 %up_maps.1 = bf16[16,64,128]{2,1,0:T(8,128)(2,1)} custom-call(s32[16]{0:T(128)} %tenant.3, s32[8]{0:T(128)} %table.3, s32[16]{0:T(128)} %placement.5, bf16[16,64,128]{2,1,0:T(8,128)(2,1)} %bitcast.11), custom_call_target="tpu_custom_call" | custom-call | tf_op jit(solution)/shard_map/up_maps/pallas_call | solution.py:229
  24.7 0.1 all-to-all-done.refs_0_
  24.8 0.0 copy-start
  24.8 6.0 %all-to-all-start.1 = ((bf16[16,64,128]{2,1,0:T(8,128)(2,1)}), bf16[16,64,128]{2,1,0:T(8,128)(2,1)S(1)}, u32[]{:S(2)}, u32[]{:S(2)}) async-start(bf16[16,64,128]{2,1,0:T(8,128)(2,1)} %up_maps.1), calls=%async_computation.1 | async-start | bytes 524288 | tf_op jit(solution)/shard_map/all_to_all | solution.py:238
  30.8 0.0 copy-done.2
  30.8 0.6 %reshape.17.refs_4_ = bf16[8,2048]{1,0:T(8,128)(2,1)} reshape(bf16[4,2,2048]{2,1,0:T(2,128)(2,1)S(1)} %copy-done.2) | data formatting | bytes 65536 | tf_op jit(solution)/shard_map/reshape | solution.py:278
  31.4 9.4 %all-to-all-done.1.refs_1_ = bf16[16,64,128]{2,1,0:T(8,128)(2,1)S(1)} async-done(((bf16[16,64,128]{2,1,0:T(8,128)(2,1)}), bf16[16,64,128]{2,1,0:T(8,128)(2,1)S(1)}, u32[]{:S(2)}, u32[]{:S(2)}) %all-to-all-start.1) | async-done | bytes 262176 | tf_op jit(solution)/shard_map/all_to_all | solution.py:238
  40.8 0.0 copy-start.1
  40.8 0.0 copy-done
  40.8 0.7 %copy-done.1 = bf16[16,64,128]{2,1,0:T(8,128)(2,1)} copy-done((bf16[16,64,128]{2,1,0:T(8,128)(2,1)}, bf16[16,64,128]{2,1,0:T(8,128)(2,1)S(1)}, u32[]{:S(2)}) %copy-start.1) | copy-done | bytes 262168
  41.5 4.6 %attend.1 = bf16[512,128]{1,0:T(8,128)(2,1)} custom-call(s32[16]{0:T(128)} %counts.3, s32[16]{0:T(128)} %last.1, s32[16]{0:T(128)} %placement.5, s32[2]{0:T(128)} %lengths.1, f32[16,16,256]{2,1,0:T(8,128)} %copy-done, bf16[16,64,128]{2,1,0:T(8,128)(2,1)} %copy-done.1, bf16[2,128,2048]{2,1,0:T(8,128)(2,1)} %refs_2_.1, bf16[512,128]{1,0:T(8,128)(2,1)} %bitcast.12, ...), custom_call_target="tpu_custom_call" | custom-call | tf_op jit(solution)/shard_map/attend/pallas_call | solution.py:279
Async XLA Ops:
  0.0 30.8 %copy-start.2 = (bf16[4,2,2048]{2,1,0:T(2,128)(2,1)S(1)}, bf16[4,2,2048]{2,1,0:T(2,128)(2,1)}, u32[]{:S(2)}) copy-start(bf16[4,2,2048]{2,1,0:T(2,128)(2,1)} %param.25) | copy-start | bytes 98308
  7.3 17.5 %all-to-all-start = ((f32[16,16,256]{2,1,0:T(8,128)}), f32[16,16,256]{2,1,0:T(8,128)S(1)}, u32[]{:S(2)}, u32[]{:S(2)}) async-start(f32[16,16,256]{2,1,0:T(8,128)} %project.1), calls=%async_computation | async-start | bytes 524288 | tf_op jit(solution)/shard_map/all_to_all | solution.py:262
  24.8 16.0 %copy-start = (f32[16,16,256]{2,1,0:T(8,128)}, f32[16,16,256]{2,1,0:T(8,128)S(1)}, u32[]{:S(2)}) copy-start(f32[16,16,256]{2,1,0:T(8,128)S(1)} %all-to-all-done.refs_0_) | copy-start | bytes 786436
  24.8 16.0 %all-to-all-start.1 = ((bf16[16,64,128]{2,1,0:T(8,128)(2,1)}), bf16[16,64,128]{2,1,0:T(8,128)(2,1)S(1)}, u32[]{:S(2)}, u32[]{:S(2)}) async-start(bf16[16,64,128]{2,1,0:T(8,128)(2,1)} %up_maps.1), calls=%async_computation.1 | async-start | bytes 524288 | tf_op jit(solution)/shard_map/all_to_all | solution.py:238
  40.8 0.7 %copy-start.1 = (bf16[16,64,128]{2,1,0:T(8,128)(2,1)}, bf16[16,64,128]{2,1,0:T(8,128)(2,1)S(1)}, u32[]{:S(2)}) copy-start(bf16[16,64,128]{2,1,0:T(8,128)(2,1)S(1)} %all-to-all-done.1.refs_1_) | copy-start | bytes 786436

commit v2 on v1

v2 whole, which is shorter than its diff:
```python
import functools

import jax
import jax.numpy as jnp
from jax import lax
from jax.experimental import pallas as pl
from jax.experimental.pallas import tpu as pltpu
from jax.sharding import PartitionSpec as P

HEADS = 64
KVH = 8
HD = 128
BLK = 8
MOSTB = 2
CAPT = MOSTB * BLK
ADAPTER_SCALE = 0.5
NEG_LARGE = -1e30
VMEM_LIMIT = 24 * 1024 * 1024
WIRE = jnp.bfloat16

SMEM_SPEC = pl.BlockSpec(memory_space=pltpu.SMEM)
VMEM_SPEC = pl.BlockSpec(memory_space=pltpu.VMEM)
ANY_SPEC = pl.BlockSpec(memory_space=pl.ANY)


def div(x, n):
    shift = n.bit_length() - 1
    return lax.shift_right_logical(x, shift) if n == 1 << shift else x // n


def mod(x, n):
    return x & (n - 1) if n & (n - 1) == 0 else x % n


def partial_kernel(
    dec_rows, chunks, tenant, table, counts, placement, hidden, down, up, out,
    d_s, mine_s, sel_s, part_s, sems,
):
    tokens = hidden.shape[0]
    local, pages, rank2 = down.shape
    features = up.shape[2]
    tenants = table.shape[0]
    requests = tenant.shape[0]
    devices = out.shape[0]
    me = lax.axis_index("tensor")
    step = local // chunks

    d_copies = []
    for c in range(chunks):
        d_copies.append(pltpu.make_async_copy(
            down.at[pl.ds(c * step, step)], d_s.at[pl.ds(c * step, step)], sems.at[c]))
        d_copies[c].start()
    my_copy = pltpu.make_async_copy(
        hidden.at[:, pl.ds(pl.multiple_of(me * local, 128), local)], mine_s, sems.at[chunks]
    )
    my_copy.start()

    rows = lax.broadcasted_iota(jnp.int32, (tenants * 16, 16 * pages), 0)
    cols = lax.broadcasted_iota(jnp.int32, (tenants * 16, 16 * pages), 1)
    page_of_row = jnp.zeros_like(rows)
    for k in range(tenants):
        page_of_row = jnp.where(div(rows, 16) == k, table[k], page_of_row)
    pick = (mod(rows, 16) == div(cols, pages)) & (mod(cols, pages) == page_of_row)
    pick = jnp.where(pick, jnp.float32(1), jnp.float32(0)).astype(jnp.bfloat16)

    if requests < devices:
        out[...] = jnp.zeros_like(out)
    for r in range(requests):
        dest = div(placement[r], dec_rows)
        out[dest, CAPT:, :features] = up[table[tenant[r]]]

    for c in range(chunks):
        d_copies[c].wait()
        for b in range(c * step // 16, (c + 1) * step // 16):
            block = d_s[pl.ds(b * 16, 16)].reshape(16 * pages, rank2)
            chosen = jnp.dot(pick, block, preferred_element_type=jnp.float32)
            sel_s[b] = chosen.astype(jnp.bfloat16)
    my_copy.wait()
    mine = mine_s[...]
    for k in range(0, tenants, 2):
        width = min(2, tenants - k)
        maps = jnp.concatenate(
            [sel_s[:, j * 16 : (j + 1) * 16, :].reshape(local, rank2) for j in range(k, k + width)],
            axis=1,
        )
        product = jnp.dot(mine, maps, preferred_element_type=jnp.float32)
        for j in range(width):
            part_s[k + j, :tokens] = product[:, j * rank2 : (j + 1) * rank2]
            part_s[k + j, tokens:] = jnp.zeros((BLK, rank2), jnp.float32)

    first = jnp.int32(0)
    for r in range(requests):
        dest = div(placement[r], dec_rows)
        start = pl.multiple_of(first * BLK, BLK)
        out[dest, :CAPT, :] = part_s[tenant[r], pl.ds(start, CAPT), :].astype(out.dtype)
        first = first + counts[r]


def base_kernel(
    dec_rows, chunks, counts, placement, hidden, weight, out, h_s, w_s, base_s, sems,
):
    tokens, width = hidden.shape
    features = weight.shape[0]
    requests = placement.shape[0]
    devices = out.shape[0]
    step = width // chunks
    h_copies, w_copies = [], []
    for c in range(chunks):
        h_copies.append(pltpu.make_async_copy(
            hidden.at[:, pl.ds(c * step, step)], h_s.at[c], sems.at[c, 0]))
        w_copies.append(pltpu.make_async_copy(
            weight.at[:, pl.ds(c * step, step)], w_s.at[c], sems.at[c, 1]))
        h_copies[c].start()
        w_copies[c].start()
    total = jnp.zeros((tokens, features), jnp.float32)
    for c in range(chunks):
        h_copies[c].wait()
        w_copies[c].wait()
        total = total + lax.dot_general(
            h_s[c], w_s[c], (((1,), (1,)), ((), ())), preferred_element_type=jnp.float32
        )
    base_s[tokens:] = jnp.zeros((BLK, HD), jnp.float32)
    if features < HD:
        base_s[...] = jnp.zeros_like(base_s)
    base_s[:tokens, :features] = total
    if requests < devices:
        out[...] = jnp.zeros_like(out)
    first = jnp.int32(0)
    for r in range(requests):
        dest = div(placement[r], dec_rows)
        start = pl.multiple_of(first * BLK, BLK)
        out[dest] = base_s[pl.ds(start, CAPT), :].astype(out.dtype)
        first = first + counts[r]


NT = (((1,), (1,)), ((), ()))


def gather_queries(query, k, group, steps, stride):
    return jnp.concatenate(
        [query[pl.ds(s * stride + k * group, group), :] for s in range(steps)], axis=0
    )


def cached_kernel(
    lengths, part, ups, cache, query, steps_kv, delta, acc, top_out, total_out,
):
    dec_rows, ctx, kv_width = cache.shape
    half_width = kv_width // 2
    heads2 = delta.shape[0]
    step_rows = KVH * dec_rows
    steps = steps_kv.shape[0] // (2 * step_rows)
    rank = ups.shape[1]
    group = HEADS // KVH * dec_rows
    q_rows = steps * group
    stride = HEADS * dec_rows

    shrunk = part[0].astype(jnp.float32)
    for i in range(1, part.shape[0]):
        shrunk = shrunk + part[i].astype(jnp.float32)
    shrunk = shrunk.astype(jnp.bfloat16)
    halves = (shrunk[:, :rank], shrunk[:, rank:])
    for i in range(heads2):
        delta[i] = ADAPTER_SCALE * jnp.dot(
            halves[i // KVH], ups[i], preferred_element_type=jnp.float32
        )

    row = lax.broadcasted_iota(jnp.int32, (q_rows, ctx), 0)
    col = lax.broadcasted_iota(jnp.int32, (q_rows, ctx), 1)
    row_slot = mod(row, dec_rows)
    cache_ok = [(row_slot == g) & (col < lengths[g]) for g in range(dec_rows)]
    row = lax.broadcasted_iota(jnp.int32, (q_rows, steps * step_rows), 0)
    col = lax.broadcasted_iota(jnp.int32, (q_rows, steps * step_rows), 1)
    step_ok = (mod(row, dec_rows) == mod(col, dec_rows)) & (div(col, step_rows) <= div(row, group))
    step_head = div(mod(col, step_rows), dec_rows)
    step_keys, step_values = (
        jnp.concatenate(
            [steps_kv[pl.ds((2 * s + half) * step_rows, step_rows), :] for s in range(steps)], axis=0
        )
        for half in range(2)
    )

    scale = HD ** (-0.5)
    for k in range(KVH):
        lanes = pl.ds(k * HD, HD)
        vlanes = pl.ds(half_width + k * HD, HD)
        q = gather_queries(query, k, group, steps, stride)
        keys = [cache[g, :, lanes] for g in range(dec_rows)] + [step_keys]
        values = [cache[g, :, vlanes] for g in range(dec_rows)] + [step_values]
        scores = [
            jnp.where(
                ok,
                lax.dot_general(q, key, NT, preferred_element_type=jnp.float32) * scale,
                NEG_LARGE,
            )
            for ok, key in zip(cache_ok + [step_ok & (step_head == k)], keys)
        ]
        top = functools.reduce(jnp.maximum, [jnp.max(s, axis=1, keepdims=True) for s in scores])
        weights = [jnp.exp(s - top) for s in scores]
        total = sum(jnp.sum(w, axis=1, keepdims=True) for w in weights)
        acc[k] = sum(
            jnp.dot(w.astype(jnp.bfloat16), v, preferred_element_type=jnp.float32)
            for w, v in zip(weights, values)
        )
        top_out[k] = jnp.broadcast_to(top, (q_rows, HD))
        total_out[k] = jnp.broadcast_to(total, (q_rows, HD))


def merge_kernel(
    dec_rows, steps, counts, last, placement, base, delta, acc, top_in, total_in, query, out,
):
    requests = placement.shape[0]
    me = lax.axis_index("tensor")
    group = HEADS // KVH * dec_rows
    q_rows = steps * group
    stride = HEADS * dec_rows

    my_slot = jnp.int32(-1)
    my_length = jnp.int32(0)
    for r in range(requests):
        hit = div(placement[r], dec_rows) == me
        my_slot = jnp.where(hit, mod(placement[r], dec_rows), my_slot)
        my_length = jnp.where(hit, (counts[r] - 1) * BLK + last[r], my_length)
    row = lax.broadcasted_iota(jnp.int32, (q_rows, CAPT), 0)
    col = lax.broadcasted_iota(jnp.int32, (q_rows, CAPT), 1)
    ok = (mod(row, dec_rows) == my_slot) & (col < my_length)

    scale = HD ** (-0.5)
    for k in range(KVH):
        q = gather_queries(query, k, group, steps, stride)
        keys = (base[k].astype(jnp.float32) + delta[k]).astype(jnp.bfloat16)
        values = (base[KVH + k].astype(jnp.float32) + delta[KVH + k]).astype(jnp.bfloat16)
        s = lax.dot_general(q, keys, NT, preferred_element_type=jnp.float32)
        s = jnp.where(ok, s * scale, NEG_LARGE)
        old = top_in[k]
        top = jnp.maximum(old, jnp.max(s, axis=1, keepdims=True))
        fade = jnp.exp(old - top)
        w = jnp.exp(s - top[:, :CAPT])
        total = total_in[k] * fade + jnp.sum(w, axis=1, keepdims=True)
        mixed = acc[k] * fade + jnp.dot(
            w.astype(jnp.bfloat16), values, preferred_element_type=jnp.float32
        )
        result = (mixed / total).astype(jnp.bfloat16)
        for s in range(steps):
            out[pl.ds(s * stride + k * group, group), :] = result[s * group : (s + 1) * group]


def body(
    hidden,
    key_value_weight,
    adapter_down_weight,
    adapter_up_weight,
    tenant,
    tenant_page_table,
    request_block_count,
    last_block_tokens,
    placement,
    key_value_cache,
    context_length,
    decode_step_query,
    step_key_value,
):
    devices = lax.axis_size("tensor")
    tokens, width = hidden.shape
    features = key_value_weight.shape[0]
    local, pages, rank2 = adapter_down_weight.shape
    rank = adapter_up_weight.shape[2]
    tenants = tenant_page_table.shape[0]
    dec_rows, ctx, kv_width = key_value_cache.shape
    steps = step_key_value.shape[0]
    params = pltpu.CompilerParams(vmem_limit_bytes=VMEM_LIMIT)

    heads2 = kv_width // HD
    group = HEADS // KVH * dec_rows
    q_rows = steps * group
    chunks = 4
    up_by_page = jnp.transpose(adapter_up_weight, (1, 2, 0))
    first_out = pl.pallas_call(
        functools.partial(partial_kernel, dec_rows, chunks),
        out_shape=jax.ShapeDtypeStruct((devices, CAPT + rank, HD), WIRE),
        in_specs=[SMEM_SPEC] * 4 + [ANY_SPEC] * 2 + [VMEM_SPEC],
        out_specs=VMEM_SPEC,
        scratch_shapes=[
            pltpu.VMEM((local, pages, rank2), jnp.bfloat16),
            pltpu.VMEM((tokens, local), jnp.bfloat16),
            pltpu.VMEM((local // 16, tenants * 16, rank2), jnp.bfloat16),
            pltpu.VMEM((tenants, tokens + BLK, rank2), jnp.float32),
            pltpu.SemaphoreType.DMA((chunks + 1,)),
        ],
        compiler_params=params,
        name="partials",
    )(
        tenant, tenant_page_table, request_block_count, placement,
        hidden, adapter_down_weight, up_by_page,
    )
    first_in = lax.all_to_all(first_out, "tensor", split_axis=0, concat_axis=0, tiled=True)

    chunks = 8
    second_out = pl.pallas_call(
        functools.partial(base_kernel, dec_rows, chunks),
        out_shape=jax.ShapeDtypeStruct((devices, CAPT, HD), WIRE),
        in_specs=[SMEM_SPEC] * 2 + [ANY_SPEC] * 2,
        out_specs=VMEM_SPEC,
        scratch_shapes=[
            pltpu.VMEM((chunks, tokens, width // chunks), jnp.bfloat16),
            pltpu.VMEM((chunks, features, width // chunks), jnp.bfloat16),
            pltpu.VMEM((tokens + BLK, HD), jnp.float32),
            pltpu.SemaphoreType.DMA((chunks, 2)),
        ],
        compiler_params=params,
        name="base",
    )(request_block_count, placement, hidden, key_value_weight)
    second_in = lax.all_to_all(second_out, "tensor", split_axis=0, concat_axis=0, tiled=True)

    query = decode_step_query.reshape(steps, dec_rows, HEADS, HD)
    query = query.transpose(0, 2, 1, 3).reshape(steps * HEADS * dec_rows, HD)
    steps_kv = step_key_value.reshape(steps, dec_rows, heads2, HD)
    steps_kv = steps_kv.transpose(0, 2, 1, 3).reshape(steps * heads2 * dec_rows, HD)
    fused = features == HD
    if fused:
        arrived = (first_in,)
        base = second_in
    else:
        pieces = HD // features
        ups = first_in[:, CAPT:, :features].reshape(heads2, pieces, rank, features)
        ups = ups.transpose(0, 2, 1, 3).reshape(heads2, rank, HD)
        arrived = (first_in[:, :CAPT], ups)
        base = second_in[:, :, :features].reshape(heads2, pieces, CAPT, features)
        base = base.transpose(0, 2, 1, 3).reshape(heads2, CAPT, HD)

    def cached(lengths, *refs):
        if fused:
            both, *rest = refs
            rest = (both.at[:, :CAPT, :], both.at[:, CAPT:, :], *rest)
        else:
            rest = refs
        cached_kernel(lengths, *rest)

    partial_state = jax.ShapeDtypeStruct((KVH, q_rows, HD), jnp.float32)
    delta, acc, top, total = pl.pallas_call(
        cached,
        out_shape=(
            jax.ShapeDtypeStruct((heads2, CAPT, HD), jnp.float32),
            partial_state,
            partial_state,
            partial_state,
        ),
        in_specs=[SMEM_SPEC] + [VMEM_SPEC] * (len(arrived) + 3),
        out_specs=(VMEM_SPEC,) * 4,
        compiler_params=params,
        name="cached",
    )(context_length, *arrived, key_value_cache, query, steps_kv)
    attended = pl.pallas_call(
        functools.partial(merge_kernel, dec_rows, steps),
        out_shape=jax.ShapeDtypeStruct((steps * HEADS * dec_rows, HD), jnp.bfloat16),
        in_specs=[SMEM_SPEC] * 3 + [VMEM_SPEC] * 6,
        out_specs=VMEM_SPEC,
        compiler_params=params,
        name="merge",
    )(
        request_block_count, last_block_tokens, placement,
        base, delta, acc, top, total, query,
    )
    attended = attended.reshape(steps, HEADS, dec_rows, HD).transpose(0, 2, 1, 3)
    return attended.reshape(steps, dec_rows, HEADS * HD)


def solution(mesh):
    return jax.shard_map(
        body,
        mesh=mesh,
        in_specs=(
            P("parts", None),
            P("tensor", None),
            P("tensor", None, None),
            P("tensor", None, None),
            P("parts"),
            P(),
            P("parts"),
            P("parts"),
            P("parts"),
            P(("parts", "tensor"), None, None),
            P(("parts", "tensor")),
            P(None, ("parts", "tensor"), None),
            P(None, ("parts", "tensor"), None),
        ),
        out_specs=P(None, ("parts", "tensor"), None),
        check_vma=False,
    )
```

time: 46.5 us -> 41.2 us (0.89)
  Pallas kernels: 21.9 us -> 11.4 us
  local copies, waits for them, and re-layouts: 1.33 us -> 9.73 us
  starting transfers between devices: 13.4 us -> 10.9 us
  waiting for transfers between devices: 9.48 us -> 8.57 us
    pallas_call x3 -> x4, Pallas kernels: 21.9 us -> 11.4 us  [the longest x1 3.53 us: body(): pl.pallas_call(functools.partial(base_kernel, dec_rows, chunks), out_shap...]
    unnamed x6 -> x32, local copies, waits for them, and re-layouts: 0.7 us -> 9.73 us
    all_to_all x2, starting transfers between devices: 13.4 us -> 10.9 us  [the longest x1 7.4 us: body(): lax.all_to_all(first_out, 'tensor', split_axis=0, concat_axis=0, tiled=True)]
    all_to_all x2, waiting for transfers between devices: 9.48 us -> 8.57 us  [the longest x1 5.92 us: body(): lax.all_to_all(first_out, 'tensor', split_axis=0, concat_axis=0, tiled=True)]
    reshape x1 -> x0, local copies, waits for them, and re-layouts: 0.63 us -> none  [body(): steps_kv = step_key_value.reshape(steps * dec_rows, kv_width)]
  transfers between devices with their start and end apart: 2 -> 2, of which waited for: 2 -> 2; matrix products, arithmetic and copies ran while one was open for 1% -> 0% of each run, Pallas kernels for 22% -> 16%
where the time goes in v2:
time: 41.2 us; the launch traced here: 40.7 us
  Pallas kernels  11.4 us (28%)
  starting transfers between devices  10.9 us (26%)
  local copies, waits for them, and re-layouts  9.73 us (24%)
  waiting for transfers between devices  8.57 us (21%)
    unnamed x32, local copies, waits for them, and re-layouts  9.73 us
    all_to_all x1, starting transfers between devices, body(): lax.all_to_all(first_out, 'tensor', split_axis=0, concat_axis=0, tiled=True)  7.4 us
    all_to_all x1, waiting for transfers between devices, body(): lax.all_to_all(first_out, 'tensor', split_axis=0, concat_axis=0, tiled=True)  5.92 us
    pallas_call x1, Pallas kernels, body(): pl.pallas_call(functools.partial(base_kernel, dec_rows, chunks), out_shap...  3.53 us
    all_to_all x1, starting transfers between devices, body(): lax.all_to_all(second_out, 'tensor', split_axis=0, concat_axis=0, tiled=T...  3.5 us
    pallas_call x1, Pallas kernels, body(): pl.pallas_call(functools.partial(partial_kernel, dec_rows, chunks), out_s...  3.06 us
    pallas_call x1, Pallas kernels, body(): pl.pallas_call(cached, out_shape=(jax.ShapeDtypeStruct((heads2, CAPT, HD)...  2.95 us
    all_to_all x1, waiting for transfers between devices, body(): lax.all_to_all(second_out, 'tensor', split_axis=0, concat_axis=0, tiled=T...  2.64 us
  transfers between devices with their start and end apart: 2, of which 2 were waited for; matrix products, arithmetic and copies ran while one was open for 0% of the time, Pallas kernels for 16%

profile of v2, /device:TPU:0, one launch (start us, length us, event | category | flops | bytes accessed | tf_op | source)
XLA Modules:
  0.0 40.7 jit_solution(3568273942016856165)
XLA Ops:
  0.0 0.0 copy-start
  0.0 1.7 %copy-done = bf16[160,8192]{1,0:T(8,128)(2,1)S(1)} copy-done((bf16[160,8192]{1,0:T(8,128)(2,1)S(1)}, bf16[160,8192]{1,0:T(8,128)(2,1)}, u32[]{:S(2)}) %copy-start) | copy-done | bytes 2621464
  1.7 0.0 copy-start.2
  1.7 1.6 %copy-done.2 = bf16[512,16,128]{2,1,0:T(8,128)(2,1)S(1)} copy-done((bf16[512,16,128]{2,1,0:T(8,128)(2,1)S(1)}, bf16[512,16,128]{2,1,0:T(8,128)(2,1)}, u32[]{:S(2)}) %copy-start.2) | copy-done | bytes 2097176
  3.3 0.0 copy-start.6
  3.3 0.9 %copy-done.6 = bf16[128,16,64]{0,2,1:T(8,128)(2,1)S(1)} copy-done((bf16[128,16,64]{0,2,1:T(8,128)(2,1)S(1)}, bf16[128,16,64]{0,2,1:T(8,128)(2,1)}, u32[]{:S(2)}) %copy-start.6) | copy-done | bytes 262168
  4.3 0.0 copy-start.8
  4.3 0.7 %copy-done.8 = s32[16]{0:T(128)S(1)} copy-done((s32[16]{0:T(128)S(1)}, s32[16]{0:T(128)}, u32[]{:S(2)}) %copy-start.8) | copy-done | bytes 88
  4.9 0.0 copy-start.10
  4.9 0.7 %copy-done.10 = s32[16]{0:T(128)S(1)} copy-done((s32[16]{0:T(128)S(1)}, s32[16]{0:T(128)}, u32[]{:S(2)}) %copy-start.10) | copy-done | bytes 88
  5.6 0.0 copy-start.12
  5.6 0.7 %copy-done.12 = s32[16]{0:T(128)S(1)} copy-done((s32[16]{0:T(128)S(1)}, s32[16]{0:T(128)}, u32[]{:S(2)}) %copy-start.12) | copy-done | bytes 88
  6.3 0.0 copy-start.13
  6.3 0.7 %copy-done.13 = s32[8]{0:T(128)S(1)} copy-done((s32[8]{0:T(128)S(1)}, s32[8]{0:T(128)}, u32[]{:S(2)}) %copy-start.13) | copy-done | bytes 56
  6.9 0.0 copy-start.1
  6.9 0.0 copy-start.9
  6.9 0.0 copy-start.11
  6.9 3.1 %partials.1 = bf16[16,80,128]{2,1,0:T(8,128)(2,1)} custom-call(s32[16]{0:T(128)S(1)} %copy-done.12, s32[8]{0:T(128)S(1)} %copy-done.13, s32[16]{0:T(128)S(1)} %copy-done.8, s32[16]{0:T(128)S(1)} %copy-done.10, bf16[160,8192]{1,0:T(8,128)(2,1)S(1)} %copy-done, bf16[512,16,128]{2,1,0:T(8,128)(2,1)S(1)} %copy-done.2, bf16[16,64,128]{2,1,0:T(8,128)(2,1)S(1)} %bitcast.18), custom_call_target="tpu_custom_call" | custom-call | tf_op jit(solution)/shard_map/partials/pallas_call | solution.py:278
  10.0 7.4 %all-to-all-start.1 = ((bf16[16,80,128]{2,1,0:T(8,128)(2,1)}), bf16[16,80,128]{2,1,0:T(8,128)(2,1)S(1)}, u32[]{:S(2)}, u32[]{:S(2)}) async-start(bf16[16,80,128]{2,1,0:T(8,128)(2,1)} %partials.1), calls=%async_computation.1 | async-start | bytes 655360 | tf_op jit(solution)/shard_map/all_to_all | solution.py:296
  17.4 0.0 copy-done.1
  17.4 0.0 copy-done.9
  17.4 0.0 copy-done.11
  17.4 0.0 copy-start.3
  17.4 1.6 %copy-done.3 = bf16[128,8192]{1,0:T(8,128)(2,1)S(1)} copy-done((bf16[128,8192]{1,0:T(8,128)(2,1)S(1)}, bf16[128,8192]{1,0:T(8,128)(2,1)}, u32[]{:S(2)}) %copy-start.3) | copy-done | bytes 2097176
  19.0 0.0 copy-start.5
  19.0 0.0 copy-start.7
  19.0 0.0 copy-start.14
  19.0 0.0 copy-start.15
  19.0 3.5 %base.1 = bf16[16,16,128]{2,1,0:T(8,128)(2,1)} custom-call(s32[16]{0:T(128)S(1)} %copy-done.9, s32[16]{0:T(128)S(1)} %copy-done.11, bf16[160,8192]{1,0:T(8,128)(2,1)S(1)} %copy-done.1, bf16[128,8192]{1,0:T(8,128)(2,1)S(1)} %copy-done.3), custom_call_target="tpu_custom_call" | custom-call | tf_op jit(solution)/shard_map/base/pallas_call | solution.py:299
  22.6 5.9 %all-to-all-done.1.refs_0_ = bf16[16,80,128]{2,1,0:T(8,128)(2,1)S(1)} async-done(((bf16[16,80,128]{2,1,0:T(8,128)(2,1)}), bf16[16,80,128]{2,1,0:T(8,128)(2,1)S(1)}, u32[]{:S(2)}, u32[]{:S(2)}) %all-to-all-start.1) | async-done | bytes 327712 | tf_op jit(solution)/shard_map/all_to_all | solution.py:296
  28.5 3.5 %all-to-all-start = ((bf16[16,16,128]{2,1,0:T(8,128)(2,1)}), bf16[16,16,128]{2,1,0:T(8,128)(2,1)S(1)}, u32[]{:S(2)}, u32[]{:S(2)}) async-start(bf16[16,16,128]{2,1,0:T(8,128)(2,1)} %base.1), calls=%async_computation | async-start | bytes 131072 | tf_op jit(solution)/shard_map/all_to_all | solution.py:313
  32.0 0.0 copy-done.5
  32.0 0.0 copy-done.7
  32.0 0.0 copy-done.14
  32.0 0.0 copy-start.4
  32.0 1.2 %copy-done.4 = bf16[2,128,2048]{2,1,0:T(8,128)(2,1)S(1)} copy-done((bf16[2,128,2048]{2,1,0:T(8,128)(2,1)S(1)}, bf16[2,128,2048]{2,1,0:T(8,128)(2,1)}, u32[]{:S(2)}) %copy-start.4) | copy-done | bytes 1048600
  33.3 3.0 %cached.1 = (f32[16,16,128]{2,1,0:T(8,128)S(1)}, f32[8,64,128]{2,1,0:T(8,128)S(1)}, f32[8,64,128]{2,1,0:T(8,128)S(1)}, f32[8,64,128]{2,1,0:T(8,128)S(1)}) custom-call(s32[2]{0:T(128)S(1)} %copy-done.14, bf16[16,80,128]{2,1,0:T(8,128)(2,1)S(1)} %all-to-all-done.1.refs_0_, bf16[2,128,2048]{2,1,0:T(8,128)(2,1)S(1)} %copy-done.4, bf16[512,128]{1,0:T(8,128)(2,1)S(1)} %bitcast.16, ...), custom_call_target="tpu_custom_call" | custom-call | tf_op jit(solution)/shard_map/cached/pallas_call | solution.py:340
  36.2 2.6 %all-to-all-done.base = bf16[16,16,128]{2,1,0:T(8,128)(2,1)S(1)} async-done(((bf16[16,16,128]{2,1,0:T(8,128)(2,1)}), bf16[16,16,128]{2,1,0:T(8,128)(2,1)S(1)}, u32[]{:S(2)}, u32[]{:S(2)}) %all-to-all-start) | async-done | bytes 65568 | tf_op jit(solution)/shard_map/all_to_all | solution.py:313
  38.9 0.0 copy-done.15
  38.9 1.8 %merge.1 = bf16[512,128]{1,0:T(8,128)(2,1)} custom-call(s32[16]{0:T(128)S(1)} %copy-done.9, s32[16]{0:T(128)S(1)} %copy-done.15, s32[16]{0:T(128)S(1)} %copy-done.11, bf16[16,16,128]{2,1,0:T(8,128)(2,1)S(1)} %all-to-all-done.base, f32[16,16,128]{2,1,0:T(8,128)S(1)} %get-tuple-element.9.delta, f32[8,64,128]{2,1,0:T(8,128)S(1)} %get-tuple-element.10.acc, ...), custom_call_target="tpu_custom_call" | custom-call | tf_op jit(solution)/shard_map/merge/pallas_call | solution.py:353
Async XLA Ops:
  0.0 1.7 %copy-start = (bf16[160,8192]{1,0:T(8,128)(2,1)S(1)}, bf16[160,8192]{1,0:T(8,128)(2,1)}, u32[]{:S(2)}) copy-start(bf16[160,8192]{1,0:T(8,128)(2,1)} %hidden.3) | copy-start | bytes 7864324
  1.7 1.6 %copy-start.2 = (bf16[512,16,128]{2,1,0:T(8,128)(2,1)S(1)}, bf16[512,16,128]{2,1,0:T(8,128)(2,1)}, u32[]{:S(2)}) copy-start(bf16[512,16,128]{2,1,0:T(8,128)(2,1)} %down.1) | copy-start | bytes 6291460
  3.3 0.9 %copy-start.6 = (bf16[128,16,64]{0,2,1:T(8,128)(2,1)S(1)}, bf16[128,16,64]{0,2,1:T(8,128)(2,1)}, u32[]{:S(2)}) copy-start(bf16[128,16,64]{0,2,1:T(8,128)(2,1)} %param.16) | copy-start | bytes 786436
  4.3 0.7 %copy-start.8 = (s32[16]{0:T(128)S(1)}, s32[16]{0:T(128)}, u32[]{:S(2)}) copy-start(s32[16]{0:T(128)} %counts.5) | copy-start | bytes 196
  4.9 0.7 %copy-start.10 = (s32[16]{0:T(128)S(1)}, s32[16]{0:T(128)}, u32[]{:S(2)}) copy-start(s32[16]{0:T(128)} %placement.5) | copy-start | bytes 196
  5.6 0.7 %copy-start.12 = (s32[16]{0:T(128)S(1)}, s32[16]{0:T(128)}, u32[]{:S(2)}) copy-start(s32[16]{0:T(128)} %tenant.1) | copy-start | bytes 196
  6.3 0.7 %copy-start.13 = (s32[8]{0:T(128)S(1)}, s32[8]{0:T(128)}, u32[]{:S(2)}) copy-start(s32[8]{0:T(128)} %table.1) | copy-start | bytes 100
  6.9 10.5 %copy-start.1 = (bf16[160,8192]{1,0:T(8,128)(2,1)S(1)}, bf16[160,8192]{1,0:T(8,128)(2,1)}, u32[]{:S(2)}) copy-start(bf16[160,8192]{1,0:T(8,128)(2,1)} %hidden.3) | copy-start | bytes 7864324
  6.9 10.5 %copy-start.9 = (s32[16]{0:T(128)S(1)}, s32[16]{0:T(128)}, u32[]{:S(2)}) copy-start(s32[16]{0:T(128)} %counts.5) | copy-start | bytes 196
  6.9 10.5 %copy-start.11 = (s32[16]{0:T(128)S(1)}, s32[16]{0:T(128)}, u32[]{:S(2)}) copy-start(s32[16]{0:T(128)} %placement.5) | copy-start | bytes 196
  10.0 18.5 %all-to-all-start.1 = ((bf16[16,80,128]{2,1,0:T(8,128)(2,1)}), bf16[16,80,128]{2,1,0:T(8,128)(2,1)S(1)}, u32[]{:S(2)}, u32[]{:S(2)}) async-start(bf16[16,80,128]{2,1,0:T(8,128)(2,1)} %partials.1), calls=%async_computation.1 | async-start | bytes 655360 | tf_op jit(solution)/shard_map/all_to_all | solution.py:296
  17.4 1.6 %copy-start.3 = (bf16[128,8192]{1,0:T(8,128)(2,1)S(1)}, bf16[128,8192]{1,0:T(8,128)(2,1)}, u32[]{:S(2)}) copy-start(bf16[128,8192]{1,0:T(8,128)(2,1)} %weight.1) | copy-start | bytes 6291460
  19.0 13.0 %copy-start.5 = (bf16[4,2,8192]{2,1,0:T(2,128)(2,1)S(1)}, bf16[4,2,8192]{2,1,0:T(2,128)(2,1)}, u32[]{:S(2)}) copy-start(bf16[4,2,8192]{2,1,0:T(2,128)(2,1)} %param.24) | copy-start | bytes 393220
  19.0 13.0 %copy-start.7 = (bf16[4,2,2048]{2,1,0:T(2,128)(2,1)S(1)}, bf16[4,2,2048]{2,1,0:T(2,128)(2,1)}, u32[]{:S(2)}) copy-start(bf16[4,2,2048]{2,1,0:T(2,128)(2,1)} %param.25) | copy-start | bytes 98308
  19.0 13.0 %copy-start.14 = (s32[2]{0:T(128)S(1)}, s32[2]{0:T(128)}, u32[]{:S(2)}) copy-start(s32[2]{0:T(128)} %lengths.1) | copy-start | bytes 28
  19.0 19.8 %copy-start.15 = (s32[16]{0:T(128)S(1)}, s32[16]{0:T(128)}, u32[]{:S(2)}) copy-start(s32[16]{0:T(128)} %last.1) | copy-start | bytes 196
  28.5 10.4 %all-to-all-start = ((bf16[16,16,128]{2,1,0:T(8,128)(2,1)}), bf16[16,16,128]{2,1,0:T(8,128)(2,1)S(1)}, u32[]{:S(2)}, u32[]{:S(2)}) async-start(bf16[16,16,128]{2,1,0:T(8,128)(2,1)} %base.1), calls=%async_computation | async-start | bytes 131072 | tf_op jit(solution)/shard_map/all_to_all | solution.py:313
  32.0 1.2 %copy-start.4 = (bf16[2,128,2048]{2,1,0:T(8,128)(2,1)S(1)}, bf16[2,128,2048]{2,1,0:T(8,128)(2,1)}, u32[]{:S(2)}) copy-start(bf16[2,128,2048]{2,1,0:T(8,128)(2,1)} %refs_1_.1) | copy-start | bytes 3145732

commit v3 on v2

v3 whole, which is shorter than its diff:
```python
import functools

import jax
import jax.numpy as jnp
from jax import lax
from jax.experimental import pallas as pl
from jax.experimental.pallas import tpu as pltpu
from jax.sharding import PartitionSpec as P

HEADS = 64
KVH = 8
HD = 128
BLK = 8
MOSTB = 2
CAPT = MOSTB * BLK
ADAPTER_SCALE = 0.5
NEG_LARGE = -1e30
PROJECT_VMEM = 60 * 1024 * 1024
ATTEND_VMEM = 16 * 1024 * 1024
WIRE = jnp.bfloat16

SMEM_SPEC = pl.BlockSpec(memory_space=pltpu.SMEM)
VMEM_SPEC = pl.BlockSpec(memory_space=pltpu.VMEM)
ANY_SPEC = pl.BlockSpec(memory_space=pl.ANY)


def div(x, n):
    shift = n.bit_length() - 1
    return lax.shift_right_logical(x, shift) if n == 1 << shift else x // n


def mod(x, n):
    return x & (n - 1) if n & (n - 1) == 0 else x % n


def project_kernel(
    dec_rows, chunks, devices, tenant, table, counts, placement, hidden, weight, down, up, *refs
):
    outs = refs[:devices]
    h_s, w_s, d_s, mine_s, u_s, sel_s, part_s, base_s, dest_table, sems = refs[devices:]
    tokens, width = hidden.shape
    features = weight.shape[0]
    local, pages, rank2 = down.shape
    tenants = table.shape[0]
    requests = tenant.shape[0]
    me = lax.axis_index("tensor")
    d_step = local // chunks
    step = width // chunks

    d_copies, h_copies, w_copies = [], [], []
    for c in range(chunks):
        d_copies.append(pltpu.make_async_copy(
            down.at[pl.ds(c * d_step, d_step)], d_s.at[pl.ds(c * d_step, d_step)], sems.at[c, 0]))
        h_copies.append(pltpu.make_async_copy(
            hidden.at[:, pl.ds(c * step, step)], h_s.at[c], sems.at[c, 1]))
        w_copies.append(pltpu.make_async_copy(
            weight.at[:, pl.ds(c * step, step)], w_s.at[c], sems.at[c, 2]))
    my_copy = pltpu.make_async_copy(
        hidden.at[:, pl.ds(pl.multiple_of(me * local, 128), local)], mine_s, sems.at[0, 3]
    )
    up_copy = pltpu.make_async_copy(up, u_s, sems.at[1, 3])
    for copy in d_copies + [my_copy, up_copy]:
        copy.start()
    for c in range(chunks):
        h_copies[c].start()
        w_copies[c].start()

    for dest in range(devices):
        dest_table[0, dest] = 0
        dest_table[1, dest] = 0
    first = jnp.int32(0)
    for r in range(requests):
        dest = div(placement[r], dec_rows)
        dest_table[0, dest] = first * BLK
        dest_table[1, dest] = tenant[r]
        first = first + counts[r]

    rows = lax.broadcasted_iota(jnp.int32, (tenants * 16, 16 * pages), 0)
    cols = lax.broadcasted_iota(jnp.int32, (tenants * 16, 16 * pages), 1)
    page_of_row = jnp.zeros_like(rows)
    for k in range(tenants):
        page_of_row = jnp.where(div(rows, 16) == k, table[k], page_of_row)
    pick = (mod(rows, 16) == div(cols, pages)) & (mod(cols, pages) == page_of_row)
    pick = jnp.where(pick, jnp.float32(1), jnp.float32(0)).astype(jnp.bfloat16)

    for c in range(chunks):
        d_copies[c].wait()
        for b in range(c * d_step // 16, (c + 1) * d_step // 16):
            block = d_s[pl.ds(b * 16, 16)].reshape(16 * pages, rank2)
            chosen = jnp.dot(pick, block, preferred_element_type=jnp.float32)
            sel_s[b] = chosen.astype(jnp.bfloat16)
    my_copy.wait()
    mine = mine_s[...]
    for k in range(0, tenants, 2):
        pair = min(2, tenants - k)
        maps = jnp.concatenate(
            [sel_s[:, j * 16 : (j + 1) * 16, :].reshape(local, rank2) for j in range(k, k + pair)],
            axis=1,
        )
        product = jnp.dot(mine, maps, preferred_element_type=jnp.float32)
        for j in range(pair):
            part_s[k + j, :tokens] = product[:, j * rank2 : (j + 1) * rank2]
            part_s[k + j, tokens:] = jnp.zeros((BLK, rank2), jnp.float32)

    total = jnp.zeros((tokens, features), jnp.float32)
    for c in range(chunks):
        h_copies[c].wait()
        w_copies[c].wait()
        total = total + lax.dot_general(
            h_s[c], w_s[c], (((1,), (1,)), ((), ())), preferred_element_type=jnp.float32
        )
    base_s[tokens:] = jnp.zeros((BLK, HD), jnp.float32)
    if features < HD:
        base_s[...] = jnp.zeros_like(base_s)
    base_s[:tokens, :features] = total

    up_copy.wait()
    for s in range(devices):
        dest = partner(me, s, devices)
        start = pl.multiple_of(dest_table[0, dest], BLK)
        who = dest_table[1, dest]
        out = outs[s]
        out[:CAPT, :] = part_s[who, pl.ds(start, CAPT), :].astype(out.dtype)
        out[CAPT : 2 * CAPT, :] = base_s[pl.ds(start, CAPT), :].astype(out.dtype)
        if features < HD:
            out[2 * CAPT :, :] = jnp.zeros_like(out[2 * CAPT :, :])
        out[2 * CAPT :, :features] = u_s[table[who]]


def partner(me, s, devices):
    return me ^ s if devices & (devices - 1) == 0 else (me + s) % devices


def sender(me, s, devices):
    return me ^ s if devices & (devices - 1) == 0 else (me + devices - s) % devices


NT = (((1,), (1,)), ((), ()))


def gather_queries(query, k, group, steps, stride):
    return jnp.concatenate(
        [query[pl.ds(s * stride + k * group, group), :] for s in range(steps)], axis=0
    )


def cached_kernel(
    lengths, cache, query, steps_kv, acc, top_out, total_out,
):
    dec_rows, ctx, kv_width = cache.shape
    half_width = kv_width // 2
    step_rows = KVH * dec_rows
    steps = steps_kv.shape[0] // (2 * step_rows)
    group = HEADS // KVH * dec_rows
    q_rows = steps * group
    stride = HEADS * dec_rows

    row = lax.broadcasted_iota(jnp.int32, (q_rows, ctx), 0)
    col = lax.broadcasted_iota(jnp.int32, (q_rows, ctx), 1)
    row_slot = mod(row, dec_rows)
    cache_ok = [(row_slot == g) & (col < lengths[g]) for g in range(dec_rows)]
    row = lax.broadcasted_iota(jnp.int32, (q_rows, steps * step_rows), 0)
    col = lax.broadcasted_iota(jnp.int32, (q_rows, steps * step_rows), 1)
    step_ok = (mod(row, dec_rows) == mod(col, dec_rows)) & (div(col, step_rows) <= div(row, group))
    step_head = div(mod(col, step_rows), dec_rows)
    step_keys, step_values = (
        jnp.concatenate(
            [steps_kv[pl.ds((2 * s + half) * step_rows, step_rows), :] for s in range(steps)], axis=0
        )
        for half in range(2)
    )

    scale = HD ** (-0.5)
    for k in range(KVH):
        lanes = pl.ds(k * HD, HD)
        vlanes = pl.ds(half_width + k * HD, HD)
        q = gather_queries(query, k, group, steps, stride)
        keys = [cache[g, :, lanes] for g in range(dec_rows)] + [step_keys]
        values = [cache[g, :, vlanes] for g in range(dec_rows)] + [step_values]
        scores = [
            jnp.where(
                ok,
                lax.dot_general(q, key, NT, preferred_element_type=jnp.float32) * scale,
                NEG_LARGE,
            )
            for ok, key in zip(cache_ok + [step_ok & (step_head == k)], keys)
        ]
        top = functools.reduce(jnp.maximum, [jnp.max(s, axis=1, keepdims=True) for s in scores])
        weights = [jnp.exp(s - top) for s in scores]
        total = sum(jnp.sum(w, axis=1, keepdims=True) for w in weights)
        acc[k] = sum(
            jnp.dot(w.astype(jnp.bfloat16), v, preferred_element_type=jnp.float32)
            for w, v in zip(weights, values)
        )
        top_out[k] = jnp.broadcast_to(top, (q_rows, HD))
        total_out[k] = jnp.broadcast_to(total, (q_rows, HD))


def merge_kernel(
    dec_rows, steps, devices, features, counts, last, placement, *refs
):
    arrived = refs[:devices]
    acc, top_in, total_in, query, out, box = refs[devices:]
    requests = placement.shape[0]
    rank = arrived[0].shape[0] - 2 * CAPT
    me = lax.axis_index("tensor")
    group = HEADS // KVH * dec_rows
    q_rows = steps * group
    stride = HEADS * dec_rows

    for s in range(devices):
        box[sender(me, s, devices)] = arrived[s][...]
    my_slot = jnp.int32(-1)
    my_length = jnp.int32(0)
    for r in range(requests):
        hit = div(placement[r], dec_rows) == me
        my_slot = jnp.where(hit, mod(placement[r], dec_rows), my_slot)
        my_length = jnp.where(hit, (counts[r] - 1) * BLK + last[r], my_length)
    row = lax.broadcasted_iota(jnp.int32, (q_rows, CAPT), 0)
    col = lax.broadcasted_iota(jnp.int32, (q_rows, CAPT), 1)
    ok = (mod(row, dec_rows) == my_slot) & (col < my_length)

    shrunk = box[0, :CAPT].astype(jnp.float32)
    for i in range(1, devices):
        shrunk = shrunk + box[i, :CAPT].astype(jnp.float32)
    shrunk = shrunk.astype(jnp.bfloat16)
    halves = (shrunk[:, :rank], shrunk[:, rank:])
    pieces = HD // features

    def fresh(i):
        base = [box[i * pieces + p, CAPT : 2 * CAPT, :features] for p in range(pieces)]
        ups = [box[i * pieces + p, 2 * CAPT :, :features] for p in range(pieces)]
        base = base[0] if pieces == 1 else jnp.concatenate(base, axis=1)
        ups = ups[0] if pieces == 1 else jnp.concatenate(ups, axis=1)
        delta = jnp.dot(halves[i // KVH], ups, preferred_element_type=jnp.float32)
        return (base.astype(jnp.float32) + ADAPTER_SCALE * delta).astype(jnp.bfloat16)

    scale = HD ** (-0.5)
    for k in range(KVH):
        q = gather_queries(query, k, group, steps, stride)
        keys, values = fresh(k), fresh(KVH + k)
        s = lax.dot_general(q, keys, NT, preferred_element_type=jnp.float32)
        s = jnp.where(ok, s * scale, NEG_LARGE)
        old = top_in[k]
        top = jnp.maximum(old, jnp.max(s, axis=1, keepdims=True))
        fade = jnp.exp(old - top)
        w = jnp.exp(s - top[:, :CAPT])
        total = total_in[k] * fade + jnp.sum(w, axis=1, keepdims=True)
        mixed = acc[k] * fade + jnp.dot(
            w.astype(jnp.bfloat16), values, preferred_element_type=jnp.float32
        )
        result = (mixed / total).astype(jnp.bfloat16)
        for s in range(steps):
            out[pl.ds(s * stride + k * group, group), :] = result[s * group : (s + 1) * group]


def body(
    hidden,
    key_value_weight,
    adapter_down_weight,
    adapter_up_weight,
    tenant,
    tenant_page_table,
    request_block_count,
    last_block_tokens,
    placement,
    key_value_cache,
    context_length,
    decode_step_query,
    step_key_value,
):
    devices = lax.axis_size("tensor")
    tokens, width = hidden.shape
    features = key_value_weight.shape[0]
    local, pages, rank2 = adapter_down_weight.shape
    rank = adapter_up_weight.shape[2]
    tenants = tenant_page_table.shape[0]
    dec_rows, ctx, kv_width = key_value_cache.shape
    steps = step_key_value.shape[0]
    heads2 = kv_width // HD
    group = HEADS // KVH * dec_rows
    q_rows = steps * group
    chunks = 4
    up_by_page = jnp.transpose(adapter_up_weight, (1, 2, 0))
    rows = 2 * CAPT + rank
    outgoing = pl.pallas_call(
        functools.partial(project_kernel, dec_rows, chunks, devices),
        out_shape=[jax.ShapeDtypeStruct((rows, HD), WIRE)] * devices,
        in_specs=[SMEM_SPEC] * 4 + [ANY_SPEC] * 4,
        out_specs=[VMEM_SPEC] * devices,
        scratch_shapes=[
            pltpu.VMEM((chunks, tokens, width // chunks), jnp.bfloat16),
            pltpu.VMEM((chunks, features, width // chunks), jnp.bfloat16),
            pltpu.VMEM((local, pages, rank2), jnp.bfloat16),
            pltpu.VMEM((tokens, local), jnp.bfloat16),
            pltpu.VMEM((pages, rank, features), jnp.bfloat16),
            pltpu.VMEM((local // 16, tenants * 16, rank2), jnp.bfloat16),
            pltpu.VMEM((tenants, tokens + BLK, rank2), jnp.float32),
            pltpu.VMEM((tokens + BLK, HD), jnp.float32),
            pltpu.SMEM((2, devices), jnp.int32),
            pltpu.SemaphoreType.DMA((chunks, 4)),
        ],
        compiler_params=pltpu.CompilerParams(vmem_limit_bytes=PROJECT_VMEM),
        name="project",
    )(
        tenant, tenant_page_table, request_block_count, placement,
        hidden, key_value_weight, adapter_down_weight, up_by_page,
    )
    arrived = [outgoing[0]]
    for s in range(1, devices):
        route = [(i, partner(i, s, devices)) for i in range(devices)]
        arrived.append(lax.ppermute(outgoing[s], "tensor", route))

    query = decode_step_query.reshape(steps, dec_rows, HEADS, HD)
    query = query.transpose(0, 2, 1, 3).reshape(steps * HEADS * dec_rows, HD)
    steps_kv = step_key_value.reshape(steps, dec_rows, heads2, HD)
    steps_kv = steps_kv.transpose(0, 2, 1, 3).reshape(steps * heads2 * dec_rows, HD)
    partial_state = jax.ShapeDtypeStruct((KVH, q_rows, HD), jnp.float32)
    acc, top, total = pl.pallas_call(
        cached_kernel,
        out_shape=(partial_state,) * 3,
        in_specs=[SMEM_SPEC] + [VMEM_SPEC] * 3,
        out_specs=(VMEM_SPEC,) * 3,
        compiler_params=pltpu.CompilerParams(vmem_limit_bytes=ATTEND_VMEM),
        name="cached",
    )(context_length, key_value_cache, query, steps_kv)
    attended = pl.pallas_call(
        functools.partial(merge_kernel, dec_rows, steps, devices, features),
        out_shape=jax.ShapeDtypeStruct((steps * HEADS * dec_rows, HD), jnp.bfloat16),
        in_specs=[SMEM_SPEC] * 3 + [VMEM_SPEC] * (devices + 4),
        out_specs=VMEM_SPEC,
        scratch_shapes=[pltpu.VMEM((devices, rows, HD), WIRE)],
        compiler_params=pltpu.CompilerParams(vmem_limit_bytes=ATTEND_VMEM),
        name="merge",
    )(
        request_block_count, last_block_tokens, placement, *arrived, acc, top, total, query,
    )
    attended = attended.reshape(steps, HEADS, dec_rows, HD).transpose(0, 2, 1, 3)
    return attended.reshape(steps, dec_rows, HEADS * HD)


def solution(mesh):
    return jax.shard_map(
        body,
        mesh=mesh,
        in_specs=(
            P("parts", None),
            P("tensor", None),
            P("tensor", None, None),
            P("tensor", None, None),
            P("parts"),
            P(),
            P("parts"),
            P("parts"),
            P("parts"),
            P(("parts", "tensor"), None, None),
            P(("parts", "tensor")),
            P(None, ("parts", "tensor"), None),
            P(None, ("parts", "tensor"), None),
        ),
        out_specs=P(None, ("parts", "tensor"), None),
        check_vma=False,
    )
```

time: 41.2 us -> 37.9 us (0.920)
  starting transfers between devices: 10.9 us -> 22.2 us
  local copies, waits for them, and re-layouts: 9.73 us -> 0.76 us
  waiting for transfers between devices: 8.57 us -> 3.19 us
    ppermute x0 -> x15, starting transfers between devices: none -> 22.2 us  [body(): arrived.append(lax.ppermute(outgoing[s], 'tensor', route))]
    all_to_all x2 -> x0, starting transfers between devices: 10.9 us -> none  [the longest x1 7.4 us: body(): lax.all_to_all(first_out, 'tensor', split_axis=0, concat_axis=0, tiled=True)]
    unnamed x32 -> x16, local copies, waits for them, and re-layouts: 9.73 us -> 0.76 us
    all_to_all x2 -> x0, waiting for transfers between devices: 8.57 us -> none  [the longest x1 5.92 us: body(): lax.all_to_all(first_out, 'tensor', split_axis=0, concat_axis=0, tiled=True)]
    ppermute x0 -> x15, waiting for transfers between devices: none -> 3.19 us  [body(): arrived.append(lax.ppermute(outgoing[s], 'tensor', route))]
    pallas_call x4 -> x3, Pallas kernels: 11.4 us -> 11.5 us  [the longest x1 6.06 us: body(): pl.pallas_call(functools.partial(project_kernel, dec_rows, chunks, device...]
  transfers between devices with their start and end apart: 2 -> 15, of which waited for: 2 -> 1; matrix products, arithmetic and copies ran while one was open for 0% -> 0% of each run, Pallas kernels for 16% -> 7%
where the time goes in v3:
time: 37.9 us; the launch traced here: 37.7 us
  starting transfers between devices  22.2 us (59%)
  Pallas kernels  11.5 us (30%)
  waiting for transfers between devices  3.19 us (8%)
  local copies, waits for them, and re-layouts  0.76 us (2%)
    ppermute x15, starting transfers between devices, body(): arrived.append(lax.ppermute(outgoing[s], 'tensor', route))  22.2 us
    pallas_call x1, Pallas kernels, body(): pl.pallas_call(functools.partial(project_kernel, dec_rows, chunks, device...  6.06 us
    ppermute x15, waiting for transfers between devices, body(): arrived.append(lax.ppermute(outgoing[s], 'tensor', route))  3.19 us
    pallas_call x1, Pallas kernels, body(): pl.pallas_call(cached_kernel, out_shape=(partial_state,) * 3, in_specs=[S...  2.82 us
    pallas_call x1, Pallas kernels, body(): pl.pallas_call(functools.partial(merge_kernel, dec_rows, steps, devices,...  2.62 us
    unnamed x16, local copies, waits for them, and re-layouts  0.76 us
  transfers between devices with their start and end apart: 15, of which 1 were waited for; matrix products, arithmetic and copies ran while one was open for 0% of the time, Pallas kernels for 7%

profile of v3, /device:TPU:0, one launch (start us, length us, event | category | flops | bytes accessed | tf_op | source)
XLA Modules:
  0.0 37.7 jit_solution(205105008436842926)
XLA Ops:
  0.0 0.0 copy-start
  0.0 0.0 copy-start.1
  0.0 0.0 copy-start.2
  0.0 0.0 copy-start.6
  0.0 0.0 copy-start.4
  0.0 0.0 copy-start.5
  0.0 0.0 copy-start.7
  0.0 6.1 %project.1 = (bf16[96,128]{1,0:T(8,128)(2,1)}, bf16[96,128]{1,0:T(8,128)(2,1)}, bf16[96,128]{1,0:T(8,128)(2,1)}, bf16[96,128]{1,0:T(8,128)(2,1)}, bf16[96,128]{1...) custom-call(s32[16]{0:T(128)} %tenant.1, s32[8]{0:T(128)} %table.1, ...), custom_call_target="tpu_custom_call" | custom-call | tf_op jit(solution)/shard_map/project/pallas_call | solution.py:286
  6.1 0.5 %collective-permute-start = (bf16[96,128]{1,0:T(8,128)(2,1)}, bf16[96,128]{1,0:T(8,128)(2,1)S(1)}, u32[]{:S(2)}, u32[]{:S(2)}) collective-permute-start(bf16[96,128]{1,0:T(8,128)(2,1)} %get-tuple-element.25), channel_id=1, source_target_pairs={{0,1},{1,0},{2,3},{3,2},{4,5},{5,4},{6,7},{7,6},{8,9},{9,8},{10,11... | collective-permute-start | bytes 73736 | tf_op jit(solution)/shard_map/ppermute | solution.py:312
  6.6 2.6 %collective-permute-start.1 = (bf16[96,128]{1,0:T(8,128)(2,1)}, bf16[96,128]{1,0:T(8,128)(2,1)S(1)}, u32[]{:S(2)}, u32[]{:S(2)}) collective-permute-start(bf16[96,128]{1,0:T(8,128)(2,1)} %get-tuple-element.26), channel_id=1, source_target_pairs={{0,2},{1,3},{2,0},{3,1},{4,6},{5,7},{6,4},{7,5},{8,10},{9,11},{10,... | collective-permute-start | bytes 73736 | tf_op jit(solution)/shard_map/ppermute | solution.py:312
  9.2 0.1 collective-permute-start.2
  9.3 1.8 %collective-permute-start.3 = (bf16[96,128]{1,0:T(8,128)(2,1)}, bf16[96,128]{1,0:T(8,128)(2,1)S(1)}, u32[]{:S(2)}, u32[]{:S(2)}) collective-permute-start(bf16[96,128]{1,0:T(8,128)(2,1)} %get-tuple-element.28), channel_id=1, source_target_pairs={{0,4},{1,5},{2,6},{3,7},{4,0},{5,1},{6,2},{7,3},{8,12},{9,13},{10,... | collective-permute-start | bytes 73736 | tf_op jit(solution)/shard_map/ppermute | solution.py:312
  11.1 0.0 collective-permute-start.4
  11.1 0.0 collective-permute-done.refs_1_
  11.1 2.6 %collective-permute-start.5 = (bf16[96,128]{1,0:T(8,128)(2,1)}, bf16[96,128]{1,0:T(8,128)(2,1)S(1)}, u32[]{:S(2)}, u32[]{:S(2)}) collective-permute-start(bf16[96,128]{1,0:T(8,128)(2,1)} %get-tuple-element.30), channel_id=1, source_target_pairs={{0,6},{1,7},{2,4},{3,5},{4,2},{5,3},{6,0},{7,1},{8,14},{9,15},{10,... | collective-permute-start | bytes 73736 | tf_op jit(solution)/shard_map/ppermute | solution.py:312
  13.7 0.0 collective-permute-done.1.refs_2_
  13.7 0.1 collective-permute-start.6
  13.9 0.0 collective-permute-done.2.refs_3_
  13.9 2.6 %collective-permute-start.7 = (bf16[96,128]{1,0:T(8,128)(2,1)}, bf16[96,128]{1,0:T(8,128)(2,1)S(1)}, u32[]{:S(2)}, u32[]{:S(2)}) collective-permute-start(bf16[96,128]{1,0:T(8,128)(2,1)} %get-tuple-element.32), channel_id=1, source_target_pairs={{0,8},{1,9},{2,10},{3,11},{4,12},{5,13},{6,14},{7,15},{8,0},{9,1},... | collective-permute-start | bytes 73736 | tf_op jit(solution)/shard_map/ppermute | solution.py:312
  16.5 0.0 collective-permute-done.3.refs_4_
  16.5 0.4 collective-permute-start.8
  16.9 0.0 collective-permute-done.4.refs_5_
  16.9 3.2 %collective-permute-start.9 = (bf16[96,128]{1,0:T(8,128)(2,1)}, bf16[96,128]{1,0:T(8,128)(2,1)S(1)}, u32[]{:S(2)}, u32[]{:S(2)}) collective-permute-start(bf16[96,128]{1,0:T(8,128)(2,1)} %get-tuple-element.34), channel_id=1, source_target_pairs={{0,10},{1,11},{2,8},{3,9},{4,14},{5,15},{6,12},{7,13},{8,2},{9,3},... | collective-permute-start | bytes 73736 | tf_op jit(solution)/shard_map/ppermute | solution.py:312
  20.1 0.0 collective-permute-done.5.refs_6_
  20.1 0.1 collective-permute-start.10
  20.2 0.0 collective-permute-done.6.refs_7_
  20.2 3.5 %collective-permute-start.11 = (bf16[96,128]{1,0:T(8,128)(2,1)}, bf16[96,128]{1,0:T(8,128)(2,1)S(1)}, u32[]{:S(2)}, u32[]{:S(2)}) collective-permute-start(bf16[96,128]{1,0:T(8,128)(2,1)} %get-tuple-element.36), channel_id=1, source_target_pairs={{0,12},{1,13},{2,14},{3,15},{4,8},{5,9},{6,10},{7,11},{8,4},{9,5},... | collective-permute-start | bytes 73736 | tf_op jit(solution)/shard_map/ppermute | solution.py:312
  23.7 0.0 collective-permute-done.7.refs_8_
  23.7 0.2 collective-permute-start.12
  24.0 0.0 collective-permute-done.8.refs_9_
  24.0 4.2 %collective-permute-start.13 = (bf16[96,128]{1,0:T(8,128)(2,1)}, bf16[96,128]{1,0:T(8,128)(2,1)S(1)}, u32[]{:S(2)}, u32[]{:S(2)}) collective-permute-start(bf16[96,128]{1,0:T(8,128)(2,1)} %get-tuple-element.38), channel_id=1, source_target_pairs={{0,14},{1,15},{2,12},{3,13},{4,10},{5,11},{6,8},{7,9},{8,6},{9,7},... | collective-permute-start | bytes 73736 | tf_op jit(solution)/shard_map/ppermute | solution.py:312
  28.2 0.0 collective-permute-done.9.refs_10_
  28.2 0.1 collective-permute-start.14
  28.3 0.0 copy-done
  28.3 0.0 copy-done.1
  28.3 0.0 copy-done.2
  28.3 0.0 copy-done.6
  28.3 2.8 %cached.1 = (f32[8,64,128]{2,1,0:T(8,128)S(1)}, f32[8,64,128]{2,1,0:T(8,128)S(1)}, f32[8,64,128]{2,1,0:T(8,128)S(1)}) custom-call(s32[2]{0:T(128)S(1)} %copy-done.6, bf16[2,128,2048]{2,1,0:T(8,128)(2,1)S(1)} %copy-done, bf16[512,128]{1,0:T(8,128)(2,1)S(1)} %bitcast.16, bf16[128,128]{1,0:T(8,128)(2,1)S(1)} %bitcast.18), custom_call_target="tpu_custom_call" | custom-call | tf_op jit(solution)/shard_map/cached/pallas_call | solution.py:319
  31.1 0.0 collective-permute-done.10.refs_11_
  31.1 0.0 collective-permute-done.11.refs_12_
  31.2 0.0 collective-permute-done.12.refs_13_
  31.2 0.0 collective-permute-done.13.refs_14_
  31.2 3.2 %collective-permute-done.14.refs_15_ = bf16[96,128]{1,0:T(8,128)(2,1)S(1)} collective-permute-done((bf16[96,128]{1,0:T(8,128)(2,1)}, bf16[96,128]{1,0:T(8,128)(2,1)S(1)}, u32[]{:S(2)}, u32[]{:S(2)}) %collective-permute-start.14) | collective-permute-done | bytes 24608 | tf_op jit(solution)/shard_map/ppermute | solution.py:312
  34.3 0.0 copy-done.4
  34.3 0.0 copy-done.5
  34.3 0.0 copy-done.7
  34.3 0.0 copy-start.3
  34.4 0.7 %copy-done.3 = bf16[96,128]{1,0:T(8,128)(2,1)S(1)} copy-done((bf16[96,128]{1,0:T(8,128)(2,1)S(1)}, bf16[96,128]{1,0:T(8,128)(2,1)}, u32[]{:S(2)}) %copy-start.3) | copy-done | bytes 24600
  35.1 2.6 %merge.1 = bf16[512,128]{1,0:T(8,128)(2,1)} custom-call(s32[16]{0:T(128)S(1)} %copy-done.4, s32[16]{0:T(128)S(1)} %copy-done.7, s32[16]{0:T(128)S(1)} %copy-done.5, bf16[96,128]{1,0:T(8,128)(2,1)S(1)} %copy-done.3, bf16[96,128]{1,0:T(8,128)(2,1)S(1)} %collective-permute-done.refs_1_, bf16[96,128]{1,0:T(8,128)(2,1)S(1)} %collective-permute-done.1.refs_2_, ...), custom_call_target="tpu_custom_call" | custom-call | tf_op jit(solution)/shard_map/merge/pallas_call | solution.py:327
Async XLA Ops:
  0.0 28.3 %copy-start = (bf16[2,128,2048]{2,1,0:T(8,128)(2,1)S(1)}, bf16[2,128,2048]{2,1,0:T(8,128)(2,1)}, u32[]{:S(2)}) copy-start(bf16[2,128,2048]{2,1,0:T(8,128)(2,1)} %cache.1) | copy-start | bytes 3145732
  0.0 28.3 %copy-start.1 = (bf16[4,2,8192]{2,1,0:T(2,128)(2,1)S(1)}, bf16[4,2,8192]{2,1,0:T(2,128)(2,1)}, u32[]{:S(2)}) copy-start(bf16[4,2,8192]{2,1,0:T(2,128)(2,1)} %param.24) | copy-start | bytes 393220
  0.0 28.3 %copy-start.2 = (bf16[4,2,2048]{2,1,0:T(2,128)(2,1)S(1)}, bf16[4,2,2048]{2,1,0:T(2,128)(2,1)}, u32[]{:S(2)}) copy-start(bf16[4,2,2048]{2,1,0:T(2,128)(2,1)} %param.25) | copy-start | bytes 98308
  0.0 28.3 %copy-start.6 = (s32[2]{0:T(128)S(1)}, s32[2]{0:T(128)}, u32[]{:S(2)}) copy-start(s32[2]{0:T(128)} %lengths.1) | copy-start | bytes 28
  0.0 34.3 %copy-start.4 = (s32[16]{0:T(128)S(1)}, s32[16]{0:T(128)}, u32[]{:S(2)}) copy-start(s32[16]{0:T(128)} %counts.3) | copy-start | bytes 196
  0.0 34.3 %copy-start.5 = (s32[16]{0:T(128)S(1)}, s32[16]{0:T(128)}, u32[]{:S(2)}) copy-start(s32[16]{0:T(128)} %placement.3) | copy-start | bytes 196
  0.0 34.3 %copy-start.7 = (s32[16]{0:T(128)S(1)}, s32[16]{0:T(128)}, u32[]{:S(2)}) copy-start(s32[16]{0:T(128)} %last.1) | copy-start | bytes 196
  6.1 5.0 %collective-permute-start = (bf16[96,128]{1,0:T(8,128)(2,1)}, bf16[96,128]{1,0:T(8,128)(2,1)S(1)}, u32[]{:S(2)}, u32[]{:S(2)}) collective-permute-start(bf16[96,128]{1,0:T(8,128)(2,1)} %get-tuple-element.25), channel_id=1, source_target_pairs={{0,1},{1,0},{2,3},{3,2},{4,5},{5,4},{6,7},{7,6},{8,9},{9,8},{10,11... | collective-permute-start | bytes 73736 | tf_op jit(solution)/shard_map/ppermute | solution.py:312
  6.6 7.1 %collective-permute-start.1 = (bf16[96,128]{1,0:T(8,128)(2,1)}, bf16[96,128]{1,0:T(8,128)(2,1)S(1)}, u32[]{:S(2)}, u32[]{:S(2)}) collective-permute-start(bf16[96,128]{1,0:T(8,128)(2,1)} %get-tuple-element.26), channel_id=1, source_target_pairs={{0,2},{1,3},{2,0},{3,1},{4,6},{5,7},{6,4},{7,5},{8,10},{9,11},{10,... | collective-permute-start | bytes 73736 | tf_op jit(solution)/shard_map/ppermute | solution.py:312
  9.2 4.6 %collective-permute-start.2 = (bf16[96,128]{1,0:T(8,128)(2,1)}, bf16[96,128]{1,0:T(8,128)(2,1)S(1)}, u32[]{:S(2)}, u32[]{:S(2)}) collective-permute-start(bf16[96,128]{1,0:T(8,128)(2,1)} %get-tuple-element.27), channel_id=1, source_target_pairs={{0,3},{1,2},{2,1},{3,0},{4,7},{5,6},{6,5},{7,4},{8,11},{9,10},{10,... | collective-permute-start | bytes 73736 | tf_op jit(solution)/shard_map/ppermute | solution.py:312
  9.3 7.2 %collective-permute-start.3 = (bf16[96,128]{1,0:T(8,128)(2,1)}, bf16[96,128]{1,0:T(8,128)(2,1)S(1)}, u32[]{:S(2)}, u32[]{:S(2)}) collective-permute-start(bf16[96,128]{1,0:T(8,128)(2,1)} %get-tuple-element.28), channel_id=1, source_target_pairs={{0,4},{1,5},{2,6},{3,7},{4,0},{5,1},{6,2},{7,3},{8,12},{9,13},{10,... | collective-permute-start | bytes 73736 | tf_op jit(solution)/shard_map/ppermute | solution.py:312
  11.1 5.8 %collective-permute-start.4 = (bf16[96,128]{1,0:T(8,128)(2,1)}, bf16[96,128]{1,0:T(8,128)(2,1)S(1)}, u32[]{:S(2)}, u32[]{:S(2)}) collective-permute-start(bf16[96,128]{1,0:T(8,128)(2,1)} %get-tuple-element.29), channel_id=1, source_target_pairs={{0,5},{1,4},{2,7},{3,6},{4,1},{5,0},{6,3},{7,2},{8,13},{9,12},{10,... | collective-permute-start | bytes 73736 | tf_op jit(solution)/shard_map/ppermute | solution.py:312
  11.1 9.0 %collective-permute-start.5 = (bf16[96,128]{1,0:T(8,128)(2,1)}, bf16[96,128]{1,0:T(8,128)(2,1)S(1)}, u32[]{:S(2)}, u32[]{:S(2)}) collective-permute-start(bf16[96,128]{1,0:T(8,128)(2,1)} %get-tuple-element.30), channel_id=1, source_target_pairs={{0,6},{1,7},{2,4},{3,5},{4,2},{5,3},{6,0},{7,1},{8,14},{9,15},{10,... | collective-permute-start | bytes 73736 | tf_op jit(solution)/shard_map/ppermute | solution.py:312
  13.7 6.4 %collective-permute-start.6 = (bf16[96,128]{1,0:T(8,128)(2,1)}, bf16[96,128]{1,0:T(8,128)(2,1)S(1)}, u32[]{:S(2)}, u32[]{:S(2)}) collective-permute-start(bf16[96,128]{1,0:T(8,128)(2,1)} %get-tuple-element.31), channel_id=1, source_target_pairs={{0,7},{1,6},{2,5},{3,4},{4,3},{5,2},{6,1},{7,0},{8,15},{9,14},{10,... | collective-permute-start | bytes 73736 | tf_op jit(solution)/shard_map/ppermute | solution.py:312
  13.9 9.9 %collective-permute-start.7 = (bf16[96,128]{1,0:T(8,128)(2,1)}, bf16[96,128]{1,0:T(8,128)(2,1)S(1)}, u32[]{:S(2)}, u32[]{:S(2)}) collective-permute-start(bf16[96,128]{1,0:T(8,128)(2,1)} %get-tuple-element.32), channel_id=1, source_target_pairs={{0,8},{1,9},{2,10},{3,11},{4,12},{5,13},{6,14},{7,15},{8,0},{9,1},... | collective-permute-start | bytes 73736 | tf_op jit(solution)/shard_map/ppermute | solution.py:312
  16.5 7.5 %collective-permute-start.8 = (bf16[96,128]{1,0:T(8,128)(2,1)}, bf16[96,128]{1,0:T(8,128)(2,1)S(1)}, u32[]{:S(2)}, u32[]{:S(2)}) collective-permute-start(bf16[96,128]{1,0:T(8,128)(2,1)} %get-tuple-element.33), channel_id=1, source_target_pairs={{0,9},{1,8},{2,11},{3,10},{4,13},{5,12},{6,15},{7,14},{8,1},{9,0},... | collective-permute-start | bytes 73736 | tf_op jit(solution)/shard_map/ppermute | solution.py:312
  16.9 11.3 %collective-permute-start.9 = (bf16[96,128]{1,0:T(8,128)(2,1)}, bf16[96,128]{1,0:T(8,128)(2,1)S(1)}, u32[]{:S(2)}, u32[]{:S(2)}) collective-permute-start(bf16[96,128]{1,0:T(8,128)(2,1)} %get-tuple-element.34), channel_id=1, source_target_pairs={{0,10},{1,11},{2,8},{3,9},{4,14},{5,15},{6,12},{7,13},{8,2},{9,3},... | collective-permute-start | bytes 73736 | tf_op jit(solution)/shard_map/ppermute | solution.py:312
  20.1 11.1 %collective-permute-start.10 = (bf16[96,128]{1,0:T(8,128)(2,1)}, bf16[96,128]{1,0:T(8,128)(2,1)S(1)}, u32[]{:S(2)}, u32[]{:S(2)}) collective-permute-start(bf16[96,128]{1,0:T(8,128)(2,1)} %get-tuple-element.35), channel_id=1, source_target_pairs={{0,11},{1,10},{2,9},{3,8},{4,15},{5,14},{6,13},{7,12},{8,3},{9,2},... | collective-permute-start | bytes 73736 | tf_op jit(solution)/shard_map/ppermute | solution.py:312
  20.2 11.0 %collective-permute-start.11 = (bf16[96,128]{1,0:T(8,128)(2,1)}, bf16[96,128]{1,0:T(8,128)(2,1)S(1)}, u32[]{:S(2)}, u32[]{:S(2)}) collective-permute-start(bf16[96,128]{1,0:T(8,128)(2,1)} %get-tuple-element.36), channel_id=1, source_target_pairs={{0,12},{1,13},{2,14},{3,15},{4,8},{5,9},{6,10},{7,11},{8,4},{9,5},... | collective-permute-start | bytes 73736 | tf_op jit(solution)/shard_map/ppermute | solution.py:312
  23.7 7.4 %collective-permute-start.12 = (bf16[96,128]{1,0:T(8,128)(2,1)}, bf16[96,128]{1,0:T(8,128)(2,1)S(1)}, u32[]{:S(2)}, u32[]{:S(2)}) collective-permute-start(bf16[96,128]{1,0:T(8,128)(2,1)} %get-tuple-element.37), channel_id=1, source_target_pairs={{0,13},{1,12},{2,15},{3,14},{4,9},{5,8},{6,11},{7,10},{8,5},{9,4},... | collective-permute-start | bytes 73736 | tf_op jit(solution)/shard_map/ppermute | solution.py:312
  24.0 7.2 %collective-permute-start.13 = (bf16[96,128]{1,0:T(8,128)(2,1)}, bf16[96,128]{1,0:T(8,128)(2,1)S(1)}, u32[]{:S(2)}, u32[]{:S(2)}) collective-permute-start(bf16[96,128]{1,0:T(8,128)(2,1)} %get-tuple-element.38), channel_id=1, source_target_pairs={{0,14},{1,15},{2,12},{3,13},{4,10},{5,11},{6,8},{7,9},{8,6},{9,7},... | collective-permute-start | bytes 73736 | tf_op jit(solution)/shard_map/ppermute | solution.py:312
  28.2 6.2 %collective-permute-start.14 = (bf16[96,128]{1,0:T(8,128)(2,1)}, bf16[96,128]{1,0:T(8,128)(2,1)S(1)}, u32[]{:S(2)}, u32[]{:S(2)}) collective-permute-start(bf16[96,128]{1,0:T(8,128)(2,1)} %get-tuple-element.39), channel_id=1, source_target_pairs={{0,15},{1,14},{2,13},{3,12},{4,11},{5,10},{6,9},{7,8},{8,7},{9,6},... | collective-permute-start | bytes 73736 | tf_op jit(solution)/shard_map/ppermute | solution.py:312
  34.3 0.7 %copy-start.3 = (bf16[96,128]{1,0:T(8,128)(2,1)S(1)}, bf16[96,128]{1,0:T(8,128)(2,1)}, u32[]{:S(2)}) copy-start(bf16[96,128]{1,0:T(8,128)(2,1)} %get-tuple-element.24.refs_0_) | copy-start | bytes 73732

commit v4 on v3

--- a/solution.py
+++ b/solution.py
@@ -34,10 +34,9 @@
 
 
 def project_kernel(
-    dec_rows, chunks, devices, tenant, table, counts, placement, hidden, weight, down, up, *refs
+    dec_rows, chunks, devices, tenant, table, counts, placement, hidden, weight, down, up, out,
+    h_s, w_s, d_s, mine_s, u_s, sel_s, part_s, base_s, dest_table, sems,
 ):
-    outs = refs[:devices]
-    h_s, w_s, d_s, mine_s, u_s, sel_s, part_s, base_s, dest_table, sems = refs[devices:]
     tokens, width = hidden.shape
     features = weight.shape[0]
     local, pages, rank2 = down.shape
@@ -115,24 +114,14 @@
     base_s[:tokens, :features] = total
 
     up_copy.wait()
-    for s in range(devices):
-        dest = partner(me, s, devices)
+    for dest in range(devices):
         start = pl.multiple_of(dest_table[0, dest], BLK)
         who = dest_table[1, dest]
-        out = outs[s]
-        out[:CAPT, :] = part_s[who, pl.ds(start, CAPT), :].astype(out.dtype)
-        out[CAPT : 2 * CAPT, :] = base_s[pl.ds(start, CAPT), :].astype(out.dtype)
+        out[dest, :CAPT, :] = part_s[who, pl.ds(start, CAPT), :].astype(out.dtype)
+        out[dest, CAPT : 2 * CAPT, :] = base_s[pl.ds(start, CAPT), :].astype(out.dtype)
         if features < HD:
-            out[2 * CAPT :, :] = jnp.zeros_like(out[2 * CAPT :, :])
-        out[2 * CAPT :, :features] = u_s[table[who]]
-
-
-def partner(me, s, devices):
-    return me ^ s if devices & (devices - 1) == 0 else (me + s) % devices
-
-
-def sender(me, s, devices):
-    return me ^ s if devices & (devices - 1) == 0 else (me + devices - s) % devices
+            out[dest, 2 * CAPT :, :] = jnp.zeros((out.shape[1] - 2 * CAPT, HD), out.dtype)
+        out[dest, 2 * CAPT :, :features] = u_s[table[who]]
 
 
 NT = (((1,), (1,)), ((), ()))
@@ -197,19 +186,16 @@
 
 
 def merge_kernel(
-    dec_rows, steps, devices, features, counts, last, placement, *refs
+    dec_rows, steps, devices, features, counts, last, placement,
+    box, acc, top_in, total_in, query, out,
 ):
-    arrived = refs[:devices]
-    acc, top_in, total_in, query, out, box = refs[devices:]
     requests = placement.shape[0]
-    rank = arrived[0].shape[0] - 2 * CAPT
+    rank = box.shape[1] - 2 * CAPT
     me = lax.axis_index("tensor")
     group = HEADS // KVH * dec_rows
     q_rows = steps * group
     stride = HEADS * dec_rows
 
-    for s in range(devices):
-        box[sender(me, s, devices)] = arrived[s][...]
     my_slot = jnp.int32(-1)
     my_length = jnp.int32(0)
     for r in range(requests):
@@ -285,9 +271,9 @@
     rows = 2 * CAPT + rank
     outgoing = pl.pallas_call(
         functools.partial(project_kernel, dec_rows, chunks, devices),
-        out_shape=[jax.ShapeDtypeStruct((rows, HD), WIRE)] * devices,
+        out_shape=jax.ShapeDtypeStruct((devices, rows, HD), WIRE),
         in_specs=[SMEM_SPEC] * 4 + [ANY_SPEC] * 4,
-        out_specs=[VMEM_SPEC] * devices,
+        out_specs=VMEM_SPEC,
         scratch_shapes=[
             pltpu.VMEM((chunks, tokens, width // chunks), jnp.bfloat16),
             pltpu.VMEM((chunks, features, width // chunks), jnp.bfloat16),
@@ -306,10 +292,7 @@
         tenant, tenant_page_table, request_block_count, placement,
         hidden, key_value_weight, adapter_down_weight, up_by_page,
     )
-    arrived = [outgoing[0]]
-    for s in range(1, devices):
-        route = [(i, partner(i, s, devices)) for i in range(devices)]
-        arrived.append(lax.ppermute(outgoing[s], "tensor", route))
+    arrived = lax.all_to_all(outgoing, "tensor", split_axis=0, concat_axis=0, tiled=True)
 
     query = decode_step_query.reshape(steps, dec_rows, HEADS, HD)
     query = query.transpose(0, 2, 1, 3).reshape(steps * HEADS * dec_rows, HD)
@@ -327,13 +310,12 @@
     attended = pl.pallas_call(
         functools.partial(merge_kernel, dec_rows, steps, devices, features),
         out_shape=jax.ShapeDtypeStruct((steps * HEADS * dec_rows, HD), jnp.bfloat16),
-        in_specs=[SMEM_SPEC] * 3 + [VMEM_SPEC] * (devices + 4),
+        in_specs=[SMEM_SPEC] * 3 + [VMEM_SPEC] * 5,
         out_specs=VMEM_SPEC,
-        scratch_shapes=[pltpu.VMEM((devices, rows, HD), WIRE)],
         compiler_params=pltpu.CompilerParams(vmem_limit_bytes=ATTEND_VMEM),
         name="merge",
     )(
-        request_block_count, last_block_tokens, placement, *arrived, acc, top, total, query,
+        request_block_count, last_block_tokens, placement, arrived, acc, top, total, query,
     )
     attended = attended.reshape(steps, HEADS, dec_rows, HD).transpose(0, 2, 1, 3)
     return attended.reshape(steps, dec_rows, HEADS * HD)

time: 37.9 us -> 28.5 us (0.75)
  starting transfers between devices: 22.2 us -> 7.41 us
  waiting for transfers between devices: 3.19 us -> 9.32 us
  local copies, waits for them, and re-layouts: 0.76 us -> 0.03 us
    ppermute x15 -> x0, starting transfers between devices: 22.2 us -> none  [body(): arrived.append(lax.ppermute(outgoing[s], 'tensor', route))]
    all_to_all x0 -> x1, waiting for transfers between devices: none -> 9.32 us  [body(): lax.all_to_all(outgoing, 'tensor', split_axis=0, concat_axis=0, tiled=True)]
    all_to_all x0 -> x1, starting transfers between devices: none -> 7.41 us  [body(): lax.all_to_all(outgoing, 'tensor', split_axis=0, concat_axis=0, tiled=True)]
    ppermute x15 -> x0, waiting for transfers between devices: 3.19 us -> none  [body(): arrived.append(lax.ppermute(outgoing[s], 'tensor', route))]
    unnamed x16 -> x14, local copies, waits for them, and re-layouts: 0.76 us -> 0.03 us
  transfers between devices with their start and end apart: 15 -> 1, of which waited for: 1 -> 1; matrix products, arithmetic and copies ran while one was open for 0% -> 0% of each run, Pallas kernels for 7% -> 10%
where the time goes in v4:
time: 28.5 us; the launch traced here: 28.3 us
  Pallas kernels  11.4 us (40%)
  waiting for transfers between devices  9.32 us (33%)
  starting transfers between devices  7.41 us (26%)
    all_to_all x1, waiting for transfers between devices, body(): lax.all_to_all(outgoing, 'tensor', split_axis=0, concat_axis=0, tiled=True)  9.32 us
    all_to_all x1, starting transfers between devices, body(): lax.all_to_all(outgoing, 'tensor', split_axis=0, concat_axis=0, tiled=True)  7.41 us
    pallas_call x1, Pallas kernels, body(): pl.pallas_call(functools.partial(project_kernel, dec_rows, chunks, device...  6.01 us
    pallas_call x1, Pallas kernels, body(): pl.pallas_call(cached_kernel, out_shape=(partial_state,) * 3, in_specs=[S...  2.83 us
    pallas_call x1, Pallas kernels, body(): pl.pallas_call(functools.partial(merge_kernel, dec_rows, steps, devices,...  2.59 us
  transfers between devices with their start and end apart: 1, of which 1 were waited for; matrix products, arithmetic and copies ran while one was open for 0% of the time, Pallas kernels for 10%

profile of v4, /device:TPU:0, one launch (start us, length us, event | category | flops | bytes accessed | tf_op | source)
XLA Modules:
  0.0 28.3 jit_solution(5595959497909849468)
XLA Ops:
  0.0 0.0 copy-start
  0.0 0.0 copy-start.1
  0.0 0.0 copy-start.2
  0.0 0.0 copy-start.5
  0.0 0.0 copy-start.3
  0.0 0.0 copy-start.4
  0.0 0.0 copy-start.6
  0.0 6.0 %project.1 = bf16[16,96,128]{2,1,0:T(8,128)(2,1)} custom-call(s32[16]{0:T(128)} %tenant.1, s32[8]{0:T(128)} %table.1, s32[16]{0:T(128)} %counts.3, s32[16]{0:T(128)} %placement.3, bf16[160,8192]{1,0:T(8,128)(2,1)} %hidden.1, bf16[128,8192]{1,0:T(8,128)(2,1)} %weight.1, bf16[512,16,128]{2,1,0:T(8,128)(2,1)} %down.1, bf16[16,64,128]{2,1,0:T(8,128)(2,1)} %bitcast.19), custom_call_target="tpu_custom_call" | custom-call | tf_op jit(solution)/shard_map/project/pallas_call | solution.py:272
  6.1 7.4 %all-to-all-start = ((bf16[16,96,128]{2,1,0:T(8,128)(2,1)}), bf16[16,96,128]{2,1,0:T(8,128)(2,1)S(1)}, u32[]{:S(2)}, u32[]{:S(2)}) async-start(bf16[16,96,128]{2,1,0:T(8,128)(2,1)} %project.1), calls=%async_computation | async-start | bytes 786432 | tf_op jit(solution)/shard_map/all_to_all | solution.py:295
  13.5 0.0 copy-done
  13.5 0.0 copy-done.1
  13.5 0.0 copy-done.2
  13.5 0.0 copy-done.5
  13.5 2.8 %cached.1 = (f32[8,64,128]{2,1,0:T(8,128)S(1)}, f32[8,64,128]{2,1,0:T(8,128)S(1)}, f32[8,64,128]{2,1,0:T(8,128)S(1)}) custom-call(s32[2]{0:T(128)S(1)} %copy-done.5, bf16[2,128,2048]{2,1,0:T(8,128)(2,1)S(1)} %copy-done, bf16[512,128]{1,0:T(8,128)(2,1)S(1)} %bitcast.16, bf16[128,128]{1,0:T(8,128)(2,1)S(1)} %bitcast.18), custom_call_target="tpu_custom_call" | custom-call | tf_op jit(solution)/shard_map/cached/pallas_call | solution.py:302
  16.4 9.3 %all-to-all-done.box = bf16[16,96,128]{2,1,0:T(8,128)(2,1)S(1)} async-done(((bf16[16,96,128]{2,1,0:T(8,128)(2,1)}), bf16[16,96,128]{2,1,0:T(8,128)(2,1)S(1)}, u32[]{:S(2)}, u32[]{:S(2)}) %all-to-all-start) | async-done | bytes 393248 | tf_op jit(solution)/shard_map/all_to_all | solution.py:295
  25.7 0.0 copy-done.3
  25.7 0.0 copy-done.4
  25.7 0.0 copy-done.6
  25.7 2.6 %merge.1 = bf16[512,128]{1,0:T(8,128)(2,1)} custom-call(s32[16]{0:T(128)S(1)} %copy-done.3, s32[16]{0:T(128)S(1)} %copy-done.6, s32[16]{0:T(128)S(1)} %copy-done.4, bf16[16,96,128]{2,1,0:T(8,128)(2,1)S(1)} %all-to-all-done.box, f32[8,64,128]{2,1,0:T(8,128)S(1)} %get-tuple-element.8.acc, f32[8,64,128]{2,1,0:T(8,128)S(1)} %get-tuple-element.9.top_in, ...), custom_call_target="tpu_custom_call" | custom-call | tf_op jit(solution)/shard_map/merge/pallas_call | solution.py:310
Async XLA Ops:
  0.0 13.5 %copy-start = (bf16[2,128,2048]{2,1,0:T(8,128)(2,1)S(1)}, bf16[2,128,2048]{2,1,0:T(8,128)(2,1)}, u32[]{:S(2)}) copy-start(bf16[2,128,2048]{2,1,0:T(8,128)(2,1)} %cache.1) | copy-start | bytes 3145732
  0.0 13.5 %copy-start.1 = (bf16[4,2,8192]{2,1,0:T(2,128)(2,1)S(1)}, bf16[4,2,8192]{2,1,0:T(2,128)(2,1)}, u32[]{:S(2)}) copy-start(bf16[4,2,8192]{2,1,0:T(2,128)(2,1)} %param.24) | copy-start | bytes 393220
  0.0 13.5 %copy-start.2 = (bf16[4,2,2048]{2,1,0:T(2,128)(2,1)S(1)}, bf16[4,2,2048]{2,1,0:T(2,128)(2,1)}, u32[]{:S(2)}) copy-start(bf16[4,2,2048]{2,1,0:T(2,128)(2,1)} %param.25) | copy-start | bytes 98308
  0.0 13.5 %copy-start.5 = (s32[2]{0:T(128)S(1)}, s32[2]{0:T(128)}, u32[]{:S(2)}) copy-start(s32[2]{0:T(128)} %lengths.1) | copy-start | bytes 28
  0.0 25.7 %copy-start.3 = (s32[16]{0:T(128)S(1)}, s32[16]{0:T(128)}, u32[]{:S(2)}) copy-start(s32[16]{0:T(128)} %counts.3) | copy-start | bytes 196
  0.0 25.7 %copy-start.4 = (s32[16]{0:T(128)S(1)}, s32[16]{0:T(128)}, u32[]{:S(2)}) copy-start(s32[16]{0:T(128)} %placement.3) | copy-start | bytes 196
  0.0 25.7 %copy-start.6 = (s32[16]{0:T(128)S(1)}, s32[16]{0:T(128)}, u32[]{:S(2)}) copy-start(s32[16]{0:T(128)} %last.1) | copy-start | bytes 196
  6.1 19.6 %all-to-all-start = ((bf16[16,96,128]{2,1,0:T(8,128)(2,1)}), bf16[16,96,128]{2,1,0:T(8,128)(2,1)S(1)}, u32[]{:S(2)}, u32[]{:S(2)}) async-start(bf16[16,96,128]{2,1,0:T(8,128)(2,1)} %project.1), calls=%async_computation | async-start | bytes 786432 | tf_op jit(solution)/shard_map/all_to_all | solution.py:295

commit v5 on v4

--- a/solution.py
+++ b/solution.py
@@ -15,7 +15,7 @@
 CAPT = MOSTB * BLK
 ADAPTER_SCALE = 0.5
 NEG_LARGE = -1e30
-PROJECT_VMEM = 60 * 1024 * 1024
+PROJECT_VMEM = 32 * 1024 * 1024
 ATTEND_VMEM = 16 * 1024 * 1024
 WIRE = jnp.bfloat16
 
@@ -34,8 +34,9 @@
 
 
 def project_kernel(
-    dec_rows, chunks, devices, tenant, table, counts, placement, hidden, weight, down, up, out,
-    h_s, w_s, d_s, mine_s, u_s, sel_s, part_s, base_s, dest_table, sems,
+    dec_rows, chunks, devices, tenant_h, table_h, counts_h, placement_h, hidden, weight, down, up, out,
+    tenant, table, counts, placement,
+    h_s, w_s, d_s, mine_s, u_s, sel_s, part_s, base_s, dest_table, sems, int_sems,
 ):
     tokens, width = hidden.shape
     features = weight.shape[0]
@@ -46,6 +47,14 @@
     d_step = local // chunks
     step = width // chunks
 
+    int_copies = [
+        pltpu.make_async_copy(src, dst, int_sems.at[i])
+        for i, (src, dst) in enumerate(
+            ((table_h, table), (tenant_h, tenant), (counts_h, counts), (placement_h, placement))
+        )
+    ]
+    for copy in int_copies:
+        copy.start()
     d_copies, h_copies, w_copies = [], [], []
     for c in range(chunks):
         d_copies.append(pltpu.make_async_copy(
@@ -64,6 +73,26 @@
         h_copies[c].start()
         w_copies[c].start()
 
+    int_copies[0].wait()
+    rows = lax.broadcasted_iota(jnp.int32, (tenants * 16, 16 * pages), 0)
+    cols = lax.broadcasted_iota(jnp.int32, (tenants * 16, 16 * pages), 1)
+    page_of_row = jnp.zeros_like(rows)
+    for k in range(tenants):
+        page_of_row = jnp.where(div(rows, 16) == k, table[k], page_of_row)
+    pick = (mod(rows, 16) == div(cols, pages)) & (mod(cols, pages) == page_of_row)
+    pick = jnp.where(pick, jnp.float32(1), jnp.float32(0)).astype(jnp.bfloat16)
+
+    for c in range(chunks):
+        d_copies[c].wait()
+        for b in range(c * d_step // 16, (c + 1) * d_step // 16, 2):
+            block = jnp.concatenate(
+                [d_s[pl.ds((b + i) * 16, 16)].reshape(16 * pages, rank2) for i in range(2)], axis=1
+            )
+            chosen = jnp.dot(pick, block, preferred_element_type=jnp.float32)
+            for i in range(2):
+                sel_s[b + i] = chosen[:, i * rank2 : (i + 1) * rank2].astype(jnp.bfloat16)
+    for copy in int_copies[1:]:
+        copy.wait()
     for dest in range(devices):
         dest_table[0, dest] = 0
         dest_table[1, dest] = 0
@@ -73,21 +102,6 @@
         dest_table[0, dest] = first * BLK
         dest_table[1, dest] = tenant[r]
         first = first + counts[r]
-
-    rows = lax.broadcasted_iota(jnp.int32, (tenants * 16, 16 * pages), 0)
-    cols = lax.broadcasted_iota(jnp.int32, (tenants * 16, 16 * pages), 1)
-    page_of_row = jnp.zeros_like(rows)
-    for k in range(tenants):
-        page_of_row = jnp.where(div(rows, 16) == k, table[k], page_of_row)
-    pick = (mod(rows, 16) == div(cols, pages)) & (mod(cols, pages) == page_of_row)
-    pick = jnp.where(pick, jnp.float32(1), jnp.float32(0)).astype(jnp.bfloat16)
-
-    for c in range(chunks):
-        d_copies[c].wait()
-        for b in range(c * d_step // 16, (c + 1) * d_step // 16):
-            block = d_s[pl.ds(b * 16, 16)].reshape(16 * pages, rank2)
-            chosen = jnp.dot(pick, block, preferred_element_type=jnp.float32)
-            sel_s[b] = chosen.astype(jnp.bfloat16)
     my_copy.wait()
     mine = mine_s[...]
     for k in range(0, tenants, 2):
@@ -134,7 +148,7 @@
 
 
 def cached_kernel(
-    lengths, cache, query, steps_kv, acc, top_out, total_out,
+    lengths, counts, last, placement, cache, query, steps_kv, acc, top_out, total_out, fresh_ok,
 ):
     dec_rows, ctx, kv_width = cache.shape
     half_width = kv_width // 2
@@ -177,35 +191,36 @@
         top = functools.reduce(jnp.maximum, [jnp.max(s, axis=1, keepdims=True) for s in scores])
         weights = [jnp.exp(s - top) for s in scores]
         total = sum(jnp.sum(w, axis=1, keepdims=True) for w in weights)
-        acc[k] = sum(
+        mixed = sum(
             jnp.dot(w.astype(jnp.bfloat16), v, preferred_element_type=jnp.float32)
             for w, v in zip(weights, values)
         )
-        top_out[k] = jnp.broadcast_to(top, (q_rows, HD))
-        total_out[k] = jnp.broadcast_to(total, (q_rows, HD))
-
-
-def merge_kernel(
-    dec_rows, steps, devices, features, counts, last, placement,
-    box, acc, top_in, total_in, query, out,
-):
-    requests = placement.shape[0]
-    rank = box.shape[1] - 2 * CAPT
-    me = lax.axis_index("tensor")
-    group = HEADS // KVH * dec_rows
-    q_rows = steps * group
-    stride = HEADS * dec_rows
+        for s in range(steps):
+            here = pl.ds(s * stride + k * group, group)
+            part = slice(s * group, (s + 1) * group)
+            acc[here, :] = mixed[part]
+            top_out[here, :] = jnp.broadcast_to(top[part], (group, HD))
+            total_out[here, :] = jnp.broadcast_to(total[part], (group, HD))
 
     my_slot = jnp.int32(-1)
     my_length = jnp.int32(0)
-    for r in range(requests):
-        hit = div(placement[r], dec_rows) == me
+    for r in range(placement.shape[0]):
+        hit = div(placement[r], dec_rows) == lax.axis_index("tensor")
         my_slot = jnp.where(hit, mod(placement[r], dec_rows), my_slot)
         my_length = jnp.where(hit, (counts[r] - 1) * BLK + last[r], my_length)
-    row = lax.broadcasted_iota(jnp.int32, (q_rows, CAPT), 0)
-    col = lax.broadcasted_iota(jnp.int32, (q_rows, CAPT), 1)
-    ok = (mod(row, dec_rows) == my_slot) & (col < my_length)
-
+    row = lax.broadcasted_iota(jnp.int32, fresh_ok.shape, 0)
+    col = lax.broadcasted_iota(jnp.int32, fresh_ok.shape, 1)
+    ok = (
+        (mod(div(row, group), KVH) == div(col, CAPT))
+        & (mod(row, dec_rows) == my_slot)
+        & (mod(col, CAPT) < my_length)
+    )
+    fresh_ok[...] = jnp.where(ok, jnp.float32(1), jnp.float32(0))
+
+
+def merge_kernel(features, box, acc, top_in, total_in, fresh_ok, query, out):
+    devices = box.shape[0]
+    rank = box.shape[1] - 2 * CAPT
     shrunk = box[0, :CAPT].astype(jnp.float32)
     for i in range(1, devices):
         shrunk = shrunk + box[i, :CAPT].astype(jnp.float32)
@@ -221,23 +236,23 @@
         delta = jnp.dot(halves[i // KVH], ups, preferred_element_type=jnp.float32)
         return (base.astype(jnp.float32) + ADAPTER_SCALE * delta).astype(jnp.bfloat16)
 
+    keys = jnp.concatenate([fresh(k) for k in range(KVH)], axis=0)
+    values = jnp.concatenate([fresh(KVH + k) for k in range(KVH)], axis=0)
     scale = HD ** (-0.5)
-    for k in range(KVH):
-        q = gather_queries(query, k, group, steps, stride)
-        keys, values = fresh(k), fresh(KVH + k)
-        s = lax.dot_general(q, keys, NT, preferred_element_type=jnp.float32)
-        s = jnp.where(ok, s * scale, NEG_LARGE)
-        old = top_in[k]
+    part = 128
+    for c in range(out.shape[0] // part):
+        here = pl.ds(c * part, part)
+        s = lax.dot_general(query[here, :], keys, NT, preferred_element_type=jnp.float32)
+        s = jnp.where(fresh_ok[here, :] > 0, s * scale, NEG_LARGE)
+        old = top_in[here, :]
         top = jnp.maximum(old, jnp.max(s, axis=1, keepdims=True))
         fade = jnp.exp(old - top)
-        w = jnp.exp(s - top[:, :CAPT])
-        total = total_in[k] * fade + jnp.sum(w, axis=1, keepdims=True)
-        mixed = acc[k] * fade + jnp.dot(
+        w = jnp.exp(s - top)
+        total = total_in[here, :] * fade + jnp.sum(w, axis=1, keepdims=True)
+        mixed = acc[here, :] * fade + jnp.dot(
             w.astype(jnp.bfloat16), values, preferred_element_type=jnp.float32
         )
-        result = (mixed / total).astype(jnp.bfloat16)
-        for s in range(steps):
-            out[pl.ds(s * stride + k * group, group), :] = result[s * group : (s + 1) * group]
+        out[here, :] = (mixed / total).astype(jnp.bfloat16)
 
 
 def body(
@@ -264,17 +279,19 @@
     dec_rows, ctx, kv_width = key_value_cache.shape
     steps = step_key_value.shape[0]
     heads2 = kv_width // HD
-    group = HEADS // KVH * dec_rows
-    q_rows = steps * group
     chunks = 4
     up_by_page = jnp.transpose(adapter_up_weight, (1, 2, 0))
     rows = 2 * CAPT + rank
     outgoing = pl.pallas_call(
         functools.partial(project_kernel, dec_rows, chunks, devices),
-        out_shape=jax.ShapeDtypeStruct((devices, rows, HD), WIRE),
-        in_specs=[SMEM_SPEC] * 4 + [ANY_SPEC] * 4,
+        out_shape=pltpu.VMEM((devices, rows, HD), WIRE),
+        in_specs=[ANY_SPEC] * 8,
         out_specs=VMEM_SPEC,
         scratch_shapes=[
+            pltpu.SMEM(tenant.shape, jnp.int32),
+            pltpu.SMEM(tenant_page_table.shape, jnp.int32),
+            pltpu.SMEM(request_block_count.shape, jnp.int32),
+            pltpu.SMEM(placement.shape, jnp.int32),
             pltpu.VMEM((chunks, tokens, width // chunks), jnp.bfloat16),
             pltpu.VMEM((chunks, features, width // chunks), jnp.bfloat16),
             pltpu.VMEM((local, pages, rank2), jnp.bfloat16),
@@ -285,12 +302,18 @@
             pltpu.VMEM((tokens + BLK, HD), jnp.float32),
             pltpu.SMEM((2, devices), jnp.int32),
             pltpu.SemaphoreType.DMA((chunks, 4)),
+            pltpu.SemaphoreType.DMA((4,)),
         ],
         compiler_params=pltpu.CompilerParams(vmem_limit_bytes=PROJECT_VMEM),
         name="project",
     )(
-        tenant, tenant_page_table, request_block_count, placement,
-        hidden, key_value_weight, adapter_down_weight, up_by_page,
+        *(
+            pltpu.with_memory_space_constraint(x, pltpu.HBM)
+            for x in (
+                tenant, tenant_page_table, request_block_count, placement,
+                hidden, key_value_weight, adapter_down_weight, up_by_page,
+            )
+        )
     )
     arrived = lax.all_to_all(outgoing, "tensor", split_axis=0, concat_axis=0, tiled=True)
 
@@ -298,25 +321,26 @@
     query = query.transpose(0, 2, 1, 3).reshape(steps * HEADS * dec_rows, HD)
     steps_kv = step_key_value.reshape(steps, dec_rows, heads2, HD)
     steps_kv = steps_kv.transpose(0, 2, 1, 3).reshape(steps * heads2 * dec_rows, HD)
-    partial_state = jax.ShapeDtypeStruct((KVH, q_rows, HD), jnp.float32)
-    acc, top, total = pl.pallas_call(
+    state = jax.ShapeDtypeStruct((steps * HEADS * dec_rows, HD), jnp.float32)
+    acc, top, total, fresh_ok = pl.pallas_call(
         cached_kernel,
-        out_shape=(partial_state,) * 3,
-        in_specs=[SMEM_SPEC] + [VMEM_SPEC] * 3,
-        out_specs=(VMEM_SPEC,) * 3,
+        out_shape=(state,) * 4,
+        in_specs=[SMEM_SPEC] * 4 + [VMEM_SPEC] * 3,
+        out_specs=(VMEM_SPEC,) * 4,
         compiler_params=pltpu.CompilerParams(vmem_limit_bytes=ATTEND_VMEM),
         name="cached",
-    )(context_length, key_value_cache, query, steps_kv)
+    )(
+        context_length, request_block_count, last_block_tokens, placement,
+        key_value_cache, query, steps_kv,
+    )
     attended = pl.pallas_call(
-        functools.partial(merge_kernel, dec_rows, steps, devices, features),
+        functools.partial(merge_kernel, features),
         out_shape=jax.ShapeDtypeStruct((steps * HEADS * dec_rows, HD), jnp.bfloat16),
-        in_specs=[SMEM_SPEC] * 3 + [VMEM_SPEC] * 5,
+        in_specs=[VMEM_SPEC] * 6,
         out_specs=VMEM_SPEC,
         compiler_params=pltpu.CompilerParams(vmem_limit_bytes=ATTEND_VMEM),
         name="merge",
-    )(
-        request_block_count, last_block_tokens, placement, arrived, acc, top, total, query,
-    )
+    )(arrived, acc, top, total, fresh_ok, query)
     attended = attended.reshape(steps, HEADS, dec_rows, HD).transpose(0, 2, 1, 3)
     return attended.reshape(steps, dec_rows, HEADS * HD)
 

time: 28.5 us -> 27 us (0.947)
  Pallas kernels: 11.4 us -> 10 us
    pallas_call x1, Pallas kernels: 6.01 us -> 5.22 us  [body(): pl.pallas_call(functools.partial(project_kernel, dec_rows, chunks, device...]
    pallas_call x2, Pallas kernels: 5.42 us -> 4.78 us  [the longest x1 2.9 us: body(): pl.pallas_call(cached_kernel, out_shape=(state,) * 4, in_specs=[SMEM_SPEC...]
  transfers between devices with their start and end apart: 1 -> 1, of which waited for: 1 -> 1; matrix products, arithmetic and copies ran while one was open for 0% -> 0% of each run, Pallas kernels for 10% -> 11%
where the time goes in v5:
time: 27 us; the launch traced here: 26.8 us
  Pallas kernels  10 us (37%)
  waiting for transfers between devices  9.22 us (34%)
  starting transfers between devices  7.41 us (27%)
    all_to_all x1, waiting for transfers between devices, body(): lax.all_to_all(outgoing, 'tensor', split_axis=0, concat_axis=0, tiled=True)  9.22 us
    all_to_all x1, starting transfers between devices, body(): lax.all_to_all(outgoing, 'tensor', split_axis=0, concat_axis=0, tiled=True)  7.41 us
    pallas_call x1, Pallas kernels, body(): pl.pallas_call(functools.partial(project_kernel, dec_rows, chunks, device...  5.22 us
    pallas_call x1, Pallas kernels, body(): pl.pallas_call(cached_kernel, out_shape=(state,) * 4, in_specs=[SMEM_SPEC...  2.9 us
    pallas_call x1, Pallas kernels, body(): pl.pallas_call(functools.partial(merge_kernel, features), out_shape=jax.S...  1.89 us
  transfers between devices with their start and end apart: 1, of which 1 were waited for; matrix products, arithmetic and copies ran while one was open for 0% of the time, Pallas kernels for 11%

profile of v5, /device:TPU:0, one launch (start us, length us, event | category | flops | bytes accessed | tf_op | source)
XLA Modules:
  0.0 26.8 jit_solution(3895906921617813432)
XLA Ops:
  0.0 0.0 copy-start
  0.0 0.0 copy-start.1
  0.0 0.0 copy-start.2
  0.0 0.0 copy-start.3
  0.0 0.0 copy-start.4
  0.0 0.0 copy-start.5
  0.0 0.0 copy-start.6
  0.0 5.2 %project.1 = bf16[16,96,128]{2,1,0:T(8,128)(2,1)} custom-call(s32[16]{0:T(128)} %tenant_h.1, s32[8]{0:T(128)} %table_h.1, s32[16]{0:T(128)} %counts.1, s32[16]{0:T(128)} %placement.1, bf16[160,8192]{1,0:T(8,128)(2,1)} %hidden.1, bf16[128,8192]{1,0:T(8,128)(2,1)} %weight.1, bf16[512,16,128]{2,1,0:T(8,128)(2,1)} %down.1, bf16[16,64,128]{2,1,0:T(8,128)(2,1)} %bitcast.19), custom_call_target="tpu_custom_call" | custom-call | tf_op jit(solution)/shard_map/project/pallas_call | solution.py:285
  5.3 7.4 %all-to-all-start = ((bf16[16,96,128]{2,1,0:T(8,128)(2,1)}), bf16[16,96,128]{2,1,0:T(8,128)(2,1)S(1)}, u32[]{:S(2)}, u32[]{:S(2)}) async-start(bf16[16,96,128]{2,1,0:T(8,128)(2,1)} %project.1), calls=%async_computation | async-start | bytes 786432 | tf_op jit(solution)/shard_map/all_to_all | solution.py:318
  12.7 0.0 copy-done
  12.7 0.0 copy-done.1
  12.7 0.0 copy-done.2
  12.7 0.0 copy-done.3
  12.7 0.0 copy-done.4
  12.7 0.0 copy-done.5
  12.7 0.0 copy-done.6
  12.8 2.9 %cached.1 = (f32[512,128]{1,0:T(8,128)S(1)}, f32[512,128]{1,0:T(8,128)S(1)}, f32[512,128]{1,0:T(8,128)S(1)}, f32[512,128]{1,0:T(8,128)S(1)}) custom-call(s32[2]{0:T(128)S(1)} %copy-done.5, s32[16]{0:T(128)S(1)} %copy-done.3, s32[16]{0:T(128)S(1)} %copy-done.6, s32[16]{0:T(128)S(1)} %copy-done.4, bf16[2,128,2048]{2,1,0:T(8,128)(2,1)S(1)} %copy-done, ...), custom_call_target="tpu_custom_call" | custom-call | tf_op jit(solution)/shard_map/cached/pallas_call | solution.py:325
  15.7 9.2 %all-to-all-done.box = bf16[16,96,128]{2,1,0:T(8,128)(2,1)S(1)} async-done(((bf16[16,96,128]{2,1,0:T(8,128)(2,1)}), bf16[16,96,128]{2,1,0:T(8,128)(2,1)S(1)}, u32[]{:S(2)}, u32[]{:S(2)}) %all-to-all-start) | async-done | bytes 393248 | tf_op jit(solution)/shard_map/all_to_all | solution.py:318
  24.9 1.9 %merge.1 = bf16[512,128]{1,0:T(8,128)(2,1)} custom-call(bf16[16,96,128]{2,1,0:T(8,128)(2,1)S(1)} %all-to-all-done.box, f32[512,128]{1,0:T(8,128)S(1)} %get-tuple-element.9.acc, f32[512,128]{1,0:T(8,128)S(1)} %get-tuple-element.10.top_in, f32[512,128]{1,0:T(8,128)S(1)} %get-tuple-element.11.total_in, f32[512,128]{1,0:T(8,128)S(1)} %get-tuple-element.12.fresh_ok, ...), custom_call_target="tpu_custom_call" | custom-call | tf_op jit(solution)/shard_map/merge/pallas_call | solution.py:336
Async XLA Ops:
  0.0 12.7 %copy-start = (bf16[2,128,2048]{2,1,0:T(8,128)(2,1)S(1)}, bf16[2,128,2048]{2,1,0:T(8,128)(2,1)}, u32[]{:S(2)}) copy-start(bf16[2,128,2048]{2,1,0:T(8,128)(2,1)} %cache.1) | copy-start | bytes 3145732
  0.0 12.7 %copy-start.1 = (bf16[4,2,8192]{2,1,0:T(2,128)(2,1)S(1)}, bf16[4,2,8192]{2,1,0:T(2,128)(2,1)}, u32[]{:S(2)}) copy-start(bf16[4,2,8192]{2,1,0:T(2,128)(2,1)} %param.24) | copy-start | bytes 393220
  0.0 12.7 %copy-start.2 = (bf16[4,2,2048]{2,1,0:T(2,128)(2,1)S(1)}, bf16[4,2,2048]{2,1,0:T(2,128)(2,1)}, u32[]{:S(2)}) copy-start(bf16[4,2,2048]{2,1,0:T(2,128)(2,1)} %param.25) | copy-start | bytes 98308
  0.0 12.7 %copy-start.3 = (s32[16]{0:T(128)S(1)}, s32[16]{0:T(128)}, u32[]{:S(2)}) copy-start(s32[16]{0:T(128)} %counts.1) | copy-start | bytes 196
  0.0 12.7 %copy-start.4 = (s32[16]{0:T(128)S(1)}, s32[16]{0:T(128)}, u32[]{:S(2)}) copy-start(s32[16]{0:T(128)} %placement.1) | copy-start | bytes 196
  0.0 12.7 %copy-start.5 = (s32[2]{0:T(128)S(1)}, s32[2]{0:T(128)}, u32[]{:S(2)}) copy-start(s32[2]{0:T(128)} %lengths.1) | copy-start | bytes 28
  0.0 12.7 %copy-start.6 = (s32[16]{0:T(128)S(1)}, s32[16]{0:T(128)}, u32[]{:S(2)}) copy-start(s32[16]{0:T(128)} %last.1) | copy-start | bytes 196
  5.3 19.6 %all-to-all-start = ((bf16[16,96,128]{2,1,0:T(8,128)(2,1)}), bf16[16,96,128]{2,1,0:T(8,128)(2,1)S(1)}, u32[]{:S(2)}, u32[]{:S(2)}) async-start(bf16[16,96,128]{2,1,0:T(8,128)(2,1)} %project.1), calls=%async_computation | async-start | bytes 786432 | tf_op jit(solution)/shard_map/all_to_all | solution.py:318

commit v6 on v5

--- a/solution.py
+++ b/solution.py
@@ -34,9 +34,9 @@
 
 
 def project_kernel(
-    dec_rows, chunks, devices, tenant_h, table_h, counts_h, placement_h, hidden, weight, down, up, out,
+    dec_rows, d_chunks, chunks, devices, tenant_h, table_h, counts_h, placement_h, hidden, weight, down, up, out,
     tenant, table, counts, placement,
-    h_s, w_s, d_s, mine_s, u_s, sel_s, part_s, base_s, dest_table, sems, int_sems,
+    h_s, w_s, d_s, mine_s, u_s, sel_s, part_s, base_s, dest_table, sems, d_sems, int_sems,
 ):
     tokens, width = hidden.shape
     features = weight.shape[0]
@@ -44,7 +44,7 @@
     tenants = table.shape[0]
     requests = tenant.shape[0]
     me = lax.axis_index("tensor")
-    d_step = local // chunks
+    d_step = local // d_chunks
     step = width // chunks
 
     int_copies = [
@@ -55,18 +55,23 @@
     ]
     for copy in int_copies:
         copy.start()
-    d_copies, h_copies, w_copies = [], [], []
-    for c in range(chunks):
-        d_copies.append(pltpu.make_async_copy(
-            down.at[pl.ds(c * d_step, d_step)], d_s.at[pl.ds(c * d_step, d_step)], sems.at[c, 0]))
-        h_copies.append(pltpu.make_async_copy(
-            hidden.at[:, pl.ds(c * step, step)], h_s.at[c], sems.at[c, 1]))
-        w_copies.append(pltpu.make_async_copy(
-            weight.at[:, pl.ds(c * step, step)], w_s.at[c], sems.at[c, 2]))
+    d_copies = [
+        pltpu.make_async_copy(
+            down.at[pl.ds(c * d_step, d_step)], d_s.at[pl.ds(c * d_step, d_step)], d_sems.at[c])
+        for c in range(d_chunks)
+    ]
+    h_copies = [
+        pltpu.make_async_copy(hidden.at[:, pl.ds(c * step, step)], h_s.at[c], sems.at[c, 0])
+        for c in range(chunks)
+    ]
+    w_copies = [
+        pltpu.make_async_copy(weight.at[:, pl.ds(c * step, step)], w_s.at[c], sems.at[c, 1])
+        for c in range(chunks)
+    ]
     my_copy = pltpu.make_async_copy(
-        hidden.at[:, pl.ds(pl.multiple_of(me * local, 128), local)], mine_s, sems.at[0, 3]
-    )
-    up_copy = pltpu.make_async_copy(up, u_s, sems.at[1, 3])
+        hidden.at[:, pl.ds(pl.multiple_of(me * local, 128), local)], mine_s, d_sems.at[d_chunks]
+    )
+    up_copy = pltpu.make_async_copy(up, u_s, d_sems.at[d_chunks + 1])
     for copy in d_copies + [my_copy, up_copy]:
         copy.start()
     for c in range(chunks):
@@ -82,7 +87,7 @@
     pick = (mod(rows, 16) == div(cols, pages)) & (mod(cols, pages) == page_of_row)
     pick = jnp.where(pick, jnp.float32(1), jnp.float32(0)).astype(jnp.bfloat16)
 
-    for c in range(chunks):
+    for c in range(d_chunks):
         d_copies[c].wait()
         for b in range(c * d_step // 16, (c + 1) * d_step // 16, 2):
             block = jnp.concatenate(
@@ -115,27 +120,27 @@
             part_s[k + j, :tokens] = product[:, j * rank2 : (j + 1) * rank2]
             part_s[k + j, tokens:] = jnp.zeros((BLK, rank2), jnp.float32)
 
-    total = jnp.zeros((tokens, features), jnp.float32)
-    for c in range(chunks):
-        h_copies[c].wait()
-        w_copies[c].wait()
-        total = total + lax.dot_general(
-            h_s[c], w_s[c], (((1,), (1,)), ((), ())), preferred_element_type=jnp.float32
-        )
-    base_s[tokens:] = jnp.zeros((BLK, HD), jnp.float32)
-    if features < HD:
-        base_s[...] = jnp.zeros_like(base_s)
-    base_s[:tokens, :features] = total
-
     up_copy.wait()
     for dest in range(devices):
         start = pl.multiple_of(dest_table[0, dest], BLK)
         who = dest_table[1, dest]
         out[dest, :CAPT, :] = part_s[who, pl.ds(start, CAPT), :].astype(out.dtype)
-        out[dest, CAPT : 2 * CAPT, :] = base_s[pl.ds(start, CAPT), :].astype(out.dtype)
         if features < HD:
             out[dest, 2 * CAPT :, :] = jnp.zeros((out.shape[1] - 2 * CAPT, HD), out.dtype)
         out[dest, 2 * CAPT :, :features] = u_s[table[who]]
+
+    total = jnp.zeros((tokens, features), jnp.float32)
+    for c in range(chunks):
+        h_copies[c].wait()
+        w_copies[c].wait()
+        total = total + lax.dot_general(h_s[c], w_s[c], NT, preferred_element_type=jnp.float32)
+    base_s[tokens:] = jnp.zeros((BLK, HD), jnp.float32)
+    if features < HD:
+        base_s[...] = jnp.zeros_like(base_s)
+    base_s[:tokens, :features] = total
+    for dest in range(devices):
+        start = pl.multiple_of(dest_table[0, dest], BLK)
+        out[dest, CAPT : 2 * CAPT, :] = base_s[pl.ds(start, CAPT), :].astype(out.dtype)
 
 
 NT = (((1,), (1,)), ((), ()))
@@ -218,29 +223,37 @@
     fresh_ok[...] = jnp.where(ok, jnp.float32(1), jnp.float32(0))
 
 
-def merge_kernel(features, box, acc, top_in, total_in, fresh_ok, query, out):
+def merge_kernel(features, box, acc, top_in, total_in, fresh_ok, query, out, result, sems):
     devices = box.shape[0]
     rank = box.shape[1] - 2 * CAPT
-    shrunk = box[0, :CAPT].astype(jnp.float32)
-    for i in range(1, devices):
-        shrunk = shrunk + box[i, :CAPT].astype(jnp.float32)
-    shrunk = shrunk.astype(jnp.bfloat16)
+    terms = [box[i, :CAPT].astype(jnp.float32) for i in range(devices)]
+    while len(terms) > 1:
+        pairs = [a + b for a, b in zip(terms[::2], terms[1::2])]
+        terms = pairs + terms[2 * len(pairs) :]
+    shrunk = terms[0].astype(jnp.bfloat16)
     halves = (shrunk[:, :rank], shrunk[:, rank:])
     pieces = HD // features
 
-    def fresh(i):
-        base = [box[i * pieces + p, CAPT : 2 * CAPT, :features] for p in range(pieces)]
-        ups = [box[i * pieces + p, 2 * CAPT :, :features] for p in range(pieces)]
-        base = base[0] if pieces == 1 else jnp.concatenate(base, axis=1)
-        ups = ups[0] if pieces == 1 else jnp.concatenate(ups, axis=1)
-        delta = jnp.dot(halves[i // KVH], ups, preferred_element_type=jnp.float32)
-        return (base.astype(jnp.float32) + ADAPTER_SCALE * delta).astype(jnp.bfloat16)
-
-    keys = jnp.concatenate([fresh(k) for k in range(KVH)], axis=0)
-    values = jnp.concatenate([fresh(KVH + k) for k in range(KVH)], axis=0)
+    def rows(i, first, count):
+        parts = [box[i * pieces + p, first : first + count, :features] for p in range(pieces)]
+        return parts[0] if pieces == 1 else jnp.concatenate(parts, axis=1)
+
+    def fresh(first):
+        made = []
+        for i in range(first, first + KVH, 2):
+            ups = jnp.concatenate([rows(i + j, 2 * CAPT, rank) for j in range(2)], axis=1)
+            delta = jnp.dot(halves[first // KVH], ups, preferred_element_type=jnp.float32)
+            for j in range(2):
+                base = rows(i + j, CAPT, CAPT).astype(jnp.float32)
+                both = base + ADAPTER_SCALE * delta[:, j * HD : (j + 1) * HD]
+                made.append(both.astype(jnp.bfloat16))
+        return jnp.concatenate(made, axis=0)
+
+    keys, values = fresh(0), fresh(KVH)
     scale = HD ** (-0.5)
-    part = 128
-    for c in range(out.shape[0] // part):
+    part = out.shape[0] // sems.shape[0]
+    copies = []
+    for c in range(sems.shape[0]):
         here = pl.ds(c * part, part)
         s = lax.dot_general(query[here, :], keys, NT, preferred_element_type=jnp.float32)
         s = jnp.where(fresh_ok[here, :] > 0, s * scale, NEG_LARGE)
@@ -252,7 +265,11 @@
         mixed = acc[here, :] * fade + jnp.dot(
             w.astype(jnp.bfloat16), values, preferred_element_type=jnp.float32
         )
-        out[here, :] = (mixed / total).astype(jnp.bfloat16)
+        result[here, :] = (mixed / total).astype(jnp.bfloat16)
+        copies.append(pltpu.make_async_copy(result.at[here, :], out.at[here, :], sems.at[c]))
+        copies[c].start()
+    for copy in copies:
+        copy.wait()
 
 
 def body(
@@ -279,11 +296,11 @@
     dec_rows, ctx, kv_width = key_value_cache.shape
     steps = step_key_value.shape[0]
     heads2 = kv_width // HD
-    chunks = 4
+    d_chunks, chunks = 4, 8
     up_by_page = jnp.transpose(adapter_up_weight, (1, 2, 0))
     rows = 2 * CAPT + rank
     outgoing = pl.pallas_call(
-        functools.partial(project_kernel, dec_rows, chunks, devices),
+        functools.partial(project_kernel, dec_rows, d_chunks, chunks, devices),
         out_shape=pltpu.VMEM((devices, rows, HD), WIRE),
         in_specs=[ANY_SPEC] * 8,
         out_specs=VMEM_SPEC,
@@ -301,7 +318,8 @@
             pltpu.VMEM((tenants, tokens + BLK, rank2), jnp.float32),
             pltpu.VMEM((tokens + BLK, HD), jnp.float32),
             pltpu.SMEM((2, devices), jnp.int32),
-            pltpu.SemaphoreType.DMA((chunks, 4)),
+            pltpu.SemaphoreType.DMA((chunks, 2)),
+            pltpu.SemaphoreType.DMA((d_chunks + 2,)),
             pltpu.SemaphoreType.DMA((4,)),
         ],
         compiler_params=pltpu.CompilerParams(vmem_limit_bytes=PROJECT_VMEM),
@@ -337,7 +355,11 @@
         functools.partial(merge_kernel, features),
         out_shape=jax.ShapeDtypeStruct((steps * HEADS * dec_rows, HD), jnp.bfloat16),
         in_specs=[VMEM_SPEC] * 6,
-        out_specs=VMEM_SPEC,
+        out_specs=ANY_SPEC,
+        scratch_shapes=[
+            pltpu.VMEM((steps * HEADS * dec_rows, HD), jnp.bfloat16),
+            pltpu.SemaphoreType.DMA((steps,)),
+        ],
         compiler_params=pltpu.CompilerParams(vmem_limit_bytes=ATTEND_VMEM),
         name="merge",
     )(arrived, acc, top, total, fresh_ok, query)

time: 27 us -> 28.2 us (1.044)
  Pallas kernels: 10 us -> 11.2 us
    pallas_call x1, Pallas kernels: 5.22 us -> 6.49 us  [body(): pl.pallas_call(functools.partial(project_kernel, dec_rows, d_chunks, chun...]
  transfers between devices with their start and end apart: 1 -> 1, of which waited for: 1 -> 1; matrix products, arithmetic and copies ran while one was open for 0% -> 0% of each run, Pallas kernels for 11% -> 10%
where the time goes in v6:
time: 28.2 us; the launch traced here: 28 us
  Pallas kernels  11.2 us (40%)
  waiting for transfers between devices  9.22 us (33%)
  starting transfers between devices  7.41 us (26%)
    all_to_all x1, waiting for transfers between devices, body(): lax.all_to_all(outgoing, 'tensor', split_axis=0, concat_axis=0, tiled=True)  9.22 us
    all_to_all x1, starting transfers between devices, body(): lax.all_to_all(outgoing, 'tensor', split_axis=0, concat_axis=0, tiled=True)  7.41 us
    pallas_call x1, Pallas kernels, body(): pl.pallas_call(functools.partial(project_kernel, dec_rows, d_chunks, chun...  6.49 us
    pallas_call x1, Pallas kernels, body(): pl.pallas_call(cached_kernel, out_shape=(state,) * 4, in_specs=[SMEM_SPEC...  2.9 us
    pallas_call x1, Pallas kernels, body(): pl.pallas_call(functools.partial(merge_kernel, features), out_shape=jax.S...  1.87 us
  transfers between devices with their start and end apart: 1, of which 1 were waited for; matrix products, arithmetic and copies ran while one was open for 0% of the time, Pallas kernels for 10%

profile of v6, /device:TPU:0, one launch (start us, length us, event | category | flops | bytes accessed | tf_op | source)
XLA Modules:
  0.0 28.0 jit_solution(13030552000404227608)
XLA Ops:
  0.0 0.0 copy-start
  0.0 0.0 copy-start.1
  0.0 0.0 copy-start.2
  0.0 0.0 copy-start.3
  0.0 0.0 copy-start.4
  0.0 0.0 copy-start.5
  0.0 0.0 copy-start.6
  0.0 6.5 %project.1 = bf16[16,96,128]{2,1,0:T(8,128)(2,1)} custom-call(s32[16]{0:T(128)} %tenant_h.1, s32[8]{0:T(128)} %table_h.1, s32[16]{0:T(128)} %counts.1, s32[16]{0:T(128)} %placement.1, bf16[160,8192]{1,0:T(8,128)(2,1)} %hidden.1, bf16[128,8192]{1,0:T(8,128)(2,1)} %weight.1, bf16[512,16,128]{2,1,0:T(8,128)(2,1)} %down.1, bf16[16,64,128]{2,1,0:T(8,128)(2,1)} %bitcast.19), custom_call_target="tpu_custom_call" | custom-call | tf_op jit(solution)/shard_map/project/pallas_call | solution.py:302
  6.5 7.4 %all-to-all-start = ((bf16[16,96,128]{2,1,0:T(8,128)(2,1)}), bf16[16,96,128]{2,1,0:T(8,128)(2,1)S(1)}, u32[]{:S(2)}, u32[]{:S(2)}) async-start(bf16[16,96,128]{2,1,0:T(8,128)(2,1)} %project.1), calls=%async_computation | async-start | bytes 786432 | tf_op jit(solution)/shard_map/all_to_all | solution.py:336
  13.9 0.0 copy-done
  14.0 0.0 copy-done.1
  14.0 0.0 copy-done.2
  14.0 0.0 copy-done.3
  14.0 0.0 copy-done.4
  14.0 0.0 copy-done.5
  14.0 0.0 copy-done.6
  14.0 2.9 %cached.1 = (f32[512,128]{1,0:T(8,128)S(1)}, f32[512,128]{1,0:T(8,128)S(1)}, f32[512,128]{1,0:T(8,128)S(1)}, f32[512,128]{1,0:T(8,128)S(1)}) custom-call(s32[2]{0:T(128)S(1)} %copy-done.5, s32[16]{0:T(128)S(1)} %copy-done.3, s32[16]{0:T(128)S(1)} %copy-done.6, s32[16]{0:T(128)S(1)} %copy-done.4, bf16[2,128,2048]{2,1,0:T(8,128)(2,1)S(1)} %copy-done, ...), custom_call_target="tpu_custom_call" | custom-call | tf_op jit(solution)/shard_map/cached/pallas_call | solution.py:343
  16.9 9.2 %all-to-all-done.box = bf16[16,96,128]{2,1,0:T(8,128)(2,1)S(1)} async-done(((bf16[16,96,128]{2,1,0:T(8,128)(2,1)}), bf16[16,96,128]{2,1,0:T(8,128)(2,1)S(1)}, u32[]{:S(2)}, u32[]{:S(2)}) %all-to-all-start) | async-done | bytes 393248 | tf_op jit(solution)/shard_map/all_to_all | solution.py:336
  26.1 1.9 %merge.1 = bf16[512,128]{1,0:T(8,128)(2,1)} custom-call(bf16[16,96,128]{2,1,0:T(8,128)(2,1)S(1)} %all-to-all-done.box, f32[512,128]{1,0:T(8,128)S(1)} %get-tuple-element.9.acc, f32[512,128]{1,0:T(8,128)S(1)} %get-tuple-element.10.top_in, f32[512,128]{1,0:T(8,128)S(1)} %get-tuple-element.11.total_in, f32[512,128]{1,0:T(8,128)S(1)} %get-tuple-element.12.fresh_ok, ...), custom_call_target="tpu_custom_call" | custom-call | tf_op jit(solution)/shard_map/merge/pallas_call | solution.py:354
Async XLA Ops:
  0.0 13.9 %copy-start = (bf16[2,128,2048]{2,1,0:T(8,128)(2,1)S(1)}, bf16[2,128,2048]{2,1,0:T(8,128)(2,1)}, u32[]{:S(2)}) copy-start(bf16[2,128,2048]{2,1,0:T(8,128)(2,1)} %cache.1) | copy-start | bytes 3145732
  0.0 14.0 %copy-start.1 = (bf16[4,2,8192]{2,1,0:T(2,128)(2,1)S(1)}, bf16[4,2,8192]{2,1,0:T(2,128)(2,1)}, u32[]{:S(2)}) copy-start(bf16[4,2,8192]{2,1,0:T(2,128)(2,1)} %param.24) | copy-start | bytes 393220
  0.0 14.0 %copy-start.2 = (bf16[4,2,2048]{2,1,0:T(2,128)(2,1)S(1)}, bf16[4,2,2048]{2,1,0:T(2,128)(2,1)}, u32[]{:S(2)}) copy-start(bf16[4,2,2048]{2,1,0:T(2,128)(2,1)} %param.25) | copy-start | bytes 98308
  0.0 14.0 %copy-start.3 = (s32[16]{0:T(128)S(1)}, s32[16]{0:T(128)}, u32[]{:S(2)}) copy-start(s32[16]{0:T(128)} %counts.1) | copy-start | bytes 196
  0.0 14.0 %copy-start.4 = (s32[16]{0:T(128)S(1)}, s32[16]{0:T(128)}, u32[]{:S(2)}) copy-start(s32[16]{0:T(128)} %placement.1) | copy-start | bytes 196
  0.0 14.0 %copy-start.5 = (s32[2]{0:T(128)S(1)}, s32[2]{0:T(128)}, u32[]{:S(2)}) copy-start(s32[2]{0:T(128)} %lengths.1) | copy-start | bytes 28
  0.0 14.0 %copy-start.6 = (s32[16]{0:T(128)S(1)}, s32[16]{0:T(128)}, u32[]{:S(2)}) copy-start(s32[16]{0:T(128)} %last.1) | copy-start | bytes 196
  6.5 19.6 %all-to-all-start = ((bf16[16,96,128]{2,1,0:T(8,128)(2,1)}), bf16[16,96,128]{2,1,0:T(8,128)(2,1)S(1)}, u32[]{:S(2)}, u32[]{:S(2)}) async-start(bf16[16,96,128]{2,1,0:T(8,128)(2,1)} %project.1), calls=%async_computation | async-start | bytes 786432 | tf_op jit(solution)/shard_map/all_to_all | solution.py:336

commit v7 on v6

--- a/solution.py
+++ b/solution.py
@@ -120,15 +120,6 @@
             part_s[k + j, :tokens] = product[:, j * rank2 : (j + 1) * rank2]
             part_s[k + j, tokens:] = jnp.zeros((BLK, rank2), jnp.float32)
 
-    up_copy.wait()
-    for dest in range(devices):
-        start = pl.multiple_of(dest_table[0, dest], BLK)
-        who = dest_table[1, dest]
-        out[dest, :CAPT, :] = part_s[who, pl.ds(start, CAPT), :].astype(out.dtype)
-        if features < HD:
-            out[dest, 2 * CAPT :, :] = jnp.zeros((out.shape[1] - 2 * CAPT, HD), out.dtype)
-        out[dest, 2 * CAPT :, :features] = u_s[table[who]]
-
     total = jnp.zeros((tokens, features), jnp.float32)
     for c in range(chunks):
         h_copies[c].wait()
@@ -138,9 +129,15 @@
     if features < HD:
         base_s[...] = jnp.zeros_like(base_s)
     base_s[:tokens, :features] = total
+    up_copy.wait()
     for dest in range(devices):
         start = pl.multiple_of(dest_table[0, dest], BLK)
+        who = dest_table[1, dest]
+        out[dest, :CAPT, :] = part_s[who, pl.ds(start, CAPT), :].astype(out.dtype)
         out[dest, CAPT : 2 * CAPT, :] = base_s[pl.ds(start, CAPT), :].astype(out.dtype)
+        if features < HD:
+            out[dest, 2 * CAPT :, :] = jnp.zeros((out.shape[1] - 2 * CAPT, HD), out.dtype)
+        out[dest, 2 * CAPT :, :features] = u_s[table[who]]
 
 
 NT = (((1,), (1,)), ((), ()))
@@ -296,7 +293,7 @@
     dec_rows, ctx, kv_width = key_value_cache.shape
     steps = step_key_value.shape[0]
     heads2 = kv_width // HD
-    d_chunks, chunks = 4, 8
+    d_chunks, chunks = 2, 2
     up_by_page = jnp.transpose(adapter_up_weight, (1, 2, 0))
     rows = 2 * CAPT + rank
     outgoing = pl.pallas_call(

time: 28.2 us -> 27 us (0.957)
  Pallas kernels: 11.2 us -> 10 us
    pallas_call x1, Pallas kernels: 6.49 us -> 5.26 us  [body(): pl.pallas_call(functools.partial(project_kernel, dec_rows, d_chunks, chun...]
  transfers between devices with their start and end apart: 1 -> 1, of which waited for: 1 -> 1; matrix products, arithmetic and copies ran while one was open for 0% -> 0% of each run, Pallas kernels for 10% -> 11%
where the time goes in v7:
time: 27 us; the launch traced here: 26.8 us
  Pallas kernels  10 us (37%)
  waiting for transfers between devices  9.22 us (34%)
  starting transfers between devices  7.41 us (27%)
    all_to_all x1, waiting for transfers between devices, body(): lax.all_to_all(outgoing, 'tensor', split_axis=0, concat_axis=0, tiled=True)  9.22 us
    all_to_all x1, starting transfers between devices, body(): lax.all_to_all(outgoing, 'tensor', split_axis=0, concat_axis=0, tiled=True)  7.41 us
    pallas_call x1, Pallas kernels, body(): pl.pallas_call(functools.partial(project_kernel, dec_rows, d_chunks, chun...  5.26 us
    pallas_call x1, Pallas kernels, body(): pl.pallas_call(cached_kernel, out_shape=(state,) * 4, in_specs=[SMEM_SPEC...  2.9 us
    pallas_call x1, Pallas kernels, body(): pl.pallas_call(functools.partial(merge_kernel, features), out_shape=jax.S...  1.87 us
  transfers between devices with their start and end apart: 1, of which 1 were waited for; matrix products, arithmetic and copies ran while one was open for 0% of the time, Pallas kernels for 11%

profile of v7, /device:TPU:0, one launch (start us, length us, event | category | flops | bytes accessed | tf_op | source)
XLA Modules:
  0.0 26.8 jit_solution(17413175366401920809)
XLA Ops:
  0.0 0.0 copy-start
  0.0 0.0 copy-start.1
  0.0 0.0 copy-start.2
  0.0 0.0 copy-start.3
  0.0 0.0 copy-start.4
  0.0 0.0 copy-start.5
  0.0 0.0 copy-start.6
  0.0 5.3 %project.1 = bf16[16,96,128]{2,1,0:T(8,128)(2,1)} custom-call(s32[16]{0:T(128)} %tenant_h.1, s32[8]{0:T(128)} %table_h.1, s32[16]{0:T(128)} %counts.1, s32[16]{0:T(128)} %placement.1, bf16[160,8192]{1,0:T(8,128)(2,1)} %hidden.1, bf16[128,8192]{1,0:T(8,128)(2,1)} %weight.1, bf16[512,16,128]{2,1,0:T(8,128)(2,1)} %down.1, bf16[16,64,128]{2,1,0:T(8,128)(2,1)} %bitcast.19), custom_call_target="tpu_custom_call" | custom-call | tf_op jit(solution)/shard_map/project/pallas_call | solution.py:299
  5.3 7.4 %all-to-all-start = ((bf16[16,96,128]{2,1,0:T(8,128)(2,1)}), bf16[16,96,128]{2,1,0:T(8,128)(2,1)S(1)}, u32[]{:S(2)}, u32[]{:S(2)}) async-start(bf16[16,96,128]{2,1,0:T(8,128)(2,1)} %project.1), calls=%async_computation | async-start | bytes 786432 | tf_op jit(solution)/shard_map/all_to_all | solution.py:333
  12.7 0.0 copy-done
  12.7 0.0 copy-done.1
  12.7 0.0 copy-done.2
  12.8 0.0 copy-done.3
  12.8 0.0 copy-done.4
  12.8 0.0 copy-done.5
  12.8 0.0 copy-done.6
  12.8 2.9 %cached.1 = (f32[512,128]{1,0:T(8,128)S(1)}, f32[512,128]{1,0:T(8,128)S(1)}, f32[512,128]{1,0:T(8,128)S(1)}, f32[512,128]{1,0:T(8,128)S(1)}) custom-call(s32[2]{0:T(128)S(1)} %copy-done.5, s32[16]{0:T(128)S(1)} %copy-done.3, s32[16]{0:T(128)S(1)} %copy-done.6, s32[16]{0:T(128)S(1)} %copy-done.4, bf16[2,128,2048]{2,1,0:T(8,128)(2,1)S(1)} %copy-done, ...), custom_call_target="tpu_custom_call" | custom-call | tf_op jit(solution)/shard_map/cached/pallas_call | solution.py:340
  15.7 9.2 %all-to-all-done.box = bf16[16,96,128]{2,1,0:T(8,128)(2,1)S(1)} async-done(((bf16[16,96,128]{2,1,0:T(8,128)(2,1)}), bf16[16,96,128]{2,1,0:T(8,128)(2,1)S(1)}, u32[]{:S(2)}, u32[]{:S(2)}) %all-to-all-start) | async-done | bytes 393248 | tf_op jit(solution)/shard_map/all_to_all | solution.py:333
  24.9 1.9 %merge.1 = bf16[512,128]{1,0:T(8,128)(2,1)} custom-call(bf16[16,96,128]{2,1,0:T(8,128)(2,1)S(1)} %all-to-all-done.box, f32[512,128]{1,0:T(8,128)S(1)} %get-tuple-element.9.acc, f32[512,128]{1,0:T(8,128)S(1)} %get-tuple-element.10.top_in, f32[512,128]{1,0:T(8,128)S(1)} %get-tuple-element.11.total_in, f32[512,128]{1,0:T(8,128)S(1)} %get-tuple-element.12.fresh_ok, ...), custom_call_target="tpu_custom_call" | custom-call | tf_op jit(solution)/shard_map/merge/pallas_call | solution.py:351
Async XLA Ops:
  0.0 12.7 %copy-start = (bf16[2,128,2048]{2,1,0:T(8,128)(2,1)S(1)}, bf16[2,128,2048]{2,1,0:T(8,128)(2,1)}, u32[]{:S(2)}) copy-start(bf16[2,128,2048]{2,1,0:T(8,128)(2,1)} %cache.1) | copy-start | bytes 3145732
  0.0 12.7 %copy-start.1 = (bf16[4,2,8192]{2,1,0:T(2,128)(2,1)S(1)}, bf16[4,2,8192]{2,1,0:T(2,128)(2,1)}, u32[]{:S(2)}) copy-start(bf16[4,2,8192]{2,1,0:T(2,128)(2,1)} %param.24) | copy-start | bytes 393220
  0.0 12.7 %copy-start.2 = (bf16[4,2,2048]{2,1,0:T(2,128)(2,1)S(1)}, bf16[4,2,2048]{2,1,0:T(2,128)(2,1)}, u32[]{:S(2)}) copy-start(bf16[4,2,2048]{2,1,0:T(2,128)(2,1)} %param.25) | copy-start | bytes 98308
  0.0 12.7 %copy-start.3 = (s32[16]{0:T(128)S(1)}, s32[16]{0:T(128)}, u32[]{:S(2)}) copy-start(s32[16]{0:T(128)} %counts.1) | copy-start | bytes 196
  0.0 12.8 %copy-start.4 = (s32[16]{0:T(128)S(1)}, s32[16]{0:T(128)}, u32[]{:S(2)}) copy-start(s32[16]{0:T(128)} %placement.1) | copy-start | bytes 196
  0.0 12.8 %copy-start.5 = (s32[2]{0:T(128)S(1)}, s32[2]{0:T(128)}, u32[]{:S(2)}) copy-start(s32[2]{0:T(128)} %lengths.1) | copy-start | bytes 28
  0.0 12.8 %copy-start.6 = (s32[16]{0:T(128)S(1)}, s32[16]{0:T(128)}, u32[]{:S(2)}) copy-start(s32[16]{0:T(128)} %last.1) | copy-start | bytes 196
  5.3 19.6 %all-to-all-start = ((bf16[16,96,128]{2,1,0:T(8,128)(2,1)}), bf16[16,96,128]{2,1,0:T(8,128)(2,1)S(1)}, u32[]{:S(2)}, u32[]{:S(2)}) async-start(bf16[16,96,128]{2,1,0:T(8,128)(2,1)} %project.1), calls=%async_computation | async-start | bytes 786432 | tf_op jit(solution)/shard_map/all_to_all | solution.py:333

commit v8 on v7

--- a/solution.py
+++ b/solution.py
@@ -34,97 +34,90 @@
 
 
 def project_kernel(
-    dec_rows, d_chunks, chunks, devices, tenant_h, table_h, counts_h, placement_h, hidden, weight, down, up, out,
+    dec_rows, cuts, tenant_h, table_h, counts_h, placement_h, hidden, weight, down, up, out,
     tenant, table, counts, placement,
-    h_s, w_s, d_s, mine_s, u_s, sel_s, part_s, base_s, dest_table, sems, d_sems, int_sems,
+    h_s, w_s, d_s, mine_s, u_s, spread_s, part_s, base_s, dest_table, hw_sems, sems,
 ):
     tokens, width = hidden.shape
     features = weight.shape[0]
     local, pages, rank2 = down.shape
-    tenants = table.shape[0]
     requests = tenant.shape[0]
+    devices = out.shape[0]
     me = lax.axis_index("tensor")
-    d_step = local // d_chunks
-    step = width // chunks
-
+
+    my_copy = pltpu.make_async_copy(
+        hidden.at[:, pl.ds(pl.multiple_of(me * local, 128), local)], mine_s, sems.at[0]
+    )
     int_copies = [
-        pltpu.make_async_copy(src, dst, int_sems.at[i])
+        pltpu.make_async_copy(src, dst, sems.at[3 + i])
         for i, (src, dst) in enumerate(
             ((table_h, table), (tenant_h, tenant), (counts_h, counts), (placement_h, placement))
         )
     ]
+    d_copy = pltpu.make_async_copy(down, d_s, sems.at[1])
+    up_copy = pltpu.make_async_copy(up, u_s, sems.at[2])
+    for copy in [my_copy] + int_copies + [d_copy]:
+        copy.start()
+    hw_copies = []
+    for c, (first, last) in enumerate(zip(cuts[:-1], cuts[1:])):
+        lanes = pl.ds(first, last - first)
+        pair = (
+            pltpu.make_async_copy(hidden.at[:, lanes], h_s.at[:, lanes], hw_sems.at[c, 0]),
+            pltpu.make_async_copy(weight.at[:, lanes], w_s.at[:, lanes], hw_sems.at[c, 1]),
+        )
+        for copy in pair:
+            copy.start()
+        hw_copies.append(pair)
+    up_copy.start()
+
+    per_tile = 256 // pages
+    tiles = 128 // per_tile
+    row = lax.broadcasted_iota(jnp.int32, (128, 256), 0)
+    col = lax.broadcasted_iota(jnp.int32, (128, 256), 1)
+    spreads = [
+        jnp.where(row == div(col, pages) + j * per_tile, jnp.float32(1), jnp.float32(0)).astype(
+            jnp.bfloat16
+        )
+        for j in range(tiles)
+    ]
     for copy in int_copies:
-        copy.start()
-    d_copies = [
-        pltpu.make_async_copy(
-            down.at[pl.ds(c * d_step, d_step)], d_s.at[pl.ds(c * d_step, d_step)], d_sems.at[c])
-        for c in range(d_chunks)
-    ]
-    h_copies = [
-        pltpu.make_async_copy(hidden.at[:, pl.ds(c * step, step)], h_s.at[c], sems.at[c, 0])
-        for c in range(chunks)
-    ]
-    w_copies = [
-        pltpu.make_async_copy(weight.at[:, pl.ds(c * step, step)], w_s.at[c], sems.at[c, 1])
-        for c in range(chunks)
-    ]
-    my_copy = pltpu.make_async_copy(
-        hidden.at[:, pl.ds(pl.multiple_of(me * local, 128), local)], mine_s, d_sems.at[d_chunks]
-    )
-    up_copy = pltpu.make_async_copy(up, u_s, d_sems.at[d_chunks + 1])
-    for copy in d_copies + [my_copy, up_copy]:
-        copy.start()
-    for c in range(chunks):
-        h_copies[c].start()
-        w_copies[c].start()
-
-    int_copies[0].wait()
-    rows = lax.broadcasted_iota(jnp.int32, (tenants * 16, 16 * pages), 0)
-    cols = lax.broadcasted_iota(jnp.int32, (tenants * 16, 16 * pages), 1)
-    page_of_row = jnp.zeros_like(rows)
-    for k in range(tenants):
-        page_of_row = jnp.where(div(rows, 16) == k, table[k], page_of_row)
-    pick = (mod(rows, 16) == div(cols, pages)) & (mod(cols, pages) == page_of_row)
-    pick = jnp.where(pick, jnp.float32(1), jnp.float32(0)).astype(jnp.bfloat16)
-
-    for c in range(d_chunks):
-        d_copies[c].wait()
-        for b in range(c * d_step // 16, (c + 1) * d_step // 16, 2):
-            block = jnp.concatenate(
-                [d_s[pl.ds((b + i) * 16, 16)].reshape(16 * pages, rank2) for i in range(2)], axis=1
-            )
-            chosen = jnp.dot(pick, block, preferred_element_type=jnp.float32)
-            for i in range(2):
-                sel_s[b + i] = chosen[:, i * rank2 : (i + 1) * rank2].astype(jnp.bfloat16)
-    for copy in int_copies[1:]:
         copy.wait()
     for dest in range(devices):
         dest_table[0, dest] = 0
         dest_table[1, dest] = 0
+    row = lax.broadcasted_iota(jnp.int32, (tokens, 128), 0)
+    page_of_token = jnp.zeros_like(row)
     first = jnp.int32(0)
     for r in range(requests):
         dest = div(placement[r], dec_rows)
+        page = table[tenant[r]]
         dest_table[0, dest] = first * BLK
-        dest_table[1, dest] = tenant[r]
+        dest_table[1, dest] = page
+        page_of_token = jnp.where(row >= first * BLK, page, page_of_token)
         first = first + counts[r]
+    own_page = mod(lax.broadcasted_iota(jnp.int32, (tokens, 128), 1), pages) == page_of_token
+    own_page = jnp.concatenate([own_page, own_page], axis=1)
+
     my_copy.wait()
-    mine = mine_s[...]
-    for k in range(0, tenants, 2):
-        pair = min(2, tenants - k)
-        maps = jnp.concatenate(
-            [sel_s[:, j * 16 : (j + 1) * 16, :].reshape(local, rank2) for j in range(k, k + pair)],
-            axis=1,
-        )
-        product = jnp.dot(mine, maps, preferred_element_type=jnp.float32)
-        for j in range(pair):
-            part_s[k + j, :tokens] = product[:, j * rank2 : (j + 1) * rank2]
-            part_s[k + j, tokens:] = jnp.zeros((BLK, rank2), jnp.float32)
+    for g in range(local // 128):
+        mine = mine_s[:, g * 128 : (g + 1) * 128]
+        for j in range(tiles):
+            wide = jnp.dot(mine, spreads[j], preferred_element_type=jnp.float32)
+            wide = jnp.where(own_page, wide, jnp.float32(0)).astype(jnp.bfloat16)
+            spread_s[:, pl.ds((g * tiles + j) * 256, 256)] = wide
+    d_copy.wait()
+    part_s[tokens:] = jnp.zeros((BLK, rank2), jnp.float32)
+    part_s[:tokens] = jnp.dot(
+        spread_s[...], d_s[...].reshape(local * pages, rank2), preferred_element_type=jnp.float32
+    )
 
     total = jnp.zeros((tokens, features), jnp.float32)
-    for c in range(chunks):
-        h_copies[c].wait()
-        w_copies[c].wait()
-        total = total + lax.dot_general(h_s[c], w_s[c], NT, preferred_element_type=jnp.float32)
+    for c, (first, last) in enumerate(zip(cuts[:-1], cuts[1:])):
+        for copy in hw_copies[c]:
+            copy.wait()
+        total = total + lax.dot_general(
+            h_s[:, first:last], w_s[:, first:last], NT, preferred_element_type=jnp.float32
+        )
     base_s[tokens:] = jnp.zeros((BLK, HD), jnp.float32)
     if features < HD:
         base_s[...] = jnp.zeros_like(base_s)
@@ -132,12 +125,11 @@
     up_copy.wait()
     for dest in range(devices):
         start = pl.multiple_of(dest_table[0, dest], BLK)
-        who = dest_table[1, dest]
-        out[dest, :CAPT, :] = part_s[who, pl.ds(start, CAPT), :].astype(out.dtype)
+        out[dest, :CAPT, :] = part_s[pl.ds(start, CAPT), :].astype(out.dtype)
         out[dest, CAPT : 2 * CAPT, :] = base_s[pl.ds(start, CAPT), :].astype(out.dtype)
         if features < HD:
             out[dest, 2 * CAPT :, :] = jnp.zeros((out.shape[1] - 2 * CAPT, HD), out.dtype)
-        out[dest, 2 * CAPT :, :features] = u_s[table[who]]
+        out[dest, 2 * CAPT :, :features] = u_s[dest_table[1, dest]]
 
 
 NT = (((1,), (1,)), ((), ()))
@@ -293,11 +285,11 @@
     dec_rows, ctx, kv_width = key_value_cache.shape
     steps = step_key_value.shape[0]
     heads2 = kv_width // HD
-    d_chunks, chunks = 2, 2
+    cuts = (0, width * 3 // 8, width * 6 // 8, width)
     up_by_page = jnp.transpose(adapter_up_weight, (1, 2, 0))
     rows = 2 * CAPT + rank
     outgoing = pl.pallas_call(
-        functools.partial(project_kernel, dec_rows, d_chunks, chunks, devices),
+        functools.partial(project_kernel, dec_rows, cuts),
         out_shape=pltpu.VMEM((devices, rows, HD), WIRE),
         in_specs=[ANY_SPEC] * 8,
         out_specs=VMEM_SPEC,
@@ -306,18 +298,17 @@
             pltpu.SMEM(tenant_page_table.shape, jnp.int32),
             pltpu.SMEM(request_block_count.shape, jnp.int32),
             pltpu.SMEM(placement.shape, jnp.int32),
-            pltpu.VMEM((chunks, tokens, width // chunks), jnp.bfloat16),
-            pltpu.VMEM((chunks, features, width // chunks), jnp.bfloat16),
+            pltpu.VMEM((tokens, width), jnp.bfloat16),
+            pltpu.VMEM((features, width), jnp.bfloat16),
             pltpu.VMEM((local, pages, rank2), jnp.bfloat16),
             pltpu.VMEM((tokens, local), jnp.bfloat16),
             pltpu.VMEM((pages, rank, features), jnp.bfloat16),
-            pltpu.VMEM((local // 16, tenants * 16, rank2), jnp.bfloat16),
-            pltpu.VMEM((tenants, tokens + BLK, rank2), jnp.float32),
+            pltpu.VMEM((tokens, local * pages), jnp.bfloat16),
+            pltpu.VMEM((tokens + BLK, rank2), jnp.float32),
             pltpu.VMEM((tokens + BLK, HD), jnp.float32),
             pltpu.SMEM((2, devices), jnp.int32),
-            pltpu.SemaphoreType.DMA((chunks, 2)),
-            pltpu.SemaphoreType.DMA((d_chunks + 2,)),
-            pltpu.SemaphoreType.DMA((4,)),
+            pltpu.SemaphoreType.DMA((len(cuts) - 1, 2)),
+            pltpu.SemaphoreType.DMA((7,)),
         ],
         compiler_params=pltpu.CompilerParams(vmem_limit_bytes=PROJECT_VMEM),
         name="project",

time: 27 us -> 27.9 us (1.033)
  Pallas kernels: 10 us -> 11 us
    pallas_call x1, Pallas kernels: 5.26 us -> 6.21 us  [body(): pl.pallas_call(functools.partial(project_kernel, dec_rows, cuts), out_sha...]
  transfers between devices with their start and end apart: 1 -> 1, of which waited for: 1 -> 1; matrix products, arithmetic and copies ran while one was open for 0% -> 0% of each run, Pallas kernels for 11% -> 10%
where the time goes in v8:
time: 27.9 us; the launch traced here: 27.7 us
  Pallas kernels  11 us (39%)
  waiting for transfers between devices  9.22 us (33%)
  starting transfers between devices  7.41 us (27%)
    all_to_all x1, waiting for transfers between devices, body(): lax.all_to_all(outgoing, 'tensor', split_axis=0, concat_axis=0, tiled=True)  9.22 us
    all_to_all x1, starting transfers between devices, body(): lax.all_to_all(outgoing, 'tensor', split_axis=0, concat_axis=0, tiled=True)  7.41 us
    pallas_call x1, Pallas kernels, body(): pl.pallas_call(functools.partial(project_kernel, dec_rows, cuts), out_sha...  6.21 us
    pallas_call x1, Pallas kernels, body(): pl.pallas_call(cached_kernel, out_shape=(state,) * 4, in_specs=[SMEM_SPEC...  2.9 us
    pallas_call x1, Pallas kernels, body(): pl.pallas_call(functools.partial(merge_kernel, features), out_shape=jax.S...  1.86 us
  transfers between devices with their start and end apart: 1, of which 1 were waited for; matrix products, arithmetic and copies ran while one was open for 0% of the time, Pallas kernels for 10%

profile of v8, /device:TPU:0, one launch (start us, length us, event | category | flops | bytes accessed | tf_op | source)
XLA Modules:
  0.0 27.7 jit_solution(13938180887151572688)
XLA Ops:
  0.0 0.0 copy-start
  0.0 0.0 copy-start.1
  0.0 0.0 copy-start.2
  0.0 0.0 copy-start.3
  0.0 0.0 copy-start.4
  0.0 0.0 copy-start.5
  0.0 0.0 copy-start.6
  0.0 6.2 %project.1 = bf16[16,96,128]{2,1,0:T(8,128)(2,1)} custom-call(s32[16]{0:T(128)} %tenant_h.1, s32[8]{0:T(128)} %table_h.1, s32[16]{0:T(128)} %counts.1, s32[16]{0:T(128)} %placement.1, bf16[160,8192]{1,0:T(8,128)(2,1)} %hidden.1, bf16[128,8192]{1,0:T(8,128)(2,1)} %weight.1, bf16[512,16,128]{2,1,0:T(8,128)(2,1)} %down.1, bf16[16,64,128]{2,1,0:T(8,128)(2,1)} %bitcast.19), custom_call_target="tpu_custom_call" | custom-call | tf_op jit(solution)/shard_map/project/pallas_call | solution.py:291
  6.3 7.4 %all-to-all-start = ((bf16[16,96,128]{2,1,0:T(8,128)(2,1)}), bf16[16,96,128]{2,1,0:T(8,128)(2,1)S(1)}, u32[]{:S(2)}, u32[]{:S(2)}) async-start(bf16[16,96,128]{2,1,0:T(8,128)(2,1)} %project.1), calls=%async_computation | async-start | bytes 786432 | tf_op jit(solution)/shard_map/all_to_all | solution.py:324
  13.7 0.0 copy-done
  13.7 0.0 copy-done.1
  13.7 0.0 copy-done.2
  13.7 0.0 copy-done.3
  13.7 0.0 copy-done.4
  13.7 0.0 copy-done.5
  13.7 0.0 copy-done.6
  13.7 2.9 %cached.1 = (f32[512,128]{1,0:T(8,128)S(1)}, f32[512,128]{1,0:T(8,128)S(1)}, f32[512,128]{1,0:T(8,128)S(1)}, f32[512,128]{1,0:T(8,128)S(1)}) custom-call(s32[2]{0:T(128)S(1)} %copy-done.5, s32[16]{0:T(128)S(1)} %copy-done.3, s32[16]{0:T(128)S(1)} %copy-done.6, s32[16]{0:T(128)S(1)} %copy-done.4, bf16[2,128,2048]{2,1,0:T(8,128)(2,1)S(1)} %copy-done, ...), custom_call_target="tpu_custom_call" | custom-call | tf_op jit(solution)/shard_map/cached/pallas_call | solution.py:331
  16.6 9.2 %all-to-all-done.box = bf16[16,96,128]{2,1,0:T(8,128)(2,1)S(1)} async-done(((bf16[16,96,128]{2,1,0:T(8,128)(2,1)}), bf16[16,96,128]{2,1,0:T(8,128)(2,1)S(1)}, u32[]{:S(2)}, u32[]{:S(2)}) %all-to-all-start) | async-done | bytes 393248 | tf_op jit(solution)/shard_map/all_to_all | solution.py:324
  25.9 1.9 %merge.1 = bf16[512,128]{1,0:T(8,128)(2,1)} custom-call(bf16[16,96,128]{2,1,0:T(8,128)(2,1)S(1)} %all-to-all-done.box, f32[512,128]{1,0:T(8,128)S(1)} %get-tuple-element.9.acc, f32[512,128]{1,0:T(8,128)S(1)} %get-tuple-element.10.top_in, f32[512,128]{1,0:T(8,128)S(1)} %get-tuple-element.11.total_in, f32[512,128]{1,0:T(8,128)S(1)} %get-tuple-element.12.fresh_ok, ...), custom_call_target="tpu_custom_call" | custom-call | tf_op jit(solution)/shard_map/merge/pallas_call | solution.py:342
Async XLA Ops:
  0.0 13.7 %copy-start = (bf16[2,128,2048]{2,1,0:T(8,128)(2,1)S(1)}, bf16[2,128,2048]{2,1,0:T(8,128)(2,1)}, u32[]{:S(2)}) copy-start(bf16[2,128,2048]{2,1,0:T(8,128)(2,1)} %cache.1) | copy-start | bytes 3145732
  0.0 13.7 %copy-start.1 = (bf16[4,2,8192]{2,1,0:T(2,128)(2,1)S(1)}, bf16[4,2,8192]{2,1,0:T(2,128)(2,1)}, u32[]{:S(2)}) copy-start(bf16[4,2,8192]{2,1,0:T(2,128)(2,1)} %param.24) | copy-start | bytes 393220
  0.0 13.7 %copy-start.2 = (bf16[4,2,2048]{2,1,0:T(2,128)(2,1)S(1)}, bf16[4,2,2048]{2,1,0:T(2,128)(2,1)}, u32[]{:S(2)}) copy-start(bf16[4,2,2048]{2,1,0:T(2,128)(2,1)} %param.25) | copy-start | bytes 98308
  0.0 13.7 %copy-start.3 = (s32[16]{0:T(128)S(1)}, s32[16]{0:T(128)}, u32[]{:S(2)}) copy-start(s32[16]{0:T(128)} %counts.1) | copy-start | bytes 196
  0.0 13.7 %copy-start.4 = (s32[16]{0:T(128)S(1)}, s32[16]{0:T(128)}, u32[]{:S(2)}) copy-start(s32[16]{0:T(128)} %placement.1) | copy-start | bytes 196
  0.0 13.7 %copy-start.5 = (s32[2]{0:T(128)S(1)}, s32[2]{0:T(128)}, u32[]{:S(2)}) copy-start(s32[2]{0:T(128)} %lengths.1) | copy-start | bytes 28
  0.0 13.7 %copy-start.6 = (s32[16]{0:T(128)S(1)}, s32[16]{0:T(128)}, u32[]{:S(2)}) copy-start(s32[16]{0:T(128)} %last.1) | copy-start | bytes 196
  6.3 19.6 %all-to-all-start = ((bf16[16,96,128]{2,1,0:T(8,128)(2,1)}), bf16[16,96,128]{2,1,0:T(8,128)(2,1)S(1)}, u32[]{:S(2)}, u32[]{:S(2)}) async-start(bf16[16,96,128]{2,1,0:T(8,128)(2,1)} %project.1), calls=%async_computation | async-start | bytes 786432 | tf_op jit(solution)/shard_map/all_to_all | solution.py:324

commit v9 on v7

--- a/solution.py
+++ b/solution.py
@@ -34,51 +34,52 @@
 
 
 def project_kernel(
-    dec_rows, d_chunks, chunks, devices, tenant_h, table_h, counts_h, placement_h, hidden, weight, down, up, out,
+    dec_rows, d_chunks, cuts, tenant_h, table_h, counts_h, placement_h, hidden, weight, down, up, out,
     tenant, table, counts, placement,
-    h_s, w_s, d_s, mine_s, u_s, sel_s, part_s, base_s, dest_table, sems, d_sems, int_sems,
+    h_s, w_s, d_s, mine_s, u_s, sel_s, part_s, base_s, dest_table, hw_sems, d_sems, sems,
 ):
     tokens, width = hidden.shape
     features = weight.shape[0]
     local, pages, rank2 = down.shape
     tenants = table.shape[0]
     requests = tenant.shape[0]
+    devices = out.shape[0]
     me = lax.axis_index("tensor")
     d_step = local // d_chunks
-    step = width // chunks
 
     int_copies = [
-        pltpu.make_async_copy(src, dst, int_sems.at[i])
+        pltpu.make_async_copy(src, dst, sems.at[2 + i])
         for i, (src, dst) in enumerate(
             ((table_h, table), (tenant_h, tenant), (counts_h, counts), (placement_h, placement))
         )
     ]
-    for copy in int_copies:
-        copy.start()
     d_copies = [
         pltpu.make_async_copy(
             down.at[pl.ds(c * d_step, d_step)], d_s.at[pl.ds(c * d_step, d_step)], d_sems.at[c])
         for c in range(d_chunks)
     ]
-    h_copies = [
-        pltpu.make_async_copy(hidden.at[:, pl.ds(c * step, step)], h_s.at[c], sems.at[c, 0])
-        for c in range(chunks)
-    ]
-    w_copies = [
-        pltpu.make_async_copy(weight.at[:, pl.ds(c * step, step)], w_s.at[c], sems.at[c, 1])
-        for c in range(chunks)
-    ]
     my_copy = pltpu.make_async_copy(
-        hidden.at[:, pl.ds(pl.multiple_of(me * local, 128), local)], mine_s, d_sems.at[d_chunks]
-    )
-    up_copy = pltpu.make_async_copy(up, u_s, d_sems.at[d_chunks + 1])
-    for copy in d_copies + [my_copy, up_copy]:
+        hidden.at[:, pl.ds(pl.multiple_of(me * local, 128), local)], mine_s, sems.at[0]
+    )
+    up_copy = pltpu.make_async_copy(up, u_s, sems.at[1])
+    for copy in int_copies + d_copies + [my_copy]:
         copy.start()
-    for c in range(chunks):
-        h_copies[c].start()
-        w_copies[c].start()
-
-    int_copies[0].wait()
+    spans = list(zip(cuts[:-1], cuts[1:]))
+    hw_copies = []
+    for c, (first, last) in enumerate(spans):
+        lanes = pl.ds(first, last - first)
+        pair = (
+            pltpu.make_async_copy(hidden.at[:, lanes], h_s.at[:, lanes], hw_sems.at[c, 0]),
+            pltpu.make_async_copy(weight.at[:, lanes], w_s.at[:, lanes], hw_sems.at[c, 1]),
+        )
+        for copy in pair:
+            copy.start()
+        hw_copies.append(pair)
+        if c == 0:
+            up_copy.start()
+
+    for copy in int_copies:
+        copy.wait()
     rows = lax.broadcasted_iota(jnp.int32, (tenants * 16, 16 * pages), 0)
     cols = lax.broadcasted_iota(jnp.int32, (tenants * 16, 16 * pages), 1)
     page_of_row = jnp.zeros_like(rows)
@@ -86,6 +87,16 @@
         page_of_row = jnp.where(div(rows, 16) == k, table[k], page_of_row)
     pick = (mod(rows, 16) == div(cols, pages)) & (mod(cols, pages) == page_of_row)
     pick = jnp.where(pick, jnp.float32(1), jnp.float32(0)).astype(jnp.bfloat16)
+    if requests < devices:
+        for dest in range(devices):
+            dest_table[0, dest] = 0
+            dest_table[1, dest] = 0
+    first = jnp.int32(0)
+    for r in range(requests):
+        dest = div(placement[r], dec_rows)
+        dest_table[0, dest] = first * BLK
+        dest_table[1, dest] = tenant[r]
+        first = first + counts[r]
 
     for c in range(d_chunks):
         d_copies[c].wait()
@@ -96,17 +107,6 @@
             chosen = jnp.dot(pick, block, preferred_element_type=jnp.float32)
             for i in range(2):
                 sel_s[b + i] = chosen[:, i * rank2 : (i + 1) * rank2].astype(jnp.bfloat16)
-    for copy in int_copies[1:]:
-        copy.wait()
-    for dest in range(devices):
-        dest_table[0, dest] = 0
-        dest_table[1, dest] = 0
-    first = jnp.int32(0)
-    for r in range(requests):
-        dest = div(placement[r], dec_rows)
-        dest_table[0, dest] = first * BLK
-        dest_table[1, dest] = tenant[r]
-        first = first + counts[r]
     my_copy.wait()
     mine = mine_s[...]
     for k in range(0, tenants, 2):
@@ -120,24 +120,29 @@
             part_s[k + j, :tokens] = product[:, j * rank2 : (j + 1) * rank2]
             part_s[k + j, tokens:] = jnp.zeros((BLK, rank2), jnp.float32)
 
-    total = jnp.zeros((tokens, features), jnp.float32)
-    for c in range(chunks):
-        h_copies[c].wait()
-        w_copies[c].wait()
-        total = total + lax.dot_general(h_s[c], w_s[c], NT, preferred_element_type=jnp.float32)
     base_s[tokens:] = jnp.zeros((BLK, HD), jnp.float32)
     if features < HD:
         base_s[...] = jnp.zeros_like(base_s)
+    total = jnp.zeros((tokens, features), jnp.float32)
+    for c, (first, last) in enumerate(spans):
+        for copy in hw_copies[c]:
+            copy.wait()
+        if c == 1:
+            up_copy.wait()
+            for dest in range(devices):
+                start = pl.multiple_of(dest_table[0, dest], BLK)
+                who = dest_table[1, dest]
+                out[dest, :CAPT, :] = part_s[who, pl.ds(start, CAPT), :].astype(out.dtype)
+                if features < HD:
+                    out[dest, 2 * CAPT :, :] = jnp.zeros((out.shape[1] - 2 * CAPT, HD), out.dtype)
+                out[dest, 2 * CAPT :, :features] = u_s[table[who]]
+        total = total + lax.dot_general(
+            h_s[:, first:last], w_s[:, first:last], NT, preferred_element_type=jnp.float32
+        )
     base_s[:tokens, :features] = total
-    up_copy.wait()
     for dest in range(devices):
         start = pl.multiple_of(dest_table[0, dest], BLK)
-        who = dest_table[1, dest]
-        out[dest, :CAPT, :] = part_s[who, pl.ds(start, CAPT), :].astype(out.dtype)
         out[dest, CAPT : 2 * CAPT, :] = base_s[pl.ds(start, CAPT), :].astype(out.dtype)
-        if features < HD:
-            out[dest, 2 * CAPT :, :] = jnp.zeros((out.shape[1] - 2 * CAPT, HD), out.dtype)
-        out[dest, 2 * CAPT :, :features] = u_s[table[who]]
 
 
 NT = (((1,), (1,)), ((), ()))
@@ -293,11 +298,12 @@
     dec_rows, ctx, kv_width = key_value_cache.shape
     steps = step_key_value.shape[0]
     heads2 = kv_width // HD
-    d_chunks, chunks = 2, 2
+    d_chunks = 2
+    cuts = (0, width * 3 // 8, width * 6 // 8, width)
     up_by_page = jnp.transpose(adapter_up_weight, (1, 2, 0))
     rows = 2 * CAPT + rank
     outgoing = pl.pallas_call(
-        functools.partial(project_kernel, dec_rows, d_chunks, chunks, devices),
+        functools.partial(project_kernel, dec_rows, d_chunks, cuts),
         out_shape=pltpu.VMEM((devices, rows, HD), WIRE),
         in_specs=[ANY_SPEC] * 8,
         out_specs=VMEM_SPEC,
@@ -306,8 +312,8 @@
             pltpu.SMEM(tenant_page_table.shape, jnp.int32),
             pltpu.SMEM(request_block_count.shape, jnp.int32),
             pltpu.SMEM(placement.shape, jnp.int32),
-            pltpu.VMEM((chunks, tokens, width // chunks), jnp.bfloat16),
-            pltpu.VMEM((chunks, features, width // chunks), jnp.bfloat16),
+            pltpu.VMEM((tokens, width), jnp.bfloat16),
+            pltpu.VMEM((features, width), jnp.bfloat16),
             pltpu.VMEM((local, pages, rank2), jnp.bfloat16),
             pltpu.VMEM((tokens, local), jnp.bfloat16),
             pltpu.VMEM((pages, rank, features), jnp.bfloat16),
@@ -315,9 +321,9 @@
             pltpu.VMEM((tenants, tokens + BLK, rank2), jnp.float32),
             pltpu.VMEM((tokens + BLK, HD), jnp.float32),
             pltpu.SMEM((2, devices), jnp.int32),
-            pltpu.SemaphoreType.DMA((chunks, 2)),
-            pltpu.SemaphoreType.DMA((d_chunks + 2,)),
-            pltpu.SemaphoreType.DMA((4,)),
+            pltpu.SemaphoreType.DMA((len(cuts) - 1, 2)),
+            pltpu.SemaphoreType.DMA((d_chunks,)),
+            pltpu.SemaphoreType.DMA((6,)),
         ],
         compiler_params=pltpu.CompilerParams(vmem_limit_bytes=PROJECT_VMEM),
         name="project",

time: 27 us -> 27.6 us (1.022)
  Pallas kernels: 10 us -> 10.6 us
    pallas_call x1, Pallas kernels: 5.26 us -> 5.89 us  [body(): pl.pallas_call(functools.partial(project_kernel, dec_rows, d_chunks, cuts...]
where the time goes in v9:
time: 27.6 us; the launch traced here: 27.4 us
  Pallas kernels  10.6 us (38%)
  waiting for transfers between devices  9.22 us (33%)
  starting transfers between devices  7.41 us (27%)
    all_to_all x1, waiting for transfers between devices, body(): lax.all_to_all(outgoing, 'tensor', split_axis=0, concat_axis=0, tiled=True)  9.22 us
    all_to_all x1, starting transfers between devices, body(): lax.all_to_all(outgoing, 'tensor', split_axis=0, concat_axis=0, tiled=True)  7.41 us
    pallas_call x1, Pallas kernels, body(): pl.pallas_call(functools.partial(project_kernel, dec_rows, d_chunks, cuts...  5.89 us
    pallas_call x1, Pallas kernels, body(): pl.pallas_call(cached_kernel, out_shape=(state,) * 4, in_specs=[SMEM_SPEC...  2.9 us
    pallas_call x1, Pallas kernels, body(): pl.pallas_call(functools.partial(merge_kernel, features), out_shape=jax.S...  1.86 us
  transfers between devices with their start and end apart: 1, of which 1 were waited for; matrix products, arithmetic and copies ran while one was open for 0% of the time, Pallas kernels for 11%

profile of v9, /device:TPU:0, one launch (start us, length us, event | category | flops | bytes accessed | tf_op | source)
XLA Modules:
  0.0 27.4 jit_solution(16516404845459546570)
XLA Ops:
  0.0 0.0 copy-start
  0.0 0.0 copy-start.1
  0.0 0.0 copy-start.2
  0.0 0.0 copy-start.3
  0.0 0.0 copy-start.4
  0.0 0.0 copy-start.5
  0.0 0.0 copy-start.6
  0.0 5.9 %project.1 = bf16[16,96,128]{2,1,0:T(8,128)(2,1)} custom-call(s32[16]{0:T(128)} %tenant_h.1, s32[8]{0:T(128)} %table_h.1, s32[16]{0:T(128)} %counts.1, s32[16]{0:T(128)} %placement.1, bf16[160,8192]{1,0:T(8,128)(2,1)} %hidden.1, bf16[128,8192]{1,0:T(8,128)(2,1)} %weight.1, bf16[512,16,128]{2,1,0:T(8,128)(2,1)} %down.1, bf16[16,64,128]{2,1,0:T(8,128)(2,1)} %bitcast.19), custom_call_target="tpu_custom_call" | custom-call | tf_op jit(solution)/shard_map/project/pallas_call | solution.py:305
  5.9 7.4 %all-to-all-start = ((bf16[16,96,128]{2,1,0:T(8,128)(2,1)}), bf16[16,96,128]{2,1,0:T(8,128)(2,1)S(1)}, u32[]{:S(2)}, u32[]{:S(2)}) async-start(bf16[16,96,128]{2,1,0:T(8,128)(2,1)} %project.1), calls=%async_computation | async-start | bytes 786432 | tf_op jit(solution)/shard_map/all_to_all | solution.py:339
  13.3 0.0 copy-done
  13.4 0.0 copy-done.1
  13.4 0.0 copy-done.2
  13.4 0.0 copy-done.3
  13.4 0.0 copy-done.4
  13.4 0.0 copy-done.5
  13.4 0.0 copy-done.6
  13.4 2.9 %cached.1 = (f32[512,128]{1,0:T(8,128)S(1)}, f32[512,128]{1,0:T(8,128)S(1)}, f32[512,128]{1,0:T(8,128)S(1)}, f32[512,128]{1,0:T(8,128)S(1)}) custom-call(s32[2]{0:T(128)S(1)} %copy-done.5, s32[16]{0:T(128)S(1)} %copy-done.3, s32[16]{0:T(128)S(1)} %copy-done.6, s32[16]{0:T(128)S(1)} %copy-done.4, bf16[2,128,2048]{2,1,0:T(8,128)(2,1)S(1)} %copy-done, ...), custom_call_target="tpu_custom_call" | custom-call | tf_op jit(solution)/shard_map/cached/pallas_call | solution.py:346
  16.3 9.2 %all-to-all-done.box = bf16[16,96,128]{2,1,0:T(8,128)(2,1)S(1)} async-done(((bf16[16,96,128]{2,1,0:T(8,128)(2,1)}), bf16[16,96,128]{2,1,0:T(8,128)(2,1)S(1)}, u32[]{:S(2)}, u32[]{:S(2)}) %all-to-all-start) | async-done | bytes 393248 | tf_op jit(solution)/shard_map/all_to_all | solution.py:339
  25.5 1.9 %merge.1 = bf16[512,128]{1,0:T(8,128)(2,1)} custom-call(bf16[16,96,128]{2,1,0:T(8,128)(2,1)S(1)} %all-to-all-done.box, f32[512,128]{1,0:T(8,128)S(1)} %get-tuple-element.9.acc, f32[512,128]{1,0:T(8,128)S(1)} %get-tuple-element.10.top_in, f32[512,128]{1,0:T(8,128)S(1)} %get-tuple-element.11.total_in, f32[512,128]{1,0:T(8,128)S(1)} %get-tuple-element.12.fresh_ok, ...), custom_call_target="tpu_custom_call" | custom-call | tf_op jit(solution)/shard_map/merge/pallas_call | solution.py:357
Async XLA Ops:
  0.0 13.3 %copy-start = (bf16[2,128,2048]{2,1,0:T(8,128)(2,1)S(1)}, bf16[2,128,2048]{2,1,0:T(8,128)(2,1)}, u32[]{:S(2)}) copy-start(bf16[2,128,2048]{2,1,0:T(8,128)(2,1)} %cache.1) | copy-start | bytes 3145732
  0.0 13.4 %copy-start.1 = (bf16[4,2,8192]{2,1,0:T(2,128)(2,1)S(1)}, bf16[4,2,8192]{2,1,0:T(2,128)(2,1)}, u32[]{:S(2)}) copy-start(bf16[4,2,8192]{2,1,0:T(2,128)(2,1)} %param.24) | copy-start | bytes 393220
  0.0 13.4 %copy-start.2 = (bf16[4,2,2048]{2,1,0:T(2,128)(2,1)S(1)}, bf16[4,2,2048]{2,1,0:T(2,128)(2,1)}, u32[]{:S(2)}) copy-start(bf16[4,2,2048]{2,1,0:T(2,128)(2,1)} %param.25) | copy-start | bytes 98308
  0.0 13.4 %copy-start.3 = (s32[16]{0:T(128)S(1)}, s32[16]{0:T(128)}, u32[]{:S(2)}) copy-start(s32[16]{0:T(128)} %counts.1) | copy-start | bytes 196
  0.0 13.4 %copy-start.4 = (s32[16]{0:T(128)S(1)}, s32[16]{0:T(128)}, u32[]{:S(2)}) copy-start(s32[16]{0:T(128)} %placement.1) | copy-start | bytes 196
  0.0 13.4 %copy-start.5 = (s32[2]{0:T(128)S(1)}, s32[2]{0:T(128)}, u32[]{:S(2)}) copy-start(s32[2]{0:T(128)} %lengths.1) | copy-start | bytes 28
  0.0 13.4 %copy-start.6 = (s32[16]{0:T(128)S(1)}, s32[16]{0:T(128)}, u32[]{:S(2)}) copy-start(s32[16]{0:T(128)} %last.1) | copy-start | bytes 196
  5.9 19.6 %all-to-all-start = ((bf16[16,96,128]{2,1,0:T(8,128)(2,1)}), bf16[16,96,128]{2,1,0:T(8,128)(2,1)S(1)}, u32[]{:S(2)}, u32[]{:S(2)}) async-start(bf16[16,96,128]{2,1,0:T(8,128)(2,1)} %project.1), calls=%async_computation | async-start | bytes 786432 | tf_op jit(solution)/shard_map/all_to_all | solution.py:339

commit v10 on v7

--- a/solution.py
+++ b/solution.py
@@ -34,49 +34,43 @@
 
 
 def project_kernel(
-    dec_rows, d_chunks, chunks, devices, tenant_h, table_h, counts_h, placement_h, hidden, weight, down, up, out,
+    dec_rows, d_chunks, chunks, tenant_h, table_h, counts_h, placement_h, hidden, weight, down, up, out,
     tenant, table, counts, placement,
-    h_s, w_s, d_s, mine_s, u_s, sel_s, part_s, base_s, dest_table, sems, d_sems, int_sems,
+    h_s, w_s, wt_s, d_s, mine_s, u_s, sel_s, part_s, base_s, dest_table, h_sems, d_sems, sems,
 ):
     tokens, width = hidden.shape
     features = weight.shape[0]
     local, pages, rank2 = down.shape
     tenants = table.shape[0]
     requests = tenant.shape[0]
+    devices = out.shape[0]
     me = lax.axis_index("tensor")
     d_step = local // d_chunks
     step = width // chunks
 
     int_copies = [
-        pltpu.make_async_copy(src, dst, int_sems.at[i])
+        pltpu.make_async_copy(src, dst, sems.at[3 + i])
         for i, (src, dst) in enumerate(
             ((table_h, table), (tenant_h, tenant), (counts_h, counts), (placement_h, placement))
         )
     ]
-    for copy in int_copies:
-        copy.start()
     d_copies = [
         pltpu.make_async_copy(
             down.at[pl.ds(c * d_step, d_step)], d_s.at[pl.ds(c * d_step, d_step)], d_sems.at[c])
         for c in range(d_chunks)
     ]
+    my_copy = pltpu.make_async_copy(
+        hidden.at[:, pl.ds(pl.multiple_of(me * local, 128), local)], mine_s, sems.at[0]
+    )
+    up_copy = pltpu.make_async_copy(up, u_s, sems.at[1])
+    w_copy = pltpu.make_async_copy(weight, w_s, sems.at[2])
     h_copies = [
-        pltpu.make_async_copy(hidden.at[:, pl.ds(c * step, step)], h_s.at[c], sems.at[c, 0])
+        pltpu.make_async_copy(
+            hidden.at[:, pl.ds(c * step, step)], h_s.at[:, pl.ds(c * step, step)], h_sems.at[c])
         for c in range(chunks)
     ]
-    w_copies = [
-        pltpu.make_async_copy(weight.at[:, pl.ds(c * step, step)], w_s.at[c], sems.at[c, 1])
-        for c in range(chunks)
-    ]
-    my_copy = pltpu.make_async_copy(
-        hidden.at[:, pl.ds(pl.multiple_of(me * local, 128), local)], mine_s, d_sems.at[d_chunks]
-    )
-    up_copy = pltpu.make_async_copy(up, u_s, d_sems.at[d_chunks + 1])
-    for copy in d_copies + [my_copy, up_copy]:
+    for copy in int_copies + d_copies + [my_copy, w_copy, up_copy] + h_copies:
         copy.start()
-    for c in range(chunks):
-        h_copies[c].start()
-        w_copies[c].start()
 
     int_copies[0].wait()
     rows = lax.broadcasted_iota(jnp.int32, (tenants * 16, 16 * pages), 0)
@@ -96,35 +90,46 @@
             chosen = jnp.dot(pick, block, preferred_element_type=jnp.float32)
             for i in range(2):
                 sel_s[b + i] = chosen[:, i * rank2 : (i + 1) * rank2].astype(jnp.bfloat16)
+    my_copy.wait()
+    w_copy.wait()
+    if features == HD:
+        wt_s[...] = w_s[...].T
+    mine = mine_s[...]
+    for k in range(0, tenants, 2):
+        pair = min(2, tenants - k)
+        maps = jnp.concatenate(
+            [sel_s[:, j * 16 : (j + 1) * 16, :].reshape(local, rank2) for j in range(k, k + pair)],
+            axis=1,
+        )
+        product = jnp.dot(mine, maps, preferred_element_type=jnp.float32)
+        for j in range(pair):
+            part_s[k + j, :tokens] = product[:, j * rank2 : (j + 1) * rank2]
+            part_s[k + j, tokens:] = jnp.zeros((BLK, rank2), jnp.float32)
     for copy in int_copies[1:]:
         copy.wait()
-    for dest in range(devices):
-        dest_table[0, dest] = 0
-        dest_table[1, dest] = 0
+    if requests < devices:
+        for dest in range(devices):
+            dest_table[0, dest] = 0
+            dest_table[1, dest] = 0
     first = jnp.int32(0)
     for r in range(requests):
         dest = div(placement[r], dec_rows)
         dest_table[0, dest] = first * BLK
         dest_table[1, dest] = tenant[r]
         first = first + counts[r]
-    my_copy.wait()
-    mine = mine_s[...]
-    for k in range(0, tenants, 2):
-        pair = min(2, tenants - k)
-        maps = jnp.concatenate(
-            [sel_s[:, j * 16 : (j + 1) * 16, :].reshape(local, rank2) for j in range(k, k + pair)],
-            axis=1,
-        )
-        product = jnp.dot(mine, maps, preferred_element_type=jnp.float32)
-        for j in range(pair):
-            part_s[k + j, :tokens] = product[:, j * rank2 : (j + 1) * rank2]
-            part_s[k + j, tokens:] = jnp.zeros((BLK, rank2), jnp.float32)
 
     total = jnp.zeros((tokens, features), jnp.float32)
     for c in range(chunks):
         h_copies[c].wait()
-        w_copies[c].wait()
-        total = total + lax.dot_general(h_s[c], w_s[c], NT, preferred_element_type=jnp.float32)
+        lanes = slice(c * step, (c + 1) * step)
+        if features == HD:
+            total = total + jnp.dot(
+                h_s[:, lanes], wt_s[lanes, :], preferred_element_type=jnp.float32
+            )
+        else:
+            total = total + lax.dot_general(
+                h_s[:, lanes], w_s[:, lanes], NT, preferred_element_type=jnp.float32
+            )
     base_s[tokens:] = jnp.zeros((BLK, HD), jnp.float32)
     if features < HD:
         base_s[...] = jnp.zeros_like(base_s)
@@ -297,7 +302,7 @@
     up_by_page = jnp.transpose(adapter_up_weight, (1, 2, 0))
     rows = 2 * CAPT + rank
     outgoing = pl.pallas_call(
-        functools.partial(project_kernel, dec_rows, d_chunks, chunks, devices),
+        functools.partial(project_kernel, dec_rows, d_chunks, chunks),
         out_shape=pltpu.VMEM((devices, rows, HD), WIRE),
         in_specs=[ANY_SPEC] * 8,
         out_specs=VMEM_SPEC,
@@ -306,8 +311,9 @@
             pltpu.SMEM(tenant_page_table.shape, jnp.int32),
             pltpu.SMEM(request_block_count.shape, jnp.int32),
             pltpu.SMEM(placement.shape, jnp.int32),
-            pltpu.VMEM((chunks, tokens, width // chunks), jnp.bfloat16),
-            pltpu.VMEM((chunks, features, width // chunks), jnp.bfloat16),
+            pltpu.VMEM((tokens, width), jnp.bfloat16),
+            pltpu.VMEM((features, width), jnp.bfloat16),
+            pltpu.VMEM((width, HD), jnp.bfloat16),
             pltpu.VMEM((local, pages, rank2), jnp.bfloat16),
             pltpu.VMEM((tokens, local), jnp.bfloat16),
             pltpu.VMEM((pages, rank, features), jnp.bfloat16),
@@ -315,9 +321,9 @@
             pltpu.VMEM((tenants, tokens + BLK, rank2), jnp.float32),
             pltpu.VMEM((tokens + BLK, HD), jnp.float32),
             pltpu.SMEM((2, devices), jnp.int32),
-            pltpu.SemaphoreType.DMA((chunks, 2)),
-            pltpu.SemaphoreType.DMA((d_chunks + 2,)),
-            pltpu.SemaphoreType.DMA((4,)),
+            pltpu.SemaphoreType.DMA((chunks,)),
+            pltpu.SemaphoreType.DMA((d_chunks,)),
+            pltpu.SemaphoreType.DMA((7,)),
         ],
         compiler_params=pltpu.CompilerParams(vmem_limit_bytes=PROJECT_VMEM),
         name="project",

time: 27 us -> 27.4 us (1.015)
  Pallas kernels: 10 us -> 10.4 us
    pallas_call x1, Pallas kernels: 5.26 us -> 5.67 us  [body(): pl.pallas_call(functools.partial(project_kernel, dec_rows, d_chunks, chun...]
where the time goes in v10:
time: 27.4 us; the launch traced here: 27.2 us
  Pallas kernels  10.4 us (38%)
  waiting for transfers between devices  9.22 us (34%)
  starting transfers between devices  7.4 us (27%)
    all_to_all x1, waiting for transfers between devices, body(): lax.all_to_all(outgoing, 'tensor', split_axis=0, concat_axis=0, tiled=True)  9.22 us
    all_to_all x1, starting transfers between devices, body(): lax.all_to_all(outgoing, 'tensor', split_axis=0, concat_axis=0, tiled=True)  7.4 us
    pallas_call x1, Pallas kernels, body(): pl.pallas_call(functools.partial(project_kernel, dec_rows, d_chunks, chun...  5.67 us
    pallas_call x1, Pallas kernels, body(): pl.pallas_call(cached_kernel, out_shape=(state,) * 4, in_specs=[SMEM_SPEC...  2.9 us
    pallas_call x1, Pallas kernels, body(): pl.pallas_call(functools.partial(merge_kernel, features), out_shape=jax.S...  1.87 us
  transfers between devices with their start and end apart: 1, of which 1 were waited for; matrix products, arithmetic and copies ran while one was open for 0% of the time, Pallas kernels for 11%

profile of v10, /device:TPU:0, one launch (start us, length us, event | category | flops | bytes accessed | tf_op | source)
XLA Modules:
  0.0 27.2 jit_solution(2905039247010566087)
XLA Ops:
  0.0 0.0 copy-start
  0.0 0.0 copy-start.1
  0.0 0.0 copy-start.2
  0.0 0.0 copy-start.3
  0.0 0.0 copy-start.4
  0.0 0.0 copy-start.5
  0.0 0.0 copy-start.6
  0.0 5.7 %project.1 = bf16[16,96,128]{2,1,0:T(8,128)(2,1)} custom-call(s32[16]{0:T(128)} %tenant_h.1, s32[8]{0:T(128)} %table_h.1, s32[16]{0:T(128)} %counts.1, s32[16]{0:T(128)} %placement.1, bf16[160,8192]{1,0:T(8,128)(2,1)} %hidden.1, bf16[128,8192]{1,0:T(8,128)(2,1)} %weight.1, bf16[512,16,128]{2,1,0:T(8,128)(2,1)} %down.1, bf16[16,64,128]{2,1,0:T(8,128)(2,1)} %bitcast.19), custom_call_target="tpu_custom_call" | custom-call | tf_op jit(solution)/shard_map/project/pallas_call | solution.py:304
  5.7 7.4 %all-to-all-start = ((bf16[16,96,128]{2,1,0:T(8,128)(2,1)}), bf16[16,96,128]{2,1,0:T(8,128)(2,1)S(1)}, u32[]{:S(2)}, u32[]{:S(2)}) async-start(bf16[16,96,128]{2,1,0:T(8,128)(2,1)} %project.1), calls=%async_computation | async-start | bytes 786432 | tf_op jit(solution)/shard_map/all_to_all | solution.py:339
  13.1 0.0 copy-done
  13.1 0.0 copy-done.1
  13.1 0.0 copy-done.2
  13.2 0.0 copy-done.3
  13.2 0.0 copy-done.4
  13.2 0.0 copy-done.5
  13.2 0.0 copy-done.6
  13.2 2.9 %cached.1 = (f32[512,128]{1,0:T(8,128)S(1)}, f32[512,128]{1,0:T(8,128)S(1)}, f32[512,128]{1,0:T(8,128)S(1)}, f32[512,128]{1,0:T(8,128)S(1)}) custom-call(s32[2]{0:T(128)S(1)} %copy-done.5, s32[16]{0:T(128)S(1)} %copy-done.3, s32[16]{0:T(128)S(1)} %copy-done.6, s32[16]{0:T(128)S(1)} %copy-done.4, bf16[2,128,2048]{2,1,0:T(8,128)(2,1)S(1)} %copy-done, ...), custom_call_target="tpu_custom_call" | custom-call | tf_op jit(solution)/shard_map/cached/pallas_call | solution.py:346
  16.1 9.2 %all-to-all-done.box = bf16[16,96,128]{2,1,0:T(8,128)(2,1)S(1)} async-done(((bf16[16,96,128]{2,1,0:T(8,128)(2,1)}), bf16[16,96,128]{2,1,0:T(8,128)(2,1)S(1)}, u32[]{:S(2)}, u32[]{:S(2)}) %all-to-all-start) | async-done | bytes 393248 | tf_op jit(solution)/shard_map/all_to_all | solution.py:339
  25.3 1.9 %merge.1 = bf16[512,128]{1,0:T(8,128)(2,1)} custom-call(bf16[16,96,128]{2,1,0:T(8,128)(2,1)S(1)} %all-to-all-done.box, f32[512,128]{1,0:T(8,128)S(1)} %get-tuple-element.9.acc, f32[512,128]{1,0:T(8,128)S(1)} %get-tuple-element.10.top_in, f32[512,128]{1,0:T(8,128)S(1)} %get-tuple-element.11.total_in, f32[512,128]{1,0:T(8,128)S(1)} %get-tuple-element.12.fresh_ok, ...), custom_call_target="tpu_custom_call" | custom-call | tf_op jit(solution)/shard_map/merge/pallas_call | solution.py:357
Async XLA Ops:
  0.0 13.1 %copy-start = (bf16[2,128,2048]{2,1,0:T(8,128)(2,1)S(1)}, bf16[2,128,2048]{2,1,0:T(8,128)(2,1)}, u32[]{:S(2)}) copy-start(bf16[2,128,2048]{2,1,0:T(8,128)(2,1)} %cache.1) | copy-start | bytes 3145732
  0.0 13.1 %copy-start.1 = (bf16[4,2,8192]{2,1,0:T(2,128)(2,1)S(1)}, bf16[4,2,8192]{2,1,0:T(2,128)(2,1)}, u32[]{:S(2)}) copy-start(bf16[4,2,8192]{2,1,0:T(2,128)(2,1)} %param.24) | copy-start | bytes 393220
  0.0 13.1 %copy-start.2 = (bf16[4,2,2048]{2,1,0:T(2,128)(2,1)S(1)}, bf16[4,2,2048]{2,1,0:T(2,128)(2,1)}, u32[]{:S(2)}) copy-start(bf16[4,2,2048]{2,1,0:T(2,128)(2,1)} %param.25) | copy-start | bytes 98308
  0.0 13.1 %copy-start.3 = (s32[16]{0:T(128)S(1)}, s32[16]{0:T(128)}, u32[]{:S(2)}) copy-start(s32[16]{0:T(128)} %counts.1) | copy-start | bytes 196
  0.0 13.2 %copy-start.4 = (s32[16]{0:T(128)S(1)}, s32[16]{0:T(128)}, u32[]{:S(2)}) copy-start(s32[16]{0:T(128)} %placement.1) | copy-start | bytes 196
  0.0 13.2 %copy-start.5 = (s32[2]{0:T(128)S(1)}, s32[2]{0:T(128)}, u32[]{:S(2)}) copy-start(s32[2]{0:T(128)} %lengths.1) | copy-start | bytes 28
  0.0 13.2 %copy-start.6 = (s32[16]{0:T(128)S(1)}, s32[16]{0:T(128)}, u32[]{:S(2)}) copy-start(s32[16]{0:T(128)} %last.1) | copy-start | bytes 196
  5.7 19.6 %all-to-all-start = ((bf16[16,96,128]{2,1,0:T(8,128)(2,1)}), bf16[16,96,128]{2,1,0:T(8,128)(2,1)S(1)}, u32[]{:S(2)}, u32[]{:S(2)}) async-start(bf16[16,96,128]{2,1,0:T(8,128)(2,1)} %project.1), calls=%async_computation | async-start | bytes 786432 | tf_op jit(solution)/shard_map/all_to_all | solution.py:339

commit v11 on v7

--- a/solution.py
+++ b/solution.py
@@ -269,6 +269,10 @@
         copy.wait()
 
 
+def in_hbm(*arrays):
+    return [pltpu.with_memory_space_constraint(x, pltpu.HBM) for x in arrays]
+
+
 def body(
     hidden,
     key_value_weight,
@@ -293,7 +297,7 @@
     dec_rows, ctx, kv_width = key_value_cache.shape
     steps = step_key_value.shape[0]
     heads2 = kv_width // HD
-    d_chunks, chunks = 2, 2
+    d_chunks, chunks = 2, 4
     up_by_page = jnp.transpose(adapter_up_weight, (1, 2, 0))
     rows = 2 * CAPT + rank
     outgoing = pl.pallas_call(
@@ -322,12 +326,9 @@
         compiler_params=pltpu.CompilerParams(vmem_limit_bytes=PROJECT_VMEM),
         name="project",
     )(
-        *(
-            pltpu.with_memory_space_constraint(x, pltpu.HBM)
-            for x in (
-                tenant, tenant_page_table, request_block_count, placement,
-                hidden, key_value_weight, adapter_down_weight, up_by_page,
-            )
+        *in_hbm(
+            tenant, tenant_page_table, request_block_count, placement,
+            hidden, key_value_weight, adapter_down_weight, up_by_page,
         )
     )
     arrived = lax.all_to_all(outgoing, "tensor", split_axis=0, concat_axis=0, tiled=True)
@@ -345,8 +346,10 @@
         compiler_params=pltpu.CompilerParams(vmem_limit_bytes=ATTEND_VMEM),
         name="cached",
     )(
-        context_length, request_block_count, last_block_tokens, placement,
-        key_value_cache, query, steps_kv,
+        *in_hbm(
+            context_length, request_block_count, last_block_tokens, placement,
+            key_value_cache, query, steps_kv,
+        )
     )
     attended = pl.pallas_call(
         functools.partial(merge_kernel, features),

time: 27 us -> 27.8 us (1.030)
  Pallas kernels: 10 us -> 11.4 us
  waiting for transfers between devices: 9.22 us -> 8.54 us
    pallas_call x1, Pallas kernels: 2.9 us -> 3.65 us  [body(): pl.pallas_call(cached_kernel, out_shape=(state,) * 4, in_specs=[SMEM_SPEC...]
    all_to_all x1, waiting for transfers between devices: 9.22 us -> 8.54 us  [body(): lax.all_to_all(outgoing, 'tensor', split_axis=0, concat_axis=0, tiled=True)]
    pallas_call x1, Pallas kernels: 5.26 us -> 5.89 us  [body(): pl.pallas_call(functools.partial(project_kernel, dec_rows, d_chunks, chun...]
  transfers between devices with their start and end apart: 1 -> 1, of which waited for: 1 -> 1; matrix products, arithmetic and copies ran while one was open for 0% -> 0% of each run, Pallas kernels for 11% -> 13%
where the time goes in v11:
time: 27.8 us; the launch traced here: 27.5 us
  Pallas kernels  11.4 us (41%)
  waiting for transfers between devices  8.54 us (31%)
  starting transfers between devices  7.53 us (27%)
    all_to_all x1, waiting for transfers between devices, body(): lax.all_to_all(outgoing, 'tensor', split_axis=0, concat_axis=0, tiled=True)  8.54 us
    all_to_all x1, starting transfers between devices, body(): lax.all_to_all(outgoing, 'tensor', split_axis=0, concat_axis=0, tiled=True)  7.53 us
    pallas_call x1, Pallas kernels, body(): pl.pallas_call(functools.partial(project_kernel, dec_rows, d_chunks, chun...  5.89 us
    pallas_call x1, Pallas kernels, body(): pl.pallas_call(cached_kernel, out_shape=(state,) * 4, in_specs=[SMEM_SPEC...  3.65 us
    pallas_call x1, Pallas kernels, body(): pl.pallas_call(functools.partial(merge_kernel, features), out_shape=jax.S...  1.87 us
  transfers between devices with their start and end apart: 1, of which 1 were waited for; matrix products, arithmetic and copies ran while one was open for 0% of the time, Pallas kernels for 13%

profile of v11, /device:TPU:0, one launch (start us, length us, event | category | flops | bytes accessed | tf_op | source)
XLA Modules:
  0.0 27.5 jit_solution(8894414063958949830)
XLA Ops:
  0.0 5.9 %project.1 = bf16[16,96,128]{2,1,0:T(8,128)(2,1)} custom-call(s32[16]{0:T(128)} %tenant_h.1, s32[8]{0:T(128)} %table_h.1, s32[16]{0:T(128)} %counts.1, s32[16]{0:T(128)} %placement.1, bf16[160,8192]{1,0:T(8,128)(2,1)} %hidden.1, bf16[128,8192]{1,0:T(8,128)(2,1)} %weight.1, bf16[512,16,128]{2,1,0:T(8,128)(2,1)} %down.1, bf16[16,64,128]{2,1,0:T(8,128)(2,1)} %bitcast.18), custom_call_target="tpu_custom_call" | custom-call | tf_op jit(solution)/shard_map/project/pallas_call | solution.py:303
  5.9 0.0 copy-start
  5.9 7.5 %all-to-all-start = ((bf16[16,96,128]{2,1,0:T(8,128)(2,1)}), bf16[16,96,128]{2,1,0:T(8,128)(2,1)S(1)}, u32[]{:S(2)}, u32[]{:S(2)}) async-start(bf16[16,96,128]{2,1,0:T(8,128)(2,1)} %project.1), calls=%async_computation | async-start | bytes 786432 | tf_op jit(solution)/shard_map/all_to_all | solution.py:334
  13.4 3.7 %cached.1 = (f32[512,128]{1,0:T(8,128)S(1)}, f32[512,128]{1,0:T(8,128)S(1)}, f32[512,128]{1,0:T(8,128)S(1)}, f32[512,128]{1,0:T(8,128)S(1)}) custom-call(s32[2]{0:T(128)} %lengths.1, s32[16]{0:T(128)} %counts.1, s32[16]{0:T(128)} %last.1, s32[16]{0:T(128)} %placement.1, bf16[2,128,2048]{2,1,0:T(8,128)(2,1)} %cache.1, bf16[512,128]{1,0:T(8,128)(2,1)} %bitcast.16, ...), custom_call_target="tpu_custom_call" | custom-call | tf_op jit(solution)/shard_map/cached/pallas_call | solution.py:341
  17.1 8.5 %all-to-all-done.box = bf16[16,96,128]{2,1,0:T(8,128)(2,1)S(1)} async-done(((bf16[16,96,128]{2,1,0:T(8,128)(2,1)}), bf16[16,96,128]{2,1,0:T(8,128)(2,1)S(1)}, u32[]{:S(2)}, u32[]{:S(2)}) %all-to-all-start) | async-done | bytes 393248 | tf_op jit(solution)/shard_map/all_to_all | solution.py:334
  25.6 0.0 copy-done
  25.6 1.9 %merge.1 = bf16[512,128]{1,0:T(8,128)(2,1)} custom-call(bf16[16,96,128]{2,1,0:T(8,128)(2,1)S(1)} %all-to-all-done.box, f32[512,128]{1,0:T(8,128)S(1)} %get-tuple-element.9.acc, f32[512,128]{1,0:T(8,128)S(1)} %get-tuple-element.10.top_in, f32[512,128]{1,0:T(8,128)S(1)} %get-tuple-element.11.total_in, f32[512,128]{1,0:T(8,128)S(1)} %get-tuple-element.12.fresh_ok, ...), custom_call_target="tpu_custom_call" | custom-call | tf_op jit(solution)/shard_map/merge/pallas_call | solution.py:354
Async XLA Ops:
  5.9 19.7 %copy-start = (bf16[4,2,8192]{2,1,0:T(2,128)(2,1)S(1)}, bf16[4,2,8192]{2,1,0:T(2,128)(2,1)}, u32[]{:S(2)}) copy-start(bf16[4,2,8192]{2,1,0:T(2,128)(2,1)} %param.24) | copy-start | bytes 393220
  5.9 19.7 %all-to-all-start = ((bf16[16,96,128]{2,1,0:T(8,128)(2,1)}), bf16[16,96,128]{2,1,0:T(8,128)(2,1)S(1)}, u32[]{:S(2)}, u32[]{:S(2)}) async-start(bf16[16,96,128]{2,1,0:T(8,128)(2,1)} %project.1), calls=%async_computation | async-start | bytes 786432 | tf_op jit(solution)/shard_map/all_to_all | solution.py:334

commit v12 on v7

--- a/solution.py
+++ b/solution.py
@@ -293,7 +293,7 @@
     dec_rows, ctx, kv_width = key_value_cache.shape
     steps = step_key_value.shape[0]
     heads2 = kv_width // HD
-    d_chunks, chunks = 2, 2
+    d_chunks, chunks = 4, 2
     up_by_page = jnp.transpose(adapter_up_weight, (1, 2, 0))
     rows = 2 * CAPT + rank
     outgoing = pl.pallas_call(

time: 27 us -> 27 us (level)
  no operation moved by 1% of the time
where the time goes in v12:
time: 27 us; the launch traced here: 26.8 us
  Pallas kernels  10 us (37%)
  waiting for transfers between devices  9.22 us (34%)
  starting transfers between devices  7.41 us (27%)
    all_to_all x1, waiting for transfers between devices, body(): lax.all_to_all(outgoing, 'tensor', split_axis=0, concat_axis=0, tiled=True)  9.22 us
    all_to_all x1, starting transfers between devices, body(): lax.all_to_all(outgoing, 'tensor', split_axis=0, concat_axis=0, tiled=True)  7.41 us
    pallas_call x1, Pallas kernels, body(): pl.pallas_call(functools.partial(project_kernel, dec_rows, d_chunks, chun...  5.28 us
    pallas_call x1, Pallas kernels, body(): pl.pallas_call(cached_kernel, out_shape=(state,) * 4, in_specs=[SMEM_SPEC...  2.9 us
    pallas_call x1, Pallas kernels, body(): pl.pallas_call(functools.partial(merge_kernel, features), out_shape=jax.S...  1.87 us
  transfers between devices with their start and end apart: 1, of which 1 were waited for; matrix products, arithmetic and copies ran while one was open for 0% of the time, Pallas kernels for 11%

profile of v12, /device:TPU:0, one launch (start us, length us, event | category | flops | bytes accessed | tf_op | source)
XLA Modules:
  0.0 26.8 jit_solution(18132449855991619032)
XLA Ops:
  0.0 0.0 copy-start
  0.0 0.0 copy-start.1
  0.0 0.0 copy-start.2
  0.0 0.0 copy-start.3
  0.0 0.0 copy-start.4
  0.0 0.0 copy-start.5
  0.0 0.0 copy-start.6
  0.0 5.3 %project.1 = bf16[16,96,128]{2,1,0:T(8,128)(2,1)} custom-call(s32[16]{0:T(128)} %tenant_h.1, s32[8]{0:T(128)} %table_h.1, s32[16]{0:T(128)} %counts.1, s32[16]{0:T(128)} %placement.1, bf16[160,8192]{1,0:T(8,128)(2,1)} %hidden.1, bf16[128,8192]{1,0:T(8,128)(2,1)} %weight.1, bf16[512,16,128]{2,1,0:T(8,128)(2,1)} %down.1, bf16[16,64,128]{2,1,0:T(8,128)(2,1)} %bitcast.19), custom_call_target="tpu_custom_call" | custom-call | tf_op jit(solution)/shard_map/project/pallas_call | solution.py:299
  5.3 7.4 %all-to-all-start = ((bf16[16,96,128]{2,1,0:T(8,128)(2,1)}), bf16[16,96,128]{2,1,0:T(8,128)(2,1)S(1)}, u32[]{:S(2)}, u32[]{:S(2)}) async-start(bf16[16,96,128]{2,1,0:T(8,128)(2,1)} %project.1), calls=%async_computation | async-start | bytes 786432 | tf_op jit(solution)/shard_map/all_to_all | solution.py:333
  12.7 0.0 copy-done
  12.8 0.0 copy-done.1
  12.8 0.0 copy-done.2
  12.8 0.0 copy-done.3
  12.8 0.0 copy-done.4
  12.8 0.0 copy-done.5
  12.8 0.0 copy-done.6
  12.8 2.9 %cached.1 = (f32[512,128]{1,0:T(8,128)S(1)}, f32[512,128]{1,0:T(8,128)S(1)}, f32[512,128]{1,0:T(8,128)S(1)}, f32[512,128]{1,0:T(8,128)S(1)}) custom-call(s32[2]{0:T(128)S(1)} %copy-done.5, s32[16]{0:T(128)S(1)} %copy-done.3, s32[16]{0:T(128)S(1)} %copy-done.6, s32[16]{0:T(128)S(1)} %copy-done.4, bf16[2,128,2048]{2,1,0:T(8,128)(2,1)S(1)} %copy-done, ...), custom_call_target="tpu_custom_call" | custom-call | tf_op jit(solution)/shard_map/cached/pallas_call | solution.py:340
  15.7 9.2 %all-to-all-done.box = bf16[16,96,128]{2,1,0:T(8,128)(2,1)S(1)} async-done(((bf16[16,96,128]{2,1,0:T(8,128)(2,1)}), bf16[16,96,128]{2,1,0:T(8,128)(2,1)S(1)}, u32[]{:S(2)}, u32[]{:S(2)}) %all-to-all-start) | async-done | bytes 393248 | tf_op jit(solution)/shard_map/all_to_all | solution.py:333
  24.9 1.9 %merge.1 = bf16[512,128]{1,0:T(8,128)(2,1)} custom-call(bf16[16,96,128]{2,1,0:T(8,128)(2,1)S(1)} %all-to-all-done.box, f32[512,128]{1,0:T(8,128)S(1)} %get-tuple-element.9.acc, f32[512,128]{1,0:T(8,128)S(1)} %get-tuple-element.10.top_in, f32[512,128]{1,0:T(8,128)S(1)} %get-tuple-element.11.total_in, f32[512,128]{1,0:T(8,128)S(1)} %get-tuple-element.12.fresh_ok, ...), custom_call_target="tpu_custom_call" | custom-call | tf_op jit(solution)/shard_map/merge/pallas_call | solution.py:351
Async XLA Ops:
  0.0 12.7 %copy-start = (bf16[2,128,2048]{2,1,0:T(8,128)(2,1)S(1)}, bf16[2,128,2048]{2,1,0:T(8,128)(2,1)}, u32[]{:S(2)}) copy-start(bf16[2,128,2048]{2,1,0:T(8,128)(2,1)} %cache.1) | copy-start | bytes 3145732
  0.0 12.8 %copy-start.1 = (bf16[4,2,8192]{2,1,0:T(2,128)(2,1)S(1)}, bf16[4,2,8192]{2,1,0:T(2,128)(2,1)}, u32[]{:S(2)}) copy-start(bf16[4,2,8192]{2,1,0:T(2,128)(2,1)} %param.24) | copy-start | bytes 393220
  0.0 12.8 %copy-start.2 = (bf16[4,2,2048]{2,1,0:T(2,128)(2,1)S(1)}, bf16[4,2,2048]{2,1,0:T(2,128)(2,1)}, u32[]{:S(2)}) copy-start(bf16[4,2,2048]{2,1,0:T(2,128)(2,1)} %param.25) | copy-start | bytes 98308
  0.0 12.8 %copy-start.3 = (s32[16]{0:T(128)S(1)}, s32[16]{0:T(128)}, u32[]{:S(2)}) copy-start(s32[16]{0:T(128)} %counts.1) | copy-start | bytes 196
  0.0 12.8 %copy-start.4 = (s32[16]{0:T(128)S(1)}, s32[16]{0:T(128)}, u32[]{:S(2)}) copy-start(s32[16]{0:T(128)} %placement.1) | copy-start | bytes 196
  0.0 12.8 %copy-start.5 = (s32[2]{0:T(128)S(1)}, s32[2]{0:T(128)}, u32[]{:S(2)}) copy-start(s32[2]{0:T(128)} %lengths.1) | copy-start | bytes 28
  0.0 12.8 %copy-start.6 = (s32[16]{0:T(128)S(1)}, s32[16]{0:T(128)}, u32[]{:S(2)}) copy-start(s32[16]{0:T(128)} %last.1) | copy-start | bytes 196
  5.3 19.6 %all-to-all-start = ((bf16[16,96,128]{2,1,0:T(8,128)(2,1)}), bf16[16,96,128]{2,1,0:T(8,128)(2,1)S(1)}, u32[]{:S(2)}, u32[]{:S(2)}) async-start(bf16[16,96,128]{2,1,0:T(8,128)(2,1)} %project.1), calls=%async_computation | async-start | bytes 786432 | tf_op jit(solution)/shard_map/all_to_all | solution.py:333

commit v13 on v12

--- a/solution.py
+++ b/solution.py
@@ -53,8 +53,6 @@
             ((table_h, table), (tenant_h, tenant), (counts_h, counts), (placement_h, placement))
         )
     ]
-    for copy in int_copies:
-        copy.start()
     d_copies = [
         pltpu.make_async_copy(
             down.at[pl.ds(c * d_step, d_step)], d_s.at[pl.ds(c * d_step, d_step)], d_sems.at[c])
@@ -72,11 +70,13 @@
         hidden.at[:, pl.ds(pl.multiple_of(me * local, 128), local)], mine_s, d_sems.at[d_chunks]
     )
     up_copy = pltpu.make_async_copy(up, u_s, d_sems.at[d_chunks + 1])
-    for copy in d_copies + [my_copy, up_copy]:
+    for copy in d_copies + int_copies[:1] + [my_copy]:
         copy.start()
     for c in range(chunks):
         h_copies[c].start()
         w_copies[c].start()
+    for copy in int_copies[1:] + [up_copy]:
+        copy.start()
 
     int_copies[0].wait()
     rows = lax.broadcasted_iota(jnp.int32, (tenants * 16, 16 * pages), 0)

time: 27 us -> 27 us (level)
  no operation moved by 1% of the time
where the time goes in v13:
time: 27 us; the launch traced here: 26.8 us
  Pallas kernels  10 us (37%)
  waiting for transfers between devices  9.22 us (34%)
  starting transfers between devices  7.41 us (27%)
    all_to_all x1, waiting for transfers between devices, body(): lax.all_to_all(outgoing, 'tensor', split_axis=0, concat_axis=0, tiled=True)  9.22 us
    all_to_all x1, starting transfers between devices, body(): lax.all_to_all(outgoing, 'tensor', split_axis=0, concat_axis=0, tiled=True)  7.41 us
    pallas_call x1, Pallas kernels, body(): pl.pallas_call(functools.partial(project_kernel, dec_rows, d_chunks, chun...  5.28 us
    pallas_call x1, Pallas kernels, body(): pl.pallas_call(cached_kernel, out_shape=(state,) * 4, in_specs=[SMEM_SPEC...  2.9 us
    pallas_call x1, Pallas kernels, body(): pl.pallas_call(functools.partial(merge_kernel, features), out_shape=jax.S...  1.87 us
  transfers between devices with their start and end apart: 1, of which 1 were waited for; matrix products, arithmetic and copies ran while one was open for 0% of the time, Pallas kernels for 11%

profile of v13, /device:TPU:0, one launch (start us, length us, event | category | flops | bytes accessed | tf_op | source)
XLA Modules:
  0.0 26.8 jit_solution(3232544763804145846)
XLA Ops:
  0.0 0.0 copy-start
  0.0 0.0 copy-start.1
  0.0 0.0 copy-start.2
  0.0 0.0 copy-start.3
  0.0 0.0 copy-start.4
  0.0 0.0 copy-start.5
  0.0 0.0 copy-start.6
  0.0 5.3 %project.1 = bf16[16,96,128]{2,1,0:T(8,128)(2,1)} custom-call(s32[16]{0:T(128)} %tenant_h.1, s32[8]{0:T(128)} %table_h.1, s32[16]{0:T(128)} %counts.1, s32[16]{0:T(128)} %placement.1, bf16[160,8192]{1,0:T(8,128)(2,1)} %hidden.1, bf16[128,8192]{1,0:T(8,128)(2,1)} %weight.1, bf16[512,16,128]{2,1,0:T(8,128)(2,1)} %down.1, bf16[16,64,128]{2,1,0:T(8,128)(2,1)} %bitcast.19), custom_call_target="tpu_custom_call" | custom-call | tf_op jit(solution)/shard_map/project/pallas_call | solution.py:299
  5.3 7.4 %all-to-all-start = ((bf16[16,96,128]{2,1,0:T(8,128)(2,1)}), bf16[16,96,128]{2,1,0:T(8,128)(2,1)S(1)}, u32[]{:S(2)}, u32[]{:S(2)}) async-start(bf16[16,96,128]{2,1,0:T(8,128)(2,1)} %project.1), calls=%async_computation | async-start | bytes 786432 | tf_op jit(solution)/shard_map/all_to_all | solution.py:333
  12.7 0.0 copy-done
  12.7 0.0 copy-done.1
  12.8 0.0 copy-done.2
  12.8 0.0 copy-done.3
  12.8 0.0 copy-done.4
  12.8 0.0 copy-done.5
  12.8 0.0 copy-done.6
  12.8 2.9 %cached.1 = (f32[512,128]{1,0:T(8,128)S(1)}, f32[512,128]{1,0:T(8,128)S(1)}, f32[512,128]{1,0:T(8,128)S(1)}, f32[512,128]{1,0:T(8,128)S(1)}) custom-call(s32[2]{0:T(128)S(1)} %copy-done.5, s32[16]{0:T(128)S(1)} %copy-done.3, s32[16]{0:T(128)S(1)} %copy-done.6, s32[16]{0:T(128)S(1)} %copy-done.4, bf16[2,128,2048]{2,1,0:T(8,128)(2,1)S(1)} %copy-done, ...), custom_call_target="tpu_custom_call" | custom-call | tf_op jit(solution)/shard_map/cached/pallas_call | solution.py:340
  15.7 9.2 %all-to-all-done.box = bf16[16,96,128]{2,1,0:T(8,128)(2,1)S(1)} async-done(((bf16[16,96,128]{2,1,0:T(8,128)(2,1)}), bf16[16,96,128]{2,1,0:T(8,128)(2,1)S(1)}, u32[]{:S(2)}, u32[]{:S(2)}) %all-to-all-start) | async-done | bytes 393248 | tf_op jit(solution)/shard_map/all_to_all | solution.py:333
  24.9 1.9 %merge.1 = bf16[512,128]{1,0:T(8,128)(2,1)} custom-call(bf16[16,96,128]{2,1,0:T(8,128)(2,1)S(1)} %all-to-all-done.box, f32[512,128]{1,0:T(8,128)S(1)} %get-tuple-element.9.acc, f32[512,128]{1,0:T(8,128)S(1)} %get-tuple-element.10.top_in, f32[512,128]{1,0:T(8,128)S(1)} %get-tuple-element.11.total_in, f32[512,128]{1,0:T(8,128)S(1)} %get-tuple-element.12.fresh_ok, ...), custom_call_target="tpu_custom_call" | custom-call | tf_op jit(solution)/shard_map/merge/pallas_call | solution.py:351
Async XLA Ops:
  0.0 12.7 %copy-start = (bf16[2,128,2048]{2,1,0:T(8,128)(2,1)S(1)}, bf16[2,128,2048]{2,1,0:T(8,128)(2,1)}, u32[]{:S(2)}) copy-start(bf16[2,128,2048]{2,1,0:T(8,128)(2,1)} %cache.1) | copy-start | bytes 3145732
  0.0 12.7 %copy-start.1 = (bf16[4,2,8192]{2,1,0:T(2,128)(2,1)S(1)}, bf16[4,2,8192]{2,1,0:T(2,128)(2,1)}, u32[]{:S(2)}) copy-start(bf16[4,2,8192]{2,1,0:T(2,128)(2,1)} %param.24) | copy-start | bytes 393220
  0.0 12.8 %copy-start.2 = (bf16[4,2,2048]{2,1,0:T(2,128)(2,1)S(1)}, bf16[4,2,2048]{2,1,0:T(2,128)(2,1)}, u32[]{:S(2)}) copy-start(bf16[4,2,2048]{2,1,0:T(2,128)(2,1)} %param.25) | copy-start | bytes 98308
  0.0 12.8 %copy-start.3 = (s32[16]{0:T(128)S(1)}, s32[16]{0:T(128)}, u32[]{:S(2)}) copy-start(s32[16]{0:T(128)} %counts.1) | copy-start | bytes 196
  0.0 12.8 %copy-start.4 = (s32[16]{0:T(128)S(1)}, s32[16]{0:T(128)}, u32[]{:S(2)}) copy-start(s32[16]{0:T(128)} %placement.1) | copy-start | bytes 196
  0.0 12.8 %copy-start.5 = (s32[2]{0:T(128)S(1)}, s32[2]{0:T(128)}, u32[]{:S(2)}) copy-start(s32[2]{0:T(128)} %lengths.1) | copy-start | bytes 28
  0.0 12.8 %copy-start.6 = (s32[16]{0:T(128)S(1)}, s32[16]{0:T(128)}, u32[]{:S(2)}) copy-start(s32[16]{0:T(128)} %last.1) | copy-start | bytes 196
  5.3 19.6 %all-to-all-start = ((bf16[16,96,128]{2,1,0:T(8,128)(2,1)}), bf16[16,96,128]{2,1,0:T(8,128)(2,1)S(1)}, u32[]{:S(2)}, u32[]{:S(2)}) async-start(bf16[16,96,128]{2,1,0:T(8,128)(2,1)} %project.1), calls=%async_computation | async-start | bytes 786432 | tf_op jit(solution)/shard_map/all_to_all | solution.py:333

commit v14 on v13

--- a/solution.py
+++ b/solution.py
@@ -124,7 +124,17 @@
     for c in range(chunks):
         h_copies[c].wait()
         w_copies[c].wait()
-        total = total + lax.dot_general(h_s[c], w_s[c], NT, preferred_element_type=jnp.float32)
+        quarter = width // chunks // 4
+        sums = [
+            lax.dot_general(
+                h_s[c, :, i * quarter : (i + 1) * quarter],
+                w_s[c, :, i * quarter : (i + 1) * quarter],
+                NT,
+                preferred_element_type=jnp.float32,
+            )
+            for i in range(4)
+        ]
+        total = total + ((sums[0] + sums[1]) + (sums[2] + sums[3]))
     base_s[tokens:] = jnp.zeros((BLK, HD), jnp.float32)
     if features < HD:
         base_s[...] = jnp.zeros_like(base_s)

time: 27 us -> 27.3 us (1.011)
  Pallas kernels: 10 us -> 10.4 us
    pallas_call x1, Pallas kernels: 5.28 us -> 5.6 us  [body(): pl.pallas_call(functools.partial(project_kernel, dec_rows, d_chunks, chun...]
where the time goes in v14:
time: 27.3 us; the launch traced here: 27.1 us
  Pallas kernels  10.4 us (38%)
  waiting for transfers between devices  9.22 us (34%)
  starting transfers between devices  7.41 us (27%)
    all_to_all x1, waiting for transfers between devices, body(): lax.all_to_all(outgoing, 'tensor', split_axis=0, concat_axis=0, tiled=True)  9.22 us
    all_to_all x1, starting transfers between devices, body(): lax.all_to_all(outgoing, 'tensor', split_axis=0, concat_axis=0, tiled=True)  7.41 us
    pallas_call x1, Pallas kernels, body(): pl.pallas_call(functools.partial(project_kernel, dec_rows, d_chunks, chun...  5.6 us
    pallas_call x1, Pallas kernels, body(): pl.pallas_call(cached_kernel, out_shape=(state,) * 4, in_specs=[SMEM_SPEC...  2.9 us
    pallas_call x1, Pallas kernels, body(): pl.pallas_call(functools.partial(merge_kernel, features), out_shape=jax.S...  1.87 us
  transfers between devices with their start and end apart: 1, of which 1 were waited for; matrix products, arithmetic and copies ran while one was open for 0% of the time, Pallas kernels for 11%

profile of v14, /device:TPU:0, one launch (start us, length us, event | category | flops | bytes accessed | tf_op | source)
XLA Modules:
  0.0 27.1 jit_solution(10755111028274558607)
XLA Ops:
  0.0 0.0 copy-start
  0.0 0.0 copy-start.1
  0.0 0.0 copy-start.2
  0.0 0.0 copy-start.3
  0.0 0.0 copy-start.4
  0.0 0.0 copy-start.5
  0.0 0.0 copy-start.6
  0.0 5.6 %project.1 = bf16[16,96,128]{2,1,0:T(8,128)(2,1)} custom-call(s32[16]{0:T(128)} %tenant_h.1, s32[8]{0:T(128)} %table_h.1, s32[16]{0:T(128)} %counts.1, s32[16]{0:T(128)} %placement.1, bf16[160,8192]{1,0:T(8,128)(2,1)} %hidden.1, bf16[128,8192]{1,0:T(8,128)(2,1)} %weight.1, bf16[512,16,128]{2,1,0:T(8,128)(2,1)} %down.1, bf16[16,64,128]{2,1,0:T(8,128)(2,1)} %bitcast.19), custom_call_target="tpu_custom_call" | custom-call | tf_op jit(solution)/shard_map/project/pallas_call | solution.py:309
  5.6 7.4 %all-to-all-start = ((bf16[16,96,128]{2,1,0:T(8,128)(2,1)}), bf16[16,96,128]{2,1,0:T(8,128)(2,1)S(1)}, u32[]{:S(2)}, u32[]{:S(2)}) async-start(bf16[16,96,128]{2,1,0:T(8,128)(2,1)} %project.1), calls=%async_computation | async-start | bytes 786432 | tf_op jit(solution)/shard_map/all_to_all | solution.py:343
  13.1 0.0 copy-done
  13.1 0.0 copy-done.1
  13.1 0.0 copy-done.2
  13.1 0.0 copy-done.3
  13.1 0.0 copy-done.4
  13.1 0.0 copy-done.5
  13.1 0.0 copy-done.6
  13.1 2.9 %cached.1 = (f32[512,128]{1,0:T(8,128)S(1)}, f32[512,128]{1,0:T(8,128)S(1)}, f32[512,128]{1,0:T(8,128)S(1)}, f32[512,128]{1,0:T(8,128)S(1)}) custom-call(s32[2]{0:T(128)S(1)} %copy-done.5, s32[16]{0:T(128)S(1)} %copy-done.3, s32[16]{0:T(128)S(1)} %copy-done.6, s32[16]{0:T(128)S(1)} %copy-done.4, bf16[2,128,2048]{2,1,0:T(8,128)(2,1)S(1)} %copy-done, ...), custom_call_target="tpu_custom_call" | custom-call | tf_op jit(solution)/shard_map/cached/pallas_call | solution.py:350
  16.0 9.2 %all-to-all-done.box = bf16[16,96,128]{2,1,0:T(8,128)(2,1)S(1)} async-done(((bf16[16,96,128]{2,1,0:T(8,128)(2,1)}), bf16[16,96,128]{2,1,0:T(8,128)(2,1)S(1)}, u32[]{:S(2)}, u32[]{:S(2)}) %all-to-all-start) | async-done | bytes 393248 | tf_op jit(solution)/shard_map/all_to_all | solution.py:343
  25.3 1.9 %merge.1 = bf16[512,128]{1,0:T(8,128)(2,1)} custom-call(bf16[16,96,128]{2,1,0:T(8,128)(2,1)S(1)} %all-to-all-done.box, f32[512,128]{1,0:T(8,128)S(1)} %get-tuple-element.9.acc, f32[512,128]{1,0:T(8,128)S(1)} %get-tuple-element.10.top_in, f32[512,128]{1,0:T(8,128)S(1)} %get-tuple-element.11.total_in, f32[512,128]{1,0:T(8,128)S(1)} %get-tuple-element.12.fresh_ok, ...), custom_call_target="tpu_custom_call" | custom-call | tf_op jit(solution)/shard_map/merge/pallas_call | solution.py:361
Async XLA Ops:
  0.0 13.1 %copy-start = (bf16[2,128,2048]{2,1,0:T(8,128)(2,1)S(1)}, bf16[2,128,2048]{2,1,0:T(8,128)(2,1)}, u32[]{:S(2)}) copy-start(bf16[2,128,2048]{2,1,0:T(8,128)(2,1)} %cache.1) | copy-start | bytes 3145732
  0.0 13.1 %copy-start.1 = (bf16[4,2,8192]{2,1,0:T(2,128)(2,1)S(1)}, bf16[4,2,8192]{2,1,0:T(2,128)(2,1)}, u32[]{:S(2)}) copy-start(bf16[4,2,8192]{2,1,0:T(2,128)(2,1)} %param.24) | copy-start | bytes 393220
  0.0 13.1 %copy-start.2 = (bf16[4,2,2048]{2,1,0:T(2,128)(2,1)S(1)}, bf16[4,2,2048]{2,1,0:T(2,128)(2,1)}, u32[]{:S(2)}) copy-start(bf16[4,2,2048]{2,1,0:T(2,128)(2,1)} %param.25) | copy-start | bytes 98308
  0.0 13.1 %copy-start.3 = (s32[16]{0:T(128)S(1)}, s32[16]{0:T(128)}, u32[]{:S(2)}) copy-start(s32[16]{0:T(128)} %counts.1) | copy-start | bytes 196
  0.0 13.1 %copy-start.4 = (s32[16]{0:T(128)S(1)}, s32[16]{0:T(128)}, u32[]{:S(2)}) copy-start(s32[16]{0:T(128)} %placement.1) | copy-start | bytes 196
  0.0 13.1 %copy-start.5 = (s32[2]{0:T(128)S(1)}, s32[2]{0:T(128)}, u32[]{:S(2)}) copy-start(s32[2]{0:T(128)} %lengths.1) | copy-start | bytes 28
  0.0 13.1 %copy-start.6 = (s32[16]{0:T(128)S(1)}, s32[16]{0:T(128)}, u32[]{:S(2)}) copy-start(s32[16]{0:T(128)} %last.1) | copy-start | bytes 196
  5.6 19.6 %all-to-all-start = ((bf16[16,96,128]{2,1,0:T(8,128)(2,1)}), bf16[16,96,128]{2,1,0:T(8,128)(2,1)S(1)}, u32[]{:S(2)}, u32[]{:S(2)}) async-start(bf16[16,96,128]{2,1,0:T(8,128)(2,1)} %project.1), calls=%async_computation | async-start | bytes 786432 | tf_op jit(solution)/shard_map/all_to_all | solution.py:343

commit v15 on v10

--- a/solution.py
+++ b/solution.py
@@ -34,9 +34,9 @@
 
 
 def project_kernel(
-    dec_rows, d_chunks, chunks, tenant_h, table_h, counts_h, placement_h, hidden, weight, down, up, out,
+    dec_rows, parts, tenant_h, table_h, counts_h, placement_h, hidden, weight, down, up, out,
     tenant, table, counts, placement,
-    h_s, w_s, wt_s, d_s, mine_s, u_s, sel_s, part_s, base_s, dest_table, h_sems, d_sems, sems,
+    h_s, w_s, wt_s, d_s, mine_s, u_s, sel_s, part_s, base_s, dest_table, w_sems, sems,
 ):
     tokens, width = hidden.shape
     features = weight.shape[0]
@@ -45,8 +45,7 @@
     requests = tenant.shape[0]
     devices = out.shape[0]
     me = lax.axis_index("tensor")
-    d_step = local // d_chunks
-    step = width // chunks
+    step = width // parts
 
     int_copies = [
         pltpu.make_async_copy(src, dst, sems.at[3 + i])
@@ -54,22 +53,18 @@
             ((table_h, table), (tenant_h, tenant), (counts_h, counts), (placement_h, placement))
         )
     ]
-    d_copies = [
+    w_copies = [
         pltpu.make_async_copy(
-            down.at[pl.ds(c * d_step, d_step)], d_s.at[pl.ds(c * d_step, d_step)], d_sems.at[c])
-        for c in range(d_chunks)
+            weight.at[:, pl.ds(c * step, step)], w_s.at[:, pl.ds(c * step, step)], w_sems.at[c])
+        for c in range(parts)
     ]
+    d_copy = pltpu.make_async_copy(down, d_s, sems.at[0])
     my_copy = pltpu.make_async_copy(
-        hidden.at[:, pl.ds(pl.multiple_of(me * local, 128), local)], mine_s, sems.at[0]
-    )
-    up_copy = pltpu.make_async_copy(up, u_s, sems.at[1])
-    w_copy = pltpu.make_async_copy(weight, w_s, sems.at[2])
-    h_copies = [
-        pltpu.make_async_copy(
-            hidden.at[:, pl.ds(c * step, step)], h_s.at[:, pl.ds(c * step, step)], h_sems.at[c])
-        for c in range(chunks)
-    ]
-    for copy in int_copies + d_copies + [my_copy, w_copy, up_copy] + h_copies:
+        hidden.at[:, pl.ds(pl.multiple_of(me * local, 128), local)], mine_s, sems.at[1]
+    )
+    h_copy = pltpu.make_async_copy(hidden, h_s, sems.at[2])
+    up_copy = pltpu.make_async_copy(up, u_s, sems.at[7])
+    for copy in w_copies + int_copies + [d_copy, my_copy, h_copy, up_copy]:
         copy.start()
 
     int_copies[0].wait()
@@ -81,19 +76,28 @@
     pick = (mod(rows, 16) == div(cols, pages)) & (mod(cols, pages) == page_of_row)
     pick = jnp.where(pick, jnp.float32(1), jnp.float32(0)).astype(jnp.bfloat16)
 
-    for c in range(d_chunks):
-        d_copies[c].wait()
-        for b in range(c * d_step // 16, (c + 1) * d_step // 16, 2):
-            block = jnp.concatenate(
-                [d_s[pl.ds((b + i) * 16, 16)].reshape(16 * pages, rank2) for i in range(2)], axis=1
-            )
-            chosen = jnp.dot(pick, block, preferred_element_type=jnp.float32)
-            for i in range(2):
-                sel_s[b + i] = chosen[:, i * rank2 : (i + 1) * rank2].astype(jnp.bfloat16)
-    my_copy.wait()
-    w_copy.wait()
-    if features == HD:
-        wt_s[...] = w_s[...].T
+    def turn(c):
+        if features == HD:
+            wt_s[pl.ds(c * step, step), :] = w_s[:, pl.ds(c * step, step)].T
+
+    early = parts // 2
+    for c in range(early):
+        w_copies[c].wait()
+        turn(c)
+    for c in range(early, parts):
+        w_copies[c].wait()
+    d_copy.wait()
+    for c in range(early, parts):
+        turn(c)
+    for b in range(0, local // 16, 2):
+        block = jnp.concatenate(
+            [d_s[pl.ds((b + i) * 16, 16)].reshape(16 * pages, rank2) for i in range(2)], axis=1
+        )
+        chosen = jnp.dot(pick, block, preferred_element_type=jnp.float32)
+        for i in range(2):
+            sel_s[b + i] = chosen[:, i * rank2 : (i + 1) * rank2].astype(jnp.bfloat16)
+    for copy in int_copies[1:] + [my_copy, h_copy, up_copy]:
+        copy.wait()
     mine = mine_s[...]
     for k in range(0, tenants, 2):
         pair = min(2, tenants - k)
@@ -105,8 +109,6 @@
         for j in range(pair):
             part_s[k + j, :tokens] = product[:, j * rank2 : (j + 1) * rank2]
             part_s[k + j, tokens:] = jnp.zeros((BLK, rank2), jnp.float32)
-    for copy in int_copies[1:]:
-        copy.wait()
     if requests < devices:
         for dest in range(devices):
             dest_table[0, dest] = 0
@@ -118,23 +120,14 @@
         dest_table[1, dest] = tenant[r]
         first = first + counts[r]
 
-    total = jnp.zeros((tokens, features), jnp.float32)
-    for c in range(chunks):
-        h_copies[c].wait()
-        lanes = slice(c * step, (c + 1) * step)
-        if features == HD:
-            total = total + jnp.dot(
-                h_s[:, lanes], wt_s[lanes, :], preferred_element_type=jnp.float32
-            )
-        else:
-            total = total + lax.dot_general(
-                h_s[:, lanes], w_s[:, lanes], NT, preferred_element_type=jnp.float32
-            )
+    if features == HD:
+        total = jnp.dot(h_s[...], wt_s[...], preferred_element_type=jnp.float32)
+    else:
+        total = lax.dot_general(h_s[...], w_s[...], NT, preferred_element_type=jnp.float32)
     base_s[tokens:] = jnp.zeros((BLK, HD), jnp.float32)
     if features < HD:
         base_s[...] = jnp.zeros_like(base_s)
     base_s[:tokens, :features] = total
-    up_copy.wait()
     for dest in range(devices):
         start = pl.multiple_of(dest_table[0, dest], BLK)
         who = dest_table[1, dest]
@@ -298,11 +291,11 @@
     dec_rows, ctx, kv_width = key_value_cache.shape
     steps = step_key_value.shape[0]
     heads2 = kv_width // HD
-    d_chunks, chunks = 2, 2
+    parts = 4
     up_by_page = jnp.transpose(adapter_up_weight, (1, 2, 0))
     rows = 2 * CAPT + rank
     outgoing = pl.pallas_call(
-        functools.partial(project_kernel, dec_rows, d_chunks, chunks),
+        functools.partial(project_kernel, dec_rows, parts),
         out_shape=pltpu.VMEM((devices, rows, HD), WIRE),
         in_specs=[ANY_SPEC] * 8,
         out_specs=VMEM_SPEC,
@@ -321,9 +314,8 @@
             pltpu.VMEM((tenants, tokens + BLK, rank2), jnp.float32),
             pltpu.VMEM((tokens + BLK, HD), jnp.float32),
             pltpu.SMEM((2, devices), jnp.int32),
-            pltpu.SemaphoreType.DMA((chunks,)),
-            pltpu.SemaphoreType.DMA((d_chunks,)),
-            pltpu.SemaphoreType.DMA((7,)),
+            pltpu.SemaphoreType.DMA((parts,)),
+            pltpu.SemaphoreType.DMA((8,)),
         ],
         compiler_params=pltpu.CompilerParams(vmem_limit_bytes=PROJECT_VMEM),
         name="project",

time: 27.4 us -> 27.2 us (level)
  no operation moved by 1% of the time
where the time goes in v15:
time: 27.2 us; the launch traced here: 27 us
  Pallas kernels  10.2 us (38%)
  waiting for transfers between devices  9.22 us (34%)
  starting transfers between devices  7.41 us (27%)
    all_to_all x1, waiting for transfers between devices, body(): lax.all_to_all(outgoing, 'tensor', split_axis=0, concat_axis=0, tiled=True)  9.22 us
    all_to_all x1, starting transfers between devices, body(): lax.all_to_all(outgoing, 'tensor', split_axis=0, concat_axis=0, tiled=True)  7.41 us
    pallas_call x1, Pallas kernels, body(): pl.pallas_call(functools.partial(project_kernel, dec_rows, parts), out_sh...  5.45 us
    pallas_call x1, Pallas kernels, body(): pl.pallas_call(cached_kernel, out_shape=(state,) * 4, in_specs=[SMEM_SPEC...  2.9 us
    pallas_call x1, Pallas kernels, body(): pl.pallas_call(functools.partial(merge_kernel, features), out_shape=jax.S...  1.87 us
  transfers between devices with their start and end apart: 1, of which 1 were waited for; matrix products, arithmetic and copies ran while one was open for 0% of the time, Pallas kernels for 11%

profile of v15, /device:TPU:0, one launch (start us, length us, event | category | flops | bytes accessed | tf_op | source)
XLA Modules:
  0.0 27.0 jit_solution(4174221172072938053)
XLA Ops:
  0.0 0.0 copy-start
  0.0 0.0 copy-start.1
  0.0 0.0 copy-start.2
  0.0 0.0 copy-start.3
  0.0 0.0 copy-start.4
  0.0 0.0 copy-start.5
  0.0 0.0 copy-start.6
  0.0 5.4 %project.1 = bf16[16,96,128]{2,1,0:T(8,128)(2,1)} custom-call(s32[16]{0:T(128)} %tenant_h.1, s32[8]{0:T(128)} %table_h.1, s32[16]{0:T(128)} %counts.1, s32[16]{0:T(128)} %placement.1, bf16[160,8192]{1,0:T(8,128)(2,1)} %hidden.1, bf16[128,8192]{1,0:T(8,128)(2,1)} %weight.1, bf16[512,16,128]{2,1,0:T(8,128)(2,1)} %down.1, bf16[16,64,128]{2,1,0:T(8,128)(2,1)} %bitcast.19), custom_call_target="tpu_custom_call" | custom-call | tf_op jit(solution)/shard_map/project/pallas_call | solution.py:297
  5.5 7.4 %all-to-all-start = ((bf16[16,96,128]{2,1,0:T(8,128)(2,1)}), bf16[16,96,128]{2,1,0:T(8,128)(2,1)S(1)}, u32[]{:S(2)}, u32[]{:S(2)}) async-start(bf16[16,96,128]{2,1,0:T(8,128)(2,1)} %project.1), calls=%async_computation | async-start | bytes 786432 | tf_op jit(solution)/shard_map/all_to_all | solution.py:331
  12.9 0.0 copy-done
  12.9 0.0 copy-done.1
  12.9 0.0 copy-done.2
  12.9 0.0 copy-done.3
  12.9 0.0 copy-done.4
  13.0 0.0 copy-done.5
  13.0 0.0 copy-done.6
  13.0 2.9 %cached.1 = (f32[512,128]{1,0:T(8,128)S(1)}, f32[512,128]{1,0:T(8,128)S(1)}, f32[512,128]{1,0:T(8,128)S(1)}, f32[512,128]{1,0:T(8,128)S(1)}) custom-call(s32[2]{0:T(128)S(1)} %copy-done.5, s32[16]{0:T(128)S(1)} %copy-done.3, s32[16]{0:T(128)S(1)} %copy-done.6, s32[16]{0:T(128)S(1)} %copy-done.4, bf16[2,128,2048]{2,1,0:T(8,128)(2,1)S(1)} %copy-done, ...), custom_call_target="tpu_custom_call" | custom-call | tf_op jit(solution)/shard_map/cached/pallas_call | solution.py:338
  15.9 9.2 %all-to-all-done.box = bf16[16,96,128]{2,1,0:T(8,128)(2,1)S(1)} async-done(((bf16[16,96,128]{2,1,0:T(8,128)(2,1)}), bf16[16,96,128]{2,1,0:T(8,128)(2,1)S(1)}, u32[]{:S(2)}, u32[]{:S(2)}) %all-to-all-start) | async-done | bytes 393248 | tf_op jit(solution)/shard_map/all_to_all | solution.py:331
  25.1 1.9 %merge.1 = bf16[512,128]{1,0:T(8,128)(2,1)} custom-call(bf16[16,96,128]{2,1,0:T(8,128)(2,1)S(1)} %all-to-all-done.box, f32[512,128]{1,0:T(8,128)S(1)} %get-tuple-element.9.acc, f32[512,128]{1,0:T(8,128)S(1)} %get-tuple-element.10.top_in, f32[512,128]{1,0:T(8,128)S(1)} %get-tuple-element.11.total_in, f32[512,128]{1,0:T(8,128)S(1)} %get-tuple-element.12.fresh_ok, ...), custom_call_target="tpu_custom_call" | custom-call | tf_op jit(solution)/shard_map/merge/pallas_call | solution.py:349
Async XLA Ops:
  0.0 12.9 %copy-start = (bf16[2,128,2048]{2,1,0:T(8,128)(2,1)S(1)}, bf16[2,128,2048]{2,1,0:T(8,128)(2,1)}, u32[]{:S(2)}) copy-start(bf16[2,128,2048]{2,1,0:T(8,128)(2,1)} %cache.1) | copy-start | bytes 3145732
  0.0 12.9 %copy-start.1 = (bf16[4,2,8192]{2,1,0:T(2,128)(2,1)S(1)}, bf16[4,2,8192]{2,1,0:T(2,128)(2,1)}, u32[]{:S(2)}) copy-start(bf16[4,2,8192]{2,1,0:T(2,128)(2,1)} %param.24) | copy-start | bytes 393220
  0.0 12.9 %copy-start.2 = (bf16[4,2,2048]{2,1,0:T(2,128)(2,1)S(1)}, bf16[4,2,2048]{2,1,0:T(2,128)(2,1)}, u32[]{:S(2)}) copy-start(bf16[4,2,2048]{2,1,0:T(2,128)(2,1)} %param.25) | copy-start | bytes 98308
  0.0 12.9 %copy-start.3 = (s32[16]{0:T(128)S(1)}, s32[16]{0:T(128)}, u32[]{:S(2)}) copy-start(s32[16]{0:T(128)} %counts.1) | copy-start | bytes 196
  0.0 12.9 %copy-start.4 = (s32[16]{0:T(128)S(1)}, s32[16]{0:T(128)}, u32[]{:S(2)}) copy-start(s32[16]{0:T(128)} %placement.1) | copy-start | bytes 196
  0.0 12.9 %copy-start.5 = (s32[2]{0:T(128)S(1)}, s32[2]{0:T(128)}, u32[]{:S(2)}) copy-start(s32[2]{0:T(128)} %lengths.1) | copy-start | bytes 28
  0.0 12.9 %copy-start.6 = (s32[16]{0:T(128)S(1)}, s32[16]{0:T(128)}, u32[]{:S(2)}) copy-start(s32[16]{0:T(128)} %last.1) | copy-start | bytes 196
  5.5 19.6 %all-to-all-start = ((bf16[16,96,128]{2,1,0:T(8,128)(2,1)}), bf16[16,96,128]{2,1,0:T(8,128)(2,1)S(1)}, u32[]{:S(2)}, u32[]{:S(2)}) async-start(bf16[16,96,128]{2,1,0:T(8,128)(2,1)} %project.1), calls=%async_computation | async-start | bytes 786432 | tf_op jit(solution)/shard_map/all_to_all | solution.py:331

commit v16 on v12

--- a/solution.py
+++ b/solution.py
@@ -346,7 +346,7 @@
         name="cached",
     )(
         context_length, request_block_count, last_block_tokens, placement,
-        key_value_cache, query, steps_kv,
+        pltpu.with_memory_space_constraint(key_value_cache, pltpu.HBM), query, steps_kv,
     )
     attended = pl.pallas_call(
         functools.partial(merge_kernel, features),

time: 27 us -> 27.1 us (level)
  Pallas kernels: 10 us -> 10.7 us
  waiting for transfers between devices: 9.22 us -> 8.55 us
    pallas_call x1, Pallas kernels: 2.9 us -> 3.58 us  [body(): pl.pallas_call(cached_kernel, out_shape=(state,) * 4, in_specs=[SMEM_SPEC...]
    all_to_all x1, waiting for transfers between devices: 9.22 us -> 8.55 us  [body(): lax.all_to_all(outgoing, 'tensor', split_axis=0, concat_axis=0, tiled=True)]
  transfers between devices with their start and end apart: 1 -> 1, of which waited for: 1 -> 1; matrix products, arithmetic and copies ran while one was open for 0% -> 0% of each run, Pallas kernels for 11% -> 13%
where the time goes in v16:
time: 27.1 us; the launch traced here: 26.8 us
  Pallas kernels  10.7 us (39%)
  waiting for transfers between devices  8.55 us (32%)
  starting transfers between devices  7.48 us (28%)
    all_to_all x1, waiting for transfers between devices, body(): lax.all_to_all(outgoing, 'tensor', split_axis=0, concat_axis=0, tiled=True)  8.55 us
    all_to_all x1, starting transfers between devices, body(): lax.all_to_all(outgoing, 'tensor', split_axis=0, concat_axis=0, tiled=True)  7.48 us
    pallas_call x1, Pallas kernels, body(): pl.pallas_call(functools.partial(project_kernel, dec_rows, d_chunks, chun...  5.24 us
    pallas_call x1, Pallas kernels, body(): pl.pallas_call(cached_kernel, out_shape=(state,) * 4, in_specs=[SMEM_SPEC...  3.58 us
    pallas_call x1, Pallas kernels, body(): pl.pallas_call(functools.partial(merge_kernel, features), out_shape=jax.S...  1.87 us
  transfers between devices with their start and end apart: 1, of which 1 were waited for; matrix products, arithmetic and copies ran while one was open for 0% of the time, Pallas kernels for 13%

profile of v16, /device:TPU:0, one launch (start us, length us, event | category | flops | bytes accessed | tf_op | source)
XLA Modules:
  0.0 26.8 jit_solution(11328880267772151668)
XLA Ops:
  0.0 0.0 copy-start
  0.0 0.0 copy-start.1
  0.0 0.0 copy-start.2
  0.0 0.0 copy-start.3
  0.0 0.0 copy-start.4
  0.0 0.0 copy-start.5
  0.0 5.2 %project.1 = bf16[16,96,128]{2,1,0:T(8,128)(2,1)} custom-call(s32[16]{0:T(128)} %tenant_h.1, s32[8]{0:T(128)} %table_h.1, s32[16]{0:T(128)} %counts.1, s32[16]{0:T(128)} %placement.1, bf16[160,8192]{1,0:T(8,128)(2,1)} %hidden.1, bf16[128,8192]{1,0:T(8,128)(2,1)} %weight.1, bf16[512,16,128]{2,1,0:T(8,128)(2,1)} %down.1, bf16[16,64,128]{2,1,0:T(8,128)(2,1)} %bitcast.19), custom_call_target="tpu_custom_call" | custom-call | tf_op jit(solution)/shard_map/project/pallas_call | solution.py:299
  5.3 7.5 %all-to-all-start = ((bf16[16,96,128]{2,1,0:T(8,128)(2,1)}), bf16[16,96,128]{2,1,0:T(8,128)(2,1)S(1)}, u32[]{:S(2)}, u32[]{:S(2)}) async-start(bf16[16,96,128]{2,1,0:T(8,128)(2,1)} %project.1), calls=%async_computation | async-start | bytes 786432 | tf_op jit(solution)/shard_map/all_to_all | solution.py:333
  12.8 0.0 copy-done
  12.8 0.0 copy-done.1
  12.8 0.0 copy-done.2
  12.8 0.0 copy-done.3
  12.8 0.0 copy-done.4
  12.8 0.0 copy-done.5
  12.8 3.6 %cached.1 = (f32[512,128]{1,0:T(8,128)S(1)}, f32[512,128]{1,0:T(8,128)S(1)}, f32[512,128]{1,0:T(8,128)S(1)}, f32[512,128]{1,0:T(8,128)S(1)}) custom-call(s32[2]{0:T(128)S(1)} %copy-done.4, s32[16]{0:T(128)S(1)} %copy-done.2, s32[16]{0:T(128)S(1)} %copy-done.5, s32[16]{0:T(128)S(1)} %copy-done.3, bf16[2,128,2048]{2,1,0:T(8,128)(2,1)} %cache.1, ...), custom_call_target="tpu_custom_call" | custom-call | tf_op jit(solution)/shard_map/cached/pallas_call | solution.py:340
  16.4 8.6 %all-to-all-done.box = bf16[16,96,128]{2,1,0:T(8,128)(2,1)S(1)} async-done(((bf16[16,96,128]{2,1,0:T(8,128)(2,1)}), bf16[16,96,128]{2,1,0:T(8,128)(2,1)S(1)}, u32[]{:S(2)}, u32[]{:S(2)}) %all-to-all-start) | async-done | bytes 393248 | tf_op jit(solution)/shard_map/all_to_all | solution.py:333
  24.9 1.9 %merge.1 = bf16[512,128]{1,0:T(8,128)(2,1)} custom-call(bf16[16,96,128]{2,1,0:T(8,128)(2,1)S(1)} %all-to-all-done.box, f32[512,128]{1,0:T(8,128)S(1)} %get-tuple-element.9.acc, f32[512,128]{1,0:T(8,128)S(1)} %get-tuple-element.10.top_in, f32[512,128]{1,0:T(8,128)S(1)} %get-tuple-element.11.total_in, f32[512,128]{1,0:T(8,128)S(1)} %get-tuple-element.12.fresh_ok, ...), custom_call_target="tpu_custom_call" | custom-call | tf_op jit(solution)/shard_map/merge/pallas_call | solution.py:351
Async XLA Ops:
  0.0 12.8 %copy-start = (bf16[4,2,8192]{2,1,0:T(2,128)(2,1)S(1)}, bf16[4,2,8192]{2,1,0:T(2,128)(2,1)}, u32[]{:S(2)}) copy-start(bf16[4,2,8192]{2,1,0:T(2,128)(2,1)} %param.24) | copy-start | bytes 393220
  0.0 12.8 %copy-start.1 = (bf16[4,2,2048]{2,1,0:T(2,128)(2,1)S(1)}, bf16[4,2,2048]{2,1,0:T(2,128)(2,1)}, u32[]{:S(2)}) copy-start(bf16[4,2,2048]{2,1,0:T(2,128)(2,1)} %param.25) | copy-start | bytes 98308
  0.0 12.8 %copy-start.2 = (s32[16]{0:T(128)S(1)}, s32[16]{0:T(128)}, u32[]{:S(2)}) copy-start(s32[16]{0:T(128)} %counts.1) | copy-start | bytes 196
  0.0 12.8 %copy-start.3 = (s32[16]{0:T(128)S(1)}, s32[16]{0:T(128)}, u32[]{:S(2)}) copy-start(s32[16]{0:T(128)} %placement.1) | copy-start | bytes 196
  0.0 12.8 %copy-start.4 = (s32[2]{0:T(128)S(1)}, s32[2]{0:T(128)}, u32[]{:S(2)}) copy-start(s32[2]{0:T(128)} %lengths.1) | copy-start | bytes 28
  0.0 12.8 %copy-start.5 = (s32[16]{0:T(128)S(1)}, s32[16]{0:T(128)}, u32[]{:S(2)}) copy-start(s32[16]{0:T(128)} %last.1) | copy-start | bytes 196
  5.3 19.7 %all-to-all-start = ((bf16[16,96,128]{2,1,0:T(8,128)(2,1)}), bf16[16,96,128]{2,1,0:T(8,128)(2,1)S(1)}, u32[]{:S(2)}, u32[]{:S(2)}) async-start(bf16[16,96,128]{2,1,0:T(8,128)(2,1)} %project.1), calls=%async_computation | async-start | bytes 786432 | tf_op jit(solution)/shard_map/all_to_all | solution.py:333

commit v17 on v12

--- a/solution.py
+++ b/solution.py
@@ -78,13 +78,9 @@
         h_copies[c].start()
         w_copies[c].start()
 
-    int_copies[0].wait()
-    rows = lax.broadcasted_iota(jnp.int32, (tenants * 16, 16 * pages), 0)
-    cols = lax.broadcasted_iota(jnp.int32, (tenants * 16, 16 * pages), 1)
-    page_of_row = jnp.zeros_like(rows)
-    for k in range(tenants):
-        page_of_row = jnp.where(div(rows, 16) == k, table[k], page_of_row)
-    pick = (mod(rows, 16) == div(cols, pages)) & (mod(cols, pages) == page_of_row)
+    rows = lax.broadcasted_iota(jnp.int32, (pages * 16, 16 * pages), 0)
+    cols = lax.broadcasted_iota(jnp.int32, (pages * 16, 16 * pages), 1)
+    pick = (mod(rows, 16) == div(cols, pages)) & (mod(cols, pages) == div(rows, 16))
     pick = jnp.where(pick, jnp.float32(1), jnp.float32(0)).astype(jnp.bfloat16)
 
     for c in range(d_chunks):
@@ -96,7 +92,7 @@
             chosen = jnp.dot(pick, block, preferred_element_type=jnp.float32)
             for i in range(2):
                 sel_s[b + i] = chosen[:, i * rank2 : (i + 1) * rank2].astype(jnp.bfloat16)
-    for copy in int_copies[1:]:
+    for copy in int_copies:
         copy.wait()
     for dest in range(devices):
         dest_table[0, dest] = 0
@@ -112,7 +108,10 @@
     for k in range(0, tenants, 2):
         pair = min(2, tenants - k)
         maps = jnp.concatenate(
-            [sel_s[:, j * 16 : (j + 1) * 16, :].reshape(local, rank2) for j in range(k, k + pair)],
+            [
+                sel_s[:, pl.ds(pl.multiple_of(table[j] * 16, 16), 16), :].reshape(local, rank2)
+                for j in range(k, k + pair)
+            ],
             axis=1,
         )
         product = jnp.dot(mine, maps, preferred_element_type=jnp.float32)
@@ -311,7 +310,7 @@
             pltpu.VMEM((local, pages, rank2), jnp.bfloat16),
             pltpu.VMEM((tokens, local), jnp.bfloat16),
             pltpu.VMEM((pages, rank, features), jnp.bfloat16),
-            pltpu.VMEM((local // 16, tenants * 16, rank2), jnp.bfloat16),
+            pltpu.VMEM((local // 16, pages * 16, rank2), jnp.bfloat16),
             pltpu.VMEM((tenants, tokens + BLK, rank2), jnp.float32),
             pltpu.VMEM((tokens + BLK, HD), jnp.float32),
             pltpu.SMEM((2, devices), jnp.int32),

time: 27 us -> 27.7 us (1.026)
  Pallas kernels: 10 us -> 10.7 us
    pallas_call x1, Pallas kernels: 5.28 us -> 5.93 us  [body(): pl.pallas_call(functools.partial(project_kernel, dec_rows, d_chunks, chun...]
where the time goes in v17:
time: 27.7 us; the launch traced here: 27.5 us
  Pallas kernels  10.7 us (39%)
  waiting for transfers between devices  9.22 us (33%)
  starting transfers between devices  7.41 us (27%)
    all_to_all x1, waiting for transfers between devices, body(): lax.all_to_all(outgoing, 'tensor', split_axis=0, concat_axis=0, tiled=True)  9.22 us
    all_to_all x1, starting transfers between devices, body(): lax.all_to_all(outgoing, 'tensor', split_axis=0, concat_axis=0, tiled=True)  7.41 us
    pallas_call x1, Pallas kernels, body(): pl.pallas_call(functools.partial(project_kernel, dec_rows, d_chunks, chun...  5.93 us
    pallas_call x1, Pallas kernels, body(): pl.pallas_call(cached_kernel, out_shape=(state,) * 4, in_specs=[SMEM_SPEC...  2.9 us
    pallas_call x1, Pallas kernels, body(): pl.pallas_call(functools.partial(merge_kernel, features), out_shape=jax.S...  1.87 us
  transfers between devices with their start and end apart: 1, of which 1 were waited for; matrix products, arithmetic and copies ran while one was open for 0% of the time, Pallas kernels for 11%

profile of v17, /device:TPU:0, one launch (start us, length us, event | category | flops | bytes accessed | tf_op | source)
XLA Modules:
  0.0 27.5 jit_solution(4913785939639260196)
XLA Ops:
  0.0 0.0 copy-start
  0.0 0.0 copy-start.1
  0.0 0.0 copy-start.2
  0.0 0.0 copy-start.3
  0.0 0.0 copy-start.4
  0.0 0.0 copy-start.5
  0.0 0.0 copy-start.6
  0.0 5.9 %project.1 = bf16[16,96,128]{2,1,0:T(8,128)(2,1)} custom-call(s32[16]{0:T(128)} %tenant_h.1, s32[8]{0:T(128)} %table_h.1, s32[16]{0:T(128)} %counts.1, s32[16]{0:T(128)} %placement.1, bf16[160,8192]{1,0:T(8,128)(2,1)} %hidden.1, bf16[128,8192]{1,0:T(8,128)(2,1)} %weight.1, bf16[512,16,128]{2,1,0:T(8,128)(2,1)} %down.1, bf16[16,64,128]{2,1,0:T(8,128)(2,1)} %bitcast.19), custom_call_target="tpu_custom_call" | custom-call | tf_op jit(solution)/shard_map/project/pallas_call | solution.py:298
  6.0 7.4 %all-to-all-start = ((bf16[16,96,128]{2,1,0:T(8,128)(2,1)}), bf16[16,96,128]{2,1,0:T(8,128)(2,1)S(1)}, u32[]{:S(2)}, u32[]{:S(2)}) async-start(bf16[16,96,128]{2,1,0:T(8,128)(2,1)} %project.1), calls=%async_computation | async-start | bytes 786432 | tf_op jit(solution)/shard_map/all_to_all | solution.py:332
  13.4 0.0 copy-done
  13.4 0.0 copy-done.1
  13.4 0.0 copy-done.2
  13.4 0.0 copy-done.3
  13.4 0.0 copy-done.4
  13.4 0.0 copy-done.5
  13.5 0.0 copy-done.6
  13.5 2.9 %cached.1 = (f32[512,128]{1,0:T(8,128)S(1)}, f32[512,128]{1,0:T(8,128)S(1)}, f32[512,128]{1,0:T(8,128)S(1)}, f32[512,128]{1,0:T(8,128)S(1)}) custom-call(s32[2]{0:T(128)S(1)} %copy-done.5, s32[16]{0:T(128)S(1)} %copy-done.3, s32[16]{0:T(128)S(1)} %copy-done.6, s32[16]{0:T(128)S(1)} %copy-done.4, bf16[2,128,2048]{2,1,0:T(8,128)(2,1)S(1)} %copy-done, ...), custom_call_target="tpu_custom_call" | custom-call | tf_op jit(solution)/shard_map/cached/pallas_call | solution.py:339
  16.4 9.2 %all-to-all-done.box = bf16[16,96,128]{2,1,0:T(8,128)(2,1)S(1)} async-done(((bf16[16,96,128]{2,1,0:T(8,128)(2,1)}), bf16[16,96,128]{2,1,0:T(8,128)(2,1)S(1)}, u32[]{:S(2)}, u32[]{:S(2)}) %all-to-all-start) | async-done | bytes 393248 | tf_op jit(solution)/shard_map/all_to_all | solution.py:332
  25.6 1.9 %merge.1 = bf16[512,128]{1,0:T(8,128)(2,1)} custom-call(bf16[16,96,128]{2,1,0:T(8,128)(2,1)S(1)} %all-to-all-done.box, f32[512,128]{1,0:T(8,128)S(1)} %get-tuple-element.9.acc, f32[512,128]{1,0:T(8,128)S(1)} %get-tuple-element.10.top_in, f32[512,128]{1,0:T(8,128)S(1)} %get-tuple-element.11.total_in, f32[512,128]{1,0:T(8,128)S(1)} %get-tuple-element.12.fresh_ok, ...), custom_call_target="tpu_custom_call" | custom-call | tf_op jit(solution)/shard_map/merge/pallas_call | solution.py:350
Async XLA Ops:
  0.0 13.4 %copy-start = (bf16[2,128,2048]{2,1,0:T(8,128)(2,1)S(1)}, bf16[2,128,2048]{2,1,0:T(8,128)(2,1)}, u32[]{:S(2)}) copy-start(bf16[2,128,2048]{2,1,0:T(8,128)(2,1)} %cache.1) | copy-start | bytes 3145732
  0.0 13.4 %copy-start.1 = (bf16[4,2,8192]{2,1,0:T(2,128)(2,1)S(1)}, bf16[4,2,8192]{2,1,0:T(2,128)(2,1)}, u32[]{:S(2)}) copy-start(bf16[4,2,8192]{2,1,0:T(2,128)(2,1)} %param.24) | copy-start | bytes 393220
  0.0 13.4 %copy-start.2 = (bf16[4,2,2048]{2,1,0:T(2,128)(2,1)S(1)}, bf16[4,2,2048]{2,1,0:T(2,128)(2,1)}, u32[]{:S(2)}) copy-start(bf16[4,2,2048]{2,1,0:T(2,128)(2,1)} %param.25) | copy-start | bytes 98308
  0.0 13.4 %copy-start.3 = (s32[16]{0:T(128)S(1)}, s32[16]{0:T(128)}, u32[]{:S(2)}) copy-start(s32[16]{0:T(128)} %counts.1) | copy-start | bytes 196
  0.0 13.4 %copy-start.4 = (s32[16]{0:T(128)S(1)}, s32[16]{0:T(128)}, u32[]{:S(2)}) copy-start(s32[16]{0:T(128)} %placement.1) | copy-start | bytes 196
  0.0 13.4 %copy-start.5 = (s32[2]{0:T(128)S(1)}, s32[2]{0:T(128)}, u32[]{:S(2)}) copy-start(s32[2]{0:T(128)} %lengths.1) | copy-start | bytes 28
  0.0 13.4 %copy-start.6 = (s32[16]{0:T(128)S(1)}, s32[16]{0:T(128)}, u32[]{:S(2)}) copy-start(s32[16]{0:T(128)} %last.1) | copy-start | bytes 196
  6.0 19.6 %all-to-all-start = ((bf16[16,96,128]{2,1,0:T(8,128)(2,1)}), bf16[16,96,128]{2,1,0:T(8,128)(2,1)S(1)}, u32[]{:S(2)}, u32[]{:S(2)}) async-start(bf16[16,96,128]{2,1,0:T(8,128)(2,1)} %project.1), calls=%async_computation | async-start | bytes 786432 | tf_op jit(solution)/shard_map/all_to_all | solution.py:332

commit v18 on v15

--- a/solution.py
+++ b/solution.py
@@ -121,7 +121,15 @@
         first = first + counts[r]
 
     if features == HD:
-        total = jnp.dot(h_s[...], wt_s[...], preferred_element_type=jnp.float32)
+        sums = [
+            jnp.dot(
+                h_s[:, c * step : (c + 1) * step],
+                wt_s[c * step : (c + 1) * step, :],
+                preferred_element_type=jnp.float32,
+            )
+            for c in range(parts)
+        ]
+        total = (sums[0] + sums[1]) + (sums[2] + sums[3])
     else:
         total = lax.dot_general(h_s[...], w_s[...], NT, preferred_element_type=jnp.float32)
     base_s[tokens:] = jnp.zeros((BLK, HD), jnp.float32)

time: 27.2 us -> 27.2 us (level)
  no operation moved by 1% of the time
where the time goes in v18:
time: 27.2 us; the launch traced here: 27 us
  Pallas kernels  10.2 us (38%)
  waiting for transfers between devices  9.22 us (34%)
  starting transfers between devices  7.41 us (27%)
    all_to_all x1, waiting for transfers between devices, body(): lax.all_to_all(outgoing, 'tensor', split_axis=0, concat_axis=0, tiled=True)  9.22 us
    all_to_all x1, starting transfers between devices, body(): lax.all_to_all(outgoing, 'tensor', split_axis=0, concat_axis=0, tiled=True)  7.41 us
    pallas_call x1, Pallas kernels, body(): pl.pallas_call(functools.partial(project_kernel, dec_rows, parts), out_sh...  5.45 us
    pallas_call x1, Pallas kernels, body(): pl.pallas_call(cached_kernel, out_shape=(state,) * 4, in_specs=[SMEM_SPEC...  2.9 us
    pallas_call x1, Pallas kernels, body(): pl.pallas_call(functools.partial(merge_kernel, features), out_shape=jax.S...  1.86 us
  transfers between devices with their start and end apart: 1, of which 1 were waited for; matrix products, arithmetic and copies ran while one was open for 0% of the time, Pallas kernels for 11%

profile of v18, /device:TPU:0, one launch (start us, length us, event | category | flops | bytes accessed | tf_op | source)
XLA Modules:
  0.0 27.0 jit_solution(12065738618307275713)
XLA Ops:
  0.0 0.0 copy-start
  0.0 0.0 copy-start.1
  0.0 0.0 copy-start.2
  0.0 0.0 copy-start.3
  0.0 0.0 copy-start.4
  0.0 0.0 copy-start.5
  0.0 0.0 copy-start.6
  0.0 5.4 %project.1 = bf16[16,96,128]{2,1,0:T(8,128)(2,1)} custom-call(s32[16]{0:T(128)} %tenant_h.1, s32[8]{0:T(128)} %table_h.1, s32[16]{0:T(128)} %counts.1, s32[16]{0:T(128)} %placement.1, bf16[160,8192]{1,0:T(8,128)(2,1)} %hidden.1, bf16[128,8192]{1,0:T(8,128)(2,1)} %weight.1, bf16[512,16,128]{2,1,0:T(8,128)(2,1)} %down.1, bf16[16,64,128]{2,1,0:T(8,128)(2,1)} %bitcast.19), custom_call_target="tpu_custom_call" | custom-call | tf_op jit(solution)/shard_map/project/pallas_call | solution.py:305
  5.5 7.4 %all-to-all-start = ((bf16[16,96,128]{2,1,0:T(8,128)(2,1)}), bf16[16,96,128]{2,1,0:T(8,128)(2,1)S(1)}, u32[]{:S(2)}, u32[]{:S(2)}) async-start(bf16[16,96,128]{2,1,0:T(8,128)(2,1)} %project.1), calls=%async_computation | async-start | bytes 786432 | tf_op jit(solution)/shard_map/all_to_all | solution.py:339
  12.9 0.0 copy-done
  12.9 0.0 copy-done.1
  12.9 0.0 copy-done.2
  12.9 0.0 copy-done.3
  12.9 0.0 copy-done.4
  13.0 0.0 copy-done.5
  13.0 0.0 copy-done.6
  13.0 2.9 %cached.1 = (f32[512,128]{1,0:T(8,128)S(1)}, f32[512,128]{1,0:T(8,128)S(1)}, f32[512,128]{1,0:T(8,128)S(1)}, f32[512,128]{1,0:T(8,128)S(1)}) custom-call(s32[2]{0:T(128)S(1)} %copy-done.5, s32[16]{0:T(128)S(1)} %copy-done.3, s32[16]{0:T(128)S(1)} %copy-done.6, s32[16]{0:T(128)S(1)} %copy-done.4, bf16[2,128,2048]{2,1,0:T(8,128)(2,1)S(1)} %copy-done, ...), custom_call_target="tpu_custom_call" | custom-call | tf_op jit(solution)/shard_map/cached/pallas_call | solution.py:346
  15.9 9.2 %all-to-all-done.box = bf16[16,96,128]{2,1,0:T(8,128)(2,1)S(1)} async-done(((bf16[16,96,128]{2,1,0:T(8,128)(2,1)}), bf16[16,96,128]{2,1,0:T(8,128)(2,1)S(1)}, u32[]{:S(2)}, u32[]{:S(2)}) %all-to-all-start) | async-done | bytes 393248 | tf_op jit(solution)/shard_map/all_to_all | solution.py:339
  25.1 1.9 %merge.1 = bf16[512,128]{1,0:T(8,128)(2,1)} custom-call(bf16[16,96,128]{2,1,0:T(8,128)(2,1)S(1)} %all-to-all-done.box, f32[512,128]{1,0:T(8,128)S(1)} %get-tuple-element.9.acc, f32[512,128]{1,0:T(8,128)S(1)} %get-tuple-element.10.top_in, f32[512,128]{1,0:T(8,128)S(1)} %get-tuple-element.11.total_in, f32[512,128]{1,0:T(8,128)S(1)} %get-tuple-element.12.fresh_ok, ...), custom_call_target="tpu_custom_call" | custom-call | tf_op jit(solution)/shard_map/merge/pallas_call | solution.py:357
Async XLA Ops:
  0.0 12.9 %copy-start = (bf16[2,128,2048]{2,1,0:T(8,128)(2,1)S(1)}, bf16[2,128,2048]{2,1,0:T(8,128)(2,1)}, u32[]{:S(2)}) copy-start(bf16[2,128,2048]{2,1,0:T(8,128)(2,1)} %cache.1) | copy-start | bytes 3145732
  0.0 12.9 %copy-start.1 = (bf16[4,2,8192]{2,1,0:T(2,128)(2,1)S(1)}, bf16[4,2,8192]{2,1,0:T(2,128)(2,1)}, u32[]{:S(2)}) copy-start(bf16[4,2,8192]{2,1,0:T(2,128)(2,1)} %param.24) | copy-start | bytes 393220
  0.0 12.9 %copy-start.2 = (bf16[4,2,2048]{2,1,0:T(2,128)(2,1)S(1)}, bf16[4,2,2048]{2,1,0:T(2,128)(2,1)}, u32[]{:S(2)}) copy-start(bf16[4,2,2048]{2,1,0:T(2,128)(2,1)} %param.25) | copy-start | bytes 98308
  0.0 12.9 %copy-start.3 = (s32[16]{0:T(128)S(1)}, s32[16]{0:T(128)}, u32[]{:S(2)}) copy-start(s32[16]{0:T(128)} %counts.1) | copy-start | bytes 196
  0.0 12.9 %copy-start.4 = (s32[16]{0:T(128)S(1)}, s32[16]{0:T(128)}, u32[]{:S(2)}) copy-start(s32[16]{0:T(128)} %placement.1) | copy-start | bytes 196
  0.0 12.9 %copy-start.5 = (s32[2]{0:T(128)S(1)}, s32[2]{0:T(128)}, u32[]{:S(2)}) copy-start(s32[2]{0:T(128)} %lengths.1) | copy-start | bytes 28
  0.0 12.9 %copy-start.6 = (s32[16]{0:T(128)S(1)}, s32[16]{0:T(128)}, u32[]{:S(2)}) copy-start(s32[16]{0:T(128)} %last.1) | copy-start | bytes 196
  5.5 19.6 %all-to-all-start = ((bf16[16,96,128]{2,1,0:T(8,128)(2,1)}), bf16[16,96,128]{2,1,0:T(8,128)(2,1)S(1)}, u32[]{:S(2)}, u32[]{:S(2)}) async-start(bf16[16,96,128]{2,1,0:T(8,128)(2,1)} %project.1), calls=%async_computation | async-start | bytes 786432 | tf_op jit(solution)/shard_map/all_to_all | solution.py:339

commit v19 on v12

--- a/solution.py
+++ b/solution.py
@@ -120,15 +120,15 @@
             part_s[k + j, :tokens] = product[:, j * rank2 : (j + 1) * rank2]
             part_s[k + j, tokens:] = jnp.zeros((BLK, rank2), jnp.float32)
 
-    total = jnp.zeros((tokens, features), jnp.float32)
+    total = jnp.zeros((features, tokens), jnp.float32)
     for c in range(chunks):
         h_copies[c].wait()
         w_copies[c].wait()
-        total = total + lax.dot_general(h_s[c], w_s[c], NT, preferred_element_type=jnp.float32)
+        total = total + lax.dot_general(w_s[c], h_s[c], NT, preferred_element_type=jnp.float32)
     base_s[tokens:] = jnp.zeros((BLK, HD), jnp.float32)
     if features < HD:
         base_s[...] = jnp.zeros_like(base_s)
-    base_s[:tokens, :features] = total
+    base_s[:tokens, :features] = total.T
     up_copy.wait()
     for dest in range(devices):
         start = pl.multiple_of(dest_table[0, dest], BLK)

time: 27 us -> 27.1 us (level)
  no operation moved by 1% of the time
where the time goes in v19:
time: 27.1 us; the launch traced here: 26.9 us
  Pallas kernels  10.1 us (37%)
  waiting for transfers between devices  9.22 us (34%)
  starting transfers between devices  7.41 us (27%)
    all_to_all x1, waiting for transfers between devices, body(): lax.all_to_all(outgoing, 'tensor', split_axis=0, concat_axis=0, tiled=True)  9.22 us
    all_to_all x1, starting transfers between devices, body(): lax.all_to_all(outgoing, 'tensor', split_axis=0, concat_axis=0, tiled=True)  7.41 us
    pallas_call x1, Pallas kernels, body(): pl.pallas_call(functools.partial(project_kernel, dec_rows, d_chunks, chun...  5.35 us
    pallas_call x1, Pallas kernels, body(): pl.pallas_call(cached_kernel, out_shape=(state,) * 4, in_specs=[SMEM_SPEC...  2.9 us
    pallas_call x1, Pallas kernels, body(): pl.pallas_call(functools.partial(merge_kernel, features), out_shape=jax.S...  1.87 us
  transfers between devices with their start and end apart: 1, of which 1 were waited for; matrix products, arithmetic and copies ran while one was open for 0% of the time, Pallas kernels for 11%

profile of v19, /device:TPU:0, one launch (start us, length us, event | category | flops | bytes accessed | tf_op | source)
XLA Modules:
  0.0 26.9 jit_solution(10361553562564460661)
XLA Ops:
  0.0 0.0 copy-start
  0.0 0.0 copy-start.1
  0.0 0.0 copy-start.2
  0.0 0.0 copy-start.3
  0.0 0.0 copy-start.4
  0.0 0.0 copy-start.5
  0.0 0.0 copy-start.6
  0.0 5.3 %project.1 = bf16[16,96,128]{2,1,0:T(8,128)(2,1)} custom-call(s32[16]{0:T(128)} %tenant_h.1, s32[8]{0:T(128)} %table_h.1, s32[16]{0:T(128)} %counts.1, s32[16]{0:T(128)} %placement.1, bf16[160,8192]{1,0:T(8,128)(2,1)} %hidden.1, bf16[128,8192]{1,0:T(8,128)(2,1)} %weight.1, bf16[512,16,128]{2,1,0:T(8,128)(2,1)} %down.1, bf16[16,64,128]{2,1,0:T(8,128)(2,1)} %bitcast.19), custom_call_target="tpu_custom_call" | custom-call | tf_op jit(solution)/shard_map/project/pallas_call | solution.py:299
  5.4 7.4 %all-to-all-start = ((bf16[16,96,128]{2,1,0:T(8,128)(2,1)}), bf16[16,96,128]{2,1,0:T(8,128)(2,1)S(1)}, u32[]{:S(2)}, u32[]{:S(2)}) async-start(bf16[16,96,128]{2,1,0:T(8,128)(2,1)} %project.1), calls=%async_computation | async-start | bytes 786432 | tf_op jit(solution)/shard_map/all_to_all | solution.py:333
  12.8 0.0 copy-done
  12.8 0.0 copy-done.1
  12.8 0.0 copy-done.2
  12.8 0.0 copy-done.3
  12.8 0.0 copy-done.4
  12.9 0.0 copy-done.5
  12.9 0.0 copy-done.6
  12.9 2.9 %cached.1 = (f32[512,128]{1,0:T(8,128)S(1)}, f32[512,128]{1,0:T(8,128)S(1)}, f32[512,128]{1,0:T(8,128)S(1)}, f32[512,128]{1,0:T(8,128)S(1)}) custom-call(s32[2]{0:T(128)S(1)} %copy-done.5, s32[16]{0:T(128)S(1)} %copy-done.3, s32[16]{0:T(128)S(1)} %copy-done.6, s32[16]{0:T(128)S(1)} %copy-done.4, bf16[2,128,2048]{2,1,0:T(8,128)(2,1)S(1)} %copy-done, ...), custom_call_target="tpu_custom_call" | custom-call | tf_op jit(solution)/shard_map/cached/pallas_call | solution.py:340
  15.8 9.2 %all-to-all-done.box = bf16[16,96,128]{2,1,0:T(8,128)(2,1)S(1)} async-done(((bf16[16,96,128]{2,1,0:T(8,128)(2,1)}), bf16[16,96,128]{2,1,0:T(8,128)(2,1)S(1)}, u32[]{:S(2)}, u32[]{:S(2)}) %all-to-all-start) | async-done | bytes 393248 | tf_op jit(solution)/shard_map/all_to_all | solution.py:333
  25.0 1.9 %merge.1 = bf16[512,128]{1,0:T(8,128)(2,1)} custom-call(bf16[16,96,128]{2,1,0:T(8,128)(2,1)S(1)} %all-to-all-done.box, f32[512,128]{1,0:T(8,128)S(1)} %get-tuple-element.9.acc, f32[512,128]{1,0:T(8,128)S(1)} %get-tuple-element.10.top_in, f32[512,128]{1,0:T(8,128)S(1)} %get-tuple-element.11.total_in, f32[512,128]{1,0:T(8,128)S(1)} %get-tuple-element.12.fresh_ok, ...), custom_call_target="tpu_custom_call" | custom-call | tf_op jit(solution)/shard_map/merge/pallas_call | solution.py:351
Async XLA Ops:
  0.0 12.8 %copy-start = (bf16[2,128,2048]{2,1,0:T(8,128)(2,1)S(1)}, bf16[2,128,2048]{2,1,0:T(8,128)(2,1)}, u32[]{:S(2)}) copy-start(bf16[2,128,2048]{2,1,0:T(8,128)(2,1)} %cache.1) | copy-start | bytes 3145732
  0.0 12.8 %copy-start.1 = (bf16[4,2,8192]{2,1,0:T(2,128)(2,1)S(1)}, bf16[4,2,8192]{2,1,0:T(2,128)(2,1)}, u32[]{:S(2)}) copy-start(bf16[4,2,8192]{2,1,0:T(2,128)(2,1)} %param.24) | copy-start | bytes 393220
  0.0 12.8 %copy-start.2 = (bf16[4,2,2048]{2,1,0:T(2,128)(2,1)S(1)}, bf16[4,2,2048]{2,1,0:T(2,128)(2,1)}, u32[]{:S(2)}) copy-start(bf16[4,2,2048]{2,1,0:T(2,128)(2,1)} %param.25) | copy-start | bytes 98308
  0.0 12.8 %copy-start.3 = (s32[16]{0:T(128)S(1)}, s32[16]{0:T(128)}, u32[]{:S(2)}) copy-start(s32[16]{0:T(128)} %counts.1) | copy-start | bytes 196
  0.0 12.8 %copy-start.4 = (s32[16]{0:T(128)S(1)}, s32[16]{0:T(128)}, u32[]{:S(2)}) copy-start(s32[16]{0:T(128)} %placement.1) | copy-start | bytes 196
  0.0 12.8 %copy-start.5 = (s32[2]{0:T(128)S(1)}, s32[2]{0:T(128)}, u32[]{:S(2)}) copy-start(s32[2]{0:T(128)} %lengths.1) | copy-start | bytes 28
  0.0 12.8 %copy-start.6 = (s32[16]{0:T(128)S(1)}, s32[16]{0:T(128)}, u32[]{:S(2)}) copy-start(s32[16]{0:T(128)} %last.1) | copy-start | bytes 196
  5.4 19.6 %all-to-all-start = ((bf16[16,96,128]{2,1,0:T(8,128)(2,1)}), bf16[16,96,128]{2,1,0:T(8,128)(2,1)S(1)}, u32[]{:S(2)}, u32[]{:S(2)}) async-start(bf16[16,96,128]{2,1,0:T(8,128)(2,1)} %project.1), calls=%async_computation | async-start | bytes 786432 | tf_op jit(solution)/shard_map/all_to_all | solution.py:333

commit v20 on v12

--- a/solution.py
+++ b/solution.py
@@ -150,7 +150,8 @@
 
 
 def cached_kernel(
-    lengths, counts, last, placement, cache, query, steps_kv, acc, top_out, total_out, fresh_ok,
+    lengths, counts, last, placement, cache, query, steps_kv,
+    query_t, acc_t, top_t, total_t, fresh_ok, acc, top_out, total_out,
 ):
     dec_rows, ctx, kv_width = cache.shape
     half_width = kv_width // 2
@@ -210,17 +211,21 @@
         hit = div(placement[r], dec_rows) == lax.axis_index("tensor")
         my_slot = jnp.where(hit, mod(placement[r], dec_rows), my_slot)
         my_length = jnp.where(hit, (counts[r] - 1) * BLK + last[r], my_length)
-    row = lax.broadcasted_iota(jnp.int32, fresh_ok.shape, 0)
-    col = lax.broadcasted_iota(jnp.int32, fresh_ok.shape, 1)
+    col = lax.broadcasted_iota(jnp.int32, fresh_ok.shape, 0)
+    row = lax.broadcasted_iota(jnp.int32, fresh_ok.shape, 1)
     ok = (
         (mod(div(row, group), KVH) == div(col, CAPT))
         & (mod(row, dec_rows) == my_slot)
         & (mod(col, CAPT) < my_length)
     )
     fresh_ok[...] = jnp.where(ok, jnp.float32(1), jnp.float32(0))
-
-
-def merge_kernel(features, box, acc, top_in, total_in, fresh_ok, query, out, result, sems):
+    query_t[...] = query[...].T
+    acc_t[...] = acc[...].T
+    top_t[...] = top_out[...].T[: top_t.shape[0]]
+    total_t[...] = total_out[...].T[: total_t.shape[0]]
+
+
+def merge_kernel(features, box, query_t, acc_t, top_t, total_t, fresh_ok, out, result, sems):
     devices = box.shape[0]
     rank = box.shape[1] - 2 * CAPT
     terms = [box[i, :CAPT].astype(jnp.float32) for i in range(devices)]
@@ -246,23 +251,24 @@
                 made.append(both.astype(jnp.bfloat16))
         return jnp.concatenate(made, axis=0)
 
-    keys, values = fresh(0), fresh(KVH)
+    keys = fresh(0)
+    values_t = fresh(KVH).T
     scale = HD ** (-0.5)
     part = out.shape[0] // sems.shape[0]
     copies = []
     for c in range(sems.shape[0]):
         here = pl.ds(c * part, part)
-        s = lax.dot_general(query[here, :], keys, NT, preferred_element_type=jnp.float32)
-        s = jnp.where(fresh_ok[here, :] > 0, s * scale, NEG_LARGE)
-        old = top_in[here, :]
-        top = jnp.maximum(old, jnp.max(s, axis=1, keepdims=True))
+        s = jnp.dot(keys, query_t[:, here], preferred_element_type=jnp.float32)
+        s = jnp.where(fresh_ok[:, here] > 0, s * scale, NEG_LARGE)
+        old = top_t[:1, here]
+        top = jnp.maximum(old, jnp.max(s, axis=0, keepdims=True))
         fade = jnp.exp(old - top)
         w = jnp.exp(s - top)
-        total = total_in[here, :] * fade + jnp.sum(w, axis=1, keepdims=True)
-        mixed = acc[here, :] * fade + jnp.dot(
-            w.astype(jnp.bfloat16), values, preferred_element_type=jnp.float32
-        )
-        result[here, :] = (mixed / total).astype(jnp.bfloat16)
+        total = total_t[:1, here] * fade + jnp.sum(w, axis=0, keepdims=True)
+        mixed = acc_t[:, here] * fade + jnp.dot(
+            values_t, w.astype(jnp.bfloat16), preferred_element_type=jnp.float32
+        )
+        result[here, :] = (mixed / total).T.astype(jnp.bfloat16)
         copies.append(pltpu.make_async_copy(result.at[here, :], out.at[here, :], sems.at[c]))
         copies[c].start()
     for copy in copies:
@@ -336,12 +342,21 @@
     query = query.transpose(0, 2, 1, 3).reshape(steps * HEADS * dec_rows, HD)
     steps_kv = step_key_value.reshape(steps, dec_rows, heads2, HD)
     steps_kv = steps_kv.transpose(0, 2, 1, 3).reshape(steps * heads2 * dec_rows, HD)
-    state = jax.ShapeDtypeStruct((steps * HEADS * dec_rows, HD), jnp.float32)
-    acc, top, total, fresh_ok = pl.pallas_call(
+    q_rows = steps * HEADS * dec_rows
+    state = jax.ShapeDtypeStruct((HD, q_rows), jnp.float32)
+    line = jax.ShapeDtypeStruct((8, q_rows), jnp.float32)
+    handed = pl.pallas_call(
         cached_kernel,
-        out_shape=(state,) * 4,
+        out_shape=(
+            jax.ShapeDtypeStruct((HD, q_rows), jnp.bfloat16),
+            state,
+            line,
+            line,
+            jax.ShapeDtypeStruct((KVH * CAPT, q_rows), jnp.float32),
+        ),
         in_specs=[SMEM_SPEC] * 4 + [VMEM_SPEC] * 3,
-        out_specs=(VMEM_SPEC,) * 4,
+        out_specs=(VMEM_SPEC,) * 5,
+        scratch_shapes=[pltpu.VMEM((q_rows, HD), jnp.float32)] * 3,
         compiler_params=pltpu.CompilerParams(vmem_limit_bytes=ATTEND_VMEM),
         name="cached",
     )(
@@ -350,16 +365,16 @@
     )
     attended = pl.pallas_call(
         functools.partial(merge_kernel, features),
-        out_shape=jax.ShapeDtypeStruct((steps * HEADS * dec_rows, HD), jnp.bfloat16),
+        out_shape=jax.ShapeDtypeStruct((q_rows, HD), jnp.bfloat16),
         in_specs=[VMEM_SPEC] * 6,
         out_specs=ANY_SPEC,
         scratch_shapes=[
-            pltpu.VMEM((steps * HEADS * dec_rows, HD), jnp.bfloat16),
+            pltpu.VMEM((q_rows, HD), jnp.bfloat16),
             pltpu.SemaphoreType.DMA((steps,)),
         ],
         compiler_params=pltpu.CompilerParams(vmem_limit_bytes=ATTEND_VMEM),
         name="merge",
-    )(arrived, acc, top, total, fresh_ok, query)
+    )(arrived, *handed)
     attended = attended.reshape(steps, HEADS, dec_rows, HD).transpose(0, 2, 1, 3)
     return attended.reshape(steps, dec_rows, HEADS * HD)
 

time: 27 us -> 26.4 us (0.978)
  Pallas kernels: 10 us -> 9.53 us
    pallas_call x1, Pallas kernels: 1.87 us -> 1.24 us  [body(): pl.pallas_call(functools.partial(merge_kernel, features), out_shape=jax.S...]
where the time goes in v20:
time: 26.4 us; the launch traced here: 26.2 us
  Pallas kernels  9.53 us (36%)
  waiting for transfers between devices  9.11 us (35%)
  starting transfers between devices  7.41 us (28%)
    all_to_all x1, waiting for transfers between devices, body(): lax.all_to_all(outgoing, 'tensor', split_axis=0, concat_axis=0, tiled=True)  9.11 us
    all_to_all x1, starting transfers between devices, body(): lax.all_to_all(outgoing, 'tensor', split_axis=0, concat_axis=0, tiled=True)  7.41 us
    pallas_call x1, Pallas kernels, body(): pl.pallas_call(functools.partial(project_kernel, dec_rows, d_chunks, chun...  5.28 us
    pallas_call x1, Pallas kernels, body(): pl.pallas_call(cached_kernel, out_shape=(jax.ShapeDtypeStruct((HD, q_rows...  3.01 us
    pallas_call x1, Pallas kernels, body(): pl.pallas_call(functools.partial(merge_kernel, features), out_shape=jax.S...  1.24 us
  transfers between devices with their start and end apart: 1, of which 1 were waited for; matrix products, arithmetic and copies ran while one was open for 0% of the time, Pallas kernels for 11%

profile of v20, /device:TPU:0, one launch (start us, length us, event | category | flops | bytes accessed | tf_op | source)
XLA Modules:
  0.0 26.2 jit_solution(9432623952473191750)
XLA Ops:
  0.0 0.0 copy-start
  0.0 0.0 copy-start.1
  0.0 0.0 copy-start.2
  0.0 0.0 copy-start.3
  0.0 0.0 copy-start.4
  0.0 0.0 copy-start.5
  0.0 0.0 copy-start.6
  0.0 5.3 %project.1 = bf16[16,96,128]{2,1,0:T(8,128)(2,1)} custom-call(s32[16]{0:T(128)} %tenant_h.1, s32[8]{0:T(128)} %table_h.1, s32[16]{0:T(128)} %counts.1, s32[16]{0:T(128)} %placement.1, bf16[160,8192]{1,0:T(8,128)(2,1)} %hidden.1, bf16[128,8192]{1,0:T(8,128)(2,1)} %weight.1, bf16[512,16,128]{2,1,0:T(8,128)(2,1)} %down.1, bf16[16,64,128]{2,1,0:T(8,128)(2,1)} %bitcast.18), custom_call_target="tpu_custom_call" | custom-call | tf_op jit(solution)/shard_map/project/pallas_call | solution.py:305
  5.3 7.4 %all-to-all-start = ((bf16[16,96,128]{2,1,0:T(8,128)(2,1)}), bf16[16,96,128]{2,1,0:T(8,128)(2,1)S(1)}, u32[]{:S(2)}, u32[]{:S(2)}) async-start(bf16[16,96,128]{2,1,0:T(8,128)(2,1)} %project.1), calls=%async_computation | async-start | bytes 786432 | tf_op jit(solution)/shard_map/all_to_all | solution.py:339
  12.7 0.0 copy-done
  12.7 0.0 copy-done.1
  12.8 0.0 copy-done.2
  12.8 0.0 copy-done.3
  12.8 0.0 copy-done.4
  12.8 0.0 copy-done.5
  12.8 0.0 copy-done.6
  12.8 3.0 %cached.1 = (bf16[128,512]{1,0:T(8,128)(2,1)S(1)}, f32[128,512]{1,0:T(8,128)S(1)}, f32[8,512]{1,0:T(8,128)S(1)}, f32[8,512]{1,0:T(8,128)S(1)}, f32[128,512]{1,0:T(8,128)S(1)}) custom-call(s32[2]{0:T(128)S(1)} %copy-done.5, s32[16]{0:T(128)S(1)} %copy-done.3, s32[16]{0:T(128)S(1)} %copy-done.6, s32[16]{0:T(128)S(1)} %copy-done.4, ...), custom_call_target="tpu_custom_call" | custom-call | tf_op jit(solution)/shard_map/cached/pallas_call | solution.py:348
  15.8 9.1 %all-to-all-done.box = bf16[16,96,128]{2,1,0:T(8,128)(2,1)S(1)} async-done(((bf16[16,96,128]{2,1,0:T(8,128)(2,1)}), bf16[16,96,128]{2,1,0:T(8,128)(2,1)S(1)}, u32[]{:S(2)}, u32[]{:S(2)}) %all-to-all-start) | async-done | bytes 393248 | tf_op jit(solution)/shard_map/all_to_all | solution.py:339
  24.9 1.2 %merge.1 = bf16[512,128]{1,0:T(8,128)(2,1)} custom-call(bf16[16,96,128]{2,1,0:T(8,128)(2,1)S(1)} %all-to-all-done.box, bf16[128,512]{1,0:T(8,128)(2,1)S(1)} %get-tuple-element.10.query_t, f32[128,512]{1,0:T(8,128)S(1)} %get-tuple-element.11.acc_t, f32[8,512]{1,0:T(8,128)S(1)} %get-tuple-element.12.top_t, f32[8,512]{1,0:T(8,128)S(1)} %get-tuple-element.13.total_t, ...), custom_call_target="tpu_custom_call" | custom-call | tf_op jit(solution)/shard_map/merge/pallas_call | solution.py:366
Async XLA Ops:
  0.0 12.7 %copy-start = (bf16[2,128,2048]{2,1,0:T(8,128)(2,1)S(1)}, bf16[2,128,2048]{2,1,0:T(8,128)(2,1)}, u32[]{:S(2)}) copy-start(bf16[2,128,2048]{2,1,0:T(8,128)(2,1)} %cache.1) | copy-start | bytes 3145732
  0.0 12.7 %copy-start.1 = (bf16[4,2,8192]{2,1,0:T(2,128)(2,1)S(1)}, bf16[4,2,8192]{2,1,0:T(2,128)(2,1)}, u32[]{:S(2)}) copy-start(bf16[4,2,8192]{2,1,0:T(2,128)(2,1)} %param.24) | copy-start | bytes 393220
  0.0 12.8 %copy-start.2 = (bf16[4,2,2048]{2,1,0:T(2,128)(2,1)S(1)}, bf16[4,2,2048]{2,1,0:T(2,128)(2,1)}, u32[]{:S(2)}) copy-start(bf16[4,2,2048]{2,1,0:T(2,128)(2,1)} %param.25) | copy-start | bytes 98308
  0.0 12.8 %copy-start.3 = (s32[16]{0:T(128)S(1)}, s32[16]{0:T(128)}, u32[]{:S(2)}) copy-start(s32[16]{0:T(128)} %counts.1) | copy-start | bytes 196
  0.0 12.8 %copy-start.4 = (s32[16]{0:T(128)S(1)}, s32[16]{0:T(128)}, u32[]{:S(2)}) copy-start(s32[16]{0:T(128)} %placement.1) | copy-start | bytes 196
  0.0 12.8 %copy-start.5 = (s32[2]{0:T(128)S(1)}, s32[2]{0:T(128)}, u32[]{:S(2)}) copy-start(s32[2]{0:T(128)} %lengths.1) | copy-start | bytes 28
  0.0 12.8 %copy-start.6 = (s32[16]{0:T(128)S(1)}, s32[16]{0:T(128)}, u32[]{:S(2)}) copy-start(s32[16]{0:T(128)} %last.1) | copy-start | bytes 196
  5.3 19.6 %all-to-all-start = ((bf16[16,96,128]{2,1,0:T(8,128)(2,1)}), bf16[16,96,128]{2,1,0:T(8,128)(2,1)S(1)}, u32[]{:S(2)}, u32[]{:S(2)}) async-start(bf16[16,96,128]{2,1,0:T(8,128)(2,1)} %project.1), calls=%async_computation | async-start | bytes 786432 | tf_op jit(solution)/shard_map/all_to_all | solution.py:339

commit v21 on v20

--- a/solution.py
+++ b/solution.py
@@ -130,14 +130,21 @@
         base_s[...] = jnp.zeros_like(base_s)
     base_s[:tokens, :features] = total
     up_copy.wait()
-    for dest in range(devices):
-        start = pl.multiple_of(dest_table[0, dest], BLK)
-        who = dest_table[1, dest]
-        out[dest, :CAPT, :] = part_s[who, pl.ds(start, CAPT), :].astype(out.dtype)
-        out[dest, CAPT : 2 * CAPT, :] = base_s[pl.ds(start, CAPT), :].astype(out.dtype)
-        if features < HD:
-            out[dest, 2 * CAPT :, :] = jnp.zeros((out.shape[1] - 2 * CAPT, HD), out.dtype)
-        out[dest, 2 * CAPT :, :features] = u_s[table[who]]
+    places = [
+        (pl.multiple_of(dest_table[0, dest], BLK), dest_table[1, dest], table[dest_table[1, dest]])
+        for dest in range(devices)
+    ]
+    for first in range(0, devices, 4):
+        group = places[first : first + 4]
+        parts = [part_s[who, pl.ds(start, CAPT), :].astype(out.dtype) for start, who, _ in group]
+        bases = [base_s[pl.ds(start, CAPT), :].astype(out.dtype) for start, _, _ in group]
+        slabs = [u_s[page] for _, _, page in group]
+        for i in range(len(group)):
+            out[first + i, :CAPT, :] = parts[i]
+            out[first + i, CAPT : 2 * CAPT, :] = bases[i]
+            if features < HD:
+                out[first + i, 2 * CAPT :, :] = jnp.zeros((out.shape[1] - 2 * CAPT, HD), out.dtype)
+            out[first + i, 2 * CAPT :, :features] = slabs[i]
 
 
 NT = (((1,), (1,)), ((), ()))

time: 26.4 us -> 26.4 us (level)
  no operation moved by 1% of the time
where the time goes in v21:
time: 26.4 us; the launch traced here: 26.2 us
  Pallas kernels  9.53 us (36%)
  waiting for transfers between devices  9.11 us (35%)
  starting transfers between devices  7.41 us (28%)
    all_to_all x1, waiting for transfers between devices, body(): lax.all_to_all(outgoing, 'tensor', split_axis=0, concat_axis=0, tiled=True)  9.11 us
    all_to_all x1, starting transfers between devices, body(): lax.all_to_all(outgoing, 'tensor', split_axis=0, concat_axis=0, tiled=True)  7.41 us
    pallas_call x1, Pallas kernels, body(): pl.pallas_call(functools.partial(project_kernel, dec_rows, d_chunks, chun...  5.28 us
    pallas_call x1, Pallas kernels, body(): pl.pallas_call(cached_kernel, out_shape=(jax.ShapeDtypeStruct((HD, q_rows...  3.01 us
    pallas_call x1, Pallas kernels, body(): pl.pallas_call(functools.partial(merge_kernel, features), out_shape=jax.S...  1.24 us
  transfers between devices with their start and end apart: 1, of which 1 were waited for; matrix products, arithmetic and copies ran while one was open for 0% of the time, Pallas kernels for 11%

profile of v21, /device:TPU:0, one launch (start us, length us, event | category | flops | bytes accessed | tf_op | source)
XLA Modules:
  0.0 26.2 jit_solution(14195733468635778532)
XLA Ops:
  0.0 0.0 copy-start
  0.0 0.0 copy-start.1
  0.0 0.0 copy-start.2
  0.0 0.0 copy-start.3
  0.0 0.0 copy-start.4
  0.0 0.0 copy-start.5
  0.0 0.0 copy-start.6
  0.0 5.3 %project.1 = bf16[16,96,128]{2,1,0:T(8,128)(2,1)} custom-call(s32[16]{0:T(128)} %tenant_h.1, s32[8]{0:T(128)} %table_h.1, s32[16]{0:T(128)} %counts.1, s32[16]{0:T(128)} %placement.1, bf16[160,8192]{1,0:T(8,128)(2,1)} %hidden.1, bf16[128,8192]{1,0:T(8,128)(2,1)} %weight.1, bf16[512,16,128]{2,1,0:T(8,128)(2,1)} %down.1, bf16[16,64,128]{2,1,0:T(8,128)(2,1)} %bitcast.18), custom_call_target="tpu_custom_call" | custom-call | tf_op jit(solution)/shard_map/project/pallas_call | solution.py:312
  5.3 7.4 %all-to-all-start = ((bf16[16,96,128]{2,1,0:T(8,128)(2,1)}), bf16[16,96,128]{2,1,0:T(8,128)(2,1)S(1)}, u32[]{:S(2)}, u32[]{:S(2)}) async-start(bf16[16,96,128]{2,1,0:T(8,128)(2,1)} %project.1), calls=%async_computation | async-start | bytes 786432 | tf_op jit(solution)/shard_map/all_to_all | solution.py:346
  12.7 0.0 copy-done
  12.7 0.0 copy-done.1
  12.8 0.0 copy-done.2
  12.8 0.0 copy-done.3
  12.8 0.0 copy-done.4
  12.8 0.0 copy-done.5
  12.8 0.0 copy-done.6
  12.8 3.0 %cached.1 = (bf16[128,512]{1,0:T(8,128)(2,1)S(1)}, f32[128,512]{1,0:T(8,128)S(1)}, f32[8,512]{1,0:T(8,128)S(1)}, f32[8,512]{1,0:T(8,128)S(1)}, f32[128,512]{1,0:T(8,128)S(1)}) custom-call(s32[2]{0:T(128)S(1)} %copy-done.5, s32[16]{0:T(128)S(1)} %copy-done.3, s32[16]{0:T(128)S(1)} %copy-done.6, s32[16]{0:T(128)S(1)} %copy-done.4, ...), custom_call_target="tpu_custom_call" | custom-call | tf_op jit(solution)/shard_map/cached/pallas_call | solution.py:355
  15.8 9.1 %all-to-all-done.box = bf16[16,96,128]{2,1,0:T(8,128)(2,1)S(1)} async-done(((bf16[16,96,128]{2,1,0:T(8,128)(2,1)}), bf16[16,96,128]{2,1,0:T(8,128)(2,1)S(1)}, u32[]{:S(2)}, u32[]{:S(2)}) %all-to-all-start) | async-done | bytes 393248 | tf_op jit(solution)/shard_map/all_to_all | solution.py:346
  24.9 1.2 %merge.1 = bf16[512,128]{1,0:T(8,128)(2,1)} custom-call(bf16[16,96,128]{2,1,0:T(8,128)(2,1)S(1)} %all-to-all-done.box, bf16[128,512]{1,0:T(8,128)(2,1)S(1)} %get-tuple-element.10.query_t, f32[128,512]{1,0:T(8,128)S(1)} %get-tuple-element.11.acc_t, f32[8,512]{1,0:T(8,128)S(1)} %get-tuple-element.12.top_t, f32[8,512]{1,0:T(8,128)S(1)} %get-tuple-element.13.total_t, ...), custom_call_target="tpu_custom_call" | custom-call | tf_op jit(solution)/shard_map/merge/pallas_call | solution.py:373
Async XLA Ops:
  0.0 12.7 %copy-start = (bf16[2,128,2048]{2,1,0:T(8,128)(2,1)S(1)}, bf16[2,128,2048]{2,1,0:T(8,128)(2,1)}, u32[]{:S(2)}) copy-start(bf16[2,128,2048]{2,1,0:T(8,128)(2,1)} %cache.1) | copy-start | bytes 3145732
  0.0 12.7 %copy-start.1 = (bf16[4,2,8192]{2,1,0:T(2,128)(2,1)S(1)}, bf16[4,2,8192]{2,1,0:T(2,128)(2,1)}, u32[]{:S(2)}) copy-start(bf16[4,2,8192]{2,1,0:T(2,128)(2,1)} %param.24) | copy-start | bytes 393220
  0.0 12.8 %copy-start.2 = (bf16[4,2,2048]{2,1,0:T(2,128)(2,1)S(1)}, bf16[4,2,2048]{2,1,0:T(2,128)(2,1)}, u32[]{:S(2)}) copy-start(bf16[4,2,2048]{2,1,0:T(2,128)(2,1)} %param.25) | copy-start | bytes 98308
  0.0 12.8 %copy-start.3 = (s32[16]{0:T(128)S(1)}, s32[16]{0:T(128)}, u32[]{:S(2)}) copy-start(s32[16]{0:T(128)} %counts.1) | copy-start | bytes 196
  0.0 12.8 %copy-start.4 = (s32[16]{0:T(128)S(1)}, s32[16]{0:T(128)}, u32[]{:S(2)}) copy-start(s32[16]{0:T(128)} %placement.1) | copy-start | bytes 196
  0.0 12.8 %copy-start.5 = (s32[2]{0:T(128)S(1)}, s32[2]{0:T(128)}, u32[]{:S(2)}) copy-start(s32[2]{0:T(128)} %lengths.1) | copy-start | bytes 28
  0.0 12.8 %copy-start.6 = (s32[16]{0:T(128)S(1)}, s32[16]{0:T(128)}, u32[]{:S(2)}) copy-start(s32[16]{0:T(128)} %last.1) | copy-start | bytes 196
  5.3 19.6 %all-to-all-start = ((bf16[16,96,128]{2,1,0:T(8,128)(2,1)}), bf16[16,96,128]{2,1,0:T(8,128)(2,1)S(1)}, u32[]{:S(2)}, u32[]{:S(2)}) async-start(bf16[16,96,128]{2,1,0:T(8,128)(2,1)} %project.1), calls=%async_computation | async-start | bytes 786432 | tf_op jit(solution)/shard_map/all_to_all | solution.py:346

commit v22 on v20

--- a/solution.py
+++ b/solution.py
@@ -36,7 +36,7 @@
 def project_kernel(
     dec_rows, d_chunks, chunks, devices, tenant_h, table_h, counts_h, placement_h, hidden, weight, down, up, out,
     tenant, table, counts, placement,
-    h_s, w_s, d_s, mine_s, u_s, sel_s, part_s, base_s, dest_table, sems, d_sems, int_sems,
+    h_s, w_s, d_s, mine_s, u_s, wide_s, part_s, base_s, dest_table, sems, d_sems, int_sems,
 ):
     tokens, width = hidden.shape
     features = weight.shape[0]
@@ -78,25 +78,11 @@
         h_copies[c].start()
         w_copies[c].start()
 
-    int_copies[0].wait()
-    rows = lax.broadcasted_iota(jnp.int32, (tenants * 16, 16 * pages), 0)
-    cols = lax.broadcasted_iota(jnp.int32, (tenants * 16, 16 * pages), 1)
-    page_of_row = jnp.zeros_like(rows)
-    for k in range(tenants):
-        page_of_row = jnp.where(div(rows, 16) == k, table[k], page_of_row)
-    pick = (mod(rows, 16) == div(cols, pages)) & (mod(cols, pages) == page_of_row)
-    pick = jnp.where(pick, jnp.float32(1), jnp.float32(0)).astype(jnp.bfloat16)
-
     for c in range(d_chunks):
         d_copies[c].wait()
-        for b in range(c * d_step // 16, (c + 1) * d_step // 16, 2):
-            block = jnp.concatenate(
-                [d_s[pl.ds((b + i) * 16, 16)].reshape(16 * pages, rank2) for i in range(2)], axis=1
-            )
-            chosen = jnp.dot(pick, block, preferred_element_type=jnp.float32)
-            for i in range(2):
-                sel_s[b + i] = chosen[:, i * rank2 : (i + 1) * rank2].astype(jnp.bfloat16)
-    for copy in int_copies[1:]:
+        part = d_s[pl.ds(c * d_step, d_step)].astype(jnp.float32)
+        wide_s[pl.ds(c * d_step * pages, d_step * pages), :] = part.reshape(d_step * pages, rank2)
+    for copy in int_copies:
         copy.wait()
     for dest in range(devices):
         dest_table[0, dest] = 0
@@ -112,7 +98,10 @@
     for k in range(0, tenants, 2):
         pair = min(2, tenants - k)
         maps = jnp.concatenate(
-            [sel_s[:, j * 16 : (j + 1) * 16, :].reshape(local, rank2) for j in range(k, k + pair)],
+            [
+                wide_s[pl.ds(table[j], local, stride=pages), :].astype(jnp.bfloat16)
+                for j in range(k, k + pair)
+            ],
             axis=1,
         )
         product = jnp.dot(mine, maps, preferred_element_type=jnp.float32)
@@ -317,7 +306,7 @@
             pltpu.VMEM((local, pages, rank2), jnp.bfloat16),
             pltpu.VMEM((tokens, local), jnp.bfloat16),
             pltpu.VMEM((pages, rank, features), jnp.bfloat16),
-            pltpu.VMEM((local // 16, tenants * 16, rank2), jnp.bfloat16),
+            pltpu.VMEM((local * pages, rank2), jnp.float32),
             pltpu.VMEM((tenants, tokens + BLK, rank2), jnp.float32),
             pltpu.VMEM((tokens + BLK, HD), jnp.float32),
             pltpu.SMEM((2, devices), jnp.int32),

time: 26.4 us -> 27.2 us (1.030)
  Pallas kernels: 9.53 us -> 10.3 us
    pallas_call x1, Pallas kernels: 5.28 us -> 6.07 us  [body(): pl.pallas_call(functools.partial(project_kernel, dec_rows, d_chunks, chun...]
where the time goes in v22:
time: 27.2 us; the launch traced here: 27 us
  Pallas kernels  10.3 us (38%)
  waiting for transfers between devices  9.11 us (33%)
  starting transfers between devices  7.41 us (27%)
    all_to_all x1, waiting for transfers between devices, body(): lax.all_to_all(outgoing, 'tensor', split_axis=0, concat_axis=0, tiled=True)  9.11 us
    all_to_all x1, starting transfers between devices, body(): lax.all_to_all(outgoing, 'tensor', split_axis=0, concat_axis=0, tiled=True)  7.41 us
    pallas_call x1, Pallas kernels, body(): pl.pallas_call(functools.partial(project_kernel, dec_rows, d_chunks, chun...  6.07 us
    pallas_call x1, Pallas kernels, body(): pl.pallas_call(cached_kernel, out_shape=(jax.ShapeDtypeStruct((HD, q_rows...  3.01 us
    pallas_call x1, Pallas kernels, body(): pl.pallas_call(functools.partial(merge_kernel, features), out_shape=jax.S...  1.24 us
  transfers between devices with their start and end apart: 1, of which 1 were waited for; matrix products, arithmetic and copies ran while one was open for 0% of the time, Pallas kernels for 11%

profile of v22, /device:TPU:0, one launch (start us, length us, event | category | flops | bytes accessed | tf_op | source)
XLA Modules:
  0.0 27.0 jit_solution(16610774272215073199)
XLA Ops:
  0.0 0.0 copy-start
  0.0 0.0 copy-start.1
  0.0 0.0 copy-start.2
  0.0 0.0 copy-start.3
  0.0 0.0 copy-start.4
  0.0 0.0 copy-start.5
  0.0 0.0 copy-start.6
  0.0 6.1 %project.1 = bf16[16,96,128]{2,1,0:T(8,128)(2,1)} custom-call(s32[16]{0:T(128)} %tenant_h.1, s32[8]{0:T(128)} %table_h.1, s32[16]{0:T(128)} %counts.1, s32[16]{0:T(128)} %placement.1, bf16[160,8192]{1,0:T(8,128)(2,1)} %hidden.1, bf16[128,8192]{1,0:T(8,128)(2,1)} %weight.1, bf16[512,16,128]{2,1,0:T(8,128)(2,1)} %down.1, bf16[16,64,128]{2,1,0:T(8,128)(2,1)} %bitcast.18), custom_call_target="tpu_custom_call" | custom-call | tf_op jit(solution)/shard_map/project/pallas_call | solution.py:294
  6.1 7.4 %all-to-all-start = ((bf16[16,96,128]{2,1,0:T(8,128)(2,1)}), bf16[16,96,128]{2,1,0:T(8,128)(2,1)S(1)}, u32[]{:S(2)}, u32[]{:S(2)}) async-start(bf16[16,96,128]{2,1,0:T(8,128)(2,1)} %project.1), calls=%async_computation | async-start | bytes 786432 | tf_op jit(solution)/shard_map/all_to_all | solution.py:328
  13.5 0.0 copy-done
  13.5 0.0 copy-done.1
  13.5 0.0 copy-done.2
  13.6 0.0 copy-done.3
  13.6 0.0 copy-done.4
  13.6 0.0 copy-done.5
  13.6 0.0 copy-done.6
  13.6 3.0 %cached.1 = (bf16[128,512]{1,0:T(8,128)(2,1)S(1)}, f32[128,512]{1,0:T(8,128)S(1)}, f32[8,512]{1,0:T(8,128)S(1)}, f32[8,512]{1,0:T(8,128)S(1)}, f32[128,512]{1,0:T(8,128)S(1)}) custom-call(s32[2]{0:T(128)S(1)} %copy-done.5, s32[16]{0:T(128)S(1)} %copy-done.3, s32[16]{0:T(128)S(1)} %copy-done.6, s32[16]{0:T(128)S(1)} %copy-done.4, ...), custom_call_target="tpu_custom_call" | custom-call | tf_op jit(solution)/shard_map/cached/pallas_call | solution.py:337
  16.6 9.1 %all-to-all-done.box = bf16[16,96,128]{2,1,0:T(8,128)(2,1)S(1)} async-done(((bf16[16,96,128]{2,1,0:T(8,128)(2,1)}), bf16[16,96,128]{2,1,0:T(8,128)(2,1)S(1)}, u32[]{:S(2)}, u32[]{:S(2)}) %all-to-all-start) | async-done | bytes 393248 | tf_op jit(solution)/shard_map/all_to_all | solution.py:328
  25.7 1.2 %merge.1 = bf16[512,128]{1,0:T(8,128)(2,1)} custom-call(bf16[16,96,128]{2,1,0:T(8,128)(2,1)S(1)} %all-to-all-done.box, bf16[128,512]{1,0:T(8,128)(2,1)S(1)} %get-tuple-element.10.query_t, f32[128,512]{1,0:T(8,128)S(1)} %get-tuple-element.11.acc_t, f32[8,512]{1,0:T(8,128)S(1)} %get-tuple-element.12.top_t, f32[8,512]{1,0:T(8,128)S(1)} %get-tuple-element.13.total_t, ...), custom_call_target="tpu_custom_call" | custom-call | tf_op jit(solution)/shard_map/merge/pallas_call | solution.py:355
Async XLA Ops:
  0.0 13.5 %copy-start = (bf16[2,128,2048]{2,1,0:T(8,128)(2,1)S(1)}, bf16[2,128,2048]{2,1,0:T(8,128)(2,1)}, u32[]{:S(2)}) copy-start(bf16[2,128,2048]{2,1,0:T(8,128)(2,1)} %cache.1) | copy-start | bytes 3145732
  0.0 13.5 %copy-start.1 = (bf16[4,2,8192]{2,1,0:T(2,128)(2,1)S(1)}, bf16[4,2,8192]{2,1,0:T(2,128)(2,1)}, u32[]{:S(2)}) copy-start(bf16[4,2,8192]{2,1,0:T(2,128)(2,1)} %param.24) | copy-start | bytes 393220
  0.0 13.5 %copy-start.2 = (bf16[4,2,2048]{2,1,0:T(2,128)(2,1)S(1)}, bf16[4,2,2048]{2,1,0:T(2,128)(2,1)}, u32[]{:S(2)}) copy-start(bf16[4,2,2048]{2,1,0:T(2,128)(2,1)} %param.25) | copy-start | bytes 98308
  0.0 13.6 %copy-start.3 = (s32[16]{0:T(128)S(1)}, s32[16]{0:T(128)}, u32[]{:S(2)}) copy-start(s32[16]{0:T(128)} %counts.1) | copy-start | bytes 196
  0.0 13.6 %copy-start.4 = (s32[16]{0:T(128)S(1)}, s32[16]{0:T(128)}, u32[]{:S(2)}) copy-start(s32[16]{0:T(128)} %placement.1) | copy-start | bytes 196
  0.0 13.6 %copy-start.5 = (s32[2]{0:T(128)S(1)}, s32[2]{0:T(128)}, u32[]{:S(2)}) copy-start(s32[2]{0:T(128)} %lengths.1) | copy-start | bytes 28
  0.0 13.6 %copy-start.6 = (s32[16]{0:T(128)S(1)}, s32[16]{0:T(128)}, u32[]{:S(2)}) copy-start(s32[16]{0:T(128)} %last.1) | copy-start | bytes 196
  6.1 19.6 %all-to-all-start = ((bf16[16,96,128]{2,1,0:T(8,128)(2,1)}), bf16[16,96,128]{2,1,0:T(8,128)(2,1)S(1)}, u32[]{:S(2)}, u32[]{:S(2)}) async-start(bf16[16,96,128]{2,1,0:T(8,128)(2,1)} %project.1), calls=%async_computation | async-start | bytes 786432 | tf_op jit(solution)/shard_map/all_to_all | solution.py:328

commit v23 on v20

--- a/solution.py
+++ b/solution.py
@@ -45,6 +45,7 @@
     requests = tenant.shape[0]
     me = lax.axis_index("tensor")
     d_step = local // d_chunks
+    wide = min(4, d_step // 16)
     step = width // chunks
 
     int_copies = [
@@ -89,12 +90,16 @@
 
     for c in range(d_chunks):
         d_copies[c].wait()
-        for b in range(c * d_step // 16, (c + 1) * d_step // 16, 2):
+        for b in range(c * d_step // 16, (c + 1) * d_step // 16, wide):
             block = jnp.concatenate(
-                [d_s[pl.ds((b + i) * 16, 16)].reshape(16 * pages, rank2) for i in range(2)], axis=1
+                [
+                    d_s[pl.ds((b + i) * 16, 16)].reshape(16 * pages, rank2)
+                    for i in range(wide)
+                ],
+                axis=1,
             )
             chosen = jnp.dot(pick, block, preferred_element_type=jnp.float32)
-            for i in range(2):
+            for i in range(wide):
                 sel_s[b + i] = chosen[:, i * rank2 : (i + 1) * rank2].astype(jnp.bfloat16)
     for copy in int_copies[1:]:
         copy.wait()
@@ -109,8 +114,8 @@
         first = first + counts[r]
     my_copy.wait()
     mine = mine_s[...]
-    for k in range(0, tenants, 2):
-        pair = min(2, tenants - k)
+    for k in range(0, tenants, 4):
+        pair = min(4, tenants - k)
         maps = jnp.concatenate(
             [sel_s[:, j * 16 : (j + 1) * 16, :].reshape(local, rank2) for j in range(k, k + pair)],
             axis=1,
@@ -242,10 +247,10 @@
 
     def fresh(first):
         made = []
-        for i in range(first, first + KVH, 2):
-            ups = jnp.concatenate([rows(i + j, 2 * CAPT, rank) for j in range(2)], axis=1)
+        for i in range(first, first + KVH, 4):
+            ups = jnp.concatenate([rows(i + j, 2 * CAPT, rank) for j in range(4)], axis=1)
             delta = jnp.dot(halves[first // KVH], ups, preferred_element_type=jnp.float32)
-            for j in range(2):
+            for j in range(4):
                 base = rows(i + j, CAPT, CAPT).astype(jnp.float32)
                 both = base + ADAPTER_SCALE * delta[:, j * HD : (j + 1) * HD]
                 made.append(both.astype(jnp.bfloat16))
@@ -370,7 +375,7 @@
         out_specs=ANY_SPEC,
         scratch_shapes=[
             pltpu.VMEM((q_rows, HD), jnp.bfloat16),
-            pltpu.SemaphoreType.DMA((steps,)),
+            pltpu.SemaphoreType.DMA((2,)),
         ],
         compiler_params=pltpu.CompilerParams(vmem_limit_bytes=ATTEND_VMEM),
         name="merge",

time: 26.4 us -> 26.4 us (level)
  no operation moved by 1% of the time
where the time goes in v23:
time: 26.4 us; the launch traced here: 26.2 us
  Pallas kernels  9.53 us (36%)
  waiting for transfers between devices  9.11 us (35%)
  starting transfers between devices  7.41 us (28%)
    all_to_all x1, waiting for transfers between devices, body(): lax.all_to_all(outgoing, 'tensor', split_axis=0, concat_axis=0, tiled=True)  9.11 us
    all_to_all x1, starting transfers between devices, body(): lax.all_to_all(outgoing, 'tensor', split_axis=0, concat_axis=0, tiled=True)  7.41 us
    pallas_call x1, Pallas kernels, body(): pl.pallas_call(functools.partial(project_kernel, dec_rows, d_chunks, chun...  5.28 us
    pallas_call x1, Pallas kernels, body(): pl.pallas_call(cached_kernel, out_shape=(jax.ShapeDtypeStruct((HD, q_rows...  3.01 us
    pallas_call x1, Pallas kernels, body(): pl.pallas_call(functools.partial(merge_kernel, features), out_shape=jax.S...  1.23 us
  transfers between devices with their start and end apart: 1, of which 1 were waited for; matrix products, arithmetic and copies ran while one was open for 0% of the time, Pallas kernels for 11%

profile of v23, /device:TPU:0, one launch (start us, length us, event | category | flops | bytes accessed | tf_op | source)
XLA Modules:
  0.0 26.2 jit_solution(915426099456392748)
XLA Ops:
  0.0 0.0 copy-start
  0.0 0.0 copy-start.1
  0.0 0.0 copy-start.2
  0.0 0.0 copy-start.3
  0.0 0.0 copy-start.4
  0.0 0.0 copy-start.5
  0.0 0.0 copy-start.6
  0.0 5.3 %project.1 = bf16[16,96,128]{2,1,0:T(8,128)(2,1)} custom-call(s32[16]{0:T(128)} %tenant_h.1, s32[8]{0:T(128)} %table_h.1, s32[16]{0:T(128)} %counts.1, s32[16]{0:T(128)} %placement.1, bf16[160,8192]{1,0:T(8,128)(2,1)} %hidden.1, bf16[128,8192]{1,0:T(8,128)(2,1)} %weight.1, bf16[512,16,128]{2,1,0:T(8,128)(2,1)} %down.1, bf16[16,64,128]{2,1,0:T(8,128)(2,1)} %bitcast.18), custom_call_target="tpu_custom_call" | custom-call | tf_op jit(solution)/shard_map/project/pallas_call | solution.py:310
  5.3 7.4 %all-to-all-start = ((bf16[16,96,128]{2,1,0:T(8,128)(2,1)}), bf16[16,96,128]{2,1,0:T(8,128)(2,1)S(1)}, u32[]{:S(2)}, u32[]{:S(2)}) async-start(bf16[16,96,128]{2,1,0:T(8,128)(2,1)} %project.1), calls=%async_computation | async-start | bytes 786432 | tf_op jit(solution)/shard_map/all_to_all | solution.py:344
  12.7 0.0 copy-done
  12.8 0.0 copy-done.1
  12.8 0.0 copy-done.2
  12.8 0.0 copy-done.3
  12.8 0.0 copy-done.4
  12.8 0.0 copy-done.5
  12.8 0.0 copy-done.6
  12.8 3.0 %cached.1 = (bf16[128,512]{1,0:T(8,128)(2,1)S(1)}, f32[128,512]{1,0:T(8,128)S(1)}, f32[8,512]{1,0:T(8,128)S(1)}, f32[8,512]{1,0:T(8,128)S(1)}, f32[128,512]{1,0:T(8,128)S(1)}) custom-call(s32[2]{0:T(128)S(1)} %copy-done.5, s32[16]{0:T(128)S(1)} %copy-done.3, s32[16]{0:T(128)S(1)} %copy-done.6, s32[16]{0:T(128)S(1)} %copy-done.4, ...), custom_call_target="tpu_custom_call" | custom-call | tf_op jit(solution)/shard_map/cached/pallas_call | solution.py:353
  15.8 9.1 %all-to-all-done.box = bf16[16,96,128]{2,1,0:T(8,128)(2,1)S(1)} async-done(((bf16[16,96,128]{2,1,0:T(8,128)(2,1)}), bf16[16,96,128]{2,1,0:T(8,128)(2,1)S(1)}, u32[]{:S(2)}, u32[]{:S(2)}) %all-to-all-start) | async-done | bytes 393248 | tf_op jit(solution)/shard_map/all_to_all | solution.py:344
  24.9 1.2 %merge.1 = bf16[512,128]{1,0:T(8,128)(2,1)} custom-call(bf16[16,96,128]{2,1,0:T(8,128)(2,1)S(1)} %all-to-all-done.box, bf16[128,512]{1,0:T(8,128)(2,1)S(1)} %get-tuple-element.10.query_t, f32[128,512]{1,0:T(8,128)S(1)} %get-tuple-element.11.acc_t, f32[8,512]{1,0:T(8,128)S(1)} %get-tuple-element.12.top_t, f32[8,512]{1,0:T(8,128)S(1)} %get-tuple-element.13.total_t, ...), custom_call_target="tpu_custom_call" | custom-call | tf_op jit(solution)/shard_map/merge/pallas_call | solution.py:371
Async XLA Ops:
  0.0 12.7 %copy-start = (bf16[2,128,2048]{2,1,0:T(8,128)(2,1)S(1)}, bf16[2,128,2048]{2,1,0:T(8,128)(2,1)}, u32[]{:S(2)}) copy-start(bf16[2,128,2048]{2,1,0:T(8,128)(2,1)} %cache.1) | copy-start | bytes 3145732
  0.0 12.8 %copy-start.1 = (bf16[4,2,8192]{2,1,0:T(2,128)(2,1)S(1)}, bf16[4,2,8192]{2,1,0:T(2,128)(2,1)}, u32[]{:S(2)}) copy-start(bf16[4,2,8192]{2,1,0:T(2,128)(2,1)} %param.24) | copy-start | bytes 393220
  0.0 12.8 %copy-start.2 = (bf16[4,2,2048]{2,1,0:T(2,128)(2,1)S(1)}, bf16[4,2,2048]{2,1,0:T(2,128)(2,1)}, u32[]{:S(2)}) copy-start(bf16[4,2,2048]{2,1,0:T(2,128)(2,1)} %param.25) | copy-start | bytes 98308
  0.0 12.8 %copy-start.3 = (s32[16]{0:T(128)S(1)}, s32[16]{0:T(128)}, u32[]{:S(2)}) copy-start(s32[16]{0:T(128)} %counts.1) | copy-start | bytes 196
  0.0 12.8 %copy-start.4 = (s32[16]{0:T(128)S(1)}, s32[16]{0:T(128)}, u32[]{:S(2)}) copy-start(s32[16]{0:T(128)} %placement.1) | copy-start | bytes 196
  0.0 12.8 %copy-start.5 = (s32[2]{0:T(128)S(1)}, s32[2]{0:T(128)}, u32[]{:S(2)}) copy-start(s32[2]{0:T(128)} %lengths.1) | copy-start | bytes 28
  0.0 12.8 %copy-start.6 = (s32[16]{0:T(128)S(1)}, s32[16]{0:T(128)}, u32[]{:S(2)}) copy-start(s32[16]{0:T(128)} %last.1) | copy-start | bytes 196
  5.3 19.6 %all-to-all-start = ((bf16[16,96,128]{2,1,0:T(8,128)(2,1)}), bf16[16,96,128]{2,1,0:T(8,128)(2,1)S(1)}, u32[]{:S(2)}, u32[]{:S(2)}) async-start(bf16[16,96,128]{2,1,0:T(8,128)(2,1)} %project.1), calls=%async_computation | async-start | bytes 786432 | tf_op jit(solution)/shard_map/all_to_all | solution.py:344

commit v24 on v20

--- a/solution.py
+++ b/solution.py
@@ -108,6 +108,8 @@
         dest_table[1, dest] = tenant[r]
         first = first + counts[r]
     my_copy.wait()
+    h_copies[0].wait()
+    w_copies[0].wait()
     mine = mine_s[...]
     for k in range(0, tenants, 2):
         pair = min(2, tenants - k)
@@ -122,8 +124,9 @@
 
     total = jnp.zeros((tokens, features), jnp.float32)
     for c in range(chunks):
-        h_copies[c].wait()
-        w_copies[c].wait()
+        if c > 0:
+            h_copies[c].wait()
+            w_copies[c].wait()
         total = total + lax.dot_general(h_s[c], w_s[c], NT, preferred_element_type=jnp.float32)
     base_s[tokens:] = jnp.zeros((BLK, HD), jnp.float32)
     if features < HD:

time: 26.4 us -> 26.4 us (level)
  no operation moved by 1% of the time
where the time goes in v24:
time: 26.4 us; the launch traced here: 26.2 us
  Pallas kernels  9.53 us (36%)
  waiting for transfers between devices  9.11 us (35%)
  starting transfers between devices  7.41 us (28%)
    all_to_all x1, waiting for transfers between devices, body(): lax.all_to_all(outgoing, 'tensor', split_axis=0, concat_axis=0, tiled=True)  9.11 us
    all_to_all x1, starting transfers between devices, body(): lax.all_to_all(outgoing, 'tensor', split_axis=0, concat_axis=0, tiled=True)  7.41 us
    pallas_call x1, Pallas kernels, body(): pl.pallas_call(functools.partial(project_kernel, dec_rows, d_chunks, chun...  5.28 us
    pallas_call x1, Pallas kernels, body(): pl.pallas_call(cached_kernel, out_shape=(jax.ShapeDtypeStruct((HD, q_rows...  3.01 us
    pallas_call x1, Pallas kernels, body(): pl.pallas_call(functools.partial(merge_kernel, features), out_shape=jax.S...  1.24 us
  transfers between devices with their start and end apart: 1, of which 1 were waited for; matrix products, arithmetic and copies ran while one was open for 0% of the time, Pallas kernels for 11%

profile of v24, /device:TPU:0, one launch (start us, length us, event | category | flops | bytes accessed | tf_op | source)
XLA Modules:
  0.0 26.2 jit_solution(14007261845914296341)
XLA Ops:
  0.0 0.0 copy-start
  0.0 0.0 copy-start.1
  0.0 0.0 copy-start.2
  0.0 0.0 copy-start.3
  0.0 0.0 copy-start.4
  0.0 0.0 copy-start.5
  0.0 0.0 copy-start.6
  0.0 5.3 %project.1 = bf16[16,96,128]{2,1,0:T(8,128)(2,1)} custom-call(s32[16]{0:T(128)} %tenant_h.1, s32[8]{0:T(128)} %table_h.1, s32[16]{0:T(128)} %counts.1, s32[16]{0:T(128)} %placement.1, bf16[160,8192]{1,0:T(8,128)(2,1)} %hidden.1, bf16[128,8192]{1,0:T(8,128)(2,1)} %weight.1, bf16[512,16,128]{2,1,0:T(8,128)(2,1)} %down.1, bf16[16,64,128]{2,1,0:T(8,128)(2,1)} %bitcast.18), custom_call_target="tpu_custom_call" | custom-call | tf_op jit(solution)/shard_map/project/pallas_call | solution.py:308
  5.3 7.4 %all-to-all-start = ((bf16[16,96,128]{2,1,0:T(8,128)(2,1)}), bf16[16,96,128]{2,1,0:T(8,128)(2,1)S(1)}, u32[]{:S(2)}, u32[]{:S(2)}) async-start(bf16[16,96,128]{2,1,0:T(8,128)(2,1)} %project.1), calls=%async_computation | async-start | bytes 786432 | tf_op jit(solution)/shard_map/all_to_all | solution.py:342
  12.7 0.0 copy-done
  12.7 0.0 copy-done.1
  12.8 0.0 copy-done.2
  12.8 0.0 copy-done.3
  12.8 0.0 copy-done.4
  12.8 0.0 copy-done.5
  12.8 0.0 copy-done.6
  12.8 3.0 %cached.1 = (bf16[128,512]{1,0:T(8,128)(2,1)S(1)}, f32[128,512]{1,0:T(8,128)S(1)}, f32[8,512]{1,0:T(8,128)S(1)}, f32[8,512]{1,0:T(8,128)S(1)}, f32[128,512]{1,0:T(8,128)S(1)}) custom-call(s32[2]{0:T(128)S(1)} %copy-done.5, s32[16]{0:T(128)S(1)} %copy-done.3, s32[16]{0:T(128)S(1)} %copy-done.6, s32[16]{0:T(128)S(1)} %copy-done.4, ...), custom_call_target="tpu_custom_call" | custom-call | tf_op jit(solution)/shard_map/cached/pallas_call | solution.py:351
  15.8 9.1 %all-to-all-done.box = bf16[16,96,128]{2,1,0:T(8,128)(2,1)S(1)} async-done(((bf16[16,96,128]{2,1,0:T(8,128)(2,1)}), bf16[16,96,128]{2,1,0:T(8,128)(2,1)S(1)}, u32[]{:S(2)}, u32[]{:S(2)}) %all-to-all-start) | async-done | bytes 393248 | tf_op jit(solution)/shard_map/all_to_all | solution.py:342
  24.9 1.2 %merge.1 = bf16[512,128]{1,0:T(8,128)(2,1)} custom-call(bf16[16,96,128]{2,1,0:T(8,128)(2,1)S(1)} %all-to-all-done.box, bf16[128,512]{1,0:T(8,128)(2,1)S(1)} %get-tuple-element.10.query_t, f32[128,512]{1,0:T(8,128)S(1)} %get-tuple-element.11.acc_t, f32[8,512]{1,0:T(8,128)S(1)} %get-tuple-element.12.top_t, f32[8,512]{1,0:T(8,128)S(1)} %get-tuple-element.13.total_t, ...), custom_call_target="tpu_custom_call" | custom-call | tf_op jit(solution)/shard_map/merge/pallas_call | solution.py:369
Async XLA Ops:
  0.0 12.7 %copy-start = (bf16[2,128,2048]{2,1,0:T(8,128)(2,1)S(1)}, bf16[2,128,2048]{2,1,0:T(8,128)(2,1)}, u32[]{:S(2)}) copy-start(bf16[2,128,2048]{2,1,0:T(8,128)(2,1)} %cache.1) | copy-start | bytes 3145732
  0.0 12.7 %copy-start.1 = (bf16[4,2,8192]{2,1,0:T(2,128)(2,1)S(1)}, bf16[4,2,8192]{2,1,0:T(2,128)(2,1)}, u32[]{:S(2)}) copy-start(bf16[4,2,8192]{2,1,0:T(2,128)(2,1)} %param.24) | copy-start | bytes 393220
  0.0 12.8 %copy-start.2 = (bf16[4,2,2048]{2,1,0:T(2,128)(2,1)S(1)}, bf16[4,2,2048]{2,1,0:T(2,128)(2,1)}, u32[]{:S(2)}) copy-start(bf16[4,2,2048]{2,1,0:T(2,128)(2,1)} %param.25) | copy-start | bytes 98308
  0.0 12.8 %copy-start.3 = (s32[16]{0:T(128)S(1)}, s32[16]{0:T(128)}, u32[]{:S(2)}) copy-start(s32[16]{0:T(128)} %counts.1) | copy-start | bytes 196
  0.0 12.8 %copy-start.4 = (s32[16]{0:T(128)S(1)}, s32[16]{0:T(128)}, u32[]{:S(2)}) copy-start(s32[16]{0:T(128)} %placement.1) | copy-start | bytes 196
  0.0 12.8 %copy-start.5 = (s32[2]{0:T(128)S(1)}, s32[2]{0:T(128)}, u32[]{:S(2)}) copy-start(s32[2]{0:T(128)} %lengths.1) | copy-start | bytes 28
  0.0 12.8 %copy-start.6 = (s32[16]{0:T(128)S(1)}, s32[16]{0:T(128)}, u32[]{:S(2)}) copy-start(s32[16]{0:T(128)} %last.1) | copy-start | bytes 196
  5.3 19.6 %all-to-all-start = ((bf16[16,96,128]{2,1,0:T(8,128)(2,1)}), bf16[16,96,128]{2,1,0:T(8,128)(2,1)S(1)}, u32[]{:S(2)}, u32[]{:S(2)}) async-start(bf16[16,96,128]{2,1,0:T(8,128)(2,1)} %project.1), calls=%async_computation | async-start | bytes 786432 | tf_op jit(solution)/shard_map/all_to_all | solution.py:342

commit v25 on v20

--- a/solution.py
+++ b/solution.py
@@ -55,11 +55,10 @@
     ]
     for copy in int_copies:
         copy.start()
-    d_copies = [
-        pltpu.make_async_copy(
-            down.at[pl.ds(c * d_step, d_step)], d_s.at[pl.ds(c * d_step, d_step)], d_sems.at[c])
-        for c in range(d_chunks)
-    ]
+    def d_copy(c):
+        rows = pl.ds(c * d_step, d_step)
+        return pltpu.make_async_copy(down.at[rows], d_s.at[rows], d_sems.at[c])
+
     h_copies = [
         pltpu.make_async_copy(hidden.at[:, pl.ds(c * step, step)], h_s.at[c], sems.at[c, 0])
         for c in range(chunks)
@@ -72,7 +71,7 @@
         hidden.at[:, pl.ds(pl.multiple_of(me * local, 128), local)], mine_s, d_sems.at[d_chunks]
     )
     up_copy = pltpu.make_async_copy(up, u_s, d_sems.at[d_chunks + 1])
-    for copy in d_copies + [my_copy, up_copy]:
+    for copy in [d_copy(c) for c in range(d_chunks)] + [my_copy, up_copy]:
         copy.start()
     for c in range(chunks):
         h_copies[c].start()
@@ -87,15 +86,26 @@
     pick = (mod(rows, 16) == div(cols, pages)) & (mod(cols, pages) == page_of_row)
     pick = jnp.where(pick, jnp.float32(1), jnp.float32(0)).astype(jnp.bfloat16)
 
-    for c in range(d_chunks):
-        d_copies[c].wait()
-        for b in range(c * d_step // 16, (c + 1) * d_step // 16, 2):
+    blocks = d_step // 16
+
+    def select(c, carry):
+        d_copy(c).wait()
+        for b in range(0, blocks, 2):
             block = jnp.concatenate(
-                [d_s[pl.ds((b + i) * 16, 16)].reshape(16 * pages, rank2) for i in range(2)], axis=1
+                [
+                    d_s[pl.ds(c * d_step + (b + i) * 16, 16)].reshape(16 * pages, rank2)
+                    for i in range(2)
+                ],
+                axis=1,
             )
             chosen = jnp.dot(pick, block, preferred_element_type=jnp.float32)
             for i in range(2):
-                sel_s[b + i] = chosen[:, i * rank2 : (i + 1) * rank2].astype(jnp.bfloat16)
+                sel_s[c * blocks + b + i] = chosen[:, i * rank2 : (i + 1) * rank2].astype(
+                    jnp.bfloat16
+                )
+        return carry
+
+    lax.fori_loop(0, d_chunks, select, 0)
     for copy in int_copies[1:]:
         copy.wait()
     for dest in range(devices):
@@ -130,14 +140,20 @@
         base_s[...] = jnp.zeros_like(base_s)
     base_s[:tokens, :features] = total
     up_copy.wait()
-    for dest in range(devices):
-        start = pl.multiple_of(dest_table[0, dest], BLK)
-        who = dest_table[1, dest]
-        out[dest, :CAPT, :] = part_s[who, pl.ds(start, CAPT), :].astype(out.dtype)
-        out[dest, CAPT : 2 * CAPT, :] = base_s[pl.ds(start, CAPT), :].astype(out.dtype)
-        if features < HD:
-            out[dest, 2 * CAPT :, :] = jnp.zeros((out.shape[1] - 2 * CAPT, HD), out.dtype)
-        out[dest, 2 * CAPT :, :features] = u_s[table[who]]
+
+    def lay_out(first, carry):
+        for i in range(4):
+            dest = first * 4 + i
+            start = pl.multiple_of(dest_table[0, dest], BLK)
+            who = dest_table[1, dest]
+            out[dest, :CAPT, :] = part_s[who, pl.ds(start, CAPT), :].astype(out.dtype)
+            out[dest, CAPT : 2 * CAPT, :] = base_s[pl.ds(start, CAPT), :].astype(out.dtype)
+            if features < HD:
+                out[dest, 2 * CAPT :, :] = jnp.zeros((out.shape[1] - 2 * CAPT, HD), out.dtype)
+            out[dest, 2 * CAPT :, :features] = u_s[table[who]]
+        return carry
+
+    lax.fori_loop(0, devices // 4, lay_out, 0)
 
 
 NT = (((1,), (1,)), ((), ()))

time: 26.4 us -> 26.4 us (level)
  no operation moved by 1% of the time
where the time goes in v25:
time: 26.4 us; the launch traced here: 26.2 us
  Pallas kernels  9.57 us (36%)
  waiting for transfers between devices  9.11 us (35%)
  starting transfers between devices  7.41 us (28%)
    all_to_all x1, waiting for transfers between devices, body(): lax.all_to_all(outgoing, 'tensor', split_axis=0, concat_axis=0, tiled=True)  9.11 us
    all_to_all x1, starting transfers between devices, body(): lax.all_to_all(outgoing, 'tensor', split_axis=0, concat_axis=0, tiled=True)  7.41 us
    pallas_call x1, Pallas kernels, body(): pl.pallas_call(functools.partial(project_kernel, dec_rows, d_chunks, chun...  5.32 us
    pallas_call x1, Pallas kernels, body(): pl.pallas_call(cached_kernel, out_shape=(jax.ShapeDtypeStruct((HD, q_rows...  3.01 us
    pallas_call x1, Pallas kernels, body(): pl.pallas_call(functools.partial(merge_kernel, features), out_shape=jax.S...  1.24 us
  transfers between devices with their start and end apart: 1, of which 1 were waited for; matrix products, arithmetic and copies ran while one was open for 0% of the time, Pallas kernels for 11%

profile of v25, /device:TPU:0, one launch (start us, length us, event | category | flops | bytes accessed | tf_op | source)
XLA Modules:
  0.0 26.2 jit_solution(1785046648106740750)
XLA Ops:
  0.0 0.0 copy-start
  0.0 0.0 copy-start.1
  0.0 0.0 copy-start.2
  0.0 0.0 copy-start.3
  0.0 0.0 copy-start.4
  0.0 0.0 copy-start.5
  0.0 0.0 copy-start.6
  0.0 5.3 %project.1 = bf16[16,96,128]{2,1,0:T(8,128)(2,1)} custom-call(s32[16]{0:T(128)} %tenant_h.1, s32[8]{0:T(128)} %table_h.1, s32[16]{0:T(128)} %counts.1, s32[16]{0:T(128)} %placement.1, bf16[160,8192]{1,0:T(8,128)(2,1)} %hidden.1, bf16[128,8192]{1,0:T(8,128)(2,1)} %weight.1, bf16[512,16,128]{2,1,0:T(8,128)(2,1)} %down.1, bf16[16,64,128]{2,1,0:T(8,128)(2,1)} %bitcast.18), custom_call_target="tpu_custom_call" | custom-call | tf_op jit(solution)/shard_map/project/pallas_call | solution.py:321
  5.4 7.4 %all-to-all-start = ((bf16[16,96,128]{2,1,0:T(8,128)(2,1)}), bf16[16,96,128]{2,1,0:T(8,128)(2,1)S(1)}, u32[]{:S(2)}, u32[]{:S(2)}) async-start(bf16[16,96,128]{2,1,0:T(8,128)(2,1)} %project.1), calls=%async_computation | async-start | bytes 786432 | tf_op jit(solution)/shard_map/all_to_all | solution.py:355
  12.8 0.0 copy-done
  12.8 0.0 copy-done.1
  12.8 0.0 copy-done.2
  12.8 0.0 copy-done.3
  12.8 0.0 copy-done.4
  12.8 0.0 copy-done.5
  12.8 0.0 copy-done.6
  12.9 3.0 %cached.1 = (bf16[128,512]{1,0:T(8,128)(2,1)S(1)}, f32[128,512]{1,0:T(8,128)S(1)}, f32[8,512]{1,0:T(8,128)S(1)}, f32[8,512]{1,0:T(8,128)S(1)}, f32[128,512]{1,0:T(8,128)S(1)}) custom-call(s32[2]{0:T(128)S(1)} %copy-done.5, s32[16]{0:T(128)S(1)} %copy-done.3, s32[16]{0:T(128)S(1)} %copy-done.6, s32[16]{0:T(128)S(1)} %copy-done.4, ...), custom_call_target="tpu_custom_call" | custom-call | tf_op jit(solution)/shard_map/cached/pallas_call | solution.py:364
  15.9 9.1 %all-to-all-done.box = bf16[16,96,128]{2,1,0:T(8,128)(2,1)S(1)} async-done(((bf16[16,96,128]{2,1,0:T(8,128)(2,1)}), bf16[16,96,128]{2,1,0:T(8,128)(2,1)S(1)}, u32[]{:S(2)}, u32[]{:S(2)}) %all-to-all-start) | async-done | bytes 393248 | tf_op jit(solution)/shard_map/all_to_all | solution.py:355
  25.0 1.2 %merge.1 = bf16[512,128]{1,0:T(8,128)(2,1)} custom-call(bf16[16,96,128]{2,1,0:T(8,128)(2,1)S(1)} %all-to-all-done.box, bf16[128,512]{1,0:T(8,128)(2,1)S(1)} %get-tuple-element.10.query_t, f32[128,512]{1,0:T(8,128)S(1)} %get-tuple-element.11.acc_t, f32[8,512]{1,0:T(8,128)S(1)} %get-tuple-element.12.top_t, f32[8,512]{1,0:T(8,128)S(1)} %get-tuple-element.13.total_t, ...), custom_call_target="tpu_custom_call" | custom-call | tf_op jit(solution)/shard_map/merge/pallas_call | solution.py:382
Async XLA Ops:
  0.0 12.8 %copy-start = (bf16[2,128,2048]{2,1,0:T(8,128)(2,1)S(1)}, bf16[2,128,2048]{2,1,0:T(8,128)(2,1)}, u32[]{:S(2)}) copy-start(bf16[2,128,2048]{2,1,0:T(8,128)(2,1)} %cache.1) | copy-start | bytes 3145732
  0.0 12.8 %copy-start.1 = (bf16[4,2,8192]{2,1,0:T(2,128)(2,1)S(1)}, bf16[4,2,8192]{2,1,0:T(2,128)(2,1)}, u32[]{:S(2)}) copy-start(bf16[4,2,8192]{2,1,0:T(2,128)(2,1)} %param.24) | copy-start | bytes 393220
  0.0 12.8 %copy-start.2 = (bf16[4,2,2048]{2,1,0:T(2,128)(2,1)S(1)}, bf16[4,2,2048]{2,1,0:T(2,128)(2,1)}, u32[]{:S(2)}) copy-start(bf16[4,2,2048]{2,1,0:T(2,128)(2,1)} %param.25) | copy-start | bytes 98308
  0.0 12.8 %copy-start.3 = (s32[16]{0:T(128)S(1)}, s32[16]{0:T(128)}, u32[]{:S(2)}) copy-start(s32[16]{0:T(128)} %counts.1) | copy-start | bytes 196
  0.0 12.8 %copy-start.4 = (s32[16]{0:T(128)S(1)}, s32[16]{0:T(128)}, u32[]{:S(2)}) copy-start(s32[16]{0:T(128)} %placement.1) | copy-start | bytes 196
  0.0 12.8 %copy-start.5 = (s32[2]{0:T(128)S(1)}, s32[2]{0:T(128)}, u32[]{:S(2)}) copy-start(s32[2]{0:T(128)} %lengths.1) | copy-start | bytes 28
  0.0 12.8 %copy-start.6 = (s32[16]{0:T(128)S(1)}, s32[16]{0:T(128)}, u32[]{:S(2)}) copy-start(s32[16]{0:T(128)} %last.1) | copy-start | bytes 196
  5.4 19.6 %all-to-all-start = ((bf16[16,96,128]{2,1,0:T(8,128)(2,1)}), bf16[16,96,128]{2,1,0:T(8,128)(2,1)S(1)}, u32[]{:S(2)}, u32[]{:S(2)}) async-start(bf16[16,96,128]{2,1,0:T(8,128)(2,1)} %project.1), calls=%async_computation | async-start | bytes 786432 | tf_op jit(solution)/shard_map/all_to_all | solution.py:355

commit v26 on v25

--- a/solution.py
+++ b/solution.py
@@ -241,9 +241,16 @@
     total_t[...] = total_out[...].T[: total_t.shape[0]]
 
 
-def merge_kernel(features, box, query_t, acc_t, top_t, total_t, fresh_ok, out, result, sems):
-    devices = box.shape[0]
-    rank = box.shape[1] - 2 * CAPT
+def merge_kernel(
+    features, kept, swapped, query_t, acc_t, top_t, total_t, fresh_ok, out, box, result, sems
+):
+    devices, size = box.shape[:2]
+    rank = size - 2 * CAPT
+    core = mod(lax.axis_index("tensor"), 2)
+    mine = pl.ds(pl.multiple_of(core * size, 16), size)
+    for chip in range(devices // 2):
+        box[2 * chip + core] = kept[chip, mine, :]
+        box[2 * chip + 1 - core] = swapped[chip, mine, :]
     terms = [box[i, :CAPT].astype(jnp.float32) for i in range(devices)]
     while len(terms) > 1:
         pairs = [a + b for a, b in zip(terms[::2], terms[1::2])]
@@ -352,7 +359,13 @@
             )
         )
     )
-    arrived = lax.all_to_all(outgoing, "tensor", split_axis=0, concat_axis=0, tiled=True)
+    chips = devices // 2
+    same_core = [[2 * chip + core for chip in range(chips)] for core in range(2)]
+    kept = lax.all_to_all(
+        outgoing.reshape(chips, 2 * rows, HD), "tensor", split_axis=0, concat_axis=0,
+        axis_index_groups=same_core, tiled=True,
+    )
+    swapped = lax.ppermute(kept, "tensor", [(i, i ^ 1) for i in range(devices)])
 
     query = decode_step_query.reshape(steps, dec_rows, HEADS, HD)
     query = query.transpose(0, 2, 1, 3).reshape(steps * HEADS * dec_rows, HD)
@@ -382,15 +395,16 @@
     attended = pl.pallas_call(
         functools.partial(merge_kernel, features),
         out_shape=jax.ShapeDtypeStruct((q_rows, HD), jnp.bfloat16),
-        in_specs=[VMEM_SPEC] * 6,
+        in_specs=[VMEM_SPEC] * 7,
         out_specs=ANY_SPEC,
         scratch_shapes=[
+            pltpu.VMEM((devices, rows, HD), WIRE),
             pltpu.VMEM((q_rows, HD), jnp.bfloat16),
             pltpu.SemaphoreType.DMA((steps,)),
         ],
         compiler_params=pltpu.CompilerParams(vmem_limit_bytes=ATTEND_VMEM),
         name="merge",
-    )(arrived, *handed)
+    )(kept, swapped, *handed)
     attended = attended.reshape(steps, HEADS, dec_rows, HD).transpose(0, 2, 1, 3)
     return attended.reshape(steps, dec_rows, HEADS * HD)
 

time: 26.4 us -> 28.2 us (1.068)
  blocking collectives: 0 us -> 19.2 us
  waiting for transfers between devices: 9.11 us -> 0.01 us
  starting transfers between devices: 7.41 us -> 0.01 us
  Pallas kernels: 9.57 us -> 8.67 us
    all_to_all x0 -> x1, blocking collectives: none -> 19.2 us  [body(): lax.all_to_all(outgoing.reshape(chips, 2 * rows, HD), 'tensor', split_axi...]
    all_to_all x1 -> x0, waiting for transfers between devices: 9.11 us -> none  [body(): lax.all_to_all(outgoing, 'tensor', split_axis=0, concat_axis=0, tiled=True)]
    all_to_all x1 -> x0, starting transfers between devices: 7.41 us -> none  [body(): lax.all_to_all(outgoing, 'tensor', split_axis=0, concat_axis=0, tiled=True)]
    pallas_call x1, Pallas kernels: 5.32 us -> 4.38 us  [body(): pl.pallas_call(functools.partial(project_kernel, dec_rows, d_chunks, chun...]
  transfers between devices with their start and end apart: 1 -> 1, of which waited for: 1 -> 0; matrix products, arithmetic and copies ran while one was open for 0% -> 0% of each run, Pallas kernels for 11% -> 11%
where the time goes in v26:
time: 28.2 us; the launch traced here: 28 us
  blocking collectives  19.2 us (68%)
  Pallas kernels  8.67 us (31%)
    all_to_all x1, blocking collectives, body(): lax.all_to_all(outgoing.reshape(chips, 2 * rows, HD), 'tensor', split_axi...  19.2 us
    pallas_call x1, Pallas kernels, body(): pl.pallas_call(functools.partial(project_kernel, dec_rows, d_chunks, chun...  4.38 us
    pallas_call x1, Pallas kernels, body(): pl.pallas_call(cached_kernel, out_shape=(jax.ShapeDtypeStruct((HD, q_rows...  3.01 us
    pallas_call x1, Pallas kernels, body(): pl.pallas_call(functools.partial(merge_kernel, features), out_shape=jax.S...  1.28 us
  transfers between devices with their start and end apart: 1, of which 0 were waited for; matrix products, arithmetic and copies ran while one was open for 0% of the time, Pallas kernels for 11%

profile of v26, /device:TPU:0, one launch (start us, length us, event | category | flops | bytes accessed | tf_op | source)
XLA Modules:
  0.0 28.0 jit_solution(16602070683546578397)
XLA Ops:
  0.0 0.0 copy-start
  0.0 0.0 copy-start.1
  0.0 0.0 copy-start.2
  0.0 0.0 copy-start.3
  0.0 0.0 copy-start.4
  0.0 0.0 copy-start.5
  0.0 0.0 copy-start.6
  0.0 4.4 %project.1 = bf16[16,96,128]{2,1,0:T(8,128)(2,1)S(1)} custom-call(s32[16]{0:T(128)} %tenant_h.1, s32[8]{0:T(128)} %table_h.1, s32[16]{0:T(128)} %counts.1, s32[16]{0:T(128)} %placement.1, bf16[160,8192]{1,0:T(8,128)(2,1)} %hidden.1, bf16[128,8192]{1,0:T(8,128)(2,1)} %weight.1, bf16[512,16,128]{2,1,0:T(8,128)(2,1)} %down.1, bf16[16,64,128]{2,1,0:T(8,128)(2,1)} %bitcast.20), custom_call_target="tpu_custom_call" | custom-call | tf_op jit(solution)/shard_map/project/pallas_call | solution.py:328
  4.4 19.2 %all_to_all.5.kept = bf16[8,192,128]{2,1,0:T(8,128)(2,1)S(1)} all-to-all(bf16[8,192,128]{2,1,0:T(8,128)(2,1)S(1)} %bitcast.17), channel_id=1, replica_groups={{0,2,4,6,8,10,12,14},{1,3,5,7,9,11,13,15},{16,18,20,22,24,26,28,30},{17..., dimensions={0} | all-to-all | bytes 786432 | tf_op jit(solution)/shard_map/all_to_all | solution.py:364
  23.6 0.0 collective-permute-start
  23.6 0.0 copy-done
  23.6 0.0 copy-done.1
  23.6 0.0 copy-done.2
  23.6 0.0 copy-done.3
  23.6 0.0 copy-done.4
  23.6 0.0 copy-done.5
  23.7 0.0 copy-done.6
  23.7 3.0 %cached.1 = (bf16[128,512]{1,0:T(8,128)(2,1)S(1)}, f32[128,512]{1,0:T(8,128)S(1)}, f32[8,512]{1,0:T(8,128)S(1)}, f32[8,512]{1,0:T(8,128)S(1)}, f32[128,512]{1,0:T(8,128)S(1)}) custom-call(s32[2]{0:T(128)S(1)} %copy-done.5, s32[16]{0:T(128)S(1)} %copy-done.3, s32[16]{0:T(128)S(1)} %copy-done.6, s32[16]{0:T(128)S(1)} %copy-done.4, ...), custom_call_target="tpu_custom_call" | custom-call | tf_op jit(solution)/shard_map/cached/pallas_call | solution.py:377
  26.7 0.0 collective-permute-done.swapped
  26.7 1.3 %merge.1 = bf16[512,128]{1,0:T(8,128)(2,1)} custom-call(bf16[8,192,128]{2,1,0:T(8,128)(2,1)S(1)} %all_to_all.5.kept, bf16[8,192,128]{2,1,0:T(8,128)(2,1)S(1)} %collective-permute-done.swapped, bf16[128,512]{1,0:T(8,128)(2,1)S(1)} %get-tuple-element.10.query_t, f32[128,512]{1,0:T(8,128)S(1)} %get-tuple-element.11.acc_t, ...), custom_call_target="tpu_custom_call" | custom-call | tf_op jit(solution)/shard_map/merge/pallas_call | solution.py:395
Async XLA Ops:
  0.0 23.6 %copy-start = (bf16[2,128,2048]{2,1,0:T(8,128)(2,1)S(1)}, bf16[2,128,2048]{2,1,0:T(8,128)(2,1)}, u32[]{:S(2)}) copy-start(bf16[2,128,2048]{2,1,0:T(8,128)(2,1)} %cache.1) | copy-start | bytes 3145732
  0.0 23.6 %copy-start.1 = (bf16[4,2,8192]{2,1,0:T(2,128)(2,1)S(1)}, bf16[4,2,8192]{2,1,0:T(2,128)(2,1)}, u32[]{:S(2)}) copy-start(bf16[4,2,8192]{2,1,0:T(2,128)(2,1)} %param.24) | copy-start | bytes 393220
  0.0 23.6 %copy-start.2 = (bf16[4,2,2048]{2,1,0:T(2,128)(2,1)S(1)}, bf16[4,2,2048]{2,1,0:T(2,128)(2,1)}, u32[]{:S(2)}) copy-start(bf16[4,2,2048]{2,1,0:T(2,128)(2,1)} %param.25) | copy-start | bytes 98308
  0.0 23.6 %copy-start.3 = (s32[16]{0:T(128)S(1)}, s32[16]{0:T(128)}, u32[]{:S(2)}) copy-start(s32[16]{0:T(128)} %counts.1) | copy-start | bytes 196
  0.0 23.6 %copy-start.4 = (s32[16]{0:T(128)S(1)}, s32[16]{0:T(128)}, u32[]{:S(2)}) copy-start(s32[16]{0:T(128)} %placement.1) | copy-start | bytes 196
  0.0 23.6 %copy-start.5 = (s32[2]{0:T(128)S(1)}, s32[2]{0:T(128)}, u32[]{:S(2)}) copy-start(s32[2]{0:T(128)} %lengths.1) | copy-start | bytes 28
  0.0 23.6 %copy-start.6 = (s32[16]{0:T(128)S(1)}, s32[16]{0:T(128)}, u32[]{:S(2)}) copy-start(s32[16]{0:T(128)} %last.1) | copy-start | bytes 196
  23.6 3.1 %collective-permute-start = (bf16[8,192,128]{2,1,0:T(8,128)(2,1)S(1)}, bf16[8,192,128]{2,1,0:T(8,128)(2,1)S(1)}, u32[]{:S(2)}, u32[]{:S(2)}) collective-permute-start(bf16[8,192,128]{2,1,0:T(8,128)(2,1)S(1)} %all_to_all.5.kept), channel_id=1, source_target_pairs={{0,1},{1,0},{2,3},{3,2},{4,5},{5,4},{6,7},{7,6},{8,9},{9,8},{10,11... | collective-permute-start | bytes 1179656 | tf_op jit(solution)/shard_map/ppermute | solution.py:368

commit v27 on v25

--- a/solution.py
+++ b/solution.py
@@ -36,12 +36,14 @@
 def project_kernel(
     dec_rows, d_chunks, chunks, devices, tenant_h, table_h, counts_h, placement_h, hidden, weight, down, up, out,
     tenant, table, counts, placement,
-    h_s, w_s, d_s, mine_s, u_s, sel_s, part_s, base_s, dest_table, sems, d_sems, int_sems,
+    h_s, w_s, d_s, mine_s, u_s, sel_s, part_s, base_s, out_s, dest_table, sems, d_sems, int_sems,
+    out_sems,
 ):
     tokens, width = hidden.shape
     features = weight.shape[0]
     local, pages, rank2 = down.shape
     tenants = table.shape[0]
+    rank = up.shape[1]
     requests = tenant.shape[0]
     me = lax.axis_index("tensor")
     d_step = local // d_chunks
@@ -117,6 +119,15 @@
         dest_table[0, dest] = first * BLK
         dest_table[1, dest] = tenant[r]
         first = first + counts[r]
+    up_copy.wait()
+    whole = features == HD
+    sent = []
+    if whole:
+        for dest in range(devices):
+            page = table[dest_table[1, dest]]
+            sent.append(pltpu.make_async_copy(
+                u_s.at[page], out.at[dest, pl.ds(2 * CAPT, rank), :], out_sems.at[dest]))
+            sent[-1].start()
     my_copy.wait()
     mine = mine_s[...]
     for k in range(0, tenants, 2):
@@ -129,6 +140,16 @@
         for j in range(pair):
             part_s[k + j, :tokens] = product[:, j * rank2 : (j + 1) * rank2]
             part_s[k + j, tokens:] = jnp.zeros((BLK, rank2), jnp.float32)
+
+    for dest in range(devices):
+        start = pl.multiple_of(dest_table[0, dest], BLK)
+        rows = part_s[dest_table[1, dest], pl.ds(start, CAPT), :]
+        out_s[dest, :CAPT, :] = rows.astype(out.dtype)
+    if whole:
+        lines = pl.ds(0, CAPT)
+        sent.append(pltpu.make_async_copy(
+            out_s.at[:, lines, :], out.at[:, lines, :], out_sems.at[devices]))
+        sent[-1].start()
 
     total = jnp.zeros((tokens, features), jnp.float32)
     for c in range(chunks):
@@ -139,21 +160,18 @@
     if features < HD:
         base_s[...] = jnp.zeros_like(base_s)
     base_s[:tokens, :features] = total
-    up_copy.wait()
-
-    def lay_out(first, carry):
-        for i in range(4):
-            dest = first * 4 + i
-            start = pl.multiple_of(dest_table[0, dest], BLK)
-            who = dest_table[1, dest]
-            out[dest, :CAPT, :] = part_s[who, pl.ds(start, CAPT), :].astype(out.dtype)
-            out[dest, CAPT : 2 * CAPT, :] = base_s[pl.ds(start, CAPT), :].astype(out.dtype)
-            if features < HD:
-                out[dest, 2 * CAPT :, :] = jnp.zeros((out.shape[1] - 2 * CAPT, HD), out.dtype)
-            out[dest, 2 * CAPT :, :features] = u_s[table[who]]
-        return carry
-
-    lax.fori_loop(0, devices // 4, lay_out, 0)
+    for dest in range(devices):
+        start = pl.multiple_of(dest_table[0, dest], BLK)
+        out_s[dest, CAPT : 2 * CAPT, :] = base_s[pl.ds(start, CAPT), :].astype(out.dtype)
+        if not whole:
+            out_s[dest, 2 * CAPT :, :] = jnp.zeros((rank, HD), out.dtype)
+            out_s[dest, 2 * CAPT :, :features] = u_s[table[dest_table[1, dest]]]
+    lines = pl.ds(CAPT, CAPT) if whole else pl.ds(0, out.shape[1])
+    sent.append(pltpu.make_async_copy(
+        out_s.at[:, lines, :], out.at[:, lines, :], out_sems.at[devices + 1]))
+    sent[-1].start()
+    for copy in sent:
+        copy.wait()
 
 
 NT = (((1,), (1,)), ((), ()))
@@ -320,9 +338,9 @@
     rows = 2 * CAPT + rank
     outgoing = pl.pallas_call(
         functools.partial(project_kernel, dec_rows, d_chunks, chunks, devices),
-        out_shape=pltpu.VMEM((devices, rows, HD), WIRE),
+        out_shape=jax.ShapeDtypeStruct((devices, rows, HD), WIRE),
         in_specs=[ANY_SPEC] * 8,
-        out_specs=VMEM_SPEC,
+        out_specs=ANY_SPEC,
         scratch_shapes=[
             pltpu.SMEM(tenant.shape, jnp.int32),
             pltpu.SMEM(tenant_page_table.shape, jnp.int32),
@@ -336,10 +354,12 @@
             pltpu.VMEM((local // 16, tenants * 16, rank2), jnp.bfloat16),
             pltpu.VMEM((tenants, tokens + BLK, rank2), jnp.float32),
             pltpu.VMEM((tokens + BLK, HD), jnp.float32),
+            pltpu.VMEM((devices, rows, HD), WIRE),
             pltpu.SMEM((2, devices), jnp.int32),
             pltpu.SemaphoreType.DMA((chunks, 2)),
             pltpu.SemaphoreType.DMA((d_chunks + 2,)),
             pltpu.SemaphoreType.DMA((4,)),
+            pltpu.SemaphoreType.DMA((devices + 2,)),
         ],
         compiler_params=pltpu.CompilerParams(vmem_limit_bytes=PROJECT_VMEM),
         name="project",

time: 26.4 us -> 26.5 us (level)
  no operation moved by 1% of the time
where the time goes in v27:
time: 26.5 us; the launch traced here: 26.3 us
  Pallas kernels  9.64 us (36%)
  waiting for transfers between devices  9.11 us (34%)
  starting transfers between devices  7.41 us (28%)
    all_to_all x1, waiting for transfers between devices, body(): lax.all_to_all(outgoing, 'tensor', split_axis=0, concat_axis=0, tiled=True)  9.11 us
    all_to_all x1, starting transfers between devices, body(): lax.all_to_all(outgoing, 'tensor', split_axis=0, concat_axis=0, tiled=True)  7.41 us
    pallas_call x1, Pallas kernels, body(): pl.pallas_call(functools.partial(project_kernel, dec_rows, d_chunks, chun...  5.4 us
    pallas_call x1, Pallas kernels, body(): pl.pallas_call(cached_kernel, out_shape=(jax.ShapeDtypeStruct((HD, q_rows...  3.01 us
    pallas_call x1, Pallas kernels, body(): pl.pallas_call(functools.partial(merge_kernel, features), out_shape=jax.S...  1.24 us
  transfers between devices with their start and end apart: 1, of which 1 were waited for; matrix products, arithmetic and copies ran while one was open for 0% of the time, Pallas kernels for 11%

profile of v27, /device:TPU:0, one launch (start us, length us, event | category | flops | bytes accessed | tf_op | source)
XLA Modules:
  0.0 26.3 jit_solution(5529997620413821424)
XLA Ops:
  0.0 0.0 copy-start
  0.0 0.0 copy-start.1
  0.0 0.0 copy-start.2
  0.0 0.0 copy-start.3
  0.0 0.0 copy-start.4
  0.0 0.0 copy-start.5
  0.0 0.0 copy-start.6
  0.0 5.4 %project.1 = bf16[16,96,128]{2,1,0:T(8,128)(2,1)} custom-call(s32[16]{0:T(128)} %tenant_h.1, s32[8]{0:T(128)} %table_h.1, s32[16]{0:T(128)} %counts.1, s32[16]{0:T(128)} %placement.1, bf16[160,8192]{1,0:T(8,128)(2,1)} %hidden.1, bf16[128,8192]{1,0:T(8,128)(2,1)} %weight.1, bf16[512,16,128]{2,1,0:T(8,128)(2,1)} %down.1, bf16[16,64,128]{2,1,0:T(8,128)(2,1)} %bitcast.18), custom_call_target="tpu_custom_call" | custom-call | tf_op jit(solution)/shard_map/project/pallas_call | solution.py:339
  5.4 7.4 %all-to-all-start = ((bf16[16,96,128]{2,1,0:T(8,128)(2,1)}), bf16[16,96,128]{2,1,0:T(8,128)(2,1)S(1)}, u32[]{:S(2)}, u32[]{:S(2)}) async-start(bf16[16,96,128]{2,1,0:T(8,128)(2,1)} %project.1), calls=%async_computation | async-start | bytes 786432 | tf_op jit(solution)/shard_map/all_to_all | solution.py:375
  12.9 0.0 copy-done
  12.9 0.0 copy-done.1
  12.9 0.0 copy-done.2
  12.9 0.0 copy-done.3
  12.9 0.0 copy-done.4
  12.9 0.0 copy-done.5
  12.9 0.0 copy-done.6
  12.9 3.0 %cached.1 = (bf16[128,512]{1,0:T(8,128)(2,1)S(1)}, f32[128,512]{1,0:T(8,128)S(1)}, f32[8,512]{1,0:T(8,128)S(1)}, f32[8,512]{1,0:T(8,128)S(1)}, f32[128,512]{1,0:T(8,128)S(1)}) custom-call(s32[2]{0:T(128)S(1)} %copy-done.5, s32[16]{0:T(128)S(1)} %copy-done.3, s32[16]{0:T(128)S(1)} %copy-done.6, s32[16]{0:T(128)S(1)} %copy-done.4, ...), custom_call_target="tpu_custom_call" | custom-call | tf_op jit(solution)/shard_map/cached/pallas_call | solution.py:384
  15.9 9.1 %all-to-all-done.box = bf16[16,96,128]{2,1,0:T(8,128)(2,1)S(1)} async-done(((bf16[16,96,128]{2,1,0:T(8,128)(2,1)}), bf16[16,96,128]{2,1,0:T(8,128)(2,1)S(1)}, u32[]{:S(2)}, u32[]{:S(2)}) %all-to-all-start) | async-done | bytes 393248 | tf_op jit(solution)/shard_map/all_to_all | solution.py:375
  25.1 1.2 %merge.1 = bf16[512,128]{1,0:T(8,128)(2,1)} custom-call(bf16[16,96,128]{2,1,0:T(8,128)(2,1)S(1)} %all-to-all-done.box, bf16[128,512]{1,0:T(8,128)(2,1)S(1)} %get-tuple-element.10.query_t, f32[128,512]{1,0:T(8,128)S(1)} %get-tuple-element.11.acc_t, f32[8,512]{1,0:T(8,128)S(1)} %get-tuple-element.12.top_t, f32[8,512]{1,0:T(8,128)S(1)} %get-tuple-element.13.total_t, ...), custom_call_target="tpu_custom_call" | custom-call | tf_op jit(solution)/shard_map/merge/pallas_call | solution.py:402
Async XLA Ops:
  0.0 12.9 %copy-start = (bf16[2,128,2048]{2,1,0:T(8,128)(2,1)S(1)}, bf16[2,128,2048]{2,1,0:T(8,128)(2,1)}, u32[]{:S(2)}) copy-start(bf16[2,128,2048]{2,1,0:T(8,128)(2,1)} %cache.1) | copy-start | bytes 3145732
  0.0 12.9 %copy-start.1 = (bf16[4,2,8192]{2,1,0:T(2,128)(2,1)S(1)}, bf16[4,2,8192]{2,1,0:T(2,128)(2,1)}, u32[]{:S(2)}) copy-start(bf16[4,2,8192]{2,1,0:T(2,128)(2,1)} %param.24) | copy-start | bytes 393220
  0.0 12.9 %copy-start.2 = (bf16[4,2,2048]{2,1,0:T(2,128)(2,1)S(1)}, bf16[4,2,2048]{2,1,0:T(2,128)(2,1)}, u32[]{:S(2)}) copy-start(bf16[4,2,2048]{2,1,0:T(2,128)(2,1)} %param.25) | copy-start | bytes 98308
  0.0 12.9 %copy-start.3 = (s32[16]{0:T(128)S(1)}, s32[16]{0:T(128)}, u32[]{:S(2)}) copy-start(s32[16]{0:T(128)} %counts.1) | copy-start | bytes 196
  0.0 12.9 %copy-start.4 = (s32[16]{0:T(128)S(1)}, s32[16]{0:T(128)}, u32[]{:S(2)}) copy-start(s32[16]{0:T(128)} %placement.1) | copy-start | bytes 196
  0.0 12.9 %copy-start.5 = (s32[2]{0:T(128)S(1)}, s32[2]{0:T(128)}, u32[]{:S(2)}) copy-start(s32[2]{0:T(128)} %lengths.1) | copy-start | bytes 28
  0.0 12.9 %copy-start.6 = (s32[16]{0:T(128)S(1)}, s32[16]{0:T(128)}, u32[]{:S(2)}) copy-start(s32[16]{0:T(128)} %last.1) | copy-start | bytes 196
  5.4 19.6 %all-to-all-start = ((bf16[16,96,128]{2,1,0:T(8,128)(2,1)}), bf16[16,96,128]{2,1,0:T(8,128)(2,1)S(1)}, u32[]{:S(2)}, u32[]{:S(2)}) async-start(bf16[16,96,128]{2,1,0:T(8,128)(2,1)} %project.1), calls=%async_computation | async-start | bytes 786432 | tf_op jit(solution)/shard_map/all_to_all | solution.py:375

commit v28 on v25

--- a/solution.py
+++ b/solution.py
@@ -33,10 +33,14 @@
     return x & (n - 1) if n & (n - 1) == 0 else x % n
 
 
-def project_kernel(
-    dec_rows, d_chunks, chunks, devices, tenant_h, table_h, counts_h, placement_h, hidden, weight, down, up, out,
-    tenant, table, counts, placement,
+def front_kernel(
+    dec_rows, d_chunks, chunks, devices,
+    tenant_h, table_h, counts_h, placement_h, lengths_h, last_h,
+    hidden, weight, down, up, cache_h, query_h, steps_h,
+    out, query_t, acc_t, top_t, total_t, fresh_ok,
+    tenant, table, counts, placement, lengths, last,
     h_s, w_s, d_s, mine_s, u_s, sel_s, part_s, base_s, dest_table, sems, d_sems, int_sems,
+    cache, query, steps_kv, acc, top_out, total_out, c_sems,
 ):
     tokens, width = hidden.shape
     features = weight.shape[0]
@@ -50,7 +54,10 @@
     int_copies = [
         pltpu.make_async_copy(src, dst, int_sems.at[i])
         for i, (src, dst) in enumerate(
-            ((table_h, table), (tenant_h, tenant), (counts_h, counts), (placement_h, placement))
+            (
+                (table_h, table), (tenant_h, tenant), (counts_h, counts), (placement_h, placement),
+                (lengths_h, lengths), (last_h, last),
+            )
         )
     ]
     for copy in int_copies:
@@ -71,7 +78,11 @@
         hidden.at[:, pl.ds(pl.multiple_of(me * local, 128), local)], mine_s, d_sems.at[d_chunks]
     )
     up_copy = pltpu.make_async_copy(up, u_s, d_sems.at[d_chunks + 1])
-    for copy in [d_copy(c) for c in range(d_chunks)] + [my_copy, up_copy]:
+    c_copies = [
+        pltpu.make_async_copy(src, dst, c_sems.at[i])
+        for i, (src, dst) in enumerate(((query_h, query), (steps_h, steps_kv), (cache_h, cache)))
+    ]
+    for copy in [d_copy(c) for c in range(d_chunks)] + [my_copy] + c_copies + [up_copy]:
         copy.start()
     for c in range(chunks):
         h_copies[c].start()
@@ -118,7 +129,15 @@
         dest_table[1, dest] = tenant[r]
         first = first + counts[r]
     my_copy.wait()
+    for copy in c_copies:
+        copy.wait()
+    head, finish = cached_parts(
+        lengths, counts, last, placement, cache, query, steps_kv,
+        query_t, acc_t, top_t, total_t, fresh_ok, acc, top_out, total_out,
+    )
     mine = mine_s[...]
+    for k in range(KVH // 2):
+        head(k)
     for k in range(0, tenants, 2):
         pair = min(2, tenants - k)
         maps = jnp.concatenate(
@@ -135,6 +154,11 @@
         h_copies[c].wait()
         w_copies[c].wait()
         total = total + lax.dot_general(h_s[c], w_s[c], NT, preferred_element_type=jnp.float32)
+        if c == 0:
+            for k in range(KVH // 2, KVH):
+                head(k)
+        if c == chunks - 1:
+            finish()
     base_s[tokens:] = jnp.zeros((BLK, HD), jnp.float32)
     if features < HD:
         base_s[...] = jnp.zeros_like(base_s)
@@ -165,7 +189,7 @@
     )
 
 
-def cached_kernel(
+def cached_parts(
     lengths, counts, last, placement, cache, query, steps_kv,
     query_t, acc_t, top_t, total_t, fresh_ok, acc, top_out, total_out,
 ):
@@ -193,7 +217,7 @@
     )
 
     scale = HD ** (-0.5)
-    for k in range(KVH):
+    def head(k):
         lanes = pl.ds(k * HD, HD)
         vlanes = pl.ds(half_width + k * HD, HD)
         q = gather_queries(query, k, group, steps, stride)
@@ -221,24 +245,27 @@
             top_out[here, :] = jnp.broadcast_to(top[part], (group, HD))
             total_out[here, :] = jnp.broadcast_to(total[part], (group, HD))
 
-    my_slot = jnp.int32(-1)
-    my_length = jnp.int32(0)
-    for r in range(placement.shape[0]):
-        hit = div(placement[r], dec_rows) == lax.axis_index("tensor")
-        my_slot = jnp.where(hit, mod(placement[r], dec_rows), my_slot)
-        my_length = jnp.where(hit, (counts[r] - 1) * BLK + last[r], my_length)
-    col = lax.broadcasted_iota(jnp.int32, fresh_ok.shape, 0)
-    row = lax.broadcasted_iota(jnp.int32, fresh_ok.shape, 1)
-    ok = (
-        (mod(div(row, group), KVH) == div(col, CAPT))
-        & (mod(row, dec_rows) == my_slot)
-        & (mod(col, CAPT) < my_length)
-    )
-    fresh_ok[...] = jnp.where(ok, jnp.float32(1), jnp.float32(0))
-    query_t[...] = query[...].T
-    acc_t[...] = acc[...].T
-    top_t[...] = top_out[...].T[: top_t.shape[0]]
-    total_t[...] = total_out[...].T[: total_t.shape[0]]
+    def finish():
+        my_slot = jnp.int32(-1)
+        my_length = jnp.int32(0)
+        for r in range(placement.shape[0]):
+            hit = div(placement[r], dec_rows) == lax.axis_index("tensor")
+            my_slot = jnp.where(hit, mod(placement[r], dec_rows), my_slot)
+            my_length = jnp.where(hit, (counts[r] - 1) * BLK + last[r], my_length)
+        col = lax.broadcasted_iota(jnp.int32, fresh_ok.shape, 0)
+        row = lax.broadcasted_iota(jnp.int32, fresh_ok.shape, 1)
+        ok = (
+            (mod(div(row, group), KVH) == div(col, CAPT))
+            & (mod(row, dec_rows) == my_slot)
+            & (mod(col, CAPT) < my_length)
+        )
+        fresh_ok[...] = jnp.where(ok, jnp.float32(1), jnp.float32(0))
+        query_t[...] = query[...].T
+        acc_t[...] = acc[...].T
+        top_t[...] = top_out[...].T[: top_t.shape[0]]
+        total_t[...] = total_out[...].T[: total_t.shape[0]]
+
+    return head, finish
 
 
 def merge_kernel(features, box, query_t, acc_t, top_t, total_t, fresh_ok, out, result, sems):
@@ -318,16 +345,30 @@
     d_chunks, chunks = 4, 2
     up_by_page = jnp.transpose(adapter_up_weight, (1, 2, 0))
     rows = 2 * CAPT + rank
-    outgoing = pl.pallas_call(
-        functools.partial(project_kernel, dec_rows, d_chunks, chunks, devices),
-        out_shape=pltpu.VMEM((devices, rows, HD), WIRE),
-        in_specs=[ANY_SPEC] * 8,
-        out_specs=VMEM_SPEC,
+    query = decode_step_query.reshape(steps, dec_rows, HEADS, HD)
+    query = query.transpose(0, 2, 1, 3).reshape(steps * HEADS * dec_rows, HD)
+    steps_kv = step_key_value.reshape(steps, dec_rows, heads2, HD)
+    steps_kv = steps_kv.transpose(0, 2, 1, 3).reshape(steps * heads2 * dec_rows, HD)
+    q_rows = steps * HEADS * dec_rows
+    outgoing, *handed = pl.pallas_call(
+        functools.partial(front_kernel, dec_rows, d_chunks, chunks, devices),
+        out_shape=(
+            pltpu.VMEM((devices, rows, HD), WIRE),
+            pltpu.VMEM((HD, q_rows), jnp.bfloat16),
+            pltpu.VMEM((HD, q_rows), jnp.float32),
+            pltpu.VMEM((8, q_rows), jnp.float32),
+            pltpu.VMEM((8, q_rows), jnp.float32),
+            pltpu.VMEM((KVH * CAPT, q_rows), jnp.float32),
+        ),
+        in_specs=[ANY_SPEC] * 13,
+        out_specs=(VMEM_SPEC,) * 6,
         scratch_shapes=[
             pltpu.SMEM(tenant.shape, jnp.int32),
             pltpu.SMEM(tenant_page_table.shape, jnp.int32),
             pltpu.SMEM(request_block_count.shape, jnp.int32),
             pltpu.SMEM(placement.shape, jnp.int32),
+            pltpu.SMEM(context_length.shape, jnp.int32),
+            pltpu.SMEM(last_block_tokens.shape, jnp.int32),
             pltpu.VMEM((chunks, tokens, width // chunks), jnp.bfloat16),
             pltpu.VMEM((chunks, features, width // chunks), jnp.bfloat16),
             pltpu.VMEM((local, pages, rank2), jnp.bfloat16),
@@ -339,45 +380,31 @@
             pltpu.SMEM((2, devices), jnp.int32),
             pltpu.SemaphoreType.DMA((chunks, 2)),
             pltpu.SemaphoreType.DMA((d_chunks + 2,)),
-            pltpu.SemaphoreType.DMA((4,)),
+            pltpu.SemaphoreType.DMA((6,)),
+            pltpu.VMEM(key_value_cache.shape, jnp.bfloat16),
+            pltpu.VMEM(query.shape, jnp.bfloat16),
+            pltpu.VMEM(steps_kv.shape, jnp.bfloat16),
+            pltpu.VMEM((q_rows, HD), jnp.float32),
+            pltpu.VMEM((q_rows, HD), jnp.float32),
+            pltpu.VMEM((q_rows, HD), jnp.float32),
+            pltpu.SemaphoreType.DMA((3,)),
         ],
         compiler_params=pltpu.CompilerParams(vmem_limit_bytes=PROJECT_VMEM),
-        name="project",
+        name="front",
     )(
         *(
             pltpu.with_memory_space_constraint(x, pltpu.HBM)
             for x in (
                 tenant, tenant_page_table, request_block_count, placement,
+                context_length, last_block_tokens,
                 hidden, key_value_weight, adapter_down_weight, up_by_page,
+                key_value_cache, query, steps_kv,
             )
         )
     )
-    arrived = lax.all_to_all(outgoing, "tensor", split_axis=0, concat_axis=0, tiled=True)
-
-    query = decode_step_query.reshape(steps, dec_rows, HEADS, HD)
-    query = query.transpose(0, 2, 1, 3).reshape(steps * HEADS * dec_rows, HD)
-    steps_kv = step_key_value.reshape(steps, dec_rows, heads2, HD)
-    steps_kv = steps_kv.transpose(0, 2, 1, 3).reshape(steps * heads2 * dec_rows, HD)
-    q_rows = steps * HEADS * dec_rows
-    state = jax.ShapeDtypeStruct((HD, q_rows), jnp.float32)
-    line = jax.ShapeDtypeStruct((8, q_rows), jnp.float32)
-    handed = pl.pallas_call(
-        cached_kernel,
-        out_shape=(
-            jax.ShapeDtypeStruct((HD, q_rows), jnp.bfloat16),
-            state,
-            line,
-            line,
-            jax.ShapeDtypeStruct((KVH * CAPT, q_rows), jnp.float32),
-        ),
-        in_specs=[SMEM_SPEC] * 4 + [VMEM_SPEC] * 3,
-        out_specs=(VMEM_SPEC,) * 5,
-        scratch_shapes=[pltpu.VMEM((q_rows, HD), jnp.float32)] * 3,
-        compiler_params=pltpu.CompilerParams(vmem_limit_bytes=ATTEND_VMEM),
-        name="cached",
-    )(
-        context_length, request_block_count, last_block_tokens, placement,
-        key_value_cache, query, steps_kv,
+    arrived = lax.all_to_all(
+        outgoing, "tensor", split_axis=0, concat_axis=0,
+        axis_index_groups=[list(range(devices))], tiled=True,
     )
     attended = pl.pallas_call(
         functools.partial(merge_kernel, features),

time: 26.4 us -> 28.1 us (1.064)
  blocking collectives: 0 us -> 19.4 us
  waiting for transfers between devices: 9.11 us -> 0 us
  starting transfers between devices: 7.41 us -> 0 us
  Pallas kernels: 9.57 us -> 8.54 us
    all_to_all x0 -> x1, blocking collectives: none -> 19.4 us  [body(): lax.all_to_all(outgoing, 'tensor', split_axis=0, concat_axis=0, axis_inde...]
    all_to_all x1 -> x0, waiting for transfers between devices: 9.11 us -> none  [body(): lax.all_to_all(outgoing, 'tensor', split_axis=0, concat_axis=0, tiled=True)]
    all_to_all x1 -> x0, starting transfers between devices: 7.41 us -> none  [body(): lax.all_to_all(outgoing, 'tensor', split_axis=0, concat_axis=0, tiled=True)]
    pallas_call x2 -> x1, Pallas kernels: 8.33 us -> 7.3 us  [body(): pl.pallas_call(functools.partial(front_kernel, dec_rows, d_chunks, chunks...]
  transfers between devices with their start and end apart: 1 -> 0, of which waited for: 1 -> 0; matrix products, arithmetic and copies ran while one was open for 0% -> 0% of each run, Pallas kernels for 11% -> 0%
where the time goes in v28:
time: 28.1 us; the launch traced here: 27.9 us
  blocking collectives  19.4 us (69%)
  Pallas kernels  8.54 us (30%)
    all_to_all x1, blocking collectives, body(): lax.all_to_all(outgoing, 'tensor', split_axis=0, concat_axis=0, axis_inde...  19.4 us
    pallas_call x1, Pallas kernels, body(): pl.pallas_call(functools.partial(front_kernel, dec_rows, d_chunks, chunks...  7.3 us
    pallas_call x1, Pallas kernels, body(): pl.pallas_call(functools.partial(merge_kernel, features), out_shape=jax.S...  1.24 us

profile of v28, /device:TPU:0, one launch (start us, length us, event | category | flops | bytes accessed | tf_op | source)
XLA Modules:
  0.0 27.9 jit_solution(14765124331791609447)
XLA Ops:
  0.0 7.3 %front.1 = (bf16[16,96,128]{2,1,0:T(8,128)(2,1)S(1)}, bf16[128,512]{1,0:T(8,128)(2,1)S(1)}, f32[128,512]{1,0:T(8,128)S(1)}, f32[8,512]{1,0:T(8,128)S(1)}, f32[8,512]{1,0:T(8,128)S(1)}, /*index=5*/f32[128,512]{1,0:T(8,128)S(1)}) custom-call(s32[16]{0:T(128)} %tenant_h.1, s32[8]{0:T(128)} %table_h.1, s32[16]{0:T(128)} %counts_h.1, s32[16]{0:T(128)} %placement_h.1, ...), custom_call_target="tpu_custom_call" | custom-call | tf_op jit(solution)/shard_map/front/pallas_call | solution.py:353
  7.3 19.4 %all_to_all.5.box = bf16[16,96,128]{2,1,0:T(8,128)(2,1)S(1)} all-to-all(bf16[16,96,128]{2,1,0:T(8,128)(2,1)S(1)} %get-tuple-element.11), channel_id=1, replica_groups={{0,1,2,3,4,5,6,7,8,9,10,11,12,13,14,15},{16,17,18,19,20,21,22,23,24,25,..., dimensions={0} | all-to-all | bytes 786432 | tf_op jit(solution)/shard_map/all_to_all | solution.py:405
  26.7 1.2 %merge.1 = bf16[512,128]{1,0:T(8,128)(2,1)} custom-call(bf16[16,96,128]{2,1,0:T(8,128)(2,1)S(1)} %all_to_all.5.box, bf16[128,512]{1,0:T(8,128)(2,1)S(1)} %get-tuple-element.12.query_t, f32[128,512]{1,0:T(8,128)S(1)} %get-tuple-element.13.acc_t, f32[8,512]{1,0:T(8,128)S(1)} %get-tuple-element.14.top_t, f32[8,512]{1,0:T(8,128)S(1)} %get-tuple-element.15.total_t, ...), custom_call_target="tpu_custom_call" | custom-call | tf_op jit(solution)/shard_map/merge/pallas_call | solution.py:409

commit v29 on v27

--- a/solution.py
+++ b/solution.py
@@ -122,12 +122,6 @@
     up_copy.wait()
     whole = features == HD
     sent = []
-    if whole:
-        for dest in range(devices):
-            page = table[dest_table[1, dest]]
-            sent.append(pltpu.make_async_copy(
-                u_s.at[page], out.at[dest, pl.ds(2 * CAPT, rank), :], out_sems.at[dest]))
-            sent[-1].start()
     my_copy.wait()
     mine = mine_s[...]
     for k in range(0, tenants, 2):
@@ -143,12 +137,14 @@
 
     for dest in range(devices):
         start = pl.multiple_of(dest_table[0, dest], BLK)
-        rows = part_s[dest_table[1, dest], pl.ds(start, CAPT), :]
-        out_s[dest, :CAPT, :] = rows.astype(out.dtype)
-    if whole:
-        lines = pl.ds(0, CAPT)
+        who = dest_table[1, dest]
+        out_s[dest, :CAPT, :] = part_s[who, pl.ds(start, CAPT), :].astype(out.dtype)
+        if not whole:
+            out_s[dest, 2 * CAPT :, :] = jnp.zeros((rank, HD), out.dtype)
+        out_s[dest, 2 * CAPT :, :features] = u_s[table[who]]
+    for i, lines in enumerate((pl.ds(0, CAPT), pl.ds(2 * CAPT, rank))):
         sent.append(pltpu.make_async_copy(
-            out_s.at[:, lines, :], out.at[:, lines, :], out_sems.at[devices]))
+            out_s.at[:, lines, :], out.at[:, lines, :], out_sems.at[i]))
         sent[-1].start()
 
     total = jnp.zeros((tokens, features), jnp.float32)
@@ -163,12 +159,9 @@
     for dest in range(devices):
         start = pl.multiple_of(dest_table[0, dest], BLK)
         out_s[dest, CAPT : 2 * CAPT, :] = base_s[pl.ds(start, CAPT), :].astype(out.dtype)
-        if not whole:
-            out_s[dest, 2 * CAPT :, :] = jnp.zeros((rank, HD), out.dtype)
-            out_s[dest, 2 * CAPT :, :features] = u_s[table[dest_table[1, dest]]]
-    lines = pl.ds(CAPT, CAPT) if whole else pl.ds(0, out.shape[1])
+    lines = pl.ds(CAPT, CAPT)
     sent.append(pltpu.make_async_copy(
-        out_s.at[:, lines, :], out.at[:, lines, :], out_sems.at[devices + 1]))
+        out_s.at[:, lines, :], out.at[:, lines, :], out_sems.at[2]))
     sent[-1].start()
     for copy in sent:
         copy.wait()
@@ -359,7 +352,7 @@
             pltpu.SemaphoreType.DMA((chunks, 2)),
             pltpu.SemaphoreType.DMA((d_chunks + 2,)),
             pltpu.SemaphoreType.DMA((4,)),
-            pltpu.SemaphoreType.DMA((devices + 2,)),
+            pltpu.SemaphoreType.DMA((3,)),
         ],
         compiler_params=pltpu.CompilerParams(vmem_limit_bytes=PROJECT_VMEM),
         name="project",

time: 26.5 us -> 26.4 us (level)
  no operation moved by 1% of the time
where the time goes in v29:
time: 26.4 us; the launch traced here: 26.2 us
  Pallas kernels  9.5 us (36%)
  waiting for transfers between devices  9.11 us (35%)
  starting transfers between devices  7.41 us (28%)
    all_to_all x1, waiting for transfers between devices, body(): lax.all_to_all(outgoing, 'tensor', split_axis=0, concat_axis=0, tiled=True)  9.11 us
    all_to_all x1, starting transfers between devices, body(): lax.all_to_all(outgoing, 'tensor', split_axis=0, concat_axis=0, tiled=True)  7.41 us
    pallas_call x1, Pallas kernels, body(): pl.pallas_call(functools.partial(project_kernel, dec_rows, d_chunks, chun...  5.25 us
    pallas_call x1, Pallas kernels, body(): pl.pallas_call(cached_kernel, out_shape=(jax.ShapeDtypeStruct((HD, q_rows...  3.01 us
    pallas_call x1, Pallas kernels, body(): pl.pallas_call(functools.partial(merge_kernel, features), out_shape=jax.S...  1.24 us
  transfers between devices with their start and end apart: 1, of which 1 were waited for; matrix products, arithmetic and copies ran while one was open for 0% of the time, Pallas kernels for 11%

profile of v29, /device:TPU:0, one launch (start us, length us, event | category | flops | bytes accessed | tf_op | source)
XLA Modules:
  0.0 26.2 jit_solution(7954972143544198441)
XLA Ops:
  0.0 0.0 copy-start
  0.0 0.0 copy-start.1
  0.0 0.0 copy-start.2
  0.0 0.0 copy-start.3
  0.0 0.0 copy-start.4
  0.0 0.0 copy-start.5
  0.0 0.0 copy-start.6
  0.0 5.3 %project.1 = bf16[16,96,128]{2,1,0:T(8,128)(2,1)} custom-call(s32[16]{0:T(128)} %tenant_h.1, s32[8]{0:T(128)} %table_h.1, s32[16]{0:T(128)} %counts.1, s32[16]{0:T(128)} %placement.1, bf16[160,8192]{1,0:T(8,128)(2,1)} %hidden.1, bf16[128,8192]{1,0:T(8,128)(2,1)} %weight.1, bf16[512,16,128]{2,1,0:T(8,128)(2,1)} %down.1, bf16[16,64,128]{2,1,0:T(8,128)(2,1)} %bitcast.18), custom_call_target="tpu_custom_call" | custom-call | tf_op jit(solution)/shard_map/project/pallas_call | solution.py:332
  5.3 7.4 %all-to-all-start = ((bf16[16,96,128]{2,1,0:T(8,128)(2,1)}), bf16[16,96,128]{2,1,0:T(8,128)(2,1)S(1)}, u32[]{:S(2)}, u32[]{:S(2)}) async-start(bf16[16,96,128]{2,1,0:T(8,128)(2,1)} %project.1), calls=%async_computation | async-start | bytes 786432 | tf_op jit(solution)/shard_map/all_to_all | solution.py:368
  12.7 0.0 copy-done
  12.7 0.0 copy-done.1
  12.7 0.0 copy-done.2
  12.7 0.0 copy-done.3
  12.8 0.0 copy-done.4
  12.8 0.0 copy-done.5
  12.8 0.0 copy-done.6
  12.8 3.0 %cached.1 = (bf16[128,512]{1,0:T(8,128)(2,1)S(1)}, f32[128,512]{1,0:T(8,128)S(1)}, f32[8,512]{1,0:T(8,128)S(1)}, f32[8,512]{1,0:T(8,128)S(1)}, f32[128,512]{1,0:T(8,128)S(1)}) custom-call(s32[2]{0:T(128)S(1)} %copy-done.5, s32[16]{0:T(128)S(1)} %copy-done.3, s32[16]{0:T(128)S(1)} %copy-done.6, s32[16]{0:T(128)S(1)} %copy-done.4, ...), custom_call_target="tpu_custom_call" | custom-call | tf_op jit(solution)/shard_map/cached/pallas_call | solution.py:377
  15.8 9.1 %all-to-all-done.box = bf16[16,96,128]{2,1,0:T(8,128)(2,1)S(1)} async-done(((bf16[16,96,128]{2,1,0:T(8,128)(2,1)}), bf16[16,96,128]{2,1,0:T(8,128)(2,1)S(1)}, u32[]{:S(2)}, u32[]{:S(2)}) %all-to-all-start) | async-done | bytes 393248 | tf_op jit(solution)/shard_map/all_to_all | solution.py:368
  24.9 1.2 %merge.1 = bf16[512,128]{1,0:T(8,128)(2,1)} custom-call(bf16[16,96,128]{2,1,0:T(8,128)(2,1)S(1)} %all-to-all-done.box, bf16[128,512]{1,0:T(8,128)(2,1)S(1)} %get-tuple-element.10.query_t, f32[128,512]{1,0:T(8,128)S(1)} %get-tuple-element.11.acc_t, f32[8,512]{1,0:T(8,128)S(1)} %get-tuple-element.12.top_t, f32[8,512]{1,0:T(8,128)S(1)} %get-tuple-element.13.total_t, ...), custom_call_target="tpu_custom_call" | custom-call | tf_op jit(solution)/shard_map/merge/pallas_call | solution.py:395
Async XLA Ops:
  0.0 12.7 %copy-start = (bf16[2,128,2048]{2,1,0:T(8,128)(2,1)S(1)}, bf16[2,128,2048]{2,1,0:T(8,128)(2,1)}, u32[]{:S(2)}) copy-start(bf16[2,128,2048]{2,1,0:T(8,128)(2,1)} %cache.1) | copy-start | bytes 3145732
  0.0 12.7 %copy-start.1 = (bf16[4,2,8192]{2,1,0:T(2,128)(2,1)S(1)}, bf16[4,2,8192]{2,1,0:T(2,128)(2,1)}, u32[]{:S(2)}) copy-start(bf16[4,2,8192]{2,1,0:T(2,128)(2,1)} %param.24) | copy-start | bytes 393220
  0.0 12.7 %copy-start.2 = (bf16[4,2,2048]{2,1,0:T(2,128)(2,1)S(1)}, bf16[4,2,2048]{2,1,0:T(2,128)(2,1)}, u32[]{:S(2)}) copy-start(bf16[4,2,2048]{2,1,0:T(2,128)(2,1)} %param.25) | copy-start | bytes 98308
  0.0 12.7 %copy-start.3 = (s32[16]{0:T(128)S(1)}, s32[16]{0:T(128)}, u32[]{:S(2)}) copy-start(s32[16]{0:T(128)} %counts.1) | copy-start | bytes 196
  0.0 12.7 %copy-start.4 = (s32[16]{0:T(128)S(1)}, s32[16]{0:T(128)}, u32[]{:S(2)}) copy-start(s32[16]{0:T(128)} %placement.1) | copy-start | bytes 196
  0.0 12.8 %copy-start.5 = (s32[2]{0:T(128)S(1)}, s32[2]{0:T(128)}, u32[]{:S(2)}) copy-start(s32[2]{0:T(128)} %lengths.1) | copy-start | bytes 28
  0.0 12.8 %copy-start.6 = (s32[16]{0:T(128)S(1)}, s32[16]{0:T(128)}, u32[]{:S(2)}) copy-start(s32[16]{0:T(128)} %last.1) | copy-start | bytes 196
  5.3 19.6 %all-to-all-start = ((bf16[16,96,128]{2,1,0:T(8,128)(2,1)}), bf16[16,96,128]{2,1,0:T(8,128)(2,1)S(1)}, u32[]{:S(2)}, u32[]{:S(2)}) async-start(bf16[16,96,128]{2,1,0:T(8,128)(2,1)} %project.1), calls=%async_computation | async-start | bytes 786432 | tf_op jit(solution)/shard_map/all_to_all | solution.py:368

commit v30 on v25

--- a/solution.py
+++ b/solution.py
@@ -73,9 +73,6 @@
     up_copy = pltpu.make_async_copy(up, u_s, d_sems.at[d_chunks + 1])
     for copy in [d_copy(c) for c in range(d_chunks)] + [my_copy, up_copy]:
         copy.start()
-    for c in range(chunks):
-        h_copies[c].start()
-        w_copies[c].start()
 
     int_copies[0].wait()
     rows = lax.broadcasted_iota(jnp.int32, (tenants * 16, 16 * pages), 0)
@@ -89,7 +86,6 @@
     blocks = d_step // 16
 
     def select(c, carry):
-        d_copy(c).wait()
         for b in range(0, blocks, 2):
             block = jnp.concatenate(
                 [
@@ -105,7 +101,13 @@
                 )
         return carry
 
-    lax.fori_loop(0, d_chunks, select, 0)
+    for c in range(d_chunks):
+        d_copy(c).wait()
+        if c == 0:
+            for h_copy, w_copy in zip(h_copies, w_copies):
+                h_copy.start()
+                w_copy.start()
+        select(c, 0)
     for copy in int_copies[1:]:
         copy.wait()
     for dest in range(devices):

time: 26.4 us -> 26.7 us (1.011)
  no operation moved by 1% of the time
where the time goes in v30:
time: 26.7 us; the launch traced here: 26.5 us
  Pallas kernels  9.82 us (37%)
  waiting for transfers between devices  9.11 us (34%)
  starting transfers between devices  7.4 us (28%)
    all_to_all x1, waiting for transfers between devices, body(): lax.all_to_all(outgoing, 'tensor', split_axis=0, concat_axis=0, tiled=True)  9.11 us
    all_to_all x1, starting transfers between devices, body(): lax.all_to_all(outgoing, 'tensor', split_axis=0, concat_axis=0, tiled=True)  7.4 us
    pallas_call x1, Pallas kernels, body(): pl.pallas_call(functools.partial(project_kernel, dec_rows, d_chunks, chun...  5.57 us
    pallas_call x1, Pallas kernels, body(): pl.pallas_call(cached_kernel, out_shape=(jax.ShapeDtypeStruct((HD, q_rows...  3.01 us
    pallas_call x1, Pallas kernels, body(): pl.pallas_call(functools.partial(merge_kernel, features), out_shape=jax.S...  1.24 us
  transfers between devices with their start and end apart: 1, of which 1 were waited for; matrix products, arithmetic and copies ran while one was open for 0% of the time, Pallas kernels for 11%

profile of v30, /device:TPU:0, one launch (start us, length us, event | category | flops | bytes accessed | tf_op | source)
XLA Modules:
  0.0 26.5 jit_solution(15673756516762339048)
XLA Ops:
  0.0 0.0 copy-start
  0.0 0.0 copy-start.1
  0.0 0.0 copy-start.2
  0.0 0.0 copy-start.3
  0.0 0.0 copy-start.4
  0.0 0.0 copy-start.5
  0.0 0.0 copy-start.6
  0.0 5.6 %project.1 = bf16[16,96,128]{2,1,0:T(8,128)(2,1)} custom-call(s32[16]{0:T(128)} %tenant_h.1, s32[8]{0:T(128)} %table_h.1, s32[16]{0:T(128)} %counts.1, s32[16]{0:T(128)} %placement.1, bf16[160,8192]{1,0:T(8,128)(2,1)} %hidden.1, bf16[128,8192]{1,0:T(8,128)(2,1)} %weight.1, bf16[512,16,128]{2,1,0:T(8,128)(2,1)} %down.1, bf16[16,64,128]{2,1,0:T(8,128)(2,1)} %bitcast.18), custom_call_target="tpu_custom_call" | custom-call | tf_op jit(solution)/shard_map/project/pallas_call | solution.py:323
  5.6 7.4 %all-to-all-start = ((bf16[16,96,128]{2,1,0:T(8,128)(2,1)}), bf16[16,96,128]{2,1,0:T(8,128)(2,1)S(1)}, u32[]{:S(2)}, u32[]{:S(2)}) async-start(bf16[16,96,128]{2,1,0:T(8,128)(2,1)} %project.1), calls=%async_computation | async-start | bytes 786432 | tf_op jit(solution)/shard_map/all_to_all | solution.py:357
  13.0 0.0 copy-done
  13.0 0.0 copy-done.1
  13.0 0.0 copy-done.2
  13.1 0.0 copy-done.3
  13.1 0.0 copy-done.4
  13.1 0.0 copy-done.5
  13.1 0.0 copy-done.6
  13.1 3.0 %cached.1 = (bf16[128,512]{1,0:T(8,128)(2,1)S(1)}, f32[128,512]{1,0:T(8,128)S(1)}, f32[8,512]{1,0:T(8,128)S(1)}, f32[8,512]{1,0:T(8,128)S(1)}, f32[128,512]{1,0:T(8,128)S(1)}) custom-call(s32[2]{0:T(128)S(1)} %copy-done.5, s32[16]{0:T(128)S(1)} %copy-done.3, s32[16]{0:T(128)S(1)} %copy-done.6, s32[16]{0:T(128)S(1)} %copy-done.4, ...), custom_call_target="tpu_custom_call" | custom-call | tf_op jit(solution)/shard_map/cached/pallas_call | solution.py:366
  16.1 9.1 %all-to-all-done.box = bf16[16,96,128]{2,1,0:T(8,128)(2,1)S(1)} async-done(((bf16[16,96,128]{2,1,0:T(8,128)(2,1)}), bf16[16,96,128]{2,1,0:T(8,128)(2,1)S(1)}, u32[]{:S(2)}, u32[]{:S(2)}) %all-to-all-start) | async-done | bytes 393248 | tf_op jit(solution)/shard_map/all_to_all | solution.py:357
  25.2 1.2 %merge.1 = bf16[512,128]{1,0:T(8,128)(2,1)} custom-call(bf16[16,96,128]{2,1,0:T(8,128)(2,1)S(1)} %all-to-all-done.box, bf16[128,512]{1,0:T(8,128)(2,1)S(1)} %get-tuple-element.10.query_t, f32[128,512]{1,0:T(8,128)S(1)} %get-tuple-element.11.acc_t, f32[8,512]{1,0:T(8,128)S(1)} %get-tuple-element.12.top_t, f32[8,512]{1,0:T(8,128)S(1)} %get-tuple-element.13.total_t, ...), custom_call_target="tpu_custom_call" | custom-call | tf_op jit(solution)/shard_map/merge/pallas_call | solution.py:384
Async XLA Ops:
  0.0 13.0 %copy-start = (bf16[2,128,2048]{2,1,0:T(8,128)(2,1)S(1)}, bf16[2,128,2048]{2,1,0:T(8,128)(2,1)}, u32[]{:S(2)}) copy-start(bf16[2,128,2048]{2,1,0:T(8,128)(2,1)} %cache.1) | copy-start | bytes 3145732
  0.0 13.0 %copy-start.1 = (bf16[4,2,8192]{2,1,0:T(2,128)(2,1)S(1)}, bf16[4,2,8192]{2,1,0:T(2,128)(2,1)}, u32[]{:S(2)}) copy-start(bf16[4,2,8192]{2,1,0:T(2,128)(2,1)} %param.24) | copy-start | bytes 393220
  0.0 13.0 %copy-start.2 = (bf16[4,2,2048]{2,1,0:T(2,128)(2,1)S(1)}, bf16[4,2,2048]{2,1,0:T(2,128)(2,1)}, u32[]{:S(2)}) copy-start(bf16[4,2,2048]{2,1,0:T(2,128)(2,1)} %param.25) | copy-start | bytes 98308
  0.0 13.0 %copy-start.3 = (s32[16]{0:T(128)S(1)}, s32[16]{0:T(128)}, u32[]{:S(2)}) copy-start(s32[16]{0:T(128)} %counts.1) | copy-start | bytes 196
  0.0 13.1 %copy-start.4 = (s32[16]{0:T(128)S(1)}, s32[16]{0:T(128)}, u32[]{:S(2)}) copy-start(s32[16]{0:T(128)} %placement.1) | copy-start | bytes 196
  0.0 13.1 %copy-start.5 = (s32[2]{0:T(128)S(1)}, s32[2]{0:T(128)}, u32[]{:S(2)}) copy-start(s32[2]{0:T(128)} %lengths.1) | copy-start | bytes 28
  0.0 13.1 %copy-start.6 = (s32[16]{0:T(128)S(1)}, s32[16]{0:T(128)}, u32[]{:S(2)}) copy-start(s32[16]{0:T(128)} %last.1) | copy-start | bytes 196
  5.6 19.6 %all-to-all-start = ((bf16[16,96,128]{2,1,0:T(8,128)(2,1)}), bf16[16,96,128]{2,1,0:T(8,128)(2,1)S(1)}, u32[]{:S(2)}, u32[]{:S(2)}) async-start(bf16[16,96,128]{2,1,0:T(8,128)(2,1)} %project.1), calls=%async_computation | async-start | bytes 786432 | tf_op jit(solution)/shard_map/all_to_all | solution.py:357

commit v31 on v29

--- a/solution.py
+++ b/solution.py
@@ -123,6 +123,8 @@
     whole = features == HD
     sent = []
     my_copy.wait()
+    h_copies[0].wait()
+    w_copies[0].wait()
     mine = mine_s[...]
     for k in range(0, tenants, 2):
         pair = min(2, tenants - k)
@@ -149,8 +151,9 @@
 
     total = jnp.zeros((tokens, features), jnp.float32)
     for c in range(chunks):
-        h_copies[c].wait()
-        w_copies[c].wait()
+        if c > 0:
+            h_copies[c].wait()
+            w_copies[c].wait()
         total = total + lax.dot_general(h_s[c], w_s[c], NT, preferred_element_type=jnp.float32)
     base_s[tokens:] = jnp.zeros((BLK, HD), jnp.float32)
     if features < HD:

time: 26.4 us -> 26.4 us (level)
  no operation moved by 1% of the time
where the time goes in v31:
time: 26.4 us; the launch traced here: 26.2 us
  Pallas kernels  9.5 us (36%)
  waiting for transfers between devices  9.11 us (35%)
  starting transfers between devices  7.41 us (28%)
    all_to_all x1, waiting for transfers between devices, body(): lax.all_to_all(outgoing, 'tensor', split_axis=0, concat_axis=0, tiled=True)  9.11 us
    all_to_all x1, starting transfers between devices, body(): lax.all_to_all(outgoing, 'tensor', split_axis=0, concat_axis=0, tiled=True)  7.41 us
    pallas_call x1, Pallas kernels, body(): pl.pallas_call(functools.partial(project_kernel, dec_rows, d_chunks, chun...  5.25 us
    pallas_call x1, Pallas kernels, body(): pl.pallas_call(cached_kernel, out_shape=(jax.ShapeDtypeStruct((HD, q_rows...  3.01 us
    pallas_call x1, Pallas kernels, body(): pl.pallas_call(functools.partial(merge_kernel, features), out_shape=jax.S...  1.24 us
  transfers between devices with their start and end apart: 1, of which 1 were waited for; matrix products, arithmetic and copies ran while one was open for 0% of the time, Pallas kernels for 11%

profile of v31, /device:TPU:0, one launch (start us, length us, event | category | flops | bytes accessed | tf_op | source)
XLA Modules:
  0.0 26.2 jit_solution(15552355032745323553)
XLA Ops:
  0.0 0.0 copy-start
  0.0 0.0 copy-start.1
  0.0 0.0 copy-start.2
  0.0 0.0 copy-start.3
  0.0 0.0 copy-start.4
  0.0 0.0 copy-start.5
  0.0 0.0 copy-start.6
  0.0 5.3 %project.1 = bf16[16,96,128]{2,1,0:T(8,128)(2,1)} custom-call(s32[16]{0:T(128)} %tenant_h.1, s32[8]{0:T(128)} %table_h.1, s32[16]{0:T(128)} %counts.1, s32[16]{0:T(128)} %placement.1, bf16[160,8192]{1,0:T(8,128)(2,1)} %hidden.1, bf16[128,8192]{1,0:T(8,128)(2,1)} %weight.1, bf16[512,16,128]{2,1,0:T(8,128)(2,1)} %down.1, bf16[16,64,128]{2,1,0:T(8,128)(2,1)} %bitcast.18), custom_call_target="tpu_custom_call" | custom-call | tf_op jit(solution)/shard_map/project/pallas_call | solution.py:335
  5.3 7.4 %all-to-all-start = ((bf16[16,96,128]{2,1,0:T(8,128)(2,1)}), bf16[16,96,128]{2,1,0:T(8,128)(2,1)S(1)}, u32[]{:S(2)}, u32[]{:S(2)}) async-start(bf16[16,96,128]{2,1,0:T(8,128)(2,1)} %project.1), calls=%async_computation | async-start | bytes 786432 | tf_op jit(solution)/shard_map/all_to_all | solution.py:371
  12.7 0.0 copy-done
  12.7 0.0 copy-done.1
  12.7 0.0 copy-done.2
  12.7 0.0 copy-done.3
  12.8 0.0 copy-done.4
  12.8 0.0 copy-done.5
  12.8 0.0 copy-done.6
  12.8 3.0 %cached.1 = (bf16[128,512]{1,0:T(8,128)(2,1)S(1)}, f32[128,512]{1,0:T(8,128)S(1)}, f32[8,512]{1,0:T(8,128)S(1)}, f32[8,512]{1,0:T(8,128)S(1)}, f32[128,512]{1,0:T(8,128)S(1)}) custom-call(s32[2]{0:T(128)S(1)} %copy-done.5, s32[16]{0:T(128)S(1)} %copy-done.3, s32[16]{0:T(128)S(1)} %copy-done.6, s32[16]{0:T(128)S(1)} %copy-done.4, ...), custom_call_target="tpu_custom_call" | custom-call | tf_op jit(solution)/shard_map/cached/pallas_call | solution.py:380
  15.8 9.1 %all-to-all-done.box = bf16[16,96,128]{2,1,0:T(8,128)(2,1)S(1)} async-done(((bf16[16,96,128]{2,1,0:T(8,128)(2,1)}), bf16[16,96,128]{2,1,0:T(8,128)(2,1)S(1)}, u32[]{:S(2)}, u32[]{:S(2)}) %all-to-all-start) | async-done | bytes 393248 | tf_op jit(solution)/shard_map/all_to_all | solution.py:371
  24.9 1.2 %merge.1 = bf16[512,128]{1,0:T(8,128)(2,1)} custom-call(bf16[16,96,128]{2,1,0:T(8,128)(2,1)S(1)} %all-to-all-done.box, bf16[128,512]{1,0:T(8,128)(2,1)S(1)} %get-tuple-element.10.query_t, f32[128,512]{1,0:T(8,128)S(1)} %get-tuple-element.11.acc_t, f32[8,512]{1,0:T(8,128)S(1)} %get-tuple-element.12.top_t, f32[8,512]{1,0:T(8,128)S(1)} %get-tuple-element.13.total_t, ...), custom_call_target="tpu_custom_call" | custom-call | tf_op jit(solution)/shard_map/merge/pallas_call | solution.py:398
Async XLA Ops:
  0.0 12.7 %copy-start = (bf16[2,128,2048]{2,1,0:T(8,128)(2,1)S(1)}, bf16[2,128,2048]{2,1,0:T(8,128)(2,1)}, u32[]{:S(2)}) copy-start(bf16[2,128,2048]{2,1,0:T(8,128)(2,1)} %cache.1) | copy-start | bytes 3145732
  0.0 12.7 %copy-start.1 = (bf16[4,2,8192]{2,1,0:T(2,128)(2,1)S(1)}, bf16[4,2,8192]{2,1,0:T(2,128)(2,1)}, u32[]{:S(2)}) copy-start(bf16[4,2,8192]{2,1,0:T(2,128)(2,1)} %param.24) | copy-start | bytes 393220
  0.0 12.7 %copy-start.2 = (bf16[4,2,2048]{2,1,0:T(2,128)(2,1)S(1)}, bf16[4,2,2048]{2,1,0:T(2,128)(2,1)}, u32[]{:S(2)}) copy-start(bf16[4,2,2048]{2,1,0:T(2,128)(2,1)} %param.25) | copy-start | bytes 98308
  0.0 12.7 %copy-start.3 = (s32[16]{0:T(128)S(1)}, s32[16]{0:T(128)}, u32[]{:S(2)}) copy-start(s32[16]{0:T(128)} %counts.1) | copy-start | bytes 196
  0.0 12.7 %copy-start.4 = (s32[16]{0:T(128)S(1)}, s32[16]{0:T(128)}, u32[]{:S(2)}) copy-start(s32[16]{0:T(128)} %placement.1) | copy-start | bytes 196
  0.0 12.8 %copy-start.5 = (s32[2]{0:T(128)S(1)}, s32[2]{0:T(128)}, u32[]{:S(2)}) copy-start(s32[2]{0:T(128)} %lengths.1) | copy-start | bytes 28
  0.0 12.8 %copy-start.6 = (s32[16]{0:T(128)S(1)}, s32[16]{0:T(128)}, u32[]{:S(2)}) copy-start(s32[16]{0:T(128)} %last.1) | copy-start | bytes 196
  5.3 19.6 %all-to-all-start = ((bf16[16,96,128]{2,1,0:T(8,128)(2,1)}), bf16[16,96,128]{2,1,0:T(8,128)(2,1)S(1)}, u32[]{:S(2)}, u32[]{:S(2)}) async-start(bf16[16,96,128]{2,1,0:T(8,128)(2,1)} %project.1), calls=%async_computation | async-start | bytes 786432 | tf_op jit(solution)/shard_map/all_to_all | solution.py:371

commit v32 on v25

--- a/solution.py
+++ b/solution.py
@@ -71,11 +71,12 @@
         hidden.at[:, pl.ds(pl.multiple_of(me * local, 128), local)], mine_s, d_sems.at[d_chunks]
     )
     up_copy = pltpu.make_async_copy(up, u_s, d_sems.at[d_chunks + 1])
-    for copy in [d_copy(c) for c in range(d_chunks)] + [my_copy, up_copy]:
+    for copy in [d_copy(c) for c in range(d_chunks)] + [my_copy]:
         copy.start()
     for c in range(chunks):
         h_copies[c].start()
         w_copies[c].start()
+    up_copy.start()
 
     int_copies[0].wait()
     rows = lax.broadcasted_iota(jnp.int32, (tenants * 16, 16 * pages), 0)

time: 26.4 us -> 26.4 us (level)
  no operation moved by 1% of the time
where the time goes in v32:
time: 26.4 us; the launch traced here: 26.2 us
  Pallas kernels  9.57 us (36%)
  waiting for transfers between devices  9.11 us (35%)
  starting transfers between devices  7.41 us (28%)
    all_to_all x1, waiting for transfers between devices, body(): lax.all_to_all(outgoing, 'tensor', split_axis=0, concat_axis=0, tiled=True)  9.11 us
    all_to_all x1, starting transfers between devices, body(): lax.all_to_all(outgoing, 'tensor', split_axis=0, concat_axis=0, tiled=True)  7.41 us
    pallas_call x1, Pallas kernels, body(): pl.pallas_call(functools.partial(project_kernel, dec_rows, d_chunks, chun...  5.32 us
    pallas_call x1, Pallas kernels, body(): pl.pallas_call(cached_kernel, out_shape=(jax.ShapeDtypeStruct((HD, q_rows...  3.01 us
    pallas_call x1, Pallas kernels, body(): pl.pallas_call(functools.partial(merge_kernel, features), out_shape=jax.S...  1.24 us
  transfers between devices with their start and end apart: 1, of which 1 were waited for; matrix products, arithmetic and copies ran while one was open for 0% of the time, Pallas kernels for 11%

profile of v32, /device:TPU:0, one launch (start us, length us, event | category | flops | bytes accessed | tf_op | source)
XLA Modules:
  0.0 26.2 jit_solution(12593140852863267725)
XLA Ops:
  0.0 0.0 copy-start
  0.0 0.0 copy-start.1
  0.0 0.0 copy-start.2
  0.0 0.0 copy-start.3
  0.0 0.0 copy-start.4
  0.0 0.0 copy-start.5
  0.0 0.0 copy-start.6
  0.0 5.3 %project.1 = bf16[16,96,128]{2,1,0:T(8,128)(2,1)} custom-call(s32[16]{0:T(128)} %tenant_h.1, s32[8]{0:T(128)} %table_h.1, s32[16]{0:T(128)} %counts.1, s32[16]{0:T(128)} %placement.1, bf16[160,8192]{1,0:T(8,128)(2,1)} %hidden.1, bf16[128,8192]{1,0:T(8,128)(2,1)} %weight.1, bf16[512,16,128]{2,1,0:T(8,128)(2,1)} %down.1, bf16[16,64,128]{2,1,0:T(8,128)(2,1)} %bitcast.18), custom_call_target="tpu_custom_call" | custom-call | tf_op jit(solution)/shard_map/project/pallas_call | solution.py:322
  5.4 7.4 %all-to-all-start = ((bf16[16,96,128]{2,1,0:T(8,128)(2,1)}), bf16[16,96,128]{2,1,0:T(8,128)(2,1)S(1)}, u32[]{:S(2)}, u32[]{:S(2)}) async-start(bf16[16,96,128]{2,1,0:T(8,128)(2,1)} %project.1), calls=%async_computation | async-start | bytes 786432 | tf_op jit(solution)/shard_map/all_to_all | solution.py:356
  12.8 0.0 copy-done
  12.8 0.0 copy-done.1
  12.8 0.0 copy-done.2
  12.8 0.0 copy-done.3
  12.8 0.0 copy-done.4
  12.8 0.0 copy-done.5
  12.8 0.0 copy-done.6
  12.9 3.0 %cached.1 = (bf16[128,512]{1,0:T(8,128)(2,1)S(1)}, f32[128,512]{1,0:T(8,128)S(1)}, f32[8,512]{1,0:T(8,128)S(1)}, f32[8,512]{1,0:T(8,128)S(1)}, f32[128,512]{1,0:T(8,128)S(1)}) custom-call(s32[2]{0:T(128)S(1)} %copy-done.5, s32[16]{0:T(128)S(1)} %copy-done.3, s32[16]{0:T(128)S(1)} %copy-done.6, s32[16]{0:T(128)S(1)} %copy-done.4, ...), custom_call_target="tpu_custom_call" | custom-call | tf_op jit(solution)/shard_map/cached/pallas_call | solution.py:365
  15.9 9.1 %all-to-all-done.box = bf16[16,96,128]{2,1,0:T(8,128)(2,1)S(1)} async-done(((bf16[16,96,128]{2,1,0:T(8,128)(2,1)}), bf16[16,96,128]{2,1,0:T(8,128)(2,1)S(1)}, u32[]{:S(2)}, u32[]{:S(2)}) %all-to-all-start) | async-done | bytes 393248 | tf_op jit(solution)/shard_map/all_to_all | solution.py:356
  25.0 1.2 %merge.1 = bf16[512,128]{1,0:T(8,128)(2,1)} custom-call(bf16[16,96,128]{2,1,0:T(8,128)(2,1)S(1)} %all-to-all-done.box, bf16[128,512]{1,0:T(8,128)(2,1)S(1)} %get-tuple-element.10.query_t, f32[128,512]{1,0:T(8,128)S(1)} %get-tuple-element.11.acc_t, f32[8,512]{1,0:T(8,128)S(1)} %get-tuple-element.12.top_t, f32[8,512]{1,0:T(8,128)S(1)} %get-tuple-element.13.total_t, ...), custom_call_target="tpu_custom_call" | custom-call | tf_op jit(solution)/shard_map/merge/pallas_call | solution.py:383
Async XLA Ops:
  0.0 12.8 %copy-start = (bf16[2,128,2048]{2,1,0:T(8,128)(2,1)S(1)}, bf16[2,128,2048]{2,1,0:T(8,128)(2,1)}, u32[]{:S(2)}) copy-start(bf16[2,128,2048]{2,1,0:T(8,128)(2,1)} %cache.1) | copy-start | bytes 3145732
  0.0 12.8 %copy-start.1 = (bf16[4,2,8192]{2,1,0:T(2,128)(2,1)S(1)}, bf16[4,2,8192]{2,1,0:T(2,128)(2,1)}, u32[]{:S(2)}) copy-start(bf16[4,2,8192]{2,1,0:T(2,128)(2,1)} %param.24) | copy-start | bytes 393220
  0.0 12.8 %copy-start.2 = (bf16[4,2,2048]{2,1,0:T(2,128)(2,1)S(1)}, bf16[4,2,2048]{2,1,0:T(2,128)(2,1)}, u32[]{:S(2)}) copy-start(bf16[4,2,2048]{2,1,0:T(2,128)(2,1)} %param.25) | copy-start | bytes 98308
  0.0 12.8 %copy-start.3 = (s32[16]{0:T(128)S(1)}, s32[16]{0:T(128)}, u32[]{:S(2)}) copy-start(s32[16]{0:T(128)} %counts.1) | copy-start | bytes 196
  0.0 12.8 %copy-start.4 = (s32[16]{0:T(128)S(1)}, s32[16]{0:T(128)}, u32[]{:S(2)}) copy-start(s32[16]{0:T(128)} %placement.1) | copy-start | bytes 196
  0.0 12.8 %copy-start.5 = (s32[2]{0:T(128)S(1)}, s32[2]{0:T(128)}, u32[]{:S(2)}) copy-start(s32[2]{0:T(128)} %lengths.1) | copy-start | bytes 28
  0.0 12.8 %copy-start.6 = (s32[16]{0:T(128)S(1)}, s32[16]{0:T(128)}, u32[]{:S(2)}) copy-start(s32[16]{0:T(128)} %last.1) | copy-start | bytes 196
  5.4 19.6 %all-to-all-start = ((bf16[16,96,128]{2,1,0:T(8,128)(2,1)}), bf16[16,96,128]{2,1,0:T(8,128)(2,1)S(1)}, u32[]{:S(2)}, u32[]{:S(2)}) async-start(bf16[16,96,128]{2,1,0:T(8,128)(2,1)} %project.1), calls=%async_computation | async-start | bytes 786432 | tf_op jit(solution)/shard_map/all_to_all | solution.py:356
